TPU v7x, 256 devices: a whole 4x4x8 slice. The times are simulated.
256 devices in a mesh: gx: 16 (over x_lo, z), gy: 16 (over y, x_hi, core).
Axes of the slice: x: 4 (x_hi: 2, x_lo: 2; x = x_hi * 2 + x_lo), y: 4, z: 8, core: 2. Of those that a mesh axis runs over, the one named last changes fastest.
Arguments:
- grad_out: bfloat16 [2048, 36864], P('gx', 'gy'), may hold values from -6 to 6
- inputs: bfloat16 [2048, 9216], P('gy', 'gx'), may hold values from -6 to 6
- weight: bfloat16 [9216, 36864], P('gx', 'gy'), may hold values from -0.0625 to 0.0625
Outputs:
- grad_in: bfloat16 [2048, 9216], P('gy', 'gx')
- grad_weight: float32 [9216, 36864], P('gx', 'gy')
All inputs are finite; a program needn't handle non-finite values.
Results may differ from a plain program's by a relative error of at most 0.001.
Values may be sent and summed in bfloat16 or wider, within the bound.
No kernel may reach another device: no remote copies, remote signals or barrier semaphores. Data moves between devices by JAX's collectives and lax.ppermute only.
A program may use at most 64 MiB of HBM per device.

v0:
```python
import jax
import jax.numpy as jnp
from jax import lax
from jax.sharding import PartitionSpec as P


def body(grad_out, inputs, weight):
    all_inputs = lax.all_gather(inputs, "gy", axis=0, tiled=True)
    total_rows = all_inputs.shape[0]
    all_grad = lax.all_gather(grad_out, "gx", axis=0, tiled=True)
    grad_in = lax.psum_scatter(
        lax.dot_general(
            all_grad, weight, (((1,), (1,)), ((), ())), preferred_element_type=jnp.float32
        ),
        "gy",
        scatter_dimension=0,
        tiled=True,
    ).astype(jnp.bfloat16)
    summed = lax.dot_general(
        all_inputs, all_grad, (((0,), (0,)), ((), ())), preferred_element_type=jnp.float32
    )
    grad_weight = summed * (1.0 / total_rows)
    return (grad_in, grad_weight)


def solution(mesh):
    return jax.shard_map(
        body,
        mesh=mesh,
        in_specs=(P("gx", "gy"), P("gy", "gx"), P("gx", "gy")),
        out_specs=(P("gy", "gx"), P("gx", "gy")),
        check_vma=False,
    )
```

profile of v0, /device:TPU:8, one launch (start us, length us, event | category | flops | bytes accessed | tf_op | source)
XLA Modules:
  0.0 278.5 jit_solution(6152370677707951547)
XLA Ops:
  7.2 0.0 copy-start
  7.2 0.0 all-gather.3.cloned.1.call-start
  7.2 0.7 all-gather.3.cloned.1.call-update
  7.9 0.0 all-gather.5.cloned.1.call-start
  8.0 0.7 all-gather.5.cloned.1.call-update
  8.7 0.0 reduce-scatter.2.cloned.1.call-start
  8.7 115.5 %all-gather.3.cloned.1.call-done = bf16[2048,2304]{1,0:T(8,128)(2,1)} async-done(((bf16[128,2304]{1,0:T(8,128)(2,1)}), bf16[2048,2304]{1,0:T(8,128)(2,1)}) %all-gather.3.cloned.1.call-update) | async-done | bytes 9437200 | tf_op jit(solution)/shard_map/all_gather | solution.py:10
  124.2 0.0 copy-done
  124.2 9.6 %fusion = f32[2048,576]{0,1:T(8,128)} fusion(bf16[2048,2304]{1,0:T(8,128)(2,1)} %all-gather.3.cloned.1.call-done, bf16[576,2304]{1,0:T(8,128)(2,1)S(1)} %copy-done), kind=kOutput, calls=%fused_computation.1 | convolution fusion | flops 5435817984 | bytes 16809984 | tf_op jit(solution)/shard_map/dot_general | solution.py:12
  133.9 0.0 reduce-scatter.2.cloned.1.call-update
  133.9 42.6 %all-gather.5.cloned.1.call-done = bf16[2048,576]{0,1:T(8,128)(2,1)} async-done(((bf16[128,576]{0,1:T(8,128)(2,1)}), bf16[2048,576]{0,1:T(8,128)(2,1)}) %all-gather.5.cloned.1.call-update) | async-done | bytes 2359312 | tf_op jit(solution)/shard_map/all_gather | solution.py:8
  176.5 11.4 %convolution_multiply_fusion = f32[576,2304]{1,0:T(8,128)} fusion(bf16[2048,576]{0,1:T(8,128)(2,1)} %all-gather.5.cloned.1.call-done, bf16[2048,2304]{1,0:T(8,128)(2,1)} %all-gather.3.cloned.1.call-done), kind=kOutput, calls=%fused_computation | convolution fusion | flops 5437145088 | bytes 17104896 | tf_op jit(solution)/shard_map/dot_general | solution.py:19
  187.9 82.5 %reduce-scatter.2.cloned.1.call-done = f32[128,576]{0,1:T(8,128)} async-done(((f32[2048,576]{0,1:T(8,128)}), f32[128,576]{0,1:T(8,128)}) %reduce-scatter.2.cloned.1.call-update) | async-done | bytes 294928 | tf_op jit(solution)/shard_map/reduce_scatter | solution.py:11
  270.4 1.6 convert_element_type.3
Async XLA Ops:
  7.2 117.1 %copy-start = (bf16[576,2304]{1,0:T(8,128)(2,1)S(1)}, bf16[576,2304]{1,0:T(8,128)(2,1)}, u32[]{:S(2)}) copy-start(bf16[576,2304]{1,0:T(8,128)(2,1)} %param.5) | copy-start | bytes 7962628
  7.2 117.1 %all-gather.3.cloned.1.call-start = ((), (), s32[]{:S(2)}) async-start(), calls=%async_computation.1 | async-start | bytes 10027008 | tf_op jit(solution)/shard_map/all_gather | solution.py:10
  7.9 168.6 %all-gather.5.cloned.1.call-start = ((), (), s32[]{:S(2)}) async-start(), calls=%async_computation.3 | async-start | bytes 2506752 | tf_op jit(solution)/shard_map/all_gather | solution.py:8
  8.7 261.7 %reduce-scatter.2.cloned.1.call-start = ((), (), s32[]{:S(2)}) async-start(), calls=%async_computation.2 | async-start | bytes 5013504 | tf_op jit(solution)/shard_map/reduce_scatter | solution.py:11
Sparse Core Ops, SparseCore 0:
  9.8 114.3 all-gather.2
  126.9 49.5 all-gather.4
  180.9 89.4 reduce-scatter.1
where the time goes:
time: 279 us
  waiting for transfers between devices  242 us (87%)
  matrix products  21 us (8%)
  between operations  13.8 us (5%)
    all_gather x1, waiting for transfers between devices, body(): all_grad = lax.all_gather(grad_out, 'gx', axis=0, tiled=True)  116 us
    reduce_scatter x1, waiting for transfers between devices, body(): lax.psum_scatter(lax.dot_general(all_grad, weight, (((1,), (1,)), ((), ()...  82.5 us
    all_gather x1, waiting for transfers between devices, body(): all_inputs = lax.all_gather(inputs, 'gy', axis=0, tiled=True)  42.6 us
    dot_general x1, matrix products, body(): lax.dot_general(all_inputs, all_grad, (((0,), (0,)), ((), ())), preferred...  11.4 us
    dot_general x1, matrix products, body(): lax.dot_general(all_grad, weight, (((1,), (1,)), ((), ())), preferred_ele...  9.62 us
  transfers between devices with their start and end apart: 3, of which 3 were waited for; matrix products, arithmetic and copies ran while one was open for 8% of the time, Pallas kernels for 0%

commit v1 on v0

v1 whole, which is shorter than its diff:
```python
import functools

import jax
import jax.numpy as jnp
from jax import lax
from jax.experimental import pallas as pl
from jax.experimental.pallas import tpu as pltpu
from jax.sharding import PartitionSpec as P

XL, Z = 2, 8
Y, XH, C = 4, 2, 2
VMEM_LIMIT = 48 << 20


def gx_pairs(dxl, dz):
    return [
        (xl * Z + z, (xl + dxl) % XL * Z + (z + dz) % Z)
        for xl in range(XL)
        for z in range(Z)
    ]


def gy_pairs(dy, dxh, dc):
    return [
        (
            (y * XH + xh) * C + c,
            ((y + dy) % Y * XH + (xh + dxh) % XH) * C + (c + dc) % C,
        )
        for y in range(Y)
        for xh in range(XH)
        for c in range(C)
    ]


def up(t):
    return lax.ppermute(t, "gx", gx_pairs(0, 1))


def down(t):
    return lax.ppermute(t, "gx", gx_pairs(0, -1))


def across(t):
    return lax.ppermute(t, "gx", gx_pairs(1, 0))


def in_y(t, dy):
    return lax.ppermute(t, "gy", gy_pairs(dy, 0, 0))


def in_xh(t):
    return lax.ppermute(t, "gy", gy_pairs(0, 1, 0))


def in_core(t):
    return lax.ppermute(t, "gy", gy_pairs(0, 0, 1))


def partial_kernel(n, depth, rows, s_ref, w_ref, *refs):
    shards, (keep_ref, send_ref) = refs[:n], refs[n:]
    c = s_ref[0]
    values = jnp.concatenate([r[...] for r in shards], axis=0)
    for out_ref, half in ((send_ref, 1 - c), (keep_ref, c)):
        w = w_ref[pl.ds(pl.multiple_of(half * depth, depth), depth), :]
        part = lax.dot_general(
            w, values, (((1,), (1,)), ((), ())), preferred_element_type=jnp.float32
        )
        for k in range(n):
            out_ref[s_ref[1 + k]] = part[:, k * rows : (k + 1) * rows]


def partial_sums(scalars, weight, shards):
    n = len(shards)
    rows, cols = shards[0].shape
    width = weight.shape[0]
    depth = width // 2
    out = jax.ShapeDtypeStruct((n, depth, rows), jnp.float32)
    whole = pl.BlockSpec(memory_space=pltpu.VMEM)
    return pl.pallas_call(
        functools.partial(partial_kernel, n, depth, rows),
        out_shape=(out, out),
        in_specs=[pl.BlockSpec(memory_space=pltpu.SMEM)] + [whole] * (1 + n),
        out_specs=(whole, whole),
        compiler_params=pltpu.CompilerParams(vmem_limit_bytes=VMEM_LIMIT),
        cost_estimate=pl.CostEstimate(
            flops=2 * width * cols * rows * n,
            bytes_accessed=2 * cols * (width + n * rows) + 4 * n * width * rows,
            transcendentals=0,
        ),
        name="partial_sums",
    )(scalars, weight, *shards)


def weight_kernel(n, rows, scale, s_ref, mine_ref, other_ref, *refs):
    shards, out_ref, x_ref, g_ref = refs[:n], refs[n], refs[n + 1], refs[n + 2]
    count = mine_ref.shape[0]

    @pl.when(pl.program_id(0) == 0)
    def _():
        for k in range(n):
            at = s_ref[k]
            here = slice(k * rows, (k + 1) * rows)

            @pl.when(at < count)
            def _():
                x_ref[:, here] = mine_ref[jnp.minimum(at, count - 1)]

            @pl.when(at >= count)
            def _():
                x_ref[:, here] = other_ref[jnp.maximum(at - count, 0)]

    for k in range(n):
        g_ref[k * rows : (k + 1) * rows, :] = shards[k][...]
    out_ref[...] = (
        jnp.dot(x_ref[...], g_ref[...], preferred_element_type=jnp.float32) * scale
    )


def weight_sums(scalars, mine, other, shards, scale):
    n = len(shards)
    rows, cols = shards[0].shape
    width = mine.shape[1]
    tile = 384
    whole = pl.BlockSpec(memory_space=pltpu.VMEM)
    return pl.pallas_call(
        functools.partial(weight_kernel, n, rows, scale),
        out_shape=jax.ShapeDtypeStruct((width, cols), jnp.float32),
        grid=(cols // tile,),
        in_specs=[pl.BlockSpec(memory_space=pltpu.SMEM), whole, whole]
        + [pl.BlockSpec((rows, tile), lambda i: (0, i))] * n,
        out_specs=pl.BlockSpec((width, tile), lambda i: (0, i)),
        scratch_shapes=[
            pltpu.VMEM((width, n * rows), jnp.bfloat16),
            pltpu.VMEM((n * rows, tile), jnp.bfloat16),
        ],
        compiler_params=pltpu.CompilerParams(vmem_limit_bytes=VMEM_LIMIT),
        cost_estimate=pl.CostEstimate(
            flops=2 * width * cols * rows * n,
            bytes_accessed=2 * rows * n * (cols + width) + 4 * width * cols,
            transcendentals=0,
        ),
        name="weight_sums",
    )(scalars, mine, other, *shards)


def body(grad_out, inputs, weight):
    ix, iy = lax.axis_index("gx"), lax.axis_index("gy")
    xl, z = ix // Z, ix % Z
    y, xh, c = iy // (XH * C), iy // C % XH, iy % C
    rows = grad_out.shape[0]

    g = grad_out
    u1, d1, gx = up(g), down(g), across(g)
    u2, d2, ux1 = up(u1), down(d1), across(u1)
    u3, d3, dx2 = up(u2), down(d2), across(d2)
    u4, dx3, ux2 = up(u3), down(dx2), across(u2)
    ux3, dx4, dx1 = up(ux2), down(dx3), across(d1)

    mine = inputs.T[None]
    both = jnp.concatenate([mine, in_xh(mine)])
    column = jnp.concatenate([both, in_y(both, 1), in_y(both, -1), in_y(both, 2)])
    other = in_core(column)

    def where(shard):
        side, dz = shard
        x = xl if side == 0 else 1 - xl
        at = (z + dz) % Z
        return x * 2 + at // 4, at // 2 % 2, at % 2

    def of_inputs(shard):
        ty, txh, tc = where(shard)
        dy = (ty - y) % Y
        n = jnp.where(dy == 3, 1, jnp.where(dy == 0, 0, dy + 1))
        k = 2 * n + (txh != xh)
        return jnp.where(tc == c, k, k + column.shape[0])

    sets = [
        [((0, 0), g), ((1, 0), gx), ((0, 4), u4), ((1, 4), dx4)],
        [((0, 1), d1), ((1, 1), dx1), ((0, -3), u3), ((1, -3), ux3)],
        [((0, 2), d2), ((1, 2), dx2), ((0, -2), u2), ((1, -2), ux2)],
        [((0, 3), d3), ((1, 3), dx3), ((0, -1), u1), ((1, -1), ux1)],
    ]
    totals = {}
    for group in ((2, 3), (0, 1)):
        slots, shards = [c], []
        for place, k in enumerate(group):
            for shard, value in sets[k]:
                slots.append((where(shard)[0] - y) % Y * len(group) + place)
                shards.append(value)
        keep, send = partial_sums(jnp.stack(slots), weight, shards)
        got = in_core(send)
        m = len(group)

        def to(r):
            return keep[r * m : (r + 1) * m] + got[r * m : (r + 1) * m]

        total = to(0) + in_y(to(1), 1) + in_y(to(3), -1) + in_y(to(2), 2)
        for place, k in enumerate(group):
            totals[k] = total[place]

    order = [s for group in sets for s in group]
    grad_weight = weight_sums(
        jnp.stack([of_inputs(s) for s, _ in order]),
        column,
        other,
        [v for _, v in order],
        1.0 / (Y * XH * C * rows),
    )

    even, odd = z // 2 % 2 == xh, (z + 1) // 2 % 2 == xh

    def pick(p, a, b):
        return jnp.where(p, a, b)

    got = in_xh(
        jnp.stack(
            [pick(even, totals[2], totals[0]), pick(odd, totals[3], totals[1])]
        )
    )
    e = (pick(even, totals[0], totals[2]) + got[0]).astype(jnp.bfloat16)
    o = (pick(odd, totals[1], totals[3]) + got[1]).astype(jnp.bfloat16)
    first = z % 2 == c
    own = pick(first, e, o)
    back = in_core(pick(first, o, e))
    grad_in = jnp.concatenate([pick(c == 0, own, back), pick(c == 0, back, own)])
    return grad_in.T, grad_weight


def solution(mesh):
    return jax.shard_map(
        body,
        mesh=mesh,
        in_specs=(P("gx", "gy"), P("gy", "gx"), P("gx", "gy")),
        out_specs=(P("gy", "gx"), P("gx", "gy")),
        check_vma=False,
    )
```

time: 279 us -> 188 us (0.67)
  waiting for transfers between devices: 242 us -> 91.9 us
  starting transfers between devices: 0.11 us -> 46.8 us
  Pallas kernels: 0 us -> 25.7 us
  matrix products: 21 us -> 0 us
  local copies, waits for them, and re-layouts: 0.01 us -> 14 us
  between operations: 13.8 us -> 1.12 us
  other arithmetic: 1.64 us -> 7.33 us
    all_gather x2 -> x0, waiting for transfers between devices: 158 us -> none  [the longest x1 116 us: body(): all_grad = lax.all_gather(grad_out, 'gx', axis=0, tiled=True)]
    ppermute x0 -> x30, waiting for transfers between devices: none -> 91.9 us  [the longest x5 31.2 us: across(): return lax.ppermute(t, 'gx', gx_pairs(1, 0))]
    reduce_scatter x1 -> x0, waiting for transfers between devices: 82.5 us -> none  [body(): lax.psum_scatter(lax.dot_general(all_grad, weight, (((1,), (1,)), ((), ()...]
    ppermute x0 -> x30, starting transfers between devices: none -> 46.8 us  [the longest x5 19.1 us: down(): return lax.ppermute(t, 'gx', gx_pairs(0, -1))]
    pallas_call x0 -> x3, Pallas kernels: none -> 25.7 us  [the longest x1 13.2 us: weight_sums(): pl.pallas_call(functools.partial(weight_kernel, n, rows, scale), out_shap...]
    dot_general x2 -> x0, matrix products: 21 us -> none  [the longest x1 11.4 us: body(): lax.dot_general(all_inputs, all_grad, (((0,), (0,)), ((), ())), preferred...]
    unnamed x2 -> x36, local copies, waits for them, and re-layouts: 0.01 us -> 13 us
    add x0 -> x4, other arithmetic: none -> 4.52 us  [the longest x2 2.46 us: to(): return keep[r * m:(r + 1) * m] + got[r * m:(r + 1) * m]]
  transfers between devices with their start and end apart: 3 -> 30, of which waited for: 3 -> 16; matrix products, arithmetic and copies ran while one was open for 8% -> 7% of each run, Pallas kernels for 0% -> 14%
where the time goes in v1:
time: 188 us; the launch traced here: 187 us
  waiting for transfers between devices  91.9 us (49%)
  starting transfers between devices  46.8 us (25%)
  Pallas kernels  25.7 us (14%)
  local copies, waits for them, and re-layouts  14 us (7%)
  other arithmetic  7.33 us (4%)
    ppermute x5, waiting for transfers between devices, across(): return lax.ppermute(t, 'gx', gx_pairs(1, 0))  31.2 us
    ppermute x5, waiting for transfers between devices, down(): return lax.ppermute(t, 'gx', gx_pairs(0, -1))  24.6 us
    ppermute x9, waiting for transfers between devices, in_y(): return lax.ppermute(t, 'gy', gy_pairs(dy, 0, 0))  20.7 us
    ppermute x5, starting transfers between devices, down(): return lax.ppermute(t, 'gx', gx_pairs(0, -1))  19.1 us
    ppermute x9, starting transfers between devices, in_y(): return lax.ppermute(t, 'gy', gy_pairs(dy, 0, 0))  14.4 us
    pallas_call x1, Pallas kernels, weight_sums(): pl.pallas_call(functools.partial(weight_kernel, n, rows, scale), out_shap...  13.2 us
    unnamed x36, local copies, waits for them, and re-layouts  13 us
    pallas_call x2, Pallas kernels, partial_sums(): pl.pallas_call(functools.partial(partial_kernel, n, depth, rows), out_sha...  12.5 us
  transfers between devices with their start and end apart: 30, of which 16 were waited for; matrix products, arithmetic and copies ran while one was open for 7% of the time, Pallas kernels for 14%

profile of v1, /device:TPU:8, one launch (start us, length us, event | category | flops | bytes accessed | tf_op | source)
XLA Modules:
  0.0 186.8 jit_solution(11806949367357411457)
XLA Ops:
  0.6 5.9 %collective-permute-start.5 = (bf16[128,2304]{1,0:T(8,128)(2,1)}, bf16[128,2304]{1,0:T(8,128)(2,1)S(1)}, u32[]{:S(2)}, u32[]{:S(2)}) collective-permute-start(bf16[128,2304]{1,0:T(8,128)(2,1)} %refs_0_.3), channel_id=1, source_target_pairs={{0,112},{16,0},{32,16},{48,32},{64,48},{80,64},{96,80},{112,96},{1... | collective-permute-start | bytes 1769480 | tf_op jit(solution)/shard_map/ppermute | solution.py:40
  6.6 12.9 %collective-permute-done.5.refs_4_ = bf16[128,2304]{1,0:T(8,128)(2,1)S(1)} collective-permute-done((bf16[128,2304]{1,0:T(8,128)(2,1)}, bf16[128,2304]{1,0:T(8,128)(2,1)S(1)}, u32[]{:S(2)}, u32[]{:S(2)}) %collective-permute-start.5) | collective-permute-done | bytes 589856 | tf_op jit(solution)/shard_map/ppermute | solution.py:40
  19.5 3.6 %collective-permute-start.6 = (bf16[128,2304]{1,0:T(8,128)(2,1)S(1)}, bf16[128,2304]{1,0:T(8,128)(2,1)S(1)}, u32[]{:S(2)}, u32[]{:S(2)}) collective-permute-start(bf16[128,2304]{1,0:T(8,128)(2,1)S(1)} %collective-permute-done.5.refs_4_), channel_id=1, source_target_pairs={{0,112},{16,0},{32,16},{48,32},{64,48},{80,64},{96,80},{112,96},{1... | collective-permute-start | bytes 1769480 | tf_op jit(solution)/shard_map/ppermute | solution.py:40
  23.1 11.7 %collective-permute-done.6.refs_0_.refs_8_ = bf16[128,2304]{1,0:T(8,128)(2,1)S(1)} collective-permute-done((bf16[128,2304]{1,0:T(8,128)(2,1)S(1)}, bf16[128,2304]{1,0:T(8,128)(2,1)S(1)}, u32[]{:S(2)}, u32[]{:S(2)}) %collective-permute-start.6) | collective-permute-done | bytes 589856 | tf_op jit(solution)/shard_map/ppermute | solution.py:40
  38.2 1.5 collective-permute-start.11
  40.5 3.2 %collective-permute-start.17 = (bf16[128,2304]{1,0:T(8,128)(2,1)S(1)}, bf16[128,2304]{1,0:T(8,128)(2,1)S(1)}, u32[]{:S(2)}, u32[]{:S(2)}) collective-permute-start(bf16[128,2304]{1,0:T(8,128)(2,1)S(1)} %collective-permute-done.6.refs_0_.refs_8_), channel_id=1, source_target_pairs={{0,112},{16,0},{32,16},{48,32},{64,48},{80,64},{96,80},{112,96},{1... | collective-permute-start | bytes 1769480 | tf_op jit(solution)/shard_map/ppermute | solution.py:40
  43.7 7.3 %collective-permute-done.7.refs_1_.refs_9_ = bf16[128,2304]{1,0:T(8,128)(2,1)S(1)} collective-permute-done((bf16[128,2304]{1,0:T(8,128)(2,1)S(1)}, bf16[128,2304]{1,0:T(8,128)(2,1)S(1)}, u32[]{:S(2)}, u32[]{:S(2)}) %collective-permute-start.7) | collective-permute-done | bytes 589856 | tf_op jit(solution)/shard_map/ppermute | solution.py:44
  51.0 3.7 %collective-permute-start.8 = (bf16[128,2304]{1,0:T(8,128)(2,1)S(1)}, bf16[128,2304]{1,0:T(8,128)(2,1)}, u32[]{:S(2)}, u32[]{:S(2)}) collective-permute-start(bf16[128,2304]{1,0:T(8,128)(2,1)S(1)} %collective-permute-done.7.refs_1_.refs_9_), channel_id=1, source_target_pairs={{0,112},{16,0},{32,16},{48,32},{64,48},{80,64},{96,80},{112,96},{1... | collective-permute-start | bytes 1769480 | tf_op jit(solution)/shard_map/ppermute | solution.py:40
  55.6 8.1 %collective-permute-done.18.refs_7_.refs_15_ = bf16[128,2304]{1,0:T(8,128)(2,1)S(1)} collective-permute-done((bf16[128,2304]{1,0:T(8,128)(2,1)S(1)}, bf16[128,2304]{1,0:T(8,128)(2,1)S(1)}, u32[]{:S(2)}, u32[]{:S(2)}) %collective-permute-start.18) | collective-permute-done | bytes 589856 | tf_op jit(solution)/shard_map/ppermute | solution.py:44
  66.0 10.4 %collective-permute-done.11.refs_3_.refs_11_ = bf16[128,2304]{1,0:T(8,128)(2,1)} collective-permute-done((bf16[128,2304]{1,0:T(8,128)(2,1)S(1)}, bf16[128,2304]{1,0:T(8,128)(2,1)}, u32[]{:S(2)}, u32[]{:S(2)}) %collective-permute-start.11) | collective-permute-done | bytes 589856 | tf_op jit(solution)/shard_map/ppermute | solution.py:44
  79.8 2.7 %collective-permute-start.9 = (bf16[128,2304]{1,0:T(8,128)(2,1)}, bf16[128,2304]{1,0:T(8,128)(2,1)}, u32[]{:S(2)}, u32[]{:S(2)}) collective-permute-start(bf16[128,2304]{1,0:T(8,128)(2,1)} %collective-permute-done.8.refs_5_.refs_13_), channel_id=1, source_target_pairs={{0,112},{16,0},{32,16},{48,32},{64,48},{80,64},{96,80},{112,96},{1... | collective-permute-start | bytes 1769480 | tf_op jit(solution)/shard_map/ppermute | solution.py:40
  86.8 5.9 %partial_sums.3 = (f32[8,288,128]{2,1,0:T(8,128)S(1)}, f32[8,288,128]{2,1,0:T(8,128)}) custom-call(s32[9]{0:T(128)S(1)} %stack.132.s_ref, bf16[576,2304]{1,0:T(8,128)(2,1)} %w_ref.3, bf16[128,2304]{1,0:T(8,128)(2,1)S(1)} %collective-permute-done.6.refs_0_.refs_8_, bf16[128,2304]{1,0:T(8,128)(2,1)S(1)} %copy-done.7, bf16[128,2304]{1,0:T(8,128)(2,1)S(1)} %copy-done.5, ...), custom_call_target="tpu_custom_call" | custom-call | flops 2717908992 | bytes 9732096 | tf_op jit(solution)/shard_map/partial_sums/pallas_call | solution.py:79
  93.3 5.5 %collective-permute-done.10.refs_5_ = bf16[128,2304]{1,0:T(8,128)(2,1)} collective-permute-done((bf16[128,2304]{1,0:T(8,128)(2,1)S(1)}, bf16[128,2304]{1,0:T(8,128)(2,1)}, u32[]{:S(2)}, u32[]{:S(2)}) %collective-permute-start.10) | collective-permute-done | bytes 589856 | tf_op jit(solution)/shard_map/ppermute | solution.py:44
  98.7 3.2 %collective-permute-done.4.refs_2_ = bf16[128,2304]{1,0:T(8,128)(2,1)} collective-permute-done((bf16[128,2304]{1,0:T(8,128)(2,1)}, bf16[128,2304]{1,0:T(8,128)(2,1)}, u32[]{:S(2)}, u32[]{:S(2)}) %collective-permute-start.4) | collective-permute-done | bytes 589856 | tf_op jit(solution)/shard_map/ppermute | solution.py:36
  101.9 6.6 %partial_sums.2 = (f32[8,288,128]{2,1,0:T(8,128)S(1)}, f32[8,288,128]{2,1,0:T(8,128)}) custom-call(s32[9]{0:T(128)S(1)} %stack.123.s_ref, bf16[576,2304]{1,0:T(8,128)(2,1)} %w_ref.3, bf16[128,2304]{1,0:T(8,128)(2,1)S(1)} %copy-done, bf16[128,2304]{1,0:T(8,128)(2,1)} %collective-permute-done.refs_1_, bf16[128,2304]{1,0:T(8,128)(2,1)} %collective-permute-done.4.refs_2_, ...), custom_call_target="tpu_custom_call" | custom-call | flops 2717908992 | bytes 9732096 | tf_op jit(solution)/shard_map/partial_sums/pallas_call | solution.py:79
  108.5 2.7 %collective-permute-start.25 = (bf16[1,576,128]{2,1,0:T(8,128)(2,1)}, bf16[1,576,128]{2,1,0:T(8,128)(2,1)}, u32[]{:S(2)}, u32[]{:S(2)}) collective-permute-start(bf16[1,576,128]{2,1,0:T(8,128)(2,1)} %bitcast.37), channel_id=1, source_target_pairs={{0,2},{1,3},{2,0},{3,1},{4,6},{5,7},{6,4},{7,5},{8,10},{9,11},{10,... | collective-permute-start | bytes 442376 | tf_op jit(solution)/shard_map/ppermute | solution.py:52
  111.2 5.3 %collective-permute-done.25 = bf16[1,576,128]{2,1,0:T(8,128)(2,1)} collective-permute-done((bf16[1,576,128]{2,1,0:T(8,128)(2,1)}, bf16[1,576,128]{2,1,0:T(8,128)(2,1)}, u32[]{:S(2)}, u32[]{:S(2)}) %collective-permute-start.25) | collective-permute-done | bytes 147488 | tf_op jit(solution)/shard_map/ppermute | solution.py:52
  117.6 1.7 collective-permute-start.26
  119.3 1.6 constant_dynamic-update-slice_fusion.4
  121.3 2.3 %collective-permute-start.28 = (bf16[2,576,128]{2,1,0:T(8,128)(2,1)S(1)}, bf16[2,576,128]{2,1,0:T(8,128)(2,1)S(1)}, u32[]{:S(2)}, u32[]{:S(2)}) collective-permute-start(bf16[2,576,128]{2,1,0:T(8,128)(2,1)S(1)} %pad_maximum_fusion.1), channel_id=1, source_target_pairs={{0,8},{1,9},{2,10},{3,11},{4,12},{5,13},{6,14},{7,15},{8,0},{9,1},... | collective-permute-start | bytes 884744 | tf_op jit(solution)/shard_map/ppermute | solution.py:48
  123.6 1.6 constant_dynamic-update-slice_fusion.3
  125.2 2.4 %collective-permute-done.26 = bf16[2,576,128]{2,1,0:T(8,128)(2,1)S(1)} collective-permute-done((bf16[2,576,128]{2,1,0:T(8,128)(2,1)S(1)}, bf16[2,576,128]{2,1,0:T(8,128)(2,1)S(1)}, u32[]{:S(2)}, u32[]{:S(2)}) %collective-permute-start.26) | collective-permute-done | bytes 294944 | tf_op jit(solution)/shard_map/ppermute | solution.py:48
  129.6 5.5 %collective-permute-start.20 = (f32[2,288,128]{2,1,0:T(8,128)S(1)}, f32[2,288,128]{2,1,0:T(8,128)S(1)}, u32[]{:S(2)}, u32[]{:S(2)}) collective-permute-start(f32[2,288,128]{2,1,0:T(8,128)S(1)} %get-tuple-element.13), channel_id=1, source_target_pairs={{0,4},{1,5},{2,6},{3,7},{4,8},{5,9},{6,10},{7,11},{8,12},{9,13},{1... | collective-permute-start | bytes 884744 | tf_op jit(solution)/shard_map/ppermute | solution.py:48
  135.8 1.5 collective-permute-start.22
  138.6 2.7 %collective-permute-start.14 = (f32[2,288,128]{2,1,0:T(8,128)S(1)}, f32[2,288,128]{2,1,0:T(8,128)S(1)}, u32[]{:S(2)}, u32[]{:S(2)}) collective-permute-start(f32[2,288,128]{2,1,0:T(8,128)S(1)} %get-tuple-element.16), channel_id=1, source_target_pairs={{0,4},{1,5},{2,6},{3,7},{4,8},{5,9},{6,10},{7,11},{8,12},{9,13},{1... | collective-permute-start | bytes 884744 | tf_op jit(solution)/shard_map/ppermute | solution.py:48
  141.5 6.1 %collective-permute-done.20 = f32[2,288,128]{2,1,0:T(8,128)S(1)} collective-permute-done((f32[2,288,128]{2,1,0:T(8,128)S(1)}, f32[2,288,128]{2,1,0:T(8,128)S(1)}, u32[]{:S(2)}, u32[]{:S(2)}) %collective-permute-start.20) | collective-permute-done | bytes 294944 | tf_op jit(solution)/shard_map/ppermute | solution.py:48
  148.4 3.6 %collective-permute-done.21 = f32[2,288,128]{2,1,0:T(8,128)S(1)} collective-permute-done((f32[2,288,128]{2,1,0:T(8,128)S(1)}, f32[2,288,128]{2,1,0:T(8,128)S(1)}, u32[]{:S(2)}, u32[]{:S(2)}) %collective-permute-start.21) | collective-permute-done | bytes 294944 | tf_op jit(solution)/shard_map/ppermute | solution.py:48
  154.1 3.6 %collective-permute-done.15 = f32[2,288,128]{2,1,0:T(8,128)S(1)} collective-permute-done((f32[2,288,128]{2,1,0:T(8,128)S(1)}, f32[2,288,128]{2,1,0:T(8,128)S(1)}, u32[]{:S(2)}, u32[]{:S(2)}) %collective-permute-start.15) | collective-permute-done | bytes 294944 | tf_op jit(solution)/shard_map/ppermute | solution.py:48
  157.7 3.8 %collective-permute-done.16 = f32[2,288,128]{2,1,0:T(8,128)S(1)} collective-permute-done((f32[2,288,128]{2,1,0:T(8,128)S(1)}, f32[2,288,128]{2,1,0:T(8,128)S(1)}, u32[]{:S(2)}, u32[]{:S(2)}) %collective-permute-start.16) | collective-permute-done | bytes 294944 | tf_op jit(solution)/shard_map/ppermute | solution.py:48
  163.4 2.8 %collective-permute-start.23 = (f32[2,288,128]{2,1,0:T(8,128)S(1)}, f32[2,288,128]{2,1,0:T(8,128)S(1)}, u32[]{:S(2)}, u32[]{:S(2)}) collective-permute-start(f32[2,288,128]{2,1,0:T(8,128)S(1)} %pad_maximum_fusion), channel_id=1, source_target_pairs={{0,2},{1,3},{2,0},{3,1},{4,6},{5,7},{6,4},{7,5},{8,10},{9,11},{10,... | collective-permute-start | bytes 884744 | tf_op jit(solution)/shard_map/ppermute | solution.py:52
  166.3 5.4 %collective-permute-done.23 = f32[2,288,128]{2,1,0:T(8,128)S(1)} collective-permute-done((f32[2,288,128]{2,1,0:T(8,128)S(1)}, f32[2,288,128]{2,1,0:T(8,128)S(1)}, u32[]{:S(2)}, u32[]{:S(2)}) %collective-permute-start.23) | collective-permute-done | bytes 294944 | tf_op jit(solution)/shard_map/ppermute | solution.py:52
  172.9 13.2 %weight_sums.1 = f32[576,2304]{1,0:T(8,128)} custom-call(s32[16]{0:T(128)S(1)} %stack.150.s_ref, bf16[8,576,128]{2,1,0:T(8,128)(2,1)} %constant_dynamic-update-slice_fusion.mine_ref, bf16[8,576,128]{2,1,0:T(8,128)(2,1)} %collective-permute-done.29.other_ref, bf16[128,2304]{1,0:T(8,128)(2,1)S(1)} %copy-done, bf16[128,2304]{1,0:T(8,128)(2,1)} %collective-permute-done.refs_1_, ...), custom_call_target="tpu_custom_call" | custom-call | flops 5435817984 | bytes 17104896 | tf_op jit(solution)/shard_map/weight_sums/pallas_call | solution.py:125
  (81 shorter events, 27.6 us)
Async XLA Ops:
  0.6 18.8 %collective-permute-start.5 = (bf16[128,2304]{1,0:T(8,128)(2,1)}, bf16[128,2304]{1,0:T(8,128)(2,1)S(1)}, u32[]{:S(2)}, u32[]{:S(2)}) collective-permute-start(bf16[128,2304]{1,0:T(8,128)(2,1)} %refs_0_.3), channel_id=1, source_target_pairs={{0,112},{16,0},{32,16},{48,32},{64,48},{80,64},{96,80},{112,96},{1... | collective-permute-start | bytes 1769480 | tf_op jit(solution)/shard_map/ppermute | solution.py:40
  6.6 16.5 %collective-permute-start.1 = (bf16[128,2304]{1,0:T(8,128)(2,1)}, bf16[128,2304]{1,0:T(8,128)(2,1)S(1)}, u32[]{:S(2)}, u32[]{:S(2)}) collective-permute-start(bf16[128,2304]{1,0:T(8,128)(2,1)} %refs_0_.3), channel_id=1, source_target_pairs={{0,16},{16,32},{32,48},{48,64},{64,80},{80,96},{96,112},{112,0},{1... | collective-permute-start | bytes 1769480 | tf_op jit(solution)/shard_map/ppermute | solution.py:36
  19.5 15.3 %collective-permute-start.6 = (bf16[128,2304]{1,0:T(8,128)(2,1)S(1)}, bf16[128,2304]{1,0:T(8,128)(2,1)S(1)}, u32[]{:S(2)}, u32[]{:S(2)}) collective-permute-start(bf16[128,2304]{1,0:T(8,128)(2,1)S(1)} %collective-permute-done.5.refs_4_), channel_id=1, source_target_pairs={{0,112},{16,0},{32,16},{48,32},{64,48},{80,64},{96,80},{112,96},{1... | collective-permute-start | bytes 1769480 | tf_op jit(solution)/shard_map/ppermute | solution.py:40
  23.1 69.7 %copy-start.1 = (bf16[128,2304]{1,0:T(8,128)(2,1)}, bf16[128,2304]{1,0:T(8,128)(2,1)S(1)}, u32[]{:S(2)}) copy-start(bf16[128,2304]{1,0:T(8,128)(2,1)S(1)} %collective-permute-done.1.refs_6_.refs_14_) | copy-start | bytes 1769476
  23.1 15.1 %collective-permute-start.2 = (bf16[128,2304]{1,0:T(8,128)(2,1)S(1)}, bf16[128,2304]{1,0:T(8,128)(2,1)S(1)}, u32[]{:S(2)}, u32[]{:S(2)}) collective-permute-start(bf16[128,2304]{1,0:T(8,128)(2,1)S(1)} %collective-permute-done.1.refs_6_.refs_14_), channel_id=1, source_target_pairs={{0,16},{16,32},{32,48},{48,64},{64,80},{80,96},{96,112},{112,0},{1... | collective-permute-start | bytes 1769480 | tf_op jit(solution)/shard_map/ppermute | solution.py:36
  34.8 58.0 %copy-start.2 = (bf16[128,2304]{1,0:T(8,128)(2,1)}, bf16[128,2304]{1,0:T(8,128)(2,1)S(1)}, u32[]{:S(2)}) copy-start(bf16[128,2304]{1,0:T(8,128)(2,1)S(1)} %collective-permute-done.6.refs_0_.refs_8_) | copy-start | bytes 1769476
  34.8 16.3 %collective-permute-start.7 = (bf16[128,2304]{1,0:T(8,128)(2,1)S(1)}, bf16[128,2304]{1,0:T(8,128)(2,1)S(1)}, u32[]{:S(2)}, u32[]{:S(2)}) collective-permute-start(bf16[128,2304]{1,0:T(8,128)(2,1)S(1)} %collective-permute-done.6.refs_0_.refs_8_), channel_id=1, source_target_pairs={{0,128},{16,144},{32,160},{48,176},{64,192},{80,208},{96,224},{112... | collective-permute-start | bytes 1769480 | tf_op jit(solution)/shard_map/ppermute | solution.py:44
  36.3 27.4 %collective-permute-start.18 = (bf16[128,2304]{1,0:T(8,128)(2,1)S(1)}, bf16[128,2304]{1,0:T(8,128)(2,1)S(1)}, u32[]{:S(2)}, u32[]{:S(2)}) collective-permute-start(bf16[128,2304]{1,0:T(8,128)(2,1)S(1)} %collective-permute-done.1.refs_6_.refs_14_), channel_id=1, source_target_pairs={{0,128},{16,144},{32,160},{48,176},{64,192},{80,208},{96,224},{112... | collective-permute-start | bytes 1769480 | tf_op jit(solution)/shard_map/ppermute | solution.py:44
  38.2 38.2 %collective-permute-start.11 = (bf16[128,2304]{1,0:T(8,128)(2,1)S(1)}, bf16[128,2304]{1,0:T(8,128)(2,1)}, u32[]{:S(2)}, u32[]{:S(2)}) collective-permute-start(bf16[128,2304]{1,0:T(8,128)(2,1)S(1)} %collective-permute-done.2.refs_2_.refs_10_), channel_id=1, source_target_pairs={{0,128},{16,144},{32,160},{48,176},{64,192},{80,208},{96,224},{112... | collective-permute-start | bytes 1769480 | tf_op jit(solution)/shard_map/ppermute | solution.py:44
  39.7 38.2 %collective-permute-start.3 = (bf16[128,2304]{1,0:T(8,128)(2,1)S(1)}, bf16[128,2304]{1,0:T(8,128)(2,1)}, u32[]{:S(2)}, u32[]{:S(2)}) collective-permute-start(bf16[128,2304]{1,0:T(8,128)(2,1)S(1)} %collective-permute-done.2.refs_2_.refs_10_), channel_id=1, source_target_pairs={{0,16},{16,32},{32,48},{48,64},{64,80},{80,96},{96,112},{112,0},{1... | collective-permute-start | bytes 1769480 | tf_op jit(solution)/shard_map/ppermute | solution.py:36
  40.5 37.4 %collective-permute-start.17 = (bf16[128,2304]{1,0:T(8,128)(2,1)S(1)}, bf16[128,2304]{1,0:T(8,128)(2,1)S(1)}, u32[]{:S(2)}, u32[]{:S(2)}) collective-permute-start(bf16[128,2304]{1,0:T(8,128)(2,1)S(1)} %collective-permute-done.6.refs_0_.refs_8_), channel_id=1, source_target_pairs={{0,112},{16,0},{32,16},{48,32},{64,48},{80,64},{96,80},{112,96},{1... | collective-permute-start | bytes 1769480 | tf_op jit(solution)/shard_map/ppermute | solution.py:40
  51.0 28.8 %collective-permute-start.8 = (bf16[128,2304]{1,0:T(8,128)(2,1)S(1)}, bf16[128,2304]{1,0:T(8,128)(2,1)}, u32[]{:S(2)}, u32[]{:S(2)}) collective-permute-start(bf16[128,2304]{1,0:T(8,128)(2,1)S(1)} %collective-permute-done.7.refs_1_.refs_9_), channel_id=1, source_target_pairs={{0,112},{16,0},{32,16},{48,32},{64,48},{80,64},{96,80},{112,96},{1... | collective-permute-start | bytes 1769480 | tf_op jit(solution)/shard_map/ppermute | solution.py:40
  64.5 28.2 %collective-permute-start = (bf16[128,2304]{1,0:T(8,128)(2,1)}, bf16[128,2304]{1,0:T(8,128)(2,1)}, u32[]{:S(2)}, u32[]{:S(2)}) collective-permute-start(bf16[128,2304]{1,0:T(8,128)(2,1)} %refs_0_.3), channel_id=1, source_target_pairs={{0,128},{16,144},{32,160},{48,176},{64,192},{80,208},{96,224},{112... | collective-permute-start | bytes 1769480 | tf_op jit(solution)/shard_map/ppermute | solution.py:44
  76.4 22.3 %collective-permute-start.10 = (bf16[128,2304]{1,0:T(8,128)(2,1)S(1)}, bf16[128,2304]{1,0:T(8,128)(2,1)}, u32[]{:S(2)}, u32[]{:S(2)}) collective-permute-start(bf16[128,2304]{1,0:T(8,128)(2,1)S(1)} %collective-permute-done.5.refs_4_), channel_id=1, source_target_pairs={{0,128},{16,144},{32,160},{48,176},{64,192},{80,208},{96,224},{112... | collective-permute-start | bytes 1769480 | tf_op jit(solution)/shard_map/ppermute | solution.py:44
  77.9 20.8 %collective-permute-start.12 = (bf16[128,2304]{1,0:T(8,128)(2,1)}, bf16[128,2304]{1,0:T(8,128)(2,1)}, u32[]{:S(2)}, u32[]{:S(2)}) collective-permute-start(bf16[128,2304]{1,0:T(8,128)(2,1)} %collective-permute-done.11.refs_3_.refs_11_), channel_id=1, source_target_pairs={{0,16},{16,32},{32,48},{48,64},{64,80},{80,96},{96,112},{112,0},{1... | collective-permute-start | bytes 1769480 | tf_op jit(solution)/shard_map/ppermute | solution.py:36
  78.8 23.1 %collective-permute-start.4 = (bf16[128,2304]{1,0:T(8,128)(2,1)}, bf16[128,2304]{1,0:T(8,128)(2,1)}, u32[]{:S(2)}, u32[]{:S(2)}) collective-permute-start(bf16[128,2304]{1,0:T(8,128)(2,1)} %collective-permute-done.3.refs_6_), channel_id=1, source_target_pairs={{0,16},{16,32},{32,48},{48,64},{64,80},{80,96},{96,112},{112,0},{1... | collective-permute-start | bytes 1769480 | tf_op jit(solution)/shard_map/ppermute | solution.py:36
  79.8 22.1 %collective-permute-start.9 = (bf16[128,2304]{1,0:T(8,128)(2,1)}, bf16[128,2304]{1,0:T(8,128)(2,1)}, u32[]{:S(2)}, u32[]{:S(2)}) collective-permute-start(bf16[128,2304]{1,0:T(8,128)(2,1)} %collective-permute-done.8.refs_5_.refs_13_), channel_id=1, source_target_pairs={{0,112},{16,0},{32,16},{48,32},{64,48},{80,64},{96,80},{112,96},{1... | collective-permute-start | bytes 1769480 | tf_op jit(solution)/shard_map/ppermute | solution.py:40
  92.8 35.6 %collective-permute-start.19 = (f32[8,288,128]{2,1,0:T(8,128)}, f32[8,288,128]{2,1,0:T(8,128)}, u32[]{:S(2)}, u32[]{:S(2)}) collective-permute-start(f32[8,288,128]{2,1,0:T(8,128)} %get-tuple-element.9), channel_id=1, source_target_pairs={{0,1},{1,0},{2,3},{3,2},{4,5},{5,4},{6,7},{7,6},{8,9},{9,8},{10,11... | collective-permute-start | bytes 3538952 | tf_op jit(solution)/shard_map/ppermute | solution.py:56
  108.5 28.8 %collective-permute-start.13 = (f32[8,288,128]{2,1,0:T(8,128)}, f32[8,288,128]{2,1,0:T(8,128)}, u32[]{:S(2)}, u32[]{:S(2)}) collective-permute-start(f32[8,288,128]{2,1,0:T(8,128)} %get-tuple-element.7), channel_id=1, source_target_pairs={{0,1},{1,0},{2,3},{3,2},{4,5},{5,4},{6,7},{7,6},{8,9},{9,8},{10,11... | collective-permute-start | bytes 3538952 | tf_op jit(solution)/shard_map/ppermute | solution.py:56
  108.5 8.1 %collective-permute-start.25 = (bf16[1,576,128]{2,1,0:T(8,128)(2,1)}, bf16[1,576,128]{2,1,0:T(8,128)(2,1)}, u32[]{:S(2)}, u32[]{:S(2)}) collective-permute-start(bf16[1,576,128]{2,1,0:T(8,128)(2,1)} %bitcast.37), channel_id=1, source_target_pairs={{0,2},{1,3},{2,0},{3,1},{4,6},{5,7},{6,4},{7,5},{8,10},{9,11},{10,... | collective-permute-start | bytes 442376 | tf_op jit(solution)/shard_map/ppermute | solution.py:52
  117.6 10.0 %collective-permute-start.26 = (bf16[2,576,128]{2,1,0:T(8,128)(2,1)S(1)}, bf16[2,576,128]{2,1,0:T(8,128)(2,1)S(1)}, u32[]{:S(2)}, u32[]{:S(2)}) collective-permute-start(bf16[2,576,128]{2,1,0:T(8,128)(2,1)S(1)} %pad_maximum_fusion.1), channel_id=1, source_target_pairs={{0,4},{1,5},{2,6},{3,7},{4,8},{5,9},{6,10},{7,11},{8,12},{9,13},{1... | collective-permute-start | bytes 884744 | tf_op jit(solution)/shard_map/ppermute | solution.py:48
  120.8 14.2 %collective-permute-start.27 = (bf16[2,576,128]{2,1,0:T(8,128)(2,1)S(1)}, bf16[2,576,128]{2,1,0:T(8,128)(2,1)S(1)}, u32[]{:S(2)}, u32[]{:S(2)}) collective-permute-start(bf16[2,576,128]{2,1,0:T(8,128)(2,1)S(1)} %pad_maximum_fusion.1), channel_id=1, source_target_pairs={{0,12},{1,13},{2,14},{3,15},{4,0},{5,1},{6,2},{7,3},{8,4},{9,5},{1... | collective-permute-start | bytes 884744 | tf_op jit(solution)/shard_map/ppermute | solution.py:48
  121.3 20.0 %collective-permute-start.28 = (bf16[2,576,128]{2,1,0:T(8,128)(2,1)S(1)}, bf16[2,576,128]{2,1,0:T(8,128)(2,1)S(1)}, u32[]{:S(2)}, u32[]{:S(2)}) collective-permute-start(bf16[2,576,128]{2,1,0:T(8,128)(2,1)S(1)} %pad_maximum_fusion.1), channel_id=1, source_target_pairs={{0,8},{1,9},{2,10},{3,11},{4,12},{5,13},{6,14},{7,15},{8,0},{9,1},... | collective-permute-start | bytes 884744 | tf_op jit(solution)/shard_map/ppermute | solution.py:48
  129.6 18.1 %collective-permute-start.20 = (f32[2,288,128]{2,1,0:T(8,128)S(1)}, f32[2,288,128]{2,1,0:T(8,128)S(1)}, u32[]{:S(2)}, u32[]{:S(2)}) collective-permute-start(f32[2,288,128]{2,1,0:T(8,128)S(1)} %get-tuple-element.13), channel_id=1, source_target_pairs={{0,4},{1,5},{2,6},{3,7},{4,8},{5,9},{6,10},{7,11},{8,12},{9,13},{1... | collective-permute-start | bytes 884744 | tf_op jit(solution)/shard_map/ppermute | solution.py:48
  135.8 16.2 %collective-permute-start.21 = (f32[2,288,128]{2,1,0:T(8,128)S(1)}, f32[2,288,128]{2,1,0:T(8,128)S(1)}, u32[]{:S(2)}, u32[]{:S(2)}) collective-permute-start(f32[2,288,128]{2,1,0:T(8,128)S(1)} %get-tuple-element.15), channel_id=1, source_target_pairs={{0,12},{1,13},{2,14},{3,15},{4,0},{5,1},{6,2},{7,3},{8,4},{9,5},{1... | collective-permute-start | bytes 884744 | tf_op jit(solution)/shard_map/ppermute | solution.py:48
  135.8 16.2 %collective-permute-start.22 = (f32[2,288,128]{2,1,0:T(8,128)S(1)}, f32[2,288,128]{2,1,0:T(8,128)S(1)}, u32[]{:S(2)}, u32[]{:S(2)}) collective-permute-start(f32[2,288,128]{2,1,0:T(8,128)S(1)} %get-tuple-element.14), channel_id=1, source_target_pairs={{0,8},{1,9},{2,10},{3,11},{4,12},{5,13},{6,14},{7,15},{8,0},{9,1},... | collective-permute-start | bytes 884744 | tf_op jit(solution)/shard_map/ppermute | solution.py:48
  138.6 15.6 %collective-permute-start.14 = (f32[2,288,128]{2,1,0:T(8,128)S(1)}, f32[2,288,128]{2,1,0:T(8,128)S(1)}, u32[]{:S(2)}, u32[]{:S(2)}) collective-permute-start(f32[2,288,128]{2,1,0:T(8,128)S(1)} %get-tuple-element.16), channel_id=1, source_target_pairs={{0,4},{1,5},{2,6},{3,7},{4,8},{5,9},{6,10},{7,11},{8,12},{9,13},{1... | collective-permute-start | bytes 884744 | tf_op jit(solution)/shard_map/ppermute | solution.py:48
  141.3 16.5 %collective-permute-start.15 = (f32[2,288,128]{2,1,0:T(8,128)S(1)}, f32[2,288,128]{2,1,0:T(8,128)S(1)}, u32[]{:S(2)}, u32[]{:S(2)}) collective-permute-start(f32[2,288,128]{2,1,0:T(8,128)S(1)} %get-tuple-element.18), channel_id=1, source_target_pairs={{0,12},{1,13},{2,14},{3,15},{4,0},{5,1},{6,2},{7,3},{8,4},{9,5},{1... | collective-permute-start | bytes 884744 | tf_op jit(solution)/shard_map/ppermute | solution.py:48
  147.7 13.9 %collective-permute-start.16 = (f32[2,288,128]{2,1,0:T(8,128)S(1)}, f32[2,288,128]{2,1,0:T(8,128)S(1)}, u32[]{:S(2)}, u32[]{:S(2)}) collective-permute-start(f32[2,288,128]{2,1,0:T(8,128)S(1)} %get-tuple-element.17), channel_id=1, source_target_pairs={{0,8},{1,9},{2,10},{3,11},{4,12},{5,13},{6,14},{7,15},{8,0},{9,1},... | collective-permute-start | bytes 884744 | tf_op jit(solution)/shard_map/ppermute | solution.py:48
  152.0 20.8 %collective-permute-start.29 = (bf16[8,576,128]{2,1,0:T(8,128)(2,1)}, bf16[8,576,128]{2,1,0:T(8,128)(2,1)}, u32[]{:S(2)}, u32[]{:S(2)}) collective-permute-start(bf16[8,576,128]{2,1,0:T(8,128)(2,1)} %constant_dynamic-update-slice_fusion.mine_ref), channel_id=1, source_target_pairs={{0,1},{1,0},{2,3},{3,2},{4,5},{5,4},{6,7},{7,6},{8,9},{9,8},{10,11... | collective-permute-start | bytes 3538952 | tf_op jit(solution)/shard_map/ppermute | solution.py:56
  163.4 8.3 %collective-permute-start.23 = (f32[2,288,128]{2,1,0:T(8,128)S(1)}, f32[2,288,128]{2,1,0:T(8,128)S(1)}, u32[]{:S(2)}, u32[]{:S(2)}) collective-permute-start(f32[2,288,128]{2,1,0:T(8,128)S(1)} %pad_maximum_fusion), channel_id=1, source_target_pairs={{0,2},{1,3},{2,0},{3,1},{4,6},{5,7},{6,4},{7,5},{8,10},{9,11},{10,... | collective-permute-start | bytes 884744 | tf_op jit(solution)/shard_map/ppermute | solution.py:52
  172.8 13.3 %collective-permute-start.24 = (bf16[288,128]{1,0:T(8,128)(2,1)S(1)}, bf16[288,128]{1,0:T(8,128)(2,1)S(1)}, u32[]{:S(2)}, u32[]{:S(2)}) collective-permute-start(bf16[288,128]{1,0:T(8,128)(2,1)S(1)} %get-tuple-element.10), channel_id=1, source_target_pairs={{0,1},{1,0},{2,3},{3,2},{4,5},{5,4},{6,7},{7,6},{8,9},{9,8},{10,11... | collective-permute-start | bytes 221192 | tf_op jit(solution)/shard_map/ppermute | solution.py:56
  (14 other events, 60.5 us)

commit v2 on v0

v2 whole, which is shorter than its diff:
```python
import functools

import jax
import jax.numpy as jnp
from jax import lax
from jax.experimental import pallas as pl
from jax.experimental.pallas import tpu as pltpu
from jax.sharding import PartitionSpec as P

XL, Z = 2, 8
Y, XH, C = 4, 2, 2
VMEM_LIMIT = 32 << 20
TIE_LIMIT = 63 << 20


def gx_pairs(dxl, dz):
    return [
        (xl * Z + z, (xl + dxl) % XL * Z + (z + dz) % Z)
        for xl in range(XL)
        for z in range(Z)
    ]


def gy_pairs(dy, dxh, dc):
    return [
        (
            (y * XH + xh) * C + c,
            ((y + dy) % Y * XH + (xh + dxh) % XH) * C + (c + dc) % C,
        )
        for y in range(Y)
        for xh in range(XH)
        for c in range(C)
    ]


def up(t):
    return lax.ppermute(t, "gx", gx_pairs(0, 1))


def down(t):
    return lax.ppermute(t, "gx", gx_pairs(0, -1))


def across(t):
    return lax.ppermute(t, "gx", gx_pairs(1, 0))


def in_y_pair(t):
    pairs = [
        ((y * XH + xh) * C + c, ((y ^ 1) * XH + xh) * C + c)
        for y in range(Y)
        for xh in range(XH)
        for c in range(C)
    ]
    return lax.ppermute(t, "gy", pairs)


def in_y(t, dy):
    return lax.ppermute(t, "gy", gy_pairs(dy, 0, 0))


def in_xh(t):
    return lax.ppermute(t, "gy", gy_pairs(0, 1, 0))


def in_core(t):
    return lax.ppermute(t, "gy", gy_pairs(0, 0, 1))


IN_HBM = pl.BlockSpec(memory_space=pltpu.HBM)
ANYWHERE = pl.BlockSpec(memory_space=pl.ANY)
VECTOR = pl.BlockSpec(memory_space=pltpu.VMEM)
SCALAR = pl.BlockSpec(memory_space=pltpu.SMEM)


def params(limit=VMEM_LIMIT):
    return pltpu.CompilerParams(vmem_limit_bytes=limit)


def tie(values, after):
    n = len(values)
    return pl.pallas_call(
        lambda *refs: None,
        out_shape=[jax.ShapeDtypeStruct(v.shape, v.dtype) for v in values],
        in_specs=[IN_HBM] * n + [ANYWHERE] * len(after),
        out_specs=[IN_HBM] * n,
        input_output_aliases={k: k for k in range(n)},
        compiler_params=params(TIE_LIMIT),
        name="tie",
    )(*values, *after)


def partial_kernel(places, s_ref, w_any, *refs):
    n = len(places)
    pieces = refs[:n]
    keep_ref, send_ref, w_ref, g_ref, sem = refs[n:]
    rows = keep_ref.shape[2]
    w_copy = pltpu.make_async_copy(w_any, w_ref, sem.at[n])
    w_copy.start()
    copies = []
    for k in range(n):
        copy = pltpu.make_async_copy(
            pieces[k], g_ref.at[pl.ds(k * rows, rows), :], sem.at[k]
        )
        copy.start()
        copies.append(copy)
    w_copy.wait()
    for first in range(0, n, 2):
        count = min(2, n - first)
        for k in range(first, first + count):
            copies[k].wait()
        sums = lax.dot_general(
            w_ref[...],
            g_ref[first * rows : (first + count) * rows, :],
            (((1,), (1,)), ((), ())),
            preferred_element_type=jnp.float32,
        )
        for k in range(count):
            group, slot = places[first + k]
            value = sums[:, k * rows : (k + 1) * rows]

            @pl.when(s_ref[0] == 1 - group)
            def _(slot=slot, value=value):
                keep_ref[slot] = value

            @pl.when(s_ref[0] == group)
            def _(slot=slot, value=value):
                send_ref[slot] = value


def partial_sums(first, weight, groups):
    places = [(g, k) for g, shards in enumerate(groups) for k in range(len(shards))]
    shards = [s for group in groups for s in group]
    n, slots = len(shards), max(len(group) for group in groups)
    rows, cols = shards[0].shape
    width = weight.shape[0]
    out = jax.ShapeDtypeStruct((slots, width, rows), jnp.float32)
    return pl.pallas_call(
        functools.partial(partial_kernel, places),
        out_shape=(out, out),
        in_specs=[SCALAR] + [IN_HBM] * (1 + n),
        out_specs=(VECTOR, VECTOR),
        scratch_shapes=[
            pltpu.VMEM((width, cols), jnp.bfloat16),
            pltpu.VMEM((n * rows, cols), jnp.bfloat16),
            pltpu.SemaphoreType.DMA((n + 1,)),
        ],
        compiler_params=params(),
        cost_estimate=pl.CostEstimate(
            flops=2 * width * cols * rows * n,
            bytes_accessed=2 * cols * (width + n * rows) + 8 * slots * width * rows,
            transcendentals=0,
        ),
        name="partial_sums",
    )(first, weight, *shards)


def place_kernel(counts, s_ref, *refs):
    pairs, outs = refs[: 2 * len(counts)], refs[2 * len(counts) :]
    k = 0
    for group, n in enumerate(counts):
        keep_ref, got_ref = pairs[2 * group], pairs[2 * group + 1]
        for i in range(n):
            for r, out_ref in enumerate(outs):

                @pl.when(s_ref[k] == r)
                def _(keep_ref=keep_ref, got_ref=got_ref, i=i, out_ref=out_ref):
                    out_ref[...] = keep_ref[i] + got_ref[i]

            k += 1


def place(ways, groups):
    counts = [kept.shape[0] for kept, _ in groups]
    out = jax.ShapeDtypeStruct(groups[0][0].shape[1:], jnp.float32)
    return pl.pallas_call(
        functools.partial(place_kernel, counts),
        out_shape=[out] * Y,
        in_specs=[SCALAR] + [VECTOR] * (2 * len(counts)),
        out_specs=[VECTOR] * Y,
        compiler_params=params(),
        name="place",
    )(ways, *[a for pair in groups for a in pair])


def merge_kernel(s_ref, *refs):
    late, early, (keep_ref, send_ref) = refs[:Y], refs[Y : 2 * Y], refs[-2:]

    def total(parts):
        return (parts[0][...] + parts[1][...]) + (parts[2][...] + parts[3][...])

    a, b = total(late), total(early)
    here = s_ref[0] == 1
    keep_ref[...] = jnp.where(here, a, b)
    send_ref[...] = jnp.where(here, b, a)


def merge(here, late, early, after):
    out = jax.ShapeDtypeStruct(late[0].shape, jnp.float32)
    return pl.pallas_call(
        merge_kernel,
        out_shape=(out, out),
        in_specs=[SCALAR] + [VECTOR] * (2 * Y) + [ANYWHERE] * len(after),
        out_specs=(VECTOR, VECTOR),
        compiler_params=params(),
        name="merge",
    )(here, *late, *early, *after)


def weight_kernel(n, tile, scale, s_ref, mine_ref, other_ref, *refs):
    pieces, (out_ref, token_ref) = refs[:n], refs[-7:-5]
    x_ref, g_ref, o_ref, in_sem, out_sem = refs[-5:]
    count, _, rows = mine_ref.shape
    copies = []
    for k in range(n):
        copy = pltpu.make_async_copy(
            pieces[k], g_ref.at[pl.ds(k * rows, rows), :], in_sem.at[k]
        )
        copy.start()
        copies.append(copy)
    token_ref[...] = jnp.zeros_like(token_ref)
    for k in range(n):
        at = s_ref[k]
        here = slice(k * rows, (k + 1) * rows)

        @pl.when(at < count)
        def _(at=at, here=here):
            x_ref[:, here] = mine_ref[jnp.minimum(at, count - 1)]

        @pl.when(at >= count)
        def _(at=at, here=here):
            x_ref[:, here] = other_ref[jnp.maximum(at - count, 0)]

    for copy in copies:
        copy.wait()
    results = []
    for t in range(g_ref.shape[1] // tile):
        columns = slice(t * tile, (t + 1) * tile)
        product = jnp.dot(
            x_ref[...], g_ref[:, columns], preferred_element_type=jnp.float32
        )
        o_ref[:, columns] = product * scale
        copy = pltpu.make_async_copy(
            o_ref.at[:, columns], out_ref.at[:, columns], out_sem.at[t]
        )
        copy.start()
        results.append(copy)
    for copy in results:
        copy.wait()


def weight_sums(scalars, mine, other, shards, scale, after):
    n = len(shards)
    rows, cols = shards[0].shape
    width = mine.shape[1]
    tile = 768
    return pl.pallas_call(
        functools.partial(weight_kernel, n, tile, scale),
        out_shape=(
            jax.ShapeDtypeStruct((width, cols), jnp.float32),
            jax.ShapeDtypeStruct((8, 128), jnp.float32),
        ),
        in_specs=[SCALAR, VECTOR, VECTOR] + [IN_HBM] * n + [ANYWHERE] * len(after),
        out_specs=(IN_HBM, VECTOR),
        scratch_shapes=[
            pltpu.VMEM((width, n * rows), jnp.bfloat16),
            pltpu.VMEM((n * rows, cols), jnp.bfloat16),
            pltpu.VMEM((width, cols), jnp.float32),
            pltpu.SemaphoreType.DMA((n,)),
            pltpu.SemaphoreType.DMA((cols // tile,)),
        ],
        compiler_params=params(),
        cost_estimate=pl.CostEstimate(
            flops=2 * width * cols * rows * n,
            bytes_accessed=2 * rows * n * (cols + width) + 4 * width * cols,
            transcendentals=0,
        ),
        name="weight_sums",
    )(scalars, mine, other, *shards, *after)


def body(grad_out, inputs, weight):
    ix, iy = lax.axis_index("gx"), lax.axis_index("gy")
    xl, z = ix // Z, ix % Z
    y, xh, c = iy // (XH * C), iy // C % XH, iy % C
    rows = grad_out.shape[0]

    at = {"g": (0, 0), "gx": (1, 0)}
    for k in range(1, 5):
        at[f"u{k}"], at[f"ux{k}"] = (0, -k), (1, -k)
        at[f"d{k}"], at[f"dx{k}"] = (0, k), (1, k)

    def where(name):
        side, dz = at[name]
        x = xl if side == 0 else 1 - xl
        place = (z + dz) % Z
        return x * 2 + place // 4, place // 2 % 2, place % 2

    sets = (
        ("g", "gx", "u4", "dx4"),
        ("d1", "dx1", "u3", "ux3"),
        ("d2", "dx2", "u2", "ux2"),
        ("d3", "dx3", "u1", "ux1"),
    )
    even = z % 2 == c
    first = jnp.stack([even]).astype(jnp.int32)
    h = {"g": grad_out}

    def partials(a, b):
        return partial_sums(first, weight, ([h[s] for s in a], [h[s] for s in b]))

    def ways(*groups):
        slots = []
        for a, b in groups:
            for k in range(max(len(a), len(b))):
                way = [(where(s[k])[0] - y) % Y if k < len(s) else -1 for s in (a, b)]
                slots.append(jnp.where(even, way[0], way[1]))
        return jnp.stack(slots).astype(jnp.int32)

    def over_y(parts):
        return [parts[0], in_y(parts[1], 1), in_y(parts[3], -1), in_y(parts[2], 2)]

    def phase(names, sends, *after):
        s = [h[name] for name in sends]
        h.update(zip(names, tie([up(s[0]), down(s[1]), across(s[2])], after)))

    mine = inputs.T[None]
    pair = in_xh(mine)
    phase(("u1", "d1", "gx"), ("g", "g", "g"), pair)
    pair = jnp.concatenate([mine, pair])
    quad = in_y_pair(pair)
    phase(("u2", "d2", "ux1"), ("u1", "d1", "u1"), quad)
    quad = jnp.concatenate([pair, quad])
    column = in_y(quad, 2)
    phase(("u3", "d3", "dx2"), ("u2", "d2", "d2"), column)
    column = jnp.concatenate([quad, column])
    other = in_core(column)

    early_a = (("d2", "dx2", "u2"), ("d3", "u1", "ux1"))
    early_b = (("ux2",), ("dx3",))
    late_a = (("g", "gx", "u4"), ("d1", "u3"))
    late_b = (("dx4",), ("dx1", "ux3"))

    keep_a, send_a = partials(*early_a)
    got_a = in_core(send_a)
    phase(("u4", "dx3", "ux2"), ("u3", "dx2", "u2"), other, keep_a, got_a)
    keep_b, send_b = partials(*early_b)
    early = place(
        ways(early_a, early_b), [(keep_a, got_a), (keep_b, in_core(send_b))]
    )
    keep_c, send_c = partials(*late_a)
    got_c = in_core(send_c)
    phase(("ux3", "dx4", "dx1"), ("ux2", "dx3", "d1"), keep_c, *early)
    early = over_y(early)
    keep_d, send_d = partials(*late_b)
    late = place(ways(late_a, late_b), [(keep_c, got_c), (keep_d, in_core(send_d))])

    def of_inputs(name):
        ty, txh, tc = where(name)
        k = (ty // 2 != y // 2) * 4 + (ty % 2 != y % 2) * 2 + (txh != xh)
        return jnp.where(tc == c, k, k + column.shape[0])

    order = [s for names in sets for s in names]
    grad_weight, token = weight_sums(
        jnp.stack([of_inputs(s) for s in order]),
        column,
        other,
        [h[s] for s in order],
        1.0 / (Y * XH * C * rows),
        late,
    )

    here = (z + jnp.where(even, 0, 1)) // 2 % 2 == xh
    keep, send = merge(
        jnp.stack([here]).astype(jnp.int32), over_y(late), early, [token]
    )
    grad_in = (keep + in_xh(send)).astype(jnp.bfloat16)
    return grad_in.T, grad_weight


def solution(mesh):
    return jax.shard_map(
        body,
        mesh=mesh,
        in_specs=(P("gx", "gy"), P("gy", "gx"), P("gx", "gy")),
        out_specs=(P("gy", "gx"), P("gx", "gy")),
        check_vma=False,
    )
```

time: 279 us -> 161 us (0.58)
  waiting for transfers between devices: 242 us -> 55.9 us
  starting transfers between devices: 0.11 us -> 44.3 us
  Pallas kernels: 0 us -> 33.2 us
  matrix products: 21 us -> 0 us
  local copies, waits for them, and re-layouts: 0.01 us -> 18.7 us
  between operations: 13.8 us -> 0.96 us
  other arithmetic: 1.64 us -> 6.83 us
    all_gather x2 -> x0, waiting for transfers between devices: 158 us -> none  [the longest x1 116 us: body(): all_grad = lax.all_gather(grad_out, 'gx', axis=0, tiled=True)]
    reduce_scatter x1 -> x0, waiting for transfers between devices: 82.5 us -> none  [body(): lax.psum_scatter(lax.dot_general(all_grad, weight, (((1,), (1,)), ((), ()...]
    ppermute x0 -> x30, waiting for transfers between devices: none -> 55.9 us  [the longest x2 18.7 us: in_xh(): return lax.ppermute(t, 'gy', gy_pairs(0, 1, 0))]
    ppermute x0 -> x30, starting transfers between devices: none -> 44.3 us  [the longest x5 16.8 us: down(): return lax.ppermute(t, 'gx', gx_pairs(0, -1))]
    pallas_call x0 -> x13, Pallas kernels: none -> 33.2 us  [the longest x4 18.2 us: partial_sums(): pl.pallas_call(functools.partial(partial_kernel, places), out_shape=(out,...]
    dot_general x2 -> x0, matrix products: 21 us -> none  [the longest x1 11.4 us: body(): lax.dot_general(all_inputs, all_grad, (((0,), (0,)), ((), ())), preferred...]
    unnamed x2 -> x76, local copies, waits for them, and re-layouts: 0.01 us -> 18.5 us
    concatenate x0 -> x3, other arithmetic: none -> 6.06 us  [the longest x1 2.38 us: body(): column = jnp.concatenate([quad, column])]
  transfers between devices with their start and end apart: 3 -> 30, of which waited for: 3 -> 13; matrix products, arithmetic and copies ran while one was open for 8% -> 4% of each run, Pallas kernels for 0% -> 21%
where the time goes in v2:
time: 161 us; the launch traced here: 160 us
  waiting for transfers between devices  55.9 us (35%)
  starting transfers between devices  44.3 us (28%)
  Pallas kernels  33.2 us (21%)
  local copies, waits for them, and re-layouts  18.7 us (12%)
  other arithmetic  6.83 us (4%)
    ppermute x2, waiting for transfers between devices, in_xh(): return lax.ppermute(t, 'gy', gy_pairs(0, 1, 0))  18.7 us
    unnamed x76, local copies, waits for them, and re-layouts  18.5 us
    pallas_call x4, Pallas kernels, partial_sums(): pl.pallas_call(functools.partial(partial_kernel, places), out_shape=(out,...  18.2 us
    ppermute x5, starting transfers between devices, down(): return lax.ppermute(t, 'gx', gx_pairs(0, -1))  16.8 us
    ppermute x5, waiting for transfers between devices, across(): return lax.ppermute(t, 'gx', gx_pairs(1, 0))  14.1 us
    ppermute x5, waiting for transfers between devices, up(): return lax.ppermute(t, 'gx', gx_pairs(0, 1))  12.1 us
    pallas_call x1, Pallas kernels, weight_sums(): pl.pallas_call(functools.partial(weight_kernel, n, tile, scale), out_shap...  11.7 us
    ppermute x7, starting transfers between devices, in_y(): return lax.ppermute(t, 'gy', gy_pairs(dy, 0, 0))  10.6 us
  transfers between devices with their start and end apart: 30, of which 13 were waited for; matrix products, arithmetic and copies ran while one was open for 4% of the time, Pallas kernels for 21%

profile of v2, /device:TPU:8, one launch (start us, length us, event | category | flops | bytes accessed | tf_op | source)
XLA Modules:
  0.0 159.9 jit_solution(16505271736826780253)
XLA Ops:
  2.2 5.9 %collective-permute-start.1 = (bf16[128,2304]{1,0:T(8,128)(2,1)}, bf16[128,2304]{1,0:T(8,128)(2,1)}, u32[]{:S(2)}, u32[]{:S(2)}) collective-permute-start(bf16[128,2304]{1,0:T(8,128)(2,1)} %refs_0_.3), channel_id=1, source_target_pairs={{0,112},{16,0},{32,16},{48,32},{64,48},{80,64},{96,80},{112,96},{1... | collective-permute-start | bytes 1769480 | tf_op jit(solution)/shard_map/ppermute | solution.py:41
  8.1 2.7 %collective-permute-start.3 = (bf16[1,576,128]{2,1,0:T(8,128)(2,1)}, bf16[1,576,128]{2,1,0:T(8,128)(2,1)}, u32[]{:S(2)}, u32[]{:S(2)}) collective-permute-start(bf16[1,576,128]{2,1,0:T(8,128)(2,1)} %bitcast.32), channel_id=1, source_target_pairs={{0,2},{1,3},{2,0},{3,1},{4,6},{5,7},{6,4},{7,5},{8,10},{9,11},{10,... | collective-permute-start | bytes 442376 | tf_op jit(solution)/shard_map/ppermute | solution.py:63
  10.8 10.7 %collective-permute-done.3.refs_3_ = bf16[1,576,128]{2,1,0:T(8,128)(2,1)} collective-permute-done((bf16[1,576,128]{2,1,0:T(8,128)(2,1)}, bf16[1,576,128]{2,1,0:T(8,128)(2,1)}, u32[]{:S(2)}, u32[]{:S(2)}) %collective-permute-start.3) | collective-permute-done | bytes 147488 | tf_op jit(solution)/shard_map/ppermute | solution.py:63
  21.5 1.7 %pad_maximum_fusion.2 = bf16[2,576,128]{2,1,0:T(8,128)(2,1)} fusion(bf16[1,576,128]{2,1,0:T(8,128)(2,1)} %collective-permute-done.3.refs_3_, bf16[1,576,128]{2,1,0:T(8,128)(2,1)} %bitcast.33), kind=kLoop, calls=%fused_computation.2 | loop fusion | flops 147456 | bytes 589824 | tf_op jit(solution)/shard_map/concatenate | solution.py:330
  24.7 1.9 %collective-permute-start.4 = (bf16[128,2304]{1,0:T(8,128)(2,1)}, bf16[128,2304]{1,0:T(8,128)(2,1)}, u32[]{:S(2)}, u32[]{:S(2)}) collective-permute-start(bf16[128,2304]{1,0:T(8,128)(2,1)} %get-tuple-element.38.refs_4_.refs_14_), channel_id=1, source_target_pairs={{0,16},{16,32},{32,48},{48,64},{64,80},{80,96},{96,112},{112,0},{1... | collective-permute-start | bytes 1769480 | tf_op jit(solution)/shard_map/ppermute | solution.py:37
  26.6 3.9 %collective-permute-start.5 = (bf16[128,2304]{1,0:T(8,128)(2,1)}, bf16[128,2304]{1,0:T(8,128)(2,1)}, u32[]{:S(2)}, u32[]{:S(2)}) collective-permute-start(bf16[128,2304]{1,0:T(8,128)(2,1)} %get-tuple-element.39.refs_3_.refs_4_), channel_id=1, source_target_pairs={{0,112},{16,0},{32,16},{48,32},{64,48},{80,64},{96,80},{112,96},{1... | collective-permute-start | bytes 1769480 | tf_op jit(solution)/shard_map/ppermute | solution.py:41
  31.3 2.0 %pad_maximum_fusion.1 = bf16[4,576,128]{2,1,0:T(8,128)(2,1)} fusion(bf16[2,576,128]{2,1,0:T(8,128)(2,1)S(1)} %collective-permute-done.7.refs_3_, bf16[1,576,128]{2,1,0:T(8,128)(2,1)} %collective-permute-done.3.refs_3_, bf16[1,576,128]{2,1,0:T(8,128)(2,1)} %bitcast.34), kind=kLoop, calls=%fused_computation.1 | loop fusion | flops 589824 | bytes 1179648 | tf_op jit(solution)/shard_map/concatenate | solution.py:333
  33.2 2.3 %collective-permute-start.11 = (bf16[4,576,128]{2,1,0:T(8,128)(2,1)}, bf16[4,576,128]{2,1,0:T(8,128)(2,1)}, u32[]{:S(2)}, u32[]{:S(2)}) collective-permute-start(bf16[4,576,128]{2,1,0:T(8,128)(2,1)} %pad_maximum_fusion.1), channel_id=1, source_target_pairs={{0,8},{1,9},{2,10},{3,11},{4,12},{5,13},{6,14},{7,15},{8,0},{9,1},... | collective-permute-start | bytes 1769480 | tf_op jit(solution)/shard_map/ppermute | solution.py:59
  35.5 3.1 %collective-permute-done.6.refs_2_ = bf16[128,2304]{1,0:T(8,128)(2,1)S(1)} collective-permute-done((bf16[128,2304]{1,0:T(8,128)(2,1)}, bf16[128,2304]{1,0:T(8,128)(2,1)S(1)}, u32[]{:S(2)}, u32[]{:S(2)}) %collective-permute-start.6) | collective-permute-done | bytes 589856 | tf_op jit(solution)/shard_map/ppermute | solution.py:45
  38.6 4.3 %collective-permute-done.4.refs_0_ = bf16[128,2304]{1,0:T(8,128)(2,1)} collective-permute-done((bf16[128,2304]{1,0:T(8,128)(2,1)}, bf16[128,2304]{1,0:T(8,128)(2,1)}, u32[]{:S(2)}, u32[]{:S(2)}) %collective-permute-start.4) | collective-permute-done | bytes 589856 | tf_op jit(solution)/shard_map/ppermute | solution.py:37
  43.0 1.8 %collective-permute-start.10 = (bf16[128,2304]{1,0:T(8,128)(2,1)}, bf16[128,2304]{1,0:T(8,128)(2,1)}, u32[]{:S(2)}, u32[]{:S(2)}) collective-permute-start(bf16[128,2304]{1,0:T(8,128)(2,1)} %get-tuple-element.41.refs_0_.refs_8_), channel_id=1, source_target_pairs={{0,128},{16,144},{32,160},{48,176},{64,192},{80,208},{96,224},{112... | collective-permute-start | bytes 1769480 | tf_op jit(solution)/shard_map/ppermute | solution.py:45
  44.8 3.1 %collective-permute-start.9 = (bf16[128,2304]{1,0:T(8,128)(2,1)}, bf16[128,2304]{1,0:T(8,128)(2,1)}, u32[]{:S(2)}, u32[]{:S(2)}) collective-permute-start(bf16[128,2304]{1,0:T(8,128)(2,1)} %get-tuple-element.41.refs_0_.refs_8_), channel_id=1, source_target_pairs={{0,112},{16,0},{32,16},{48,32},{64,48},{80,64},{96,80},{112,96},{1... | collective-permute-start | bytes 1769480 | tf_op jit(solution)/shard_map/ppermute | solution.py:41
  48.3 2.4 %pad_maximum_fusion.mine_ref = bf16[8,576,128]{2,1,0:T(8,128)(2,1)} fusion(bf16[4,576,128]{2,1,0:T(8,128)(2,1)} %collective-permute-done.11.refs_3_, bf16[2,576,128]{2,1,0:T(8,128)(2,1)} %copy-done.37, bf16[1,576,128]{2,1,0:T(8,128)(2,1)} %collective-permute-done.3.refs_3_, bf16[1,576,128]{2,1,0:T(8,128)(2,1)} %bitcast.35), kind=kLoop, calls=%fused_computation | loop fusion | flops 1769472 | bytes 2359296 | tf_op jit(solution)/shard_map/concatenate | solution.py:336
  50.7 6.7 %collective-permute-done.8.refs_0_ = bf16[128,2304]{1,0:T(8,128)(2,1)S(1)} collective-permute-done((bf16[128,2304]{1,0:T(8,128)(2,1)}, bf16[128,2304]{1,0:T(8,128)(2,1)S(1)}, u32[]{:S(2)}, u32[]{:S(2)}) %collective-permute-start.8) | collective-permute-done | bytes 589856 | tf_op jit(solution)/shard_map/ppermute | solution.py:37
  58.3 1.7 %copy-done = bf16[576,2304]{1,0:T(8,128)(2,1)S(1)} copy-done((bf16[576,2304]{1,0:T(8,128)(2,1)S(1)}, bf16[576,2304]{1,0:T(8,128)(2,1)}, u32[]{:S(2)}) %copy-start) | copy-done | bytes 2654232
  61.1 5.6 %partial_sums.4 = (f32[3,576,128]{2,1,0:T(8,128)S(1)}, f32[3,576,128]{2,1,0:T(8,128)S(1)}) custom-call(s32[1]{0:T(128)} %bitcast.6.s_ref, bf16[576,2304]{1,0:T(8,128)(2,1)S(1)} %copy-done, bf16[128,2304]{1,0:T(8,128)(2,1)} %get-tuple-element.41.refs_0_.refs_8_, bf16[128,2304]{1,0:T(8,128)(2,1)} %get-tuple-element.43.refs_1_.refs_9_, ...), custom_call_target="tpu_custom_call" | custom-call | flops 2038431744 | bytes 7962624 | tf_op jit(solution)/shard_map/partial_sums/pallas_call | solution.py:138
  67.6 1.7 %collective-permute-start.14 = (bf16[128,2304]{1,0:T(8,128)(2,1)}, bf16[128,2304]{1,0:T(8,128)(2,1)S(1)}, u32[]{:S(2)}, u32[]{:S(2)}) collective-permute-start(bf16[128,2304]{1,0:T(8,128)(2,1)} %get-tuple-element.40.refs_2_.refs_10_), channel_id=1, source_target_pairs={{0,128},{16,144},{32,160},{48,176},{64,192},{80,208},{96,224},{112... | collective-permute-start | bytes 1769480 | tf_op jit(solution)/shard_map/ppermute | solution.py:45
  70.5 2.1 %collective-permute-start.13 = (bf16[128,2304]{1,0:T(8,128)(2,1)}, bf16[128,2304]{1,0:T(8,128)(2,1)S(1)}, u32[]{:S(2)}, u32[]{:S(2)}) collective-permute-start(bf16[128,2304]{1,0:T(8,128)(2,1)} %get-tuple-element.43.refs_1_.refs_9_), channel_id=1, source_target_pairs={{0,112},{16,0},{32,16},{48,32},{64,48},{80,64},{96,80},{112,96},{1... | collective-permute-start | bytes 1769480 | tf_op jit(solution)/shard_map/ppermute | solution.py:41
  72.6 11.0 %collective-permute-done.14.refs_2_ = bf16[128,2304]{1,0:T(8,128)(2,1)S(1)} collective-permute-done((bf16[128,2304]{1,0:T(8,128)(2,1)}, bf16[128,2304]{1,0:T(8,128)(2,1)S(1)}, u32[]{:S(2)}, u32[]{:S(2)}) %collective-permute-start.14) | collective-permute-done | bytes 589856 | tf_op jit(solution)/shard_map/ppermute | solution.py:45
  89.4 1.7 %collective-permute-start.19 = (bf16[128,2304]{1,0:T(8,128)(2,1)}, bf16[128,2304]{1,0:T(8,128)(2,1)}, u32[]{:S(2)}, u32[]{:S(2)}) collective-permute-start(bf16[128,2304]{1,0:T(8,128)(2,1)} %get-tuple-element.52.refs_1_.refs_13_), channel_id=1, source_target_pairs={{0,112},{16,0},{32,16},{48,32},{64,48},{80,64},{96,80},{112,96},{1... | collective-permute-start | bytes 1769480 | tf_op jit(solution)/shard_map/ppermute | solution.py:41
  91.2 1.7 %copy-done.1 = bf16[576,2304]{1,0:T(8,128)(2,1)S(1)} copy-done((bf16[576,2304]{1,0:T(8,128)(2,1)S(1)}, bf16[576,2304]{1,0:T(8,128)(2,1)}, u32[]{:S(2)}) %copy-start.1) | copy-done | bytes 2654232
  99.2 5.7 %partial_sums.5 = (f32[3,576,128]{2,1,0:T(8,128)S(1)}, f32[3,576,128]{2,1,0:T(8,128)}) custom-call(s32[1]{0:T(128)} %bitcast.6.s_ref, bf16[576,2304]{1,0:T(8,128)(2,1)S(1)} %copy-done.2, bf16[128,2304]{1,0:T(8,128)(2,1)S(1)} %copy-done.35, bf16[128,2304]{1,0:T(8,128)(2,1)S(1)} %copy-done.26, bf16[128,2304]{1,0:T(8,128)(2,1)S(1)} %copy-done.19, ...), custom_call_target="tpu_custom_call" | custom-call | flops 1698693120 | bytes 7372800 | tf_op jit(solution)/shard_map/partial_sums/pallas_call | solution.py:138
  109.7 1.7 %copy-done.3 = bf16[576,2304]{1,0:T(8,128)(2,1)S(1)} copy-done((bf16[576,2304]{1,0:T(8,128)(2,1)S(1)}, bf16[576,2304]{1,0:T(8,128)(2,1)}, u32[]{:S(2)}) %copy-start.3) | copy-done | bytes 2654232
  111.4 5.4 %partial_sums.7 = (f32[2,576,128]{2,1,0:T(8,128)S(1)}, f32[2,576,128]{2,1,0:T(8,128)}) custom-call(s32[1]{0:T(128)} %bitcast.6.s_ref, bf16[576,2304]{1,0:T(8,128)(2,1)S(1)} %copy-done.3, bf16[128,2304]{1,0:T(8,128)(2,1)} %get-tuple-element.59.refs_0_.refs_3_, bf16[128,2304]{1,0:T(8,128)(2,1)} %get-tuple-element.60.refs_1_.refs_5_, ...), custom_call_target="tpu_custom_call" | custom-call | flops 1019215872 | bytes 5603328 | tf_op jit(solution)/shard_map/partial_sums/pallas_call | solution.py:138
  117.4 2.4 %collective-permute-start.26 = (f32[576,128]{1,0:T(8,128)}, f32[576,128]{1,0:T(8,128)S(1)}, u32[]{:S(2)}, u32[]{:S(2)}) collective-permute-start(f32[576,128]{1,0:T(8,128)} %get-tuple-element.56.refs_5_), channel_id=1, source_target_pairs={{0,4},{1,5},{2,6},{3,7},{4,8},{5,9},{6,10},{7,11},{8,12},{9,13},{1... | collective-permute-start | bytes 884744 | tf_op jit(solution)/shard_map/ppermute | solution.py:59
  120.0 1.9 %collective-permute-start.28 = (f32[576,128]{1,0:T(8,128)S(1)}, f32[576,128]{1,0:T(8,128)S(1)}, u32[]{:S(2)}, u32[]{:S(2)}) collective-permute-start(f32[576,128]{1,0:T(8,128)S(1)} %copy-done.34), channel_id=1, source_target_pairs={{0,8},{1,9},{2,10},{3,11},{4,12},{5,13},{6,14},{7,15},{8,0},{9,1},... | collective-permute-start | bytes 884744 | tf_op jit(solution)/shard_map/ppermute | solution.py:59
  122.0 1.9 %collective-permute-start.27 = (f32[576,128]{1,0:T(8,128)S(1)}, f32[576,128]{1,0:T(8,128)S(1)}, u32[]{:S(2)}, u32[]{:S(2)}) collective-permute-start(f32[576,128]{1,0:T(8,128)S(1)} %copy-done.32), channel_id=1, source_target_pairs={{0,12},{1,13},{2,14},{3,15},{4,0},{5,1},{6,2},{7,3},{8,4},{9,5},{1... | collective-permute-start | bytes 884744 | tf_op jit(solution)/shard_map/ppermute | solution.py:59
  125.8 1.9 %collective-permute-start.24 = (f32[576,128]{1,0:T(8,128)S(1)}, f32[576,128]{1,0:T(8,128)S(1)}, u32[]{:S(2)}, u32[]{:S(2)}) collective-permute-start(f32[576,128]{1,0:T(8,128)S(1)} %get-tuple-element.66.refs_19_), channel_id=1, source_target_pairs={{0,12},{1,13},{2,14},{3,15},{4,0},{5,1},{6,2},{7,3},{8,4},{9,5},{1... | collective-permute-start | bytes 884744 | tf_op jit(solution)/shard_map/ppermute | solution.py:59
  127.7 6.2 %collective-permute-done.26.refs_5_ = f32[576,128]{1,0:T(8,128)S(1)} collective-permute-done((f32[576,128]{1,0:T(8,128)}, f32[576,128]{1,0:T(8,128)S(1)}, u32[]{:S(2)}, u32[]{:S(2)}) %collective-permute-start.26) | collective-permute-done | bytes 294944 | tf_op jit(solution)/shard_map/ppermute | solution.py:59
  135.0 11.7 %weight_sums.1 = (f32[576,2304]{1,0:T(8,128)}, f32[8,128]{1,0:T(8,128)S(1)}) custom-call(s32[16]{0:T(128)S(1)} %stack.113.s_ref, bf16[8,576,128]{2,1,0:T(8,128)(2,1)} %pad_maximum_fusion.mine_ref, bf16[8,576,128]{2,1,0:T(8,128)(2,1)} %collective-permute-done.15.refs_3_.other_ref, bf16[128,2304]{1,0:T(8,128)(2,1)S(1)} %copy-done.36, ...), custom_call_target="tpu_custom_call" | custom-call | flops 5435817984 | bytes 17104896 | tf_op jit(solution)/shard_map/weight_sums/pallas_call | solution.py:257
  146.8 2.8 %collective-permute-done.25.refs_3_ = f32[576,128]{1,0:T(8,128)S(1)} collective-permute-done((f32[576,128]{1,0:T(8,128)S(1)}, f32[576,128]{1,0:T(8,128)S(1)}, u32[]{:S(2)}, u32[]{:S(2)}) %collective-permute-start.25) | collective-permute-done | bytes 294944 | tf_op jit(solution)/shard_map/ppermute | solution.py:59
  151.1 8.1 %collective-permute-done.29 = f32[576,128]{1,0:T(8,128)S(1)} collective-permute-done((f32[576,128]{1,0:T(8,128)S(1)}, f32[576,128]{1,0:T(8,128)S(1)}, u32[]{:S(2)}, u32[]{:S(2)}) %collective-permute-start.29) | collective-permute-done | bytes 294944 | tf_op jit(solution)/shard_map/ppermute | solution.py:63
  (124 shorter events, 30.9 us)
Async XLA Ops:
  0.6 23.0 %collective-permute-start.2 = (bf16[128,2304]{1,0:T(8,128)(2,1)}, bf16[128,2304]{1,0:T(8,128)(2,1)S(1)}, u32[]{:S(2)}, u32[]{:S(2)}) collective-permute-start(bf16[128,2304]{1,0:T(8,128)(2,1)} %refs_0_.3), channel_id=1, source_target_pairs={{0,128},{16,144},{32,160},{48,176},{64,192},{80,208},{96,224},{112... | collective-permute-start | bytes 1769480 | tf_op jit(solution)/shard_map/ppermute | solution.py:45
  2.2 21.4 %collective-permute-start.1 = (bf16[128,2304]{1,0:T(8,128)(2,1)}, bf16[128,2304]{1,0:T(8,128)(2,1)}, u32[]{:S(2)}, u32[]{:S(2)}) collective-permute-start(bf16[128,2304]{1,0:T(8,128)(2,1)} %refs_0_.3), channel_id=1, source_target_pairs={{0,112},{16,0},{32,16},{48,32},{64,48},{80,64},{96,80},{112,96},{1... | collective-permute-start | bytes 1769480 | tf_op jit(solution)/shard_map/ppermute | solution.py:41
  8.1 16.0 %collective-permute-start = (bf16[128,2304]{1,0:T(8,128)(2,1)}, bf16[128,2304]{1,0:T(8,128)(2,1)}, u32[]{:S(2)}, u32[]{:S(2)}) collective-permute-start(bf16[128,2304]{1,0:T(8,128)(2,1)} %refs_0_.3), channel_id=1, source_target_pairs={{0,16},{16,32},{32,48},{48,64},{64,80},{80,96},{96,112},{112,0},{1... | collective-permute-start | bytes 1769480 | tf_op jit(solution)/shard_map/ppermute | solution.py:37
  8.1 13.4 %collective-permute-start.3 = (bf16[1,576,128]{2,1,0:T(8,128)(2,1)}, bf16[1,576,128]{2,1,0:T(8,128)(2,1)}, u32[]{:S(2)}, u32[]{:S(2)}) collective-permute-start(bf16[1,576,128]{2,1,0:T(8,128)(2,1)} %bitcast.32), channel_id=1, source_target_pairs={{0,2},{1,3},{2,0},{3,1},{4,6},{5,7},{6,4},{7,5},{8,10},{9,11},{10,... | collective-permute-start | bytes 442376 | tf_op jit(solution)/shard_map/ppermute | solution.py:63
  23.2 8.1 %collective-permute-start.7 = (bf16[2,576,128]{2,1,0:T(8,128)(2,1)}, bf16[2,576,128]{2,1,0:T(8,128)(2,1)S(1)}, u32[]{:S(2)}, u32[]{:S(2)}) collective-permute-start(bf16[2,576,128]{2,1,0:T(8,128)(2,1)} %pad_maximum_fusion.2), channel_id=1, source_target_pairs={{0,4},{1,5},{2,6},{3,7},{4,0},{5,1},{6,2},{7,3},{8,12},{9,13},{10,... | collective-permute-start | bytes 884744 | tf_op jit(solution)/shard_map/ppermute | solution.py:55
  24.5 14.1 %collective-permute-start.6 = (bf16[128,2304]{1,0:T(8,128)(2,1)}, bf16[128,2304]{1,0:T(8,128)(2,1)S(1)}, u32[]{:S(2)}, u32[]{:S(2)}) collective-permute-start(bf16[128,2304]{1,0:T(8,128)(2,1)} %get-tuple-element.38.refs_4_.refs_14_), channel_id=1, source_target_pairs={{0,128},{16,144},{32,160},{48,176},{64,192},{80,208},{96,224},{112... | collective-permute-start | bytes 1769480 | tf_op jit(solution)/shard_map/ppermute | solution.py:45
  24.7 18.2 %collective-permute-start.4 = (bf16[128,2304]{1,0:T(8,128)(2,1)}, bf16[128,2304]{1,0:T(8,128)(2,1)}, u32[]{:S(2)}, u32[]{:S(2)}) collective-permute-start(bf16[128,2304]{1,0:T(8,128)(2,1)} %get-tuple-element.38.refs_4_.refs_14_), channel_id=1, source_target_pairs={{0,16},{16,32},{32,48},{48,64},{64,80},{80,96},{96,112},{112,0},{1... | collective-permute-start | bytes 1769480 | tf_op jit(solution)/shard_map/ppermute | solution.py:37
  26.6 16.2 %collective-permute-start.5 = (bf16[128,2304]{1,0:T(8,128)(2,1)}, bf16[128,2304]{1,0:T(8,128)(2,1)}, u32[]{:S(2)}, u32[]{:S(2)}) collective-permute-start(bf16[128,2304]{1,0:T(8,128)(2,1)} %get-tuple-element.39.refs_3_.refs_4_), channel_id=1, source_target_pairs={{0,112},{16,0},{32,16},{48,32},{64,48},{80,64},{96,80},{112,96},{1... | collective-permute-start | bytes 1769480 | tf_op jit(solution)/shard_map/ppermute | solution.py:41
  33.2 15.1 %collective-permute-start.11 = (bf16[4,576,128]{2,1,0:T(8,128)(2,1)}, bf16[4,576,128]{2,1,0:T(8,128)(2,1)}, u32[]{:S(2)}, u32[]{:S(2)}) collective-permute-start(bf16[4,576,128]{2,1,0:T(8,128)(2,1)} %pad_maximum_fusion.1), channel_id=1, source_target_pairs={{0,8},{1,9},{2,10},{3,11},{4,12},{5,13},{6,14},{7,15},{8,0},{9,1},... | collective-permute-start | bytes 1769480 | tf_op jit(solution)/shard_map/ppermute | solution.py:59
  42.9 14.5 %collective-permute-start.8 = (bf16[128,2304]{1,0:T(8,128)(2,1)}, bf16[128,2304]{1,0:T(8,128)(2,1)S(1)}, u32[]{:S(2)}, u32[]{:S(2)}) collective-permute-start(bf16[128,2304]{1,0:T(8,128)(2,1)} %get-tuple-element.40.refs_2_.refs_10_), channel_id=1, source_target_pairs={{0,16},{16,32},{32,48},{48,64},{64,80},{80,96},{96,112},{112,0},{1... | collective-permute-start | bytes 1769480 | tf_op jit(solution)/shard_map/ppermute | solution.py:37
  43.0 14.5 %collective-permute-start.10 = (bf16[128,2304]{1,0:T(8,128)(2,1)}, bf16[128,2304]{1,0:T(8,128)(2,1)}, u32[]{:S(2)}, u32[]{:S(2)}) collective-permute-start(bf16[128,2304]{1,0:T(8,128)(2,1)} %get-tuple-element.41.refs_0_.refs_8_), channel_id=1, source_target_pairs={{0,128},{16,144},{32,160},{48,176},{64,192},{80,208},{96,224},{112... | collective-permute-start | bytes 1769480 | tf_op jit(solution)/shard_map/ppermute | solution.py:45
  44.8 13.4 %collective-permute-start.9 = (bf16[128,2304]{1,0:T(8,128)(2,1)}, bf16[128,2304]{1,0:T(8,128)(2,1)}, u32[]{:S(2)}, u32[]{:S(2)}) collective-permute-start(bf16[128,2304]{1,0:T(8,128)(2,1)} %get-tuple-element.41.refs_0_.refs_8_), channel_id=1, source_target_pairs={{0,112},{16,0},{32,16},{48,32},{64,48},{80,64},{96,80},{112,96},{1... | collective-permute-start | bytes 1769480 | tf_op jit(solution)/shard_map/ppermute | solution.py:41
  50.7 34.6 %collective-permute-start.15 = (bf16[8,576,128]{2,1,0:T(8,128)(2,1)}, bf16[8,576,128]{2,1,0:T(8,128)(2,1)}, u32[]{:S(2)}, u32[]{:S(2)}) collective-permute-start(bf16[8,576,128]{2,1,0:T(8,128)(2,1)} %pad_maximum_fusion.mine_ref), channel_id=1, source_target_pairs={{0,1},{1,0},{2,3},{3,2},{4,5},{5,4},{6,7},{7,6},{8,9},{9,8},{10,11... | collective-permute-start | bytes 3538952 | tf_op jit(solution)/shard_map/ppermute | solution.py:67
  67.6 18.4 %collective-permute-start.16 = (f32[3,576,128]{2,1,0:T(8,128)S(1)}, f32[3,576,128]{2,1,0:T(8,128)S(1)}, u32[]{:S(2)}, u32[]{:S(2)}) collective-permute-start(f32[3,576,128]{2,1,0:T(8,128)S(1)} %get-tuple-element.47), channel_id=1, source_target_pairs={{0,1},{1,0},{2,3},{3,2},{4,5},{5,4},{6,7},{7,6},{8,9},{9,8},{10,11... | collective-permute-start | bytes 2654216 | tf_op jit(solution)/shard_map/ppermute | solution.py:67
  67.6 16.0 %collective-permute-start.14 = (bf16[128,2304]{1,0:T(8,128)(2,1)}, bf16[128,2304]{1,0:T(8,128)(2,1)S(1)}, u32[]{:S(2)}, u32[]{:S(2)}) collective-permute-start(bf16[128,2304]{1,0:T(8,128)(2,1)} %get-tuple-element.40.refs_2_.refs_10_), channel_id=1, source_target_pairs={{0,128},{16,144},{32,160},{48,176},{64,192},{80,208},{96,224},{112... | collective-permute-start | bytes 1769480 | tf_op jit(solution)/shard_map/ppermute | solution.py:45
  69.3 16.7 %collective-permute-start.12 = (bf16[128,2304]{1,0:T(8,128)(2,1)S(1)}, bf16[128,2304]{1,0:T(8,128)(2,1)S(1)}, u32[]{:S(2)}, u32[]{:S(2)}) collective-permute-start(bf16[128,2304]{1,0:T(8,128)(2,1)S(1)} %copy-done.22), channel_id=1, source_target_pairs={{0,16},{16,32},{32,48},{48,64},{64,80},{80,96},{96,112},{112,0},{1... | collective-permute-start | bytes 1769480 | tf_op jit(solution)/shard_map/ppermute | solution.py:37
  70.5 15.5 %collective-permute-start.13 = (bf16[128,2304]{1,0:T(8,128)(2,1)}, bf16[128,2304]{1,0:T(8,128)(2,1)S(1)}, u32[]{:S(2)}, u32[]{:S(2)}) collective-permute-start(bf16[128,2304]{1,0:T(8,128)(2,1)} %get-tuple-element.43.refs_1_.refs_9_), channel_id=1, source_target_pairs={{0,112},{16,0},{32,16},{48,32},{64,48},{80,64},{96,80},{112,96},{1... | collective-permute-start | bytes 1769480 | tf_op jit(solution)/shard_map/ppermute | solution.py:41
  83.6 26.1 %collective-permute-start.20 = (bf16[128,2304]{1,0:T(8,128)(2,1)}, bf16[128,2304]{1,0:T(8,128)(2,1)}, u32[]{:S(2)}, u32[]{:S(2)}) collective-permute-start(bf16[128,2304]{1,0:T(8,128)(2,1)} %get-tuple-element.39.refs_3_.refs_4_), channel_id=1, source_target_pairs={{0,128},{16,144},{32,160},{48,176},{64,192},{80,208},{96,224},{112... | collective-permute-start | bytes 1769480 | tf_op jit(solution)/shard_map/ppermute | solution.py:45
  87.9 21.7 %collective-permute-start.18 = (bf16[128,2304]{1,0:T(8,128)(2,1)}, bf16[128,2304]{1,0:T(8,128)(2,1)}, u32[]{:S(2)}, u32[]{:S(2)}) collective-permute-start(bf16[128,2304]{1,0:T(8,128)(2,1)} %get-tuple-element.51.refs_0_.refs_11_), channel_id=1, source_target_pairs={{0,16},{16,32},{32,48},{48,64},{64,80},{80,96},{96,112},{112,0},{1... | collective-permute-start | bytes 1769480 | tf_op jit(solution)/shard_map/ppermute | solution.py:37
  89.4 20.2 %collective-permute-start.19 = (bf16[128,2304]{1,0:T(8,128)(2,1)}, bf16[128,2304]{1,0:T(8,128)(2,1)}, u32[]{:S(2)}, u32[]{:S(2)}) collective-permute-start(bf16[128,2304]{1,0:T(8,128)(2,1)} %get-tuple-element.52.refs_1_.refs_13_), channel_id=1, source_target_pairs={{0,112},{16,0},{32,16},{48,32},{64,48},{80,64},{96,80},{112,96},{1... | collective-permute-start | bytes 1769480 | tf_op jit(solution)/shard_map/ppermute | solution.py:41
  96.5 9.5 %collective-permute-start.21 = (f32[1,576,128]{2,1,0:T(8,128)S(1)}, f32[1,576,128]{2,1,0:T(8,128)S(1)}, u32[]{:S(2)}, u32[]{:S(2)}) collective-permute-start(f32[1,576,128]{2,1,0:T(8,128)S(1)} %get-tuple-element.54), channel_id=1, source_target_pairs={{0,1},{1,0},{2,3},{3,2},{4,5},{5,4},{6,7},{7,6},{8,9},{9,8},{10,11... | collective-permute-start | bytes 884744 | tf_op jit(solution)/shard_map/ppermute | solution.py:67
  105.9 18.0 %collective-permute-start.17 = (f32[3,576,128]{2,1,0:T(8,128)}, f32[3,576,128]{2,1,0:T(8,128)}, u32[]{:S(2)}, u32[]{:S(2)}) collective-permute-start(f32[3,576,128]{2,1,0:T(8,128)} %get-tuple-element.50), channel_id=1, source_target_pairs={{0,1},{1,0},{2,3},{3,2},{4,5},{5,4},{6,7},{7,6},{8,9},{9,8},{10,11... | collective-permute-start | bytes 2654216 | tf_op jit(solution)/shard_map/ppermute | solution.py:67
  116.9 7.0 %collective-permute-start.22 = (f32[2,576,128]{2,1,0:T(8,128)}, f32[2,576,128]{2,1,0:T(8,128)S(1)}, u32[]{:S(2)}, u32[]{:S(2)}) collective-permute-start(f32[2,576,128]{2,1,0:T(8,128)} %get-tuple-element.63), channel_id=1, source_target_pairs={{0,1},{1,0},{2,3},{3,2},{4,5},{5,4},{6,7},{7,6},{8,9},{9,8},{10,11... | collective-permute-start | bytes 1769480 | tf_op jit(solution)/shard_map/ppermute | solution.py:67
  117.4 16.4 %collective-permute-start.26 = (f32[576,128]{1,0:T(8,128)}, f32[576,128]{1,0:T(8,128)S(1)}, u32[]{:S(2)}, u32[]{:S(2)}) collective-permute-start(f32[576,128]{1,0:T(8,128)} %get-tuple-element.56.refs_5_), channel_id=1, source_target_pairs={{0,4},{1,5},{2,6},{3,7},{4,8},{5,9},{6,10},{7,11},{8,12},{9,13},{1... | collective-permute-start | bytes 884744 | tf_op jit(solution)/shard_map/ppermute | solution.py:59
  119.9 14.0 %copy-start.30 = (bf16[128,2304]{1,0:T(8,128)(2,1)S(1)}, bf16[128,2304]{1,0:T(8,128)(2,1)}, u32[]{:S(2)}) copy-start(bf16[128,2304]{1,0:T(8,128)(2,1)} %get-tuple-element.45.refs_5_.refs_15_) | copy-start | bytes 1769476
  120.0 26.7 %collective-permute-start.28 = (f32[576,128]{1,0:T(8,128)S(1)}, f32[576,128]{1,0:T(8,128)S(1)}, u32[]{:S(2)}, u32[]{:S(2)}) collective-permute-start(f32[576,128]{1,0:T(8,128)S(1)} %copy-done.34), channel_id=1, source_target_pairs={{0,8},{1,9},{2,10},{3,11},{4,12},{5,13},{6,14},{7,15},{8,0},{9,1},... | collective-permute-start | bytes 884744 | tf_op jit(solution)/shard_map/ppermute | solution.py:59
  122.0 24.8 %collective-permute-start.27 = (f32[576,128]{1,0:T(8,128)S(1)}, f32[576,128]{1,0:T(8,128)S(1)}, u32[]{:S(2)}, u32[]{:S(2)}) collective-permute-start(f32[576,128]{1,0:T(8,128)S(1)} %copy-done.32), channel_id=1, source_target_pairs={{0,12},{1,13},{2,14},{3,15},{4,0},{5,1},{6,2},{7,3},{8,4},{9,5},{1... | collective-permute-start | bytes 884744 | tf_op jit(solution)/shard_map/ppermute | solution.py:59
  125.5 21.2 %collective-permute-start.23 = (f32[576,128]{1,0:T(8,128)S(1)}, f32[576,128]{1,0:T(8,128)S(1)}, u32[]{:S(2)}, u32[]{:S(2)}) collective-permute-start(f32[576,128]{1,0:T(8,128)S(1)} %get-tuple-element.65.refs_17_), channel_id=1, source_target_pairs={{0,4},{1,5},{2,6},{3,7},{4,8},{5,9},{6,10},{7,11},{8,12},{9,13},{1... | collective-permute-start | bytes 884744 | tf_op jit(solution)/shard_map/ppermute | solution.py:59
  125.8 21.0 %collective-permute-start.24 = (f32[576,128]{1,0:T(8,128)S(1)}, f32[576,128]{1,0:T(8,128)S(1)}, u32[]{:S(2)}, u32[]{:S(2)}) collective-permute-start(f32[576,128]{1,0:T(8,128)S(1)} %get-tuple-element.66.refs_19_), channel_id=1, source_target_pairs={{0,12},{1,13},{2,14},{3,15},{4,0},{5,1},{6,2},{7,3},{8,4},{9,5},{1... | collective-permute-start | bytes 884744 | tf_op jit(solution)/shard_map/ppermute | solution.py:59
  133.9 15.7 %collective-permute-start.25 = (f32[576,128]{1,0:T(8,128)S(1)}, f32[576,128]{1,0:T(8,128)S(1)}, u32[]{:S(2)}, u32[]{:S(2)}) collective-permute-start(f32[576,128]{1,0:T(8,128)S(1)} %get-tuple-element.67.refs_18_), channel_id=1, source_target_pairs={{0,8},{1,9},{2,10},{3,11},{4,12},{5,13},{6,14},{7,15},{8,0},{9,1},... | collective-permute-start | bytes 884744 | tf_op jit(solution)/shard_map/ppermute | solution.py:59
  135.0 14.6 %copy-start.17 = (f32[576,128]{1,0:T(8,128)S(1)}, f32[576,128]{1,0:T(8,128)}, u32[]{:S(2)}) copy-start(f32[576,128]{1,0:T(8,128)} %copy-done.16) | copy-start | bytes 884740
  149.7 9.4 %collective-permute-start.29 = (f32[576,128]{1,0:T(8,128)S(1)}, f32[576,128]{1,0:T(8,128)S(1)}, u32[]{:S(2)}, u32[]{:S(2)}) collective-permute-start(f32[576,128]{1,0:T(8,128)S(1)} %get-tuple-element.70), channel_id=1, source_target_pairs={{0,2},{1,3},{2,0},{3,1},{4,6},{5,7},{6,4},{7,5},{8,10},{9,11},{10,... | collective-permute-start | bytes 884744 | tf_op jit(solution)/shard_map/ppermute | solution.py:63
  (36 other events, 136.4 us)

commit v3 on v2

--- a/solution.py
+++ b/solution.py
@@ -9,8 +9,7 @@
 
 XL, Z = 2, 8
 Y, XH, C = 4, 2, 2
-VMEM_LIMIT = 32 << 20
-TIE_LIMIT = 63 << 20
+VMEM_LIMIT = 63 << 20
 
 
 def gx_pairs(dxl, dz):
@@ -73,8 +72,8 @@
 SCALAR = pl.BlockSpec(memory_space=pltpu.SMEM)
 
 
-def params(limit=VMEM_LIMIT):
-    return pltpu.CompilerParams(vmem_limit_bytes=limit)
+def params():
+    return pltpu.CompilerParams(vmem_limit_bytes=VMEM_LIMIT)
 
 
 def tie(values, after):
@@ -85,15 +84,40 @@
         in_specs=[IN_HBM] * n + [ANYWHERE] * len(after),
         out_specs=[IN_HBM] * n,
         input_output_aliases={k: k for k in range(n)},
-        compiler_params=params(TIE_LIMIT),
+        compiler_params=params(),
         name="tie",
     )(*values, *after)
+
+
+def stack_kernel(a_ref, b_ref, *refs):
+    out_ref, sem = refs[-2:]
+    n = a_ref.shape[0]
+    copies = [
+        pltpu.make_async_copy(a_ref, out_ref.at[pl.ds(0, n)], sem.at[0]),
+        pltpu.make_async_copy(b_ref, out_ref.at[pl.ds(n, n)], sem.at[1]),
+    ]
+    for copy in copies:
+        copy.start()
+    for copy in copies:
+        copy.wait()
+
+
+def stack(a, b, after):
+    return pl.pallas_call(
+        stack_kernel,
+        out_shape=jax.ShapeDtypeStruct((2 * a.shape[0],) + a.shape[1:], a.dtype),
+        in_specs=[IN_HBM] * 2 + [ANYWHERE] * len(after),
+        out_specs=IN_HBM,
+        scratch_shapes=[pltpu.SemaphoreType.DMA((2,))],
+        compiler_params=params(),
+        name="stack",
+    )(a, b, *after)
 
 
 def partial_kernel(places, s_ref, w_any, *refs):
     n = len(places)
     pieces = refs[:n]
-    keep_ref, send_ref, w_ref, g_ref, sem = refs[n:]
+    keep_ref, send_ref, w_ref, g_ref, sem = refs[-5:]
     rows = keep_ref.shape[2]
     w_copy = pltpu.make_async_copy(w_any, w_ref, sem.at[n])
     w_copy.start()
@@ -111,7 +135,7 @@
             copies[k].wait()
         sums = lax.dot_general(
             w_ref[...],
-            g_ref[first * rows : (first + count) * rows, :],
+            g_ref[first * rows : (first + 2) * rows, :],
             (((1,), (1,)), ((), ())),
             preferred_element_type=jnp.float32,
         )
@@ -128,7 +152,7 @@
                 send_ref[slot] = value
 
 
-def partial_sums(first, weight, groups):
+def partial_sums(first, weight, groups, after):
     places = [(g, k) for g, shards in enumerate(groups) for k in range(len(shards))]
     shards = [s for group in groups for s in group]
     n, slots = len(shards), max(len(group) for group in groups)
@@ -138,11 +162,11 @@
     return pl.pallas_call(
         functools.partial(partial_kernel, places),
         out_shape=(out, out),
-        in_specs=[SCALAR] + [IN_HBM] * (1 + n),
+        in_specs=[SCALAR] + [IN_HBM] * (1 + n) + [ANYWHERE] * len(after),
         out_specs=(VECTOR, VECTOR),
         scratch_shapes=[
             pltpu.VMEM((width, cols), jnp.bfloat16),
-            pltpu.VMEM((n * rows, cols), jnp.bfloat16),
+            pltpu.VMEM(((n + n % 2) * rows, cols), jnp.bfloat16),
             pltpu.SemaphoreType.DMA((n + 1,)),
         ],
         compiler_params=params(),
@@ -152,7 +176,7 @@
             transcendentals=0,
         ),
         name="partial_sums",
-    )(first, weight, *shards)
+    )(first, weight, *shards, *after)
 
 
 def place_kernel(counts, s_ref, *refs):
@@ -306,8 +330,9 @@
     first = jnp.stack([even]).astype(jnp.int32)
     h = {"g": grad_out}
 
-    def partials(a, b):
-        return partial_sums(first, weight, ([h[s] for s in a], [h[s] for s in b]))
+    def partials(a, b, *after):
+        groups = [h[s] for s in a], [h[s] for s in b]
+        return partial_sums(first, weight, groups, after)
 
     def ways(*groups):
         slots = []
@@ -327,13 +352,13 @@
     mine = inputs.T[None]
     pair = in_xh(mine)
     phase(("u1", "d1", "gx"), ("g", "g", "g"), pair)
-    pair = jnp.concatenate([mine, pair])
+    pair = stack(mine, pair, [h["u1"]])
     quad = in_y_pair(pair)
-    phase(("u2", "d2", "ux1"), ("u1", "d1", "u1"), quad)
-    quad = jnp.concatenate([pair, quad])
+    phase(("u2", "d2", "ux1"), ("u1", "d1", "u1"), pair)
+    quad = stack(pair, quad, [h["u2"]])
     column = in_y(quad, 2)
-    phase(("u3", "d3", "dx2"), ("u2", "d2", "d2"), column)
-    column = jnp.concatenate([quad, column])
+    phase(("u3", "d3", "dx2"), ("u2", "d2", "d2"), quad)
+    column = stack(quad, column, [h["u3"]])
     other = in_core(column)
 
     early_a = (("d2", "dx2", "u2"), ("d3", "u1", "ux1"))
@@ -343,16 +368,16 @@
 
     keep_a, send_a = partials(*early_a)
     got_a = in_core(send_a)
-    phase(("u4", "dx3", "ux2"), ("u3", "dx2", "u2"), other, keep_a, got_a)
+    phase(("u4", "dx3", "ux2"), ("u3", "dx2", "u2"), column, keep_a)
     keep_b, send_b = partials(*early_b)
     early = place(
         ways(early_a, early_b), [(keep_a, got_a), (keep_b, in_core(send_b))]
     )
     keep_c, send_c = partials(*late_a)
     got_c = in_core(send_c)
-    phase(("ux3", "dx4", "dx1"), ("ux2", "dx3", "d1"), keep_c, *early)
     early = over_y(early)
-    keep_d, send_d = partials(*late_b)
+    phase(("ux3", "dx4", "dx1"), ("ux2", "dx3", "d1"), keep_c, other)
+    keep_d, send_d = partials(*late_b, early[1], early[2])
     late = place(ways(late_a, late_b), [(keep_c, got_c), (keep_d, in_core(send_d))])
 
     def of_inputs(name):

time: 161 us -> 203 us (1.26)
  Pallas kernels: 33.2 us -> 112 us
  waiting for transfers between devices: 55.9 us -> 37.6 us
  local copies, waits for them, and re-layouts: 18.7 us -> 7.82 us
  starting transfers between devices: 44.3 us -> 38.5 us
  other arithmetic: 6.83 us -> 2.27 us
    pallas_call x0 -> x3, Pallas kernels: none -> 65.9 us  [stack(): pl.pallas_call(stack_kernel, out_shape=jax.ShapeDtypeStruct((2 * a.shape[...]
    unnamed x76 -> x28, local copies, waits for them, and re-layouts: 18.5 us -> 6.51 us
    ppermute x5, waiting for transfers between devices: 14.1 us -> 3.78 us  [across(): return lax.ppermute(t, 'gx', gx_pairs(1, 0))]
    ppermute x5, waiting for transfers between devices: 12.1 us -> 2.04 us  [up(): return lax.ppermute(t, 'gx', gx_pairs(0, 1))]
    pallas_call x4, Pallas kernels: 18.2 us -> 25 us  [partial_sums(): pl.pallas_call(functools.partial(partial_kernel, places), out_shape=(out,...]
    concatenate x3 -> x0, other arithmetic: 6.06 us -> none  [the longest x1 2.38 us: body(): column = jnp.concatenate([quad, column])]
    pallas_call x2, Pallas kernels: 3.11 us -> 5.91 us  [place(): pl.pallas_call(functools.partial(place_kernel, counts), out_shape=[out] *...]
    ppermute x5, starting transfers between devices: 7.01 us -> 4.42 us  [across(): return lax.ppermute(t, 'gx', gx_pairs(1, 0))]
  transfers between devices with their start and end apart: 30 -> 30, of which waited for: 13 -> 12; matrix products, arithmetic and copies ran while one was open for 4% -> 1% of each run, Pallas kernels for 21% -> 55%
where the time goes in v3:
time: 203 us; the launch traced here: 201 us
  Pallas kernels  112 us (55%)
  starting transfers between devices  38.5 us (19%)
  waiting for transfers between devices  37.6 us (19%)
  local copies, waits for them, and re-layouts  7.82 us (4%)
  other arithmetic  2.27 us (1%)
  between operations  2.26 us (1%)
    pallas_call x3, Pallas kernels, stack(): pl.pallas_call(stack_kernel, out_shape=jax.ShapeDtypeStruct((2 * a.shape[...  65.9 us
    pallas_call x4, Pallas kernels, partial_sums(): pl.pallas_call(functools.partial(partial_kernel, places), out_shape=(out,...  25 us
    ppermute x2, waiting for transfers between devices, in_xh(): return lax.ppermute(t, 'gy', gy_pairs(0, 1, 0))  19.3 us
    ppermute x5, starting transfers between devices, down(): return lax.ppermute(t, 'gx', gx_pairs(0, -1))  15.9 us
    pallas_call x1, Pallas kernels, weight_sums(): pl.pallas_call(functools.partial(weight_kernel, n, tile, scale), out_shap...  13 us
    ppermute x7, starting transfers between devices, in_y(): return lax.ppermute(t, 'gy', gy_pairs(dy, 0, 0))  10.3 us
    ppermute x7, waiting for transfers between devices, in_y(): return lax.ppermute(t, 'gy', gy_pairs(dy, 0, 0))  9.53 us
    unnamed x28, local copies, waits for them, and re-layouts  6.51 us
  transfers between devices with their start and end apart: 30, of which 12 were waited for; matrix products, arithmetic and copies ran while one was open for 1% of the time, Pallas kernels for 55%

profile of v3, /device:TPU:8, one launch (start us, length us, event | category | flops | bytes accessed | tf_op | source)
XLA Modules:
  0.0 200.8 jit_solution(3885912792659232800)
XLA Ops:
  0.6 1.6 collective-permute-start.2
  2.2 5.9 %collective-permute-start.1 = (bf16[128,2304]{1,0:T(8,128)(2,1)}, bf16[128,2304]{1,0:T(8,128)(2,1)S(1)}, u32[]{:S(2)}, u32[]{:S(2)}) collective-permute-start(bf16[128,2304]{1,0:T(8,128)(2,1)} %refs_0_.3), channel_id=1, source_target_pairs={{0,112},{16,0},{32,16},{48,32},{64,48},{80,64},{96,80},{112,96},{1... | collective-permute-start | bytes 1769480 | tf_op jit(solution)/shard_map/ppermute | solution.py:40
  8.1 2.7 %collective-permute-start.3 = (bf16[1,576,128]{2,1,0:T(8,128)(2,1)}, bf16[1,576,128]{2,1,0:T(8,128)(2,1)S(1)}, u32[]{:S(2)}, u32[]{:S(2)}) collective-permute-start(bf16[1,576,128]{2,1,0:T(8,128)(2,1)} %bitcast.32), channel_id=1, source_target_pairs={{0,2},{1,3},{2,0},{3,1},{4,6},{5,7},{6,4},{7,5},{8,10},{9,11},{10,... | collective-permute-start | bytes 442376 | tf_op jit(solution)/shard_map/ppermute | solution.py:62
  10.8 10.6 %collective-permute-done.3.refs_3_.b_ref = bf16[1,576,128]{2,1,0:T(8,128)(2,1)S(1)} collective-permute-done((bf16[1,576,128]{2,1,0:T(8,128)(2,1)}, bf16[1,576,128]{2,1,0:T(8,128)(2,1)S(1)}, u32[]{:S(2)}, u32[]{:S(2)}) %collective-permute-start.3) | collective-permute-done | bytes 147488 | tf_op jit(solution)/shard_map/ppermute | solution.py:62
  24.8 4.9 %collective-permute-start.5 = (bf16[128,2304]{1,0:T(8,128)(2,1)}, bf16[128,2304]{1,0:T(8,128)(2,1)}, u32[]{:S(2)}, u32[]{:S(2)}) collective-permute-start(bf16[128,2304]{1,0:T(8,128)(2,1)} %get-tuple-element.39.refs_3_.refs_4_), channel_id=1, source_target_pairs={{0,112},{16,0},{32,16},{48,32},{64,48},{80,64},{96,80},{112,96},{1... | collective-permute-start | bytes 1769480 | tf_op jit(solution)/shard_map/ppermute | solution.py:40
  30.0 10.1 %stack.117.refs_3_.a_ref = bf16[2,576,128]{2,1,0:T(8,128)(2,1)} custom-call(bf16[1,576,128]{2,1,0:T(8,128)(2,1)} %bitcast.33, bf16[1,576,128]{2,1,0:T(8,128)(2,1)} %copy-done.8, bf16[128,2304]{1,0:T(8,128)(2,1)} %get-tuple-element.38.refs_0_.refs_4_.refs_14_), custom_call_target="tpu_custom_call" | custom-call | tf_op jit(solution)/shard_map/stack/pallas_call | solution.py:106
  40.6 1.2 collective-permute-done.5.refs_1_
  41.8 2.2 %collective-permute-done.6.refs_2_ = bf16[128,2304]{1,0:T(8,128)(2,1)} collective-permute-done((bf16[128,2304]{1,0:T(8,128)(2,1)}, bf16[128,2304]{1,0:T(8,128)(2,1)}, u32[]{:S(2)}, u32[]{:S(2)}) %collective-permute-start.6) | collective-permute-done | bytes 589856 | tf_op jit(solution)/shard_map/ppermute | solution.py:44
  44.0 1.1 collective-permute-done.4.refs_0_
  45.9 1.7 collective-permute-start.9
  47.7 2.0 %collective-permute-start.7 = (bf16[128,2304]{1,0:T(8,128)(2,1)}, bf16[128,2304]{1,0:T(8,128)(2,1)S(1)}, u32[]{:S(2)}, u32[]{:S(2)}) collective-permute-start(bf16[128,2304]{1,0:T(8,128)(2,1)} %get-tuple-element.40.refs_0_.refs_2_.refs_10_), channel_id=1, source_target_pairs={{0,16},{16,32},{32,48},{48,64},{64,80},{80,96},{96,112},{112,0},{1... | collective-permute-start | bytes 1769480 | tf_op jit(solution)/shard_map/ppermute | solution.py:36
  50.4 19.0 %stack.118.refs_3_.a_ref = bf16[4,576,128]{2,1,0:T(8,128)(2,1)} custom-call(bf16[2,576,128]{2,1,0:T(8,128)(2,1)} %stack.117.refs_3_.a_ref, bf16[2,576,128]{2,1,0:T(8,128)(2,1)} %copy-done.10, bf16[128,2304]{1,0:T(8,128)(2,1)} %get-tuple-element.40.refs_0_.refs_2_.refs_10_), custom_call_target="tpu_custom_call" | custom-call | tf_op jit(solution)/shard_map/stack/pallas_call | solution.py:106
  69.4 2.4 %collective-permute-start.14 = (bf16[4,576,128]{2,1,0:T(8,128)(2,1)}, bf16[4,576,128]{2,1,0:T(8,128)(2,1)}, u32[]{:S(2)}, u32[]{:S(2)}) collective-permute-start(bf16[4,576,128]{2,1,0:T(8,128)(2,1)} %stack.118.refs_3_.a_ref), channel_id=1, source_target_pairs={{0,8},{1,9},{2,10},{3,11},{4,12},{5,13},{6,14},{7,15},{8,0},{9,1},... | collective-permute-start | bytes 1769480 | tf_op jit(solution)/shard_map/ppermute | solution.py:58
  72.9 2.4 %collective-permute-start.12 = (bf16[128,2304]{1,0:T(8,128)(2,1)}, bf16[128,2304]{1,0:T(8,128)(2,1)}, u32[]{:S(2)}, u32[]{:S(2)}) collective-permute-start(bf16[128,2304]{1,0:T(8,128)(2,1)} %get-tuple-element.43.refs_1_.refs_9_), channel_id=1, source_target_pairs={{0,112},{16,0},{32,16},{48,32},{64,48},{80,64},{96,80},{112,96},{1... | collective-permute-start | bytes 1769480 | tf_op jit(solution)/shard_map/ppermute | solution.py:40
  75.4 7.8 %collective-permute-done.14.b_ref = bf16[4,576,128]{2,1,0:T(8,128)(2,1)} collective-permute-done((bf16[4,576,128]{2,1,0:T(8,128)(2,1)}, bf16[4,576,128]{2,1,0:T(8,128)(2,1)}, u32[]{:S(2)}, u32[]{:S(2)}) %collective-permute-start.14) | collective-permute-done | bytes 589856 | tf_op jit(solution)/shard_map/ppermute | solution.py:58
  83.2 36.9 %stack.119.refs_3_.mine_ref = bf16[8,576,128]{2,1,0:T(8,128)(2,1)} custom-call(bf16[4,576,128]{2,1,0:T(8,128)(2,1)} %stack.118.refs_3_.a_ref, bf16[4,576,128]{2,1,0:T(8,128)(2,1)} %collective-permute-done.14.b_ref, bf16[128,2304]{1,0:T(8,128)(2,1)} %get-tuple-element.42.refs_0_.refs_4_.refs_6_), custom_call_target="tpu_custom_call" | custom-call | tf_op jit(solution)/shard_map/stack/pallas_call | solution.py:106
  120.2 7.6 %partial_sums.4 = (f32[3,576,128]{2,1,0:T(8,128)}, f32[3,576,128]{2,1,0:T(8,128)}) custom-call(s32[1]{0:T(128)} %bitcast.6.s_ref, bf16[576,2304]{1,0:T(8,128)(2,1)} %w_any.7, bf16[128,2304]{1,0:T(8,128)(2,1)} %get-tuple-element.41.refs_0_.refs_8_, bf16[128,2304]{1,0:T(8,128)(2,1)} %get-tuple-element.43.refs_1_.refs_9_, ...), custom_call_target="tpu_custom_call" | custom-call | flops 2038431744 | bytes 7962624 | tf_op jit(solution)/shard_map/partial_sums/pallas_call | solution.py:162
  129.0 3.8 %partial_sums.6 = (f32[1,576,128]{2,1,0:T(8,128)}, f32[1,576,128]{2,1,0:T(8,128)}) custom-call(s32[1]{0:T(128)} %bitcast.6.s_ref, bf16[576,2304]{1,0:T(8,128)(2,1)} %w_any.7, bf16[128,2304]{1,0:T(8,128)(2,1)} %get-tuple-element.50.refs_0_.refs_11_, bf16[128,2304]{1,0:T(8,128)(2,1)} %get-tuple-element.51.refs_1_.refs_13_), custom_call_target="tpu_custom_call" | custom-call | flops 679477248 | bytes 4423680 | tf_op jit(solution)/shard_map/partial_sums/pallas_call | solution.py:162
  133.0 1.7 collective-permute-done.21.refs_3_
  134.6 2.7 %collective-permute-start.17 = (bf16[128,2304]{1,0:T(8,128)(2,1)}, bf16[128,2304]{1,0:T(8,128)(2,1)}, u32[]{:S(2)}, u32[]{:S(2)}) collective-permute-start(bf16[128,2304]{1,0:T(8,128)(2,1)} %get-tuple-element.51.refs_1_.refs_13_), channel_id=1, source_target_pairs={{0,112},{16,0},{32,16},{48,32},{64,48},{80,64},{96,80},{112,96},{1... | collective-permute-start | bytes 1769480 | tf_op jit(solution)/shard_map/ppermute | solution.py:40
  137.9 2.8 %place.2 = (f32[576,128]{1,0:T(8,128)}, f32[576,128]{1,0:T(8,128)}, f32[576,128]{1,0:T(8,128)}, f32[576,128]{1,0:T(8,128)}) custom-call(s32[4]{0:T(128)} %pad_add_fusion.s_ref, f32[3,576,128]{2,1,0:T(8,128)} %get-tuple-element.46.refs_4_.refs_0_, f32[3,576,128]{2,1,0:T(8,128)} %collective-permute-done.20.refs_1_, f32[1,576,128]{2,1,0:T(8,128)} %get-tuple-element.56.refs_2_, ...), custom_call_target="tpu_custom_call" | custom-call | tf_op jit(solution)/shard_map/place/pallas_call | solution.py:200
  140.8 1.6 collective-permute-start.22
  142.3 1.6 collective-permute-done.18.refs_2_
  144.4 7.4 %partial_sums.5 = (f32[3,576,128]{2,1,0:T(8,128)}, f32[3,576,128]{2,1,0:T(8,128)}) custom-call(s32[1]{0:T(128)} %bitcast.6.s_ref, bf16[576,2304]{1,0:T(8,128)(2,1)} %w_any.7, bf16[128,2304]{1,0:T(8,128)(2,1)} %refs_0_.3, bf16[128,2304]{1,0:T(8,128)(2,1)} %get-tuple-element.37.refs_1_, bf16[128,2304]{1,0:T(8,128)(2,1)} %get-tuple-element.47.refs_2_, ...), custom_call_target="tpu_custom_call" | custom-call | flops 1698693120 | bytes 7372800 | tf_op jit(solution)/shard_map/partial_sums/pallas_call | solution.py:162
  152.6 6.3 %partial_sums.7 = (f32[2,576,128]{2,1,0:T(8,128)}, f32[2,576,128]{2,1,0:T(8,128)}) custom-call(s32[1]{0:T(128)} %bitcast.6.s_ref, bf16[576,2304]{1,0:T(8,128)(2,1)} %w_any.7, bf16[128,2304]{1,0:T(8,128)(2,1)} %get-tuple-element.52.refs_0_.refs_3_, bf16[128,2304]{1,0:T(8,128)(2,1)} %get-tuple-element.53.refs_1_.refs_5_, ...), custom_call_target="tpu_custom_call" | custom-call | flops 1019215872 | bytes 5603328 | tf_op jit(solution)/shard_map/partial_sums/pallas_call | solution.py:162
  162.4 3.4 %collective-permute-start.28 = (f32[576,128]{1,0:T(8,128)}, f32[576,128]{1,0:T(8,128)S(1)}, u32[]{:S(2)}, u32[]{:S(2)}) collective-permute-start(f32[576,128]{1,0:T(8,128)} %get-tuple-element.67), channel_id=1, source_target_pairs={{0,8},{1,9},{2,10},{3,11},{4,12},{5,13},{6,14},{7,15},{8,0},{9,1},... | collective-permute-start | bytes 884744 | tf_op jit(solution)/shard_map/ppermute | solution.py:58
  166.6 3.1 %place.3 = (f32[576,128]{1,0:T(8,128)}, f32[576,128]{1,0:T(8,128)}, f32[576,128]{1,0:T(8,128)}, f32[576,128]{1,0:T(8,128)}) custom-call(s32[5]{0:T(128)} %stack.94.s_ref, f32[3,576,128]{2,1,0:T(8,128)} %get-tuple-element.48.refs_3_.refs_0_, f32[3,576,128]{2,1,0:T(8,128)} %collective-permute-done.15.refs_1_, f32[2,576,128]{2,1,0:T(8,128)} %get-tuple-element.60.refs_2_, ...), custom_call_target="tpu_custom_call" | custom-call | tf_op jit(solution)/shard_map/place/pallas_call | solution.py:200
  169.7 1.1 collective-permute-start.25
  172.2 13.0 %weight_sums.1 = (f32[576,2304]{1,0:T(8,128)}, f32[8,128]{1,0:T(8,128)}) custom-call(s32[16]{0:T(128)} %stack.116.s_ref, bf16[8,576,128]{2,1,0:T(8,128)(2,1)} %stack.119.refs_3_.mine_ref, bf16[8,576,128]{2,1,0:T(8,128)(2,1)} %collective-permute-done.19.refs_4_.other_ref, bf16[128,2304]{1,0:T(8,128)(2,1)} %refs_0_.3, ...), custom_call_target="tpu_custom_call" | custom-call | flops 5435817984 | bytes 17104896 | tf_op jit(solution)/shard_map/weight_sums/pallas_call | solution.py:281
  187.0 2.5 %merge.1 = (f32[576,128]{1,0:T(8,128)}, f32[576,128]{1,0:T(8,128)}) custom-call(s32[1]{0:T(128)} %bitcast.s_ref, f32[576,128]{1,0:T(8,128)} %get-tuple-element.62.refs_16_.refs_0_, f32[576,128]{1,0:T(8,128)} %copy-done.12, f32[576,128]{1,0:T(8,128)} %copy-done.13, f32[576,128]{1,0:T(8,128)} %collective-permute-done.27.refs_3_, ...), custom_call_target="tpu_custom_call" | custom-call | tf_op jit(solution)/shard_map/merge/pallas_call | solution.py:224
  190.3 8.8 %collective-permute-done.29 = f32[576,128]{1,0:T(8,128)S(1)} collective-permute-done((f32[576,128]{1,0:T(8,128)}, f32[576,128]{1,0:T(8,128)S(1)}, u32[]{:S(2)}, u32[]{:S(2)}) %collective-permute-start.29) | collective-permute-done | bytes 294944 | tf_op jit(solution)/shard_map/ppermute | solution.py:62
  199.1 1.7 fusion
  (76 shorter events, 17.2 us)
Async XLA Ops:
  0.6 20.7 %collective-permute-start.2 = (bf16[128,2304]{1,0:T(8,128)(2,1)}, bf16[128,2304]{1,0:T(8,128)(2,1)S(1)}, u32[]{:S(2)}, u32[]{:S(2)}) collective-permute-start(bf16[128,2304]{1,0:T(8,128)(2,1)} %refs_0_.3), channel_id=1, source_target_pairs={{0,128},{16,144},{32,160},{48,176},{64,192},{80,208},{96,224},{112... | collective-permute-start | bytes 1769480 | tf_op jit(solution)/shard_map/ppermute | solution.py:44
  2.2 20.0 %collective-permute-start.1 = (bf16[128,2304]{1,0:T(8,128)(2,1)}, bf16[128,2304]{1,0:T(8,128)(2,1)S(1)}, u32[]{:S(2)}, u32[]{:S(2)}) collective-permute-start(bf16[128,2304]{1,0:T(8,128)(2,1)} %refs_0_.3), channel_id=1, source_target_pairs={{0,112},{16,0},{32,16},{48,32},{64,48},{80,64},{96,80},{112,96},{1... | collective-permute-start | bytes 1769480 | tf_op jit(solution)/shard_map/ppermute | solution.py:40
  8.1 15.9 %collective-permute-start = (bf16[128,2304]{1,0:T(8,128)(2,1)}, bf16[128,2304]{1,0:T(8,128)(2,1)S(1)}, u32[]{:S(2)}, u32[]{:S(2)}) collective-permute-start(bf16[128,2304]{1,0:T(8,128)(2,1)} %refs_0_.3), channel_id=1, source_target_pairs={{0,16},{16,32},{32,48},{48,64},{64,80},{80,96},{96,112},{112,0},{1... | collective-permute-start | bytes 1769480 | tf_op jit(solution)/shard_map/ppermute | solution.py:36
  8.1 13.3 %collective-permute-start.3 = (bf16[1,576,128]{2,1,0:T(8,128)(2,1)}, bf16[1,576,128]{2,1,0:T(8,128)(2,1)S(1)}, u32[]{:S(2)}, u32[]{:S(2)}) collective-permute-start(bf16[1,576,128]{2,1,0:T(8,128)(2,1)} %bitcast.32), channel_id=1, source_target_pairs={{0,2},{1,3},{2,0},{3,1},{4,6},{5,7},{6,4},{7,5},{8,10},{9,11},{10,... | collective-permute-start | bytes 442376 | tf_op jit(solution)/shard_map/ppermute | solution.py:62
  24.8 17.0 %collective-permute-start.5 = (bf16[128,2304]{1,0:T(8,128)(2,1)}, bf16[128,2304]{1,0:T(8,128)(2,1)}, u32[]{:S(2)}, u32[]{:S(2)}) collective-permute-start(bf16[128,2304]{1,0:T(8,128)(2,1)} %get-tuple-element.39.refs_3_.refs_4_), channel_id=1, source_target_pairs={{0,112},{16,0},{32,16},{48,32},{64,48},{80,64},{96,80},{112,96},{1... | collective-permute-start | bytes 1769480 | tf_op jit(solution)/shard_map/ppermute | solution.py:40
  29.8 14.2 %collective-permute-start.6 = (bf16[128,2304]{1,0:T(8,128)(2,1)}, bf16[128,2304]{1,0:T(8,128)(2,1)}, u32[]{:S(2)}, u32[]{:S(2)}) collective-permute-start(bf16[128,2304]{1,0:T(8,128)(2,1)} %get-tuple-element.38.refs_0_.refs_4_.refs_14_), channel_id=1, source_target_pairs={{0,128},{16,144},{32,160},{48,176},{64,192},{80,208},{96,224},{112... | collective-permute-start | bytes 1769480 | tf_op jit(solution)/shard_map/ppermute | solution.py:44
  30.0 15.1 %collective-permute-start.4 = (bf16[128,2304]{1,0:T(8,128)(2,1)}, bf16[128,2304]{1,0:T(8,128)(2,1)S(1)}, u32[]{:S(2)}, u32[]{:S(2)}) collective-permute-start(bf16[128,2304]{1,0:T(8,128)(2,1)} %get-tuple-element.38.refs_0_.refs_4_.refs_14_), channel_id=1, source_target_pairs={{0,16},{16,32},{32,48},{48,64},{64,80},{80,96},{96,112},{112,0},{1... | collective-permute-start | bytes 1769480 | tf_op jit(solution)/shard_map/ppermute | solution.py:36
  40.0 9.7 %collective-permute-start.10 = (bf16[2,576,128]{2,1,0:T(8,128)(2,1)}, bf16[2,576,128]{2,1,0:T(8,128)(2,1)S(1)}, u32[]{:S(2)}, u32[]{:S(2)}) collective-permute-start(bf16[2,576,128]{2,1,0:T(8,128)(2,1)} %stack.117.refs_3_.a_ref), channel_id=1, source_target_pairs={{0,4},{1,5},{2,6},{3,7},{4,0},{5,1},{6,2},{7,3},{8,12},{9,13},{10,... | collective-permute-start | bytes 884744 | tf_op jit(solution)/shard_map/ppermute | solution.py:54
  45.9 26.1 %collective-permute-start.9 = (bf16[128,2304]{1,0:T(8,128)(2,1)}, bf16[128,2304]{1,0:T(8,128)(2,1)}, u32[]{:S(2)}, u32[]{:S(2)}) collective-permute-start(bf16[128,2304]{1,0:T(8,128)(2,1)} %get-tuple-element.41.refs_0_.refs_8_), channel_id=1, source_target_pairs={{0,128},{16,144},{32,160},{48,176},{64,192},{80,208},{96,224},{112... | collective-permute-start | bytes 1769480 | tf_op jit(solution)/shard_map/ppermute | solution.py:44
  47.7 24.4 %collective-permute-start.8 = (bf16[128,2304]{1,0:T(8,128)(2,1)}, bf16[128,2304]{1,0:T(8,128)(2,1)}, u32[]{:S(2)}, u32[]{:S(2)}) collective-permute-start(bf16[128,2304]{1,0:T(8,128)(2,1)} %get-tuple-element.41.refs_0_.refs_8_), channel_id=1, source_target_pairs={{0,112},{16,0},{32,16},{48,32},{64,48},{80,64},{96,80},{112,96},{1... | collective-permute-start | bytes 1769480 | tf_op jit(solution)/shard_map/ppermute | solution.py:40
  47.7 24.4 %collective-permute-start.7 = (bf16[128,2304]{1,0:T(8,128)(2,1)}, bf16[128,2304]{1,0:T(8,128)(2,1)S(1)}, u32[]{:S(2)}, u32[]{:S(2)}) collective-permute-start(bf16[128,2304]{1,0:T(8,128)(2,1)} %get-tuple-element.40.refs_0_.refs_2_.refs_10_), channel_id=1, source_target_pairs={{0,16},{16,32},{32,48},{48,64},{64,80},{80,96},{96,112},{112,0},{1... | collective-permute-start | bytes 1769480 | tf_op jit(solution)/shard_map/ppermute | solution.py:36
  69.4 13.8 %collective-permute-start.14 = (bf16[4,576,128]{2,1,0:T(8,128)(2,1)}, bf16[4,576,128]{2,1,0:T(8,128)(2,1)}, u32[]{:S(2)}, u32[]{:S(2)}) collective-permute-start(bf16[4,576,128]{2,1,0:T(8,128)(2,1)} %stack.118.refs_3_.a_ref), channel_id=1, source_target_pairs={{0,8},{1,9},{2,10},{3,11},{4,12},{5,13},{6,14},{7,15},{8,0},{9,1},... | collective-permute-start | bytes 1769480 | tf_op jit(solution)/shard_map/ppermute | solution.py:58
  71.8 56.6 %collective-permute-start.13 = (bf16[128,2304]{1,0:T(8,128)(2,1)}, bf16[128,2304]{1,0:T(8,128)(2,1)}, u32[]{:S(2)}, u32[]{:S(2)}) collective-permute-start(bf16[128,2304]{1,0:T(8,128)(2,1)} %get-tuple-element.40.refs_0_.refs_2_.refs_10_), channel_id=1, source_target_pairs={{0,128},{16,144},{32,160},{48,176},{64,192},{80,208},{96,224},{112... | collective-permute-start | bytes 1769480 | tf_op jit(solution)/shard_map/ppermute | solution.py:44
  72.9 56.0 %collective-permute-start.12 = (bf16[128,2304]{1,0:T(8,128)(2,1)}, bf16[128,2304]{1,0:T(8,128)(2,1)}, u32[]{:S(2)}, u32[]{:S(2)}) collective-permute-start(bf16[128,2304]{1,0:T(8,128)(2,1)} %get-tuple-element.43.refs_1_.refs_9_), channel_id=1, source_target_pairs={{0,112},{16,0},{32,16},{48,32},{64,48},{80,64},{96,80},{112,96},{1... | collective-permute-start | bytes 1769480 | tf_op jit(solution)/shard_map/ppermute | solution.py:40
  75.3 53.6 %collective-permute-start.11 = (bf16[128,2304]{1,0:T(8,128)(2,1)}, bf16[128,2304]{1,0:T(8,128)(2,1)}, u32[]{:S(2)}, u32[]{:S(2)}) collective-permute-start(bf16[128,2304]{1,0:T(8,128)(2,1)} %get-tuple-element.42.refs_0_.refs_4_.refs_6_), channel_id=1, source_target_pairs={{0,16},{16,32},{32,48},{48,64},{64,80},{80,96},{96,112},{112,0},{1... | collective-permute-start | bytes 1769480 | tf_op jit(solution)/shard_map/ppermute | solution.py:36
  120.1 31.7 %collective-permute-start.19 = (bf16[8,576,128]{2,1,0:T(8,128)(2,1)}, bf16[8,576,128]{2,1,0:T(8,128)(2,1)}, u32[]{:S(2)}, u32[]{:S(2)}) collective-permute-start(bf16[8,576,128]{2,1,0:T(8,128)(2,1)} %stack.119.refs_3_.mine_ref), channel_id=1, source_target_pairs={{0,1},{1,0},{2,3},{3,2},{4,5},{5,4},{6,7},{7,6},{8,9},{9,8},{10,11... | collective-permute-start | bytes 3538952 | tf_op jit(solution)/shard_map/ppermute | solution.py:66
  127.8 10.1 %collective-permute-start.20 = (f32[3,576,128]{2,1,0:T(8,128)}, f32[3,576,128]{2,1,0:T(8,128)}, u32[]{:S(2)}, u32[]{:S(2)}) collective-permute-start(f32[3,576,128]{2,1,0:T(8,128)} %get-tuple-element.55), channel_id=1, source_target_pairs={{0,1},{1,0},{2,3},{3,2},{4,5},{5,4},{6,7},{7,6},{8,9},{9,8},{10,11... | collective-permute-start | bytes 2654216 | tf_op jit(solution)/shard_map/ppermute | solution.py:66
  128.4 15.6 %collective-permute-start.18 = (bf16[128,2304]{1,0:T(8,128)(2,1)}, bf16[128,2304]{1,0:T(8,128)(2,1)S(1)}, u32[]{:S(2)}, u32[]{:S(2)}) collective-permute-start(bf16[128,2304]{1,0:T(8,128)(2,1)} %get-tuple-element.39.refs_3_.refs_4_), channel_id=1, source_target_pairs={{0,128},{16,144},{32,160},{48,176},{64,192},{80,208},{96,224},{112... | collective-permute-start | bytes 1769480 | tf_op jit(solution)/shard_map/ppermute | solution.py:44
  132.8 1.9 collective-permute-start.21
  132.9 19.0 %collective-permute-start.16 = (bf16[128,2304]{1,0:T(8,128)(2,1)}, bf16[128,2304]{1,0:T(8,128)(2,1)}, u32[]{:S(2)}, u32[]{:S(2)}) collective-permute-start(bf16[128,2304]{1,0:T(8,128)(2,1)} %get-tuple-element.50.refs_0_.refs_11_), channel_id=1, source_target_pairs={{0,16},{16,32},{32,48},{48,64},{64,80},{80,96},{96,112},{112,0},{1... | collective-permute-start | bytes 1769480 | tf_op jit(solution)/shard_map/ppermute | solution.py:36
  134.6 3.3 %copy-start.9 = (f32[1,576,128]{2,1,0:T(8,128)}, f32[1,576,128]{2,1,0:T(8,128)S(1)}, u32[]{:S(2)}) copy-start(f32[1,576,128]{2,1,0:T(8,128)S(1)} %collective-permute-done.21.refs_3_) | copy-start | bytes 884740
  134.6 17.2 %collective-permute-start.17 = (bf16[128,2304]{1,0:T(8,128)(2,1)}, bf16[128,2304]{1,0:T(8,128)(2,1)}, u32[]{:S(2)}, u32[]{:S(2)}) collective-permute-start(bf16[128,2304]{1,0:T(8,128)(2,1)} %get-tuple-element.51.refs_1_.refs_13_), channel_id=1, source_target_pairs={{0,112},{16,0},{32,16},{48,32},{64,48},{80,64},{96,80},{112,96},{1... | collective-permute-start | bytes 1769480 | tf_op jit(solution)/shard_map/ppermute | solution.py:40
  140.8 11.1 %collective-permute-start.22 = (f32[576,128]{1,0:T(8,128)}, f32[576,128]{1,0:T(8,128)S(1)}, u32[]{:S(2)}, u32[]{:S(2)}) collective-permute-start(f32[576,128]{1,0:T(8,128)} %get-tuple-element.58), channel_id=1, source_target_pairs={{0,4},{1,5},{2,6},{3,7},{4,8},{5,9},{6,10},{7,11},{8,12},{9,13},{1... | collective-permute-start | bytes 884744 | tf_op jit(solution)/shard_map/ppermute | solution.py:58
  143.9 7.8 %copy-start.3 = (bf16[128,2304]{1,0:T(8,128)(2,1)}, bf16[128,2304]{1,0:T(8,128)(2,1)S(1)}, u32[]{:S(2)}) copy-start(bf16[128,2304]{1,0:T(8,128)(2,1)S(1)} %collective-permute-done.18.refs_2_) | copy-start | bytes 1769476
  143.9 8.6 %collective-permute-start.23 = (f32[576,128]{1,0:T(8,128)}, f32[576,128]{1,0:T(8,128)}, u32[]{:S(2)}, u32[]{:S(2)}) collective-permute-start(f32[576,128]{1,0:T(8,128)} %get-tuple-element.59), channel_id=1, source_target_pairs={{0,12},{1,13},{2,14},{3,15},{4,0},{5,1},{6,2},{7,3},{8,4},{9,5},{1... | collective-permute-start | bytes 884744 | tf_op jit(solution)/shard_map/ppermute | solution.py:58
  151.8 14.0 %collective-permute-start.15 = (f32[3,576,128]{2,1,0:T(8,128)}, f32[3,576,128]{2,1,0:T(8,128)}, u32[]{:S(2)}, u32[]{:S(2)}) collective-permute-start(f32[3,576,128]{2,1,0:T(8,128)} %get-tuple-element.49), channel_id=1, source_target_pairs={{0,1},{1,0},{2,3},{3,2},{4,5},{5,4},{6,7},{7,6},{8,9},{9,8},{10,11... | collective-permute-start | bytes 2654216 | tf_op jit(solution)/shard_map/ppermute | solution.py:66
  158.9 6.9 %collective-permute-start.24 = (f32[2,576,128]{2,1,0:T(8,128)}, f32[2,576,128]{2,1,0:T(8,128)S(1)}, u32[]{:S(2)}, u32[]{:S(2)}) collective-permute-start(f32[2,576,128]{2,1,0:T(8,128)} %get-tuple-element.61), channel_id=1, source_target_pairs={{0,1},{1,0},{2,3},{3,2},{4,5},{5,4},{6,7},{7,6},{8,9},{9,8},{10,11... | collective-permute-start | bytes 1769480 | tf_op jit(solution)/shard_map/ppermute | solution.py:66
  162.4 22.8 %collective-permute-start.28 = (f32[576,128]{1,0:T(8,128)}, f32[576,128]{1,0:T(8,128)S(1)}, u32[]{:S(2)}, u32[]{:S(2)}) collective-permute-start(f32[576,128]{1,0:T(8,128)} %get-tuple-element.67), channel_id=1, source_target_pairs={{0,8},{1,9},{2,10},{3,11},{4,12},{5,13},{6,14},{7,15},{8,0},{9,1},... | collective-permute-start | bytes 884744 | tf_op jit(solution)/shard_map/ppermute | solution.py:58
  169.7 15.5 %collective-permute-start.25 = (f32[576,128]{1,0:T(8,128)}, f32[576,128]{1,0:T(8,128)S(1)}, u32[]{:S(2)}, u32[]{:S(2)}) collective-permute-start(f32[576,128]{1,0:T(8,128)} %get-tuple-element.63.refs_17_), channel_id=1, source_target_pairs={{0,4},{1,5},{2,6},{3,7},{4,8},{5,9},{6,10},{7,11},{8,12},{9,13},{1... | collective-permute-start | bytes 884744 | tf_op jit(solution)/shard_map/ppermute | solution.py:58
  170.8 15.4 %collective-permute-start.26 = (f32[576,128]{1,0:T(8,128)}, f32[576,128]{1,0:T(8,128)S(1)}, u32[]{:S(2)}, u32[]{:S(2)}) collective-permute-start(f32[576,128]{1,0:T(8,128)} %get-tuple-element.64.refs_19_), channel_id=1, source_target_pairs={{0,12},{1,13},{2,14},{3,15},{4,0},{5,1},{6,2},{7,3},{8,4},{9,5},{1... | collective-permute-start | bytes 884744 | tf_op jit(solution)/shard_map/ppermute | solution.py:58
  171.7 14.6 %collective-permute-start.27 = (f32[576,128]{1,0:T(8,128)}, f32[576,128]{1,0:T(8,128)}, u32[]{:S(2)}, u32[]{:S(2)}) collective-permute-start(f32[576,128]{1,0:T(8,128)} %get-tuple-element.65.refs_18_), channel_id=1, source_target_pairs={{0,8},{1,9},{2,10},{3,11},{4,12},{5,13},{6,14},{7,15},{8,0},{9,1},... | collective-permute-start | bytes 884744 | tf_op jit(solution)/shard_map/ppermute | solution.py:58
  189.5 9.6 %collective-permute-start.29 = (f32[576,128]{1,0:T(8,128)}, f32[576,128]{1,0:T(8,128)S(1)}, u32[]{:S(2)}, u32[]{:S(2)}) collective-permute-start(f32[576,128]{1,0:T(8,128)} %get-tuple-element.70), channel_id=1, source_target_pairs={{0,2},{1,3},{2,0},{3,1},{4,6},{5,7},{6,4},{7,5},{8,10},{9,11},{10,... | collective-permute-start | bytes 884744 | tf_op jit(solution)/shard_map/ppermute | solution.py:62
  (12 other events, 12.1 us)

commit v4 on v3

--- a/solution.py
+++ b/solution.py
@@ -62,6 +62,25 @@
     return lax.ppermute(t, "gy", gy_pairs(0, 1, 0))
 
 
+def late_here(z, xh, c):
+    return (z + (z % 2 != c)) // 2 % 2 == xh
+
+
+def in_xh_where(t, late):
+    pairs = []
+    for xl in range(XL):
+        for z in range(Z):
+            for y in range(Y):
+                for xh in range(XH):
+                    for c in range(C):
+                        if late_here(z, xh, c) == late:
+                            at = ((xl * Z + z) * Y + y) * XH
+                            pairs.append(
+                                ((at + xh) * C + c, (at + 1 - xh) * C + c)
+                            )
+    return lax.ppermute(t, ("gx", "gy"), pairs)
+
+
 def in_core(t):
     return lax.ppermute(t, "gy", gy_pairs(0, 0, 1))
 
@@ -89,29 +108,61 @@
     )(*values, *after)
 
 
+def touch_kernel(a_ref, out_ref):
+    out_ref[...] = a_ref[...]
+
+
+def touch(a):
+    return pl.pallas_call(
+        touch_kernel,
+        out_shape=jax.ShapeDtypeStruct(a.shape, a.dtype),
+        in_specs=[VECTOR],
+        out_specs=VECTOR,
+        compiler_params=params(),
+        name="touch",
+    )(a)
+
+
 def stack_kernel(a_ref, b_ref, *refs):
-    out_ref, sem = refs[-2:]
     n = a_ref.shape[0]
-    copies = [
-        pltpu.make_async_copy(a_ref, out_ref.at[pl.ds(0, n)], sem.at[0]),
-        pltpu.make_async_copy(b_ref, out_ref.at[pl.ds(n, n)], sem.at[1]),
-    ]
-    for copy in copies:
-        copy.start()
-    for copy in copies:
-        copy.wait()
+    refs[-1][:n] = a_ref[...]
+    refs[-1][n:] = b_ref[...]
 
 
 def stack(a, b, after):
     return pl.pallas_call(
         stack_kernel,
         out_shape=jax.ShapeDtypeStruct((2 * a.shape[0],) + a.shape[1:], a.dtype),
-        in_specs=[IN_HBM] * 2 + [ANYWHERE] * len(after),
-        out_specs=IN_HBM,
-        scratch_shapes=[pltpu.SemaphoreType.DMA((2,))],
+        in_specs=[VECTOR] * 2 + [ANYWHERE] * len(after),
+        out_specs=VECTOR,
         compiler_params=params(),
         name="stack",
     )(a, b, *after)
+
+
+PARTS = 4
+
+
+def load_weight(w_any, w_ref, sem, first):
+    part = w_ref.shape[0] // PARTS
+    copies = []
+    for k in range(PARTS):
+        rows = pl.ds(k * part, part)
+        copy = pltpu.make_async_copy(
+            w_any.at[rows, :], w_ref.at[rows, :], sem.at[first + k]
+        )
+        copy.start()
+        copies.append(copy)
+    return copies
+
+
+def product(w_ref, g_ref):
+    return lax.dot_general(
+        w_ref[...],
+        g_ref[...],
+        (((1,), (1,)), ((), ())),
+        preferred_element_type=jnp.float32,
+    )
 
 
 def partial_kernel(places, s_ref, w_any, *refs):
@@ -119,37 +170,27 @@
     pieces = refs[:n]
     keep_ref, send_ref, w_ref, g_ref, sem = refs[-5:]
     rows = keep_ref.shape[2]
-    w_copy = pltpu.make_async_copy(w_any, w_ref, sem.at[n])
-    w_copy.start()
-    copies = []
+    copies = load_weight(w_any, w_ref, sem, n)
     for k in range(n):
         copy = pltpu.make_async_copy(
             pieces[k], g_ref.at[pl.ds(k * rows, rows), :], sem.at[k]
         )
         copy.start()
         copies.append(copy)
-    w_copy.wait()
-    for first in range(0, n, 2):
-        count = min(2, n - first)
-        for k in range(first, first + count):
-            copies[k].wait()
-        sums = lax.dot_general(
-            w_ref[...],
-            g_ref[first * rows : (first + 2) * rows, :],
-            (((1,), (1,)), ((), ())),
-            preferred_element_type=jnp.float32,
-        )
-        for k in range(count):
-            group, slot = places[first + k]
-            value = sums[:, k * rows : (k + 1) * rows]
-
-            @pl.when(s_ref[0] == 1 - group)
-            def _(slot=slot, value=value):
-                keep_ref[slot] = value
-
-            @pl.when(s_ref[0] == group)
-            def _(slot=slot, value=value):
-                send_ref[slot] = value
+    for copy in copies:
+        copy.wait()
+    sums = product(w_ref, g_ref)
+    for k in range(n):
+        group, slot = places[k]
+        value = sums[:, k * rows : (k + 1) * rows]
+
+        @pl.when(s_ref[0] == 1 - group)
+        def _(slot=slot, value=value):
+            keep_ref[slot] = value
+
+        @pl.when(s_ref[0] == group)
+        def _(slot=slot, value=value):
+            send_ref[slot] = value
 
 
 def partial_sums(first, weight, groups, after):
@@ -166,8 +207,8 @@
         out_specs=(VECTOR, VECTOR),
         scratch_shapes=[
             pltpu.VMEM((width, cols), jnp.bfloat16),
-            pltpu.VMEM(((n + n % 2) * rows, cols), jnp.bfloat16),
-            pltpu.SemaphoreType.DMA((n + 1,)),
+            pltpu.VMEM((n * rows, cols), jnp.bfloat16),
+            pltpu.SemaphoreType.DMA((n + PARTS,)),
         ],
         compiler_params=params(),
         cost_estimate=pl.CostEstimate(
@@ -179,6 +220,50 @@
     )(first, weight, *shards, *after)
 
 
+def chosen_kernel(n, s_ref, w_any, *refs):
+    out_ref, w_ref, g_ref, sem = refs[-4:]
+    rows = out_ref.shape[2]
+    copies = load_weight(w_any, w_ref, sem, n)
+    for k in range(n):
+        target = g_ref.at[pl.ds(k * rows, rows), :]
+        for group in range(2):
+
+            @pl.when(s_ref[0] == group)
+            def _(source=refs[group * n + k], target=target, k=k):
+                pltpu.make_async_copy(source, target, sem.at[k]).start()
+
+        copies.append(pltpu.make_async_copy(refs[k], target, sem.at[k]))
+    for copy in copies:
+        copy.wait()
+    sums = product(w_ref, g_ref)
+    for k in range(n):
+        out_ref[k] = sums[:, k * rows : (k + 1) * rows]
+
+
+def chosen_sums(which, weight, groups, after):
+    n = len(groups[0])
+    rows, cols = groups[0][0].shape
+    width = weight.shape[0]
+    return pl.pallas_call(
+        functools.partial(chosen_kernel, n),
+        out_shape=jax.ShapeDtypeStruct((n, width, rows), jnp.float32),
+        in_specs=[SCALAR] + [IN_HBM] * (1 + 2 * n) + [ANYWHERE] * len(after),
+        out_specs=VECTOR,
+        scratch_shapes=[
+            pltpu.VMEM((width, cols), jnp.bfloat16),
+            pltpu.VMEM((n * rows, cols), jnp.bfloat16),
+            pltpu.SemaphoreType.DMA((n + PARTS,)),
+        ],
+        compiler_params=params(),
+        cost_estimate=pl.CostEstimate(
+            flops=2 * width * cols * rows * n,
+            bytes_accessed=2 * cols * (width + n * rows) + 4 * n * width * rows,
+            transcendentals=0,
+        ),
+        name="chosen_sums",
+    )(which, weight, *groups[0], *groups[1], *after)
+
+
 def place_kernel(counts, s_ref, *refs):
     pairs, outs = refs[: 2 * len(counts)], refs[2 * len(counts) :]
     k = 0
@@ -207,28 +292,20 @@
     )(ways, *[a for pair in groups for a in pair])
 
 
-def merge_kernel(s_ref, *refs):
-    late, early, (keep_ref, send_ref) = refs[:Y], refs[Y : 2 * Y], refs[-2:]
-
-    def total(parts):
-        return (parts[0][...] + parts[1][...]) + (parts[2][...] + parts[3][...])
-
-    a, b = total(late), total(early)
-    here = s_ref[0] == 1
-    keep_ref[...] = jnp.where(here, a, b)
-    send_ref[...] = jnp.where(here, b, a)
-
-
-def merge(here, late, early, after):
-    out = jax.ShapeDtypeStruct(late[0].shape, jnp.float32)
+def merge_kernel(*refs):
+    a, b, c, d = refs[:Y]
+    refs[-1][...] = (a[...] + b[...]) + (c[...] + d[...])
+
+
+def merge(parts, after):
     return pl.pallas_call(
         merge_kernel,
-        out_shape=(out, out),
-        in_specs=[SCALAR] + [VECTOR] * (2 * Y) + [ANYWHERE] * len(after),
-        out_specs=(VECTOR, VECTOR),
+        out_shape=jax.ShapeDtypeStruct(parts[0].shape, jnp.float32),
+        in_specs=[VECTOR] * Y + [ANYWHERE] * len(after),
+        out_specs=VECTOR,
         compiler_params=params(),
         name="merge",
-    )(here, *late, *early, *after)
+    )(*parts, *after)
 
 
 def weight_kernel(n, tile, scale, s_ref, mine_ref, other_ref, *refs):
@@ -337,7 +414,7 @@
     def ways(*groups):
         slots = []
         for a, b in groups:
-            for k in range(max(len(a), len(b))):
+            for k in range(max(len(a), len(b), 1)):
                 way = [(where(s[k])[0] - y) % Y if k < len(s) else -1 for s in (a, b)]
                 slots.append(jnp.where(even, way[0], way[1]))
         return jnp.stack(slots).astype(jnp.int32)
@@ -349,7 +426,7 @@
         s = [h[name] for name in sends]
         h.update(zip(names, tie([up(s[0]), down(s[1]), across(s[2])], after)))
 
-    mine = inputs.T[None]
+    mine = touch(inputs.T[None])
     pair = in_xh(mine)
     phase(("u1", "d1", "gx"), ("g", "g", "g"), pair)
     pair = stack(mine, pair, [h["u1"]])
@@ -357,28 +434,34 @@
     phase(("u2", "d2", "ux1"), ("u1", "d1", "u1"), pair)
     quad = stack(pair, quad, [h["u2"]])
     column = in_y(quad, 2)
-    phase(("u3", "d3", "dx2"), ("u2", "d2", "d2"), quad)
+    first_early = (("d2", "u2"), ("u1", "ux1"))
+    keep_a, send_a = partials(*first_early)
+    got_a = in_core(send_a)
+    phase(("u3", "d3", "dx2"), ("u2", "d2", "d2"), quad, keep_a)
     column = stack(quad, column, [h["u3"]])
     other = in_core(column)
-
-    early_a = (("d2", "dx2", "u2"), ("d3", "u1", "ux1"))
-    early_b = (("ux2",), ("dx3",))
-    late_a = (("g", "gx", "u4"), ("d1", "u3"))
-    late_b = (("dx4",), ("dx1", "ux3"))
-
-    keep_a, send_a = partials(*early_a)
-    got_a = in_core(send_a)
-    phase(("u4", "dx3", "ux2"), ("u3", "dx2", "u2"), column, keep_a)
-    keep_b, send_b = partials(*early_b)
+    mixed = (("dx2", "g", "gx"), ("d3", "d1", "u3"))
+    keep_b, send_b = partials(*mixed)
+    got_b = in_core(send_b)
+    phase(("u4", "dx3", "ux2"), ("u3", "dx2", "u2"), column, got_a, keep_b)
+    last_early = (("ux2",), ("dx3",))
+    keep_c, send_c = partials(*last_early)
+    got_c = in_core(send_c)
+    none = ((), ())
     early = place(
-        ways(early_a, early_b), [(keep_a, got_a), (keep_b, in_core(send_b))]
-    )
-    keep_c, send_c = partials(*late_a)
-    got_c = in_core(send_c)
+        ways(first_early, (mixed[0][:1], mixed[1][:1]), none, none, last_early),
+        [(keep_a, got_a), (keep_b, got_b), (keep_c, got_c)],
+    )
+    phase(("ux3", "dx4", "dx1"), ("ux2", "dx3", "d1"), other, *early)
     early = over_y(early)
-    phase(("ux3", "dx4", "dx1"), ("ux2", "dx3", "d1"), keep_c, other)
-    keep_d, send_d = partials(*late_b, early[1], early[2])
-    late = place(ways(late_a, late_b), [(keep_c, got_c), (keep_d, in_core(send_d))])
+    last = (("u4", "dx4"), ("dx1", "ux3"))
+    groups = [[h[s] for s in group] for group in last]
+    got_d = in_core(chosen_sums(first, weight, groups, early[1:3]))
+    keep_d = chosen_sums(1 - first, weight, groups, [])
+    late = place(
+        ways(none, (mixed[0][1:], mixed[1][1:]), last),
+        [(keep_b, got_b), (keep_d, got_d)],
+    )
 
     def of_inputs(name):
         ty, txh, tc = where(name)
@@ -395,12 +478,12 @@
         late,
     )
 
-    here = (z + jnp.where(even, 0, 1)) // 2 % 2 == xh
-    keep, send = merge(
-        jnp.stack([here]).astype(jnp.int32), over_y(late), early, [token]
-    )
-    grad_in = (keep + in_xh(send)).astype(jnp.bfloat16)
-    return grad_in.T, grad_weight
+    early = merge(early, late)
+    got_early = in_xh_where(early, True)
+    late = merge(over_y(late), [token, got_early])
+    got_late = in_xh_where(late, False)
+    grad_in = jnp.where(late_here(z, xh, c), late + got_late, early + got_early)
+    return grad_in.astype(jnp.bfloat16).T, grad_weight
 
 
 def solution(mesh):

time: 203 us -> 164 us (0.81)
  Pallas kernels: 112 us -> 54.1 us
  waiting for transfers between devices: 37.6 us -> 55.7 us
  starting transfers between devices: 38.5 us -> 43.4 us
    pallas_call x3, Pallas kernels: 65.9 us -> 6.04 us  [stack(): pl.pallas_call(stack_kernel, out_shape=jax.ShapeDtypeStruct((2 * a.shape[...]
    ppermute x5, waiting for transfers between devices: 1.22 us -> 13.5 us  [down(): return lax.ppermute(t, 'gx', gx_pairs(0, -1))]
    pallas_call x1 -> x5, Pallas kernels: 2.55 us -> 13.2 us  [the longest x2 7.59 us: chosen_sums(): pl.pallas_call(functools.partial(chosen_kernel, n), out_shape=jax.ShapeDt...]
    ppermute x2 -> x1, waiting for transfers between devices: 19.3 us -> 8.97 us  [in_xh(): return lax.ppermute(t, 'gy', gy_pairs(0, 1, 0))]
    pallas_call x4 -> x3, Pallas kernels: 25 us -> 15.5 us  [partial_sums(): pl.pallas_call(functools.partial(partial_kernel, places), out_shape=(out,...]
    ppermute x0 -> x2, waiting for transfers between devices: none -> 8.98 us  [in_xh_where(): return lax.ppermute(t, ('gx', 'gy'), pairs)]
    ppermute x5, waiting for transfers between devices: 3.78 us -> 10.2 us  [across(): return lax.ppermute(t, 'gx', gx_pairs(1, 0))]
    ppermute x5, waiting for transfers between devices: 2.04 us -> 7.17 us  [up(): return lax.ppermute(t, 'gx', gx_pairs(0, 1))]
  transfers between devices with their start and end apart: 30 -> 31, of which waited for: 12 -> 13; matrix products, arithmetic and copies ran while one was open for 1% -> 1% of each run, Pallas kernels for 55% -> 30%
where the time goes in v4:
time: 164 us; the launch traced here: 163 us
  waiting for transfers between devices  55.7 us (34%)
  Pallas kernels  54.1 us (33%)
  starting transfers between devices  43.4 us (26%)
  local copies, waits for them, and re-layouts  7.5 us (5%)
  other arithmetic  1.77 us (1%)
    pallas_call x3, Pallas kernels, partial_sums(): pl.pallas_call(functools.partial(partial_kernel, places), out_shape=(out,...  15.5 us
    ppermute x5, waiting for transfers between devices, down(): return lax.ppermute(t, 'gx', gx_pairs(0, -1))  13.5 us
    pallas_call x1, Pallas kernels, weight_sums(): pl.pallas_call(functools.partial(weight_kernel, n, tile, scale), out_shap...  13 us
    ppermute x5, starting transfers between devices, down(): return lax.ppermute(t, 'gx', gx_pairs(0, -1))  12.8 us
    ppermute x7, starting transfers between devices, in_y(): return lax.ppermute(t, 'gy', gy_pairs(dy, 0, 0))  12 us
    ppermute x5, waiting for transfers between devices, across(): return lax.ppermute(t, 'gx', gx_pairs(1, 0))  10.2 us
    ppermute x2, waiting for transfers between devices, in_xh_where(): return lax.ppermute(t, ('gx', 'gy'), pairs)  8.98 us
    ppermute x1, waiting for transfers between devices, in_xh(): return lax.ppermute(t, 'gy', gy_pairs(0, 1, 0))  8.97 us
  transfers between devices with their start and end apart: 31, of which 13 were waited for; matrix products, arithmetic and copies ran while one was open for 1% of the time, Pallas kernels for 30%

profile of v4, /device:TPU:8, one launch (start us, length us, event | category | flops | bytes accessed | tf_op | source)
XLA Modules:
  0.0 163.4 jit_solution(3004805380513697103)
XLA Ops:
  2.2 5.9 %collective-permute-start.1 = (bf16[128,2304]{1,0:T(8,128)(2,1)}, bf16[128,2304]{1,0:T(8,128)(2,1)}, u32[]{:S(2)}, u32[]{:S(2)}) collective-permute-start(bf16[128,2304]{1,0:T(8,128)(2,1)} %refs_0_.1), channel_id=1, source_target_pairs={{0,112},{16,0},{32,16},{48,32},{64,48},{80,64},{96,80},{112,96},{1... | collective-permute-start | bytes 1769480 | tf_op jit(solution)/shard_map/ppermute | solution.py:40
  9.6 2.7 %collective-permute-start.3 = (bf16[1,576,128]{2,1,0:T(8,128)(2,1)}, bf16[1,576,128]{2,1,0:T(8,128)(2,1)S(1)}, u32[]{:S(2)}, u32[]{:S(2)}) collective-permute-start(bf16[1,576,128]{2,1,0:T(8,128)(2,1)} %touch.1.a_ref), channel_id=1, source_target_pairs={{0,2},{1,3},{2,0},{3,1},{4,6},{5,7},{6,4},{7,5},{8,10},{9,11},{10,... | collective-permute-start | bytes 442376 | tf_op jit(solution)/shard_map/ppermute | solution.py:62
  12.4 9.0 %collective-permute-done.3.refs_3_.b_ref = bf16[1,576,128]{2,1,0:T(8,128)(2,1)S(1)} collective-permute-done((bf16[1,576,128]{2,1,0:T(8,128)(2,1)}, bf16[1,576,128]{2,1,0:T(8,128)(2,1)S(1)}, u32[]{:S(2)}, u32[]{:S(2)}) %collective-permute-start.3) | collective-permute-done | bytes 147488 | tf_op jit(solution)/shard_map/ppermute | solution.py:62
  21.4 2.6 %collective-permute-done.refs_0_ = bf16[128,2304]{1,0:T(8,128)(2,1)S(1)} collective-permute-done((bf16[128,2304]{1,0:T(8,128)(2,1)}, bf16[128,2304]{1,0:T(8,128)(2,1)S(1)}, u32[]{:S(2)}, u32[]{:S(2)}) %collective-permute-start) | collective-permute-done | bytes 589856 | tf_op jit(solution)/shard_map/ppermute | solution.py:36
  24.8 3.9 %collective-permute-start.5 = (bf16[128,2304]{1,0:T(8,128)(2,1)}, bf16[128,2304]{1,0:T(8,128)(2,1)}, u32[]{:S(2)}, u32[]{:S(2)}) collective-permute-start(bf16[128,2304]{1,0:T(8,128)(2,1)} %get-tuple-element.34.refs_4_), channel_id=1, source_target_pairs={{0,112},{16,0},{32,16},{48,32},{64,48},{80,64},{96,80},{112,96},{1... | collective-permute-start | bytes 1769480 | tf_op jit(solution)/shard_map/ppermute | solution.py:40
  31.1 9.6 %collective-permute-done.5.refs_1_ = bf16[128,2304]{1,0:T(8,128)(2,1)} collective-permute-done((bf16[128,2304]{1,0:T(8,128)(2,1)}, bf16[128,2304]{1,0:T(8,128)(2,1)}, u32[]{:S(2)}, u32[]{:S(2)}) %collective-permute-start.5) | collective-permute-done | bytes 589856 | tf_op jit(solution)/shard_map/ppermute | solution.py:40
  40.7 2.2 %collective-permute-done.6.refs_2_ = bf16[128,2304]{1,0:T(8,128)(2,1)} collective-permute-done((bf16[128,2304]{1,0:T(8,128)(2,1)}, bf16[128,2304]{1,0:T(8,128)(2,1)}, u32[]{:S(2)}, u32[]{:S(2)}) %collective-permute-start.6) | collective-permute-done | bytes 589856 | tf_op jit(solution)/shard_map/ppermute | solution.py:44
  46.6 2.0 %collective-permute-start.7 = (bf16[128,2304]{1,0:T(8,128)(2,1)}, bf16[128,2304]{1,0:T(8,128)(2,1)S(1)}, u32[]{:S(2)}, u32[]{:S(2)}) collective-permute-start(bf16[128,2304]{1,0:T(8,128)(2,1)} %get-tuple-element.35.refs_0_.refs_1_.refs_10_), channel_id=1, source_target_pairs={{0,16},{16,32},{32,48},{48,64},{64,80},{80,96},{96,112},{112,0},{1... | collective-permute-start | bytes 1769480 | tf_op jit(solution)/shard_map/ppermute | solution.py:36
  49.4 1.9 %stack.116.refs_3_.a_ref = bf16[4,576,128]{2,1,0:T(8,128)(2,1)} custom-call(bf16[2,576,128]{2,1,0:T(8,128)(2,1)} %stack.115.refs_3_.a_ref, bf16[2,576,128]{2,1,0:T(8,128)(2,1)} %copy-done.11, bf16[128,2304]{1,0:T(8,128)(2,1)} %get-tuple-element.35.refs_0_.refs_1_.refs_10_), custom_call_target="tpu_custom_call" | custom-call | tf_op jit(solution)/shard_map/stack/pallas_call | solution.py:133
  51.3 2.3 %collective-permute-start.15 = (bf16[4,576,128]{2,1,0:T(8,128)(2,1)}, bf16[4,576,128]{2,1,0:T(8,128)(2,1)}, u32[]{:S(2)}, u32[]{:S(2)}) collective-permute-start(bf16[4,576,128]{2,1,0:T(8,128)(2,1)} %stack.116.refs_3_.a_ref), channel_id=1, source_target_pairs={{0,8},{1,9},{2,10},{3,11},{4,12},{5,13},{6,14},{7,15},{8,0},{9,1},... | collective-permute-start | bytes 1769480 | tf_op jit(solution)/shard_map/ppermute | solution.py:58
  53.9 5.2 %partial_sums.3 = (f32[2,576,128]{2,1,0:T(8,128)}, f32[2,576,128]{2,1,0:T(8,128)}) custom-call(s32[1]{0:T(128)} %bitcast.4.s_ref, bf16[576,2304]{1,0:T(8,128)(2,1)} %w_any.9, bf16[128,2304]{1,0:T(8,128)(2,1)} %get-tuple-element.36.refs_0_.refs_8_, bf16[128,2304]{1,0:T(8,128)(2,1)} %get-tuple-element.35.refs_0_.refs_1_.refs_10_, ...), custom_call_target="tpu_custom_call" | custom-call | flops 1358954496 | bytes 6193152 | tf_op jit(solution)/shard_map/partial_sums/pallas_call | solution.py:203
  59.0 2.4 %collective-permute-done.9.refs_2_ = bf16[128,2304]{1,0:T(8,128)(2,1)} collective-permute-done((bf16[128,2304]{1,0:T(8,128)(2,1)}, bf16[128,2304]{1,0:T(8,128)(2,1)}, u32[]{:S(2)}, u32[]{:S(2)}) %collective-permute-start.9) | collective-permute-done | bytes 589856 | tf_op jit(solution)/shard_map/ppermute | solution.py:44
  65.0 2.4 %stack.117.refs_3_.mine_ref = bf16[8,576,128]{2,1,0:T(8,128)(2,1)} custom-call(bf16[4,576,128]{2,1,0:T(8,128)(2,1)} %stack.116.refs_3_.a_ref, bf16[4,576,128]{2,1,0:T(8,128)(2,1)} %collective-permute-done.15.b_ref, bf16[128,2304]{1,0:T(8,128)(2,1)} %get-tuple-element.42.refs_5_.refs_0_.refs_6_), custom_call_target="tpu_custom_call" | custom-call | tf_op jit(solution)/shard_map/stack/pallas_call | solution.py:133
  67.4 6.5 %partial_sums.4 = (f32[3,576,128]{2,1,0:T(8,128)}, f32[3,576,128]{2,1,0:T(8,128)}) custom-call(s32[1]{0:T(128)} %bitcast.4.s_ref, bf16[576,2304]{1,0:T(8,128)(2,1)} %w_any.9, bf16[128,2304]{1,0:T(8,128)(2,1)} %get-tuple-element.39.refs_0_.refs_9_, bf16[128,2304]{1,0:T(8,128)(2,1)} %refs_0_.1, bf16[128,2304]{1,0:T(8,128)(2,1)} %get-tuple-element.40.refs_2_.refs_1_, ...), custom_call_target="tpu_custom_call" | custom-call | flops 2038431744 | bytes 7962624 | tf_op jit(solution)/shard_map/partial_sums/pallas_call | solution.py:203
  74.5 3.9 %collective-permute-done.13.refs_1_ = bf16[128,2304]{1,0:T(8,128)(2,1)} collective-permute-done((bf16[128,2304]{1,0:T(8,128)(2,1)}, bf16[128,2304]{1,0:T(8,128)(2,1)}, u32[]{:S(2)}, u32[]{:S(2)}) %collective-permute-start.13) | collective-permute-done | bytes 589856 | tf_op jit(solution)/shard_map/ppermute | solution.py:40
  80.5 3.8 %partial_sums.5 = (f32[1,576,128]{2,1,0:T(8,128)}, f32[1,576,128]{2,1,0:T(8,128)}) custom-call(s32[1]{0:T(128)} %bitcast.4.s_ref, bf16[576,2304]{1,0:T(8,128)(2,1)} %w_any.9, bf16[128,2304]{1,0:T(8,128)(2,1)} %get-tuple-element.47.refs_0_.refs_11_, bf16[128,2304]{1,0:T(8,128)(2,1)} %get-tuple-element.48.refs_1_.refs_13_), custom_call_target="tpu_custom_call" | custom-call | flops 679477248 | bytes 4423680 | tf_op jit(solution)/shard_map/partial_sums/pallas_call | solution.py:203
  86.7 2.7 %collective-permute-start.18 = (bf16[128,2304]{1,0:T(8,128)(2,1)}, bf16[128,2304]{1,0:T(8,128)(2,1)}, u32[]{:S(2)}, u32[]{:S(2)}) collective-permute-start(bf16[128,2304]{1,0:T(8,128)(2,1)} %get-tuple-element.48.refs_1_.refs_13_), channel_id=1, source_target_pairs={{0,112},{16,0},{32,16},{48,32},{64,48},{80,64},{96,80},{112,96},{1... | collective-permute-start | bytes 1769480 | tf_op jit(solution)/shard_map/ppermute | solution.py:40
  90.0 3.3 %place.2 = (f32[576,128]{1,0:T(8,128)}, f32[576,128]{1,0:T(8,128)}, f32[576,128]{1,0:T(8,128)}, f32[576,128]{1,0:T(8,128)}) custom-call(s32[6]{0:T(128)} %stack.97.s_ref, f32[2,576,128]{2,1,0:T(8,128)} %get-tuple-element.38.refs_4_.refs_0_, f32[2,576,128]{2,1,0:T(8,128)} %collective-permute-done.16.refs_4_.refs_1_, ...), custom_call_target="tpu_custom_call" | custom-call | tf_op jit(solution)/shard_map/place/pallas_call | solution.py:285
  94.8 5.5 %collective-permute-done.19.refs_2_ = bf16[128,2304]{1,0:T(8,128)(2,1)S(1)} collective-permute-done((bf16[128,2304]{1,0:T(8,128)(2,1)}, bf16[128,2304]{1,0:T(8,128)(2,1)S(1)}, u32[]{:S(2)}, u32[]{:S(2)}) %collective-permute-start.19) | collective-permute-done | bytes 589856 | tf_op jit(solution)/shard_map/ppermute | solution.py:44
  100.8 2.2 %collective-permute-done.17.refs_0_ = bf16[128,2304]{1,0:T(8,128)(2,1)} collective-permute-done((bf16[128,2304]{1,0:T(8,128)(2,1)}, bf16[128,2304]{1,0:T(8,128)(2,1)}, u32[]{:S(2)}, u32[]{:S(2)}) %collective-permute-start.17) | collective-permute-done | bytes 589856 | tf_op jit(solution)/shard_map/ppermute | solution.py:36
  103.1 6.3 %collective-permute-done.23.refs_5_.refs_2_ = f32[576,128]{1,0:T(8,128)} collective-permute-done((f32[576,128]{1,0:T(8,128)}, f32[576,128]{1,0:T(8,128)}, u32[]{:S(2)}, u32[]{:S(2)}) %collective-permute-start.23) | collective-permute-done | bytes 294944 | tf_op jit(solution)/shard_map/ppermute | solution.py:58
  109.3 3.8 %chosen_sums.3 = f32[2,576,128]{2,1,0:T(8,128)} custom-call(s32[1]{0:T(128)} %bitcast.4.s_ref, bf16[576,2304]{1,0:T(8,128)(2,1)} %w_any.9, bf16[128,2304]{1,0:T(8,128)(2,1)} %get-tuple-element.46.refs_0_.refs_2_, bf16[128,2304]{1,0:T(8,128)(2,1)} %get-tuple-element.55.refs_1_.refs_3_, bf16[128,2304]{1,0:T(8,128)(2,1)} %get-tuple-element.56.refs_2_.refs_5_, ...), custom_call_target="tpu_custom_call" | custom-call | flops 679477248 | bytes 4423680 | tf_op jit(solution)/shard_map/chosen_sums/pallas_call | solution.py:247
  113.2 3.8 %collective-permute-start.28 = (f32[576,128]{1,0:T(8,128)}, f32[576,128]{1,0:T(8,128)}, u32[]{:S(2)}, u32[]{:S(2)}) collective-permute-start(f32[576,128]{1,0:T(8,128)} %get-tuple-element.53.refs_6_), channel_id=1, source_target_pairs={{0,8},{1,9},{2,10},{3,11},{4,12},{5,13},{6,14},{7,15},{8,0},{9,1},... | collective-permute-start | bytes 884744 | tf_op jit(solution)/shard_map/ppermute | solution.py:58
  118.3 3.8 %chosen_sums.2.refs_2_ = f32[2,576,128]{2,1,0:T(8,128)} custom-call(s32[1]{0:T(128)S(6)} %sub.250.s_ref, bf16[576,2304]{1,0:T(8,128)(2,1)} %w_any.9, bf16[128,2304]{1,0:T(8,128)(2,1)} %get-tuple-element.46.refs_0_.refs_2_, bf16[128,2304]{1,0:T(8,128)(2,1)} %get-tuple-element.55.refs_1_.refs_3_, bf16[128,2304]{1,0:T(8,128)(2,1)} %get-tuple-element.56.refs_2_.refs_5_, ...), custom_call_target="tpu_custom_call" | custom-call | flops 679477248 | bytes 4423680 | tf_op jit(solution)/shard_map/chosen_sums/pallas_call | solution.py:247
  122.9 3.1 %place.3 = (f32[576,128]{1,0:T(8,128)}, f32[576,128]{1,0:T(8,128)}, f32[576,128]{1,0:T(8,128)}, f32[576,128]{1,0:T(8,128)}) custom-call(s32[5]{0:T(128)} %stack.92.s_ref, f32[3,576,128]{2,1,0:T(8,128)} %get-tuple-element.43.refs_5_.refs_2_.refs_0_, f32[3,576,128]{2,1,0:T(8,128)} %collective-permute-done.11.refs_3_.refs_1_, ...), custom_call_target="tpu_custom_call" | custom-call | tf_op jit(solution)/shard_map/place/pallas_call | solution.py:285
  126.0 2.0 %collective-permute-start.26 = (f32[576,128]{1,0:T(8,128)}, f32[576,128]{1,0:T(8,128)}, u32[]{:S(2)}, u32[]{:S(2)}) collective-permute-start(f32[576,128]{1,0:T(8,128)} %get-tuple-element.60.refs_19_.refs_7_), channel_id=1, source_target_pairs={{0,12},{1,13},{2,14},{3,15},{4,0},{5,1},{6,2},{7,3},{8,4},{9,5},{1... | collective-permute-start | bytes 884744 | tf_op jit(solution)/shard_map/ppermute | solution.py:58
  128.0 1.8 %collective-permute-start.27 = (f32[576,128]{1,0:T(8,128)}, f32[576,128]{1,0:T(8,128)}, u32[]{:S(2)}, u32[]{:S(2)}) collective-permute-start(f32[576,128]{1,0:T(8,128)} %get-tuple-element.61.refs_18_.refs_6_), channel_id=1, source_target_pairs={{0,8},{1,9},{2,10},{3,11},{4,12},{5,13},{6,14},{7,15},{8,0},{9,1},... | collective-permute-start | bytes 884744 | tf_op jit(solution)/shard_map/ppermute | solution.py:58
  129.9 2.0 %merge.2 = f32[576,128]{1,0:T(8,128)} custom-call(f32[576,128]{1,0:T(8,128)} %get-tuple-element.51.refs_4_.refs_0_, f32[576,128]{1,0:T(8,128)} %copy-done.5, f32[576,128]{1,0:T(8,128)} %collective-permute-done.23.refs_5_.refs_2_, f32[576,128]{1,0:T(8,128)} %collective-permute-done.28.refs_3_, f32[576,128]{1,0:T(8,128)} %get-tuple-element.58.refs_16_.refs_4_.refs_0_, ...), custom_call_target="tpu_custom_call" | custom-call | tf_op jit(solution)/shard_map/merge/pallas_call | solution.py:301
  131.9 3.6 %collective-permute-start.29 = (f32[576,128]{1,0:T(8,128)}, f32[576,128]{1,0:T(8,128)S(1)}, u32[]{:S(2)}, u32[]{:S(2)}) collective-permute-start(f32[576,128]{1,0:T(8,128)} %merge.2), channel_id=1, source_target_pairs={{0,2},{1,3},{4,6},{5,7},{8,10},{9,11},{12,14},{13,15},{17,19},{18,... | collective-permute-start | bytes 884744 | tf_op jit(solution)/shard_map/ppermute | solution.py:81
  135.5 13.0 %weight_sums.1 = (f32[576,2304]{1,0:T(8,128)}, f32[8,128]{1,0:T(8,128)}) custom-call(s32[16]{0:T(128)} %stack.114.s_ref, bf16[8,576,128]{2,1,0:T(8,128)(2,1)} %stack.117.refs_3_.mine_ref, bf16[8,576,128]{2,1,0:T(8,128)(2,1)} %collective-permute-done.20.refs_3_.other_ref, bf16[128,2304]{1,0:T(8,128)(2,1)} %refs_0_.1, ...), custom_call_target="tpu_custom_call" | custom-call | flops 5435817984 | bytes 17104896 | tf_op jit(solution)/shard_map/weight_sums/pallas_call | solution.py:358
  149.3 2.0 %merge.3 = f32[576,128]{1,0:T(8,128)} custom-call(f32[576,128]{1,0:T(8,128)} %get-tuple-element.58.refs_16_.refs_4_.refs_0_, f32[576,128]{1,0:T(8,128)} %copy-done.10, f32[576,128]{1,0:T(8,128)} %collective-permute-done.26.refs_2_, f32[576,128]{1,0:T(8,128)} %collective-permute-done.27.refs_3_, f32[8,128]{1,0:T(8,128)} %get-tuple-element.62.refs_4_, ...), custom_call_target="tpu_custom_call" | custom-call | tf_op jit(solution)/shard_map/merge/pallas_call | solution.py:301
  152.6 9.0 %collective-permute-done.30 = f32[576,128]{1,0:T(8,128)S(1)} collective-permute-done((f32[576,128]{1,0:T(8,128)}, f32[576,128]{1,0:T(8,128)S(1)}, u32[]{:S(2)}, u32[]{:S(2)}) %collective-permute-start.30) | collective-permute-done | bytes 294944 | tf_op jit(solution)/shard_map/ppermute | solution.py:81
  (79 shorter events, 28.2 us)
Async XLA Ops:
  0.6 20.7 %collective-permute-start.2 = (bf16[128,2304]{1,0:T(8,128)(2,1)}, bf16[128,2304]{1,0:T(8,128)(2,1)}, u32[]{:S(2)}, u32[]{:S(2)}) collective-permute-start(bf16[128,2304]{1,0:T(8,128)(2,1)} %refs_0_.1), channel_id=1, source_target_pairs={{0,128},{16,144},{32,160},{48,176},{64,192},{80,208},{96,224},{112... | collective-permute-start | bytes 1769480 | tf_op jit(solution)/shard_map/ppermute | solution.py:44
  2.2 19.2 %collective-permute-start.1 = (bf16[128,2304]{1,0:T(8,128)(2,1)}, bf16[128,2304]{1,0:T(8,128)(2,1)}, u32[]{:S(2)}, u32[]{:S(2)}) collective-permute-start(bf16[128,2304]{1,0:T(8,128)(2,1)} %refs_0_.1), channel_id=1, source_target_pairs={{0,112},{16,0},{32,16},{48,32},{64,48},{80,64},{96,80},{112,96},{1... | collective-permute-start | bytes 1769480 | tf_op jit(solution)/shard_map/ppermute | solution.py:40
  8.1 15.9 %collective-permute-start = (bf16[128,2304]{1,0:T(8,128)(2,1)}, bf16[128,2304]{1,0:T(8,128)(2,1)S(1)}, u32[]{:S(2)}, u32[]{:S(2)}) collective-permute-start(bf16[128,2304]{1,0:T(8,128)(2,1)} %refs_0_.1), channel_id=1, source_target_pairs={{0,16},{16,32},{32,48},{48,64},{64,80},{80,96},{96,112},{112,0},{1... | collective-permute-start | bytes 1769480 | tf_op jit(solution)/shard_map/ppermute | solution.py:36
  9.6 11.7 %collective-permute-start.3 = (bf16[1,576,128]{2,1,0:T(8,128)(2,1)}, bf16[1,576,128]{2,1,0:T(8,128)(2,1)S(1)}, u32[]{:S(2)}, u32[]{:S(2)}) collective-permute-start(bf16[1,576,128]{2,1,0:T(8,128)(2,1)} %touch.1.a_ref), channel_id=1, source_target_pairs={{0,2},{1,3},{2,0},{3,1},{4,6},{5,7},{6,4},{7,5},{8,10},{9,11},{10,... | collective-permute-start | bytes 442376 | tf_op jit(solution)/shard_map/ppermute | solution.py:62
  24.8 15.9 %collective-permute-start.5 = (bf16[128,2304]{1,0:T(8,128)(2,1)}, bf16[128,2304]{1,0:T(8,128)(2,1)}, u32[]{:S(2)}, u32[]{:S(2)}) collective-permute-start(bf16[128,2304]{1,0:T(8,128)(2,1)} %get-tuple-element.34.refs_4_), channel_id=1, source_target_pairs={{0,112},{16,0},{32,16},{48,32},{64,48},{80,64},{96,80},{112,96},{1... | collective-permute-start | bytes 1769480 | tf_op jit(solution)/shard_map/ppermute | solution.py:40
  28.7 14.2 %collective-permute-start.6 = (bf16[128,2304]{1,0:T(8,128)(2,1)}, bf16[128,2304]{1,0:T(8,128)(2,1)}, u32[]{:S(2)}, u32[]{:S(2)}) collective-permute-start(bf16[128,2304]{1,0:T(8,128)(2,1)} %get-tuple-element.33.refs_0_.refs_2_.refs_14_), channel_id=1, source_target_pairs={{0,128},{16,144},{32,160},{48,176},{64,192},{80,208},{96,224},{112... | collective-permute-start | bytes 1769480 | tf_op jit(solution)/shard_map/ppermute | solution.py:44
  28.9 15.1 %collective-permute-start.4 = (bf16[128,2304]{1,0:T(8,128)(2,1)}, bf16[128,2304]{1,0:T(8,128)(2,1)S(1)}, u32[]{:S(2)}, u32[]{:S(2)}) collective-permute-start(bf16[128,2304]{1,0:T(8,128)(2,1)} %get-tuple-element.33.refs_0_.refs_2_.refs_14_), channel_id=1, source_target_pairs={{0,16},{16,32},{32,48},{48,64},{64,80},{80,96},{96,112},{112,0},{1... | collective-permute-start | bytes 1769480 | tf_op jit(solution)/shard_map/ppermute | solution.py:36
  30.7 18.0 %collective-permute-start.10 = (bf16[2,576,128]{2,1,0:T(8,128)(2,1)}, bf16[2,576,128]{2,1,0:T(8,128)(2,1)S(1)}, u32[]{:S(2)}, u32[]{:S(2)}) collective-permute-start(bf16[2,576,128]{2,1,0:T(8,128)(2,1)} %stack.115.refs_3_.a_ref), channel_id=1, source_target_pairs={{0,4},{1,5},{2,6},{3,7},{4,0},{5,1},{6,2},{7,3},{8,12},{9,13},{10,... | collective-permute-start | bytes 884744 | tf_op jit(solution)/shard_map/ppermute | solution.py:54
  44.9 16.6 %collective-permute-start.9 = (bf16[128,2304]{1,0:T(8,128)(2,1)}, bf16[128,2304]{1,0:T(8,128)(2,1)}, u32[]{:S(2)}, u32[]{:S(2)}) collective-permute-start(bf16[128,2304]{1,0:T(8,128)(2,1)} %get-tuple-element.36.refs_0_.refs_8_), channel_id=1, source_target_pairs={{0,128},{16,144},{32,160},{48,176},{64,192},{80,208},{96,224},{112... | collective-permute-start | bytes 1769480 | tf_op jit(solution)/shard_map/ppermute | solution.py:44
  46.6 14.8 %collective-permute-start.8 = (bf16[128,2304]{1,0:T(8,128)(2,1)}, bf16[128,2304]{1,0:T(8,128)(2,1)}, u32[]{:S(2)}, u32[]{:S(2)}) collective-permute-start(bf16[128,2304]{1,0:T(8,128)(2,1)} %get-tuple-element.36.refs_0_.refs_8_), channel_id=1, source_target_pairs={{0,112},{16,0},{32,16},{48,32},{64,48},{80,64},{96,80},{112,96},{1... | collective-permute-start | bytes 1769480 | tf_op jit(solution)/shard_map/ppermute | solution.py:40
  46.6 14.8 %collective-permute-start.7 = (bf16[128,2304]{1,0:T(8,128)(2,1)}, bf16[128,2304]{1,0:T(8,128)(2,1)S(1)}, u32[]{:S(2)}, u32[]{:S(2)}) collective-permute-start(bf16[128,2304]{1,0:T(8,128)(2,1)} %get-tuple-element.35.refs_0_.refs_1_.refs_10_), channel_id=1, source_target_pairs={{0,16},{16,32},{32,48},{48,64},{64,80},{80,96},{96,112},{112,0},{1... | collective-permute-start | bytes 1769480 | tf_op jit(solution)/shard_map/ppermute | solution.py:36
  51.3 13.7 %collective-permute-start.15 = (bf16[4,576,128]{2,1,0:T(8,128)(2,1)}, bf16[4,576,128]{2,1,0:T(8,128)(2,1)}, u32[]{:S(2)}, u32[]{:S(2)}) collective-permute-start(bf16[4,576,128]{2,1,0:T(8,128)(2,1)} %stack.116.refs_3_.a_ref), channel_id=1, source_target_pairs={{0,8},{1,9},{2,10},{3,11},{4,12},{5,13},{6,14},{7,15},{8,0},{9,1},... | collective-permute-start | bytes 1769480 | tf_op jit(solution)/shard_map/ppermute | solution.py:58
  53.6 20.3 %collective-permute-start.14 = (bf16[128,2304]{1,0:T(8,128)(2,1)}, bf16[128,2304]{1,0:T(8,128)(2,1)}, u32[]{:S(2)}, u32[]{:S(2)}) collective-permute-start(bf16[128,2304]{1,0:T(8,128)(2,1)} %get-tuple-element.35.refs_0_.refs_1_.refs_10_), channel_id=1, source_target_pairs={{0,128},{16,144},{32,160},{48,176},{64,192},{80,208},{96,224},{112... | collective-permute-start | bytes 1769480 | tf_op jit(solution)/shard_map/ppermute | solution.py:44
  61.5 13.0 %collective-permute-start.16 = (f32[2,576,128]{2,1,0:T(8,128)}, f32[2,576,128]{2,1,0:T(8,128)}, u32[]{:S(2)}, u32[]{:S(2)}) collective-permute-start(f32[2,576,128]{2,1,0:T(8,128)} %get-tuple-element.45), channel_id=1, source_target_pairs={{0,1},{1,0},{2,3},{3,2},{4,5},{5,4},{6,7},{7,6},{8,9},{9,8},{10,11... | collective-permute-start | bytes 1769480 | tf_op jit(solution)/shard_map/ppermute | solution.py:85
  62.3 16.1 %collective-permute-start.13 = (bf16[128,2304]{1,0:T(8,128)(2,1)}, bf16[128,2304]{1,0:T(8,128)(2,1)}, u32[]{:S(2)}, u32[]{:S(2)}) collective-permute-start(bf16[128,2304]{1,0:T(8,128)(2,1)} %get-tuple-element.39.refs_0_.refs_9_), channel_id=1, source_target_pairs={{0,112},{16,0},{32,16},{48,32},{64,48},{80,64},{96,80},{112,96},{1... | collective-permute-start | bytes 1769480 | tf_op jit(solution)/shard_map/ppermute | solution.py:40
  62.7 16.9 %collective-permute-start.12 = (bf16[128,2304]{1,0:T(8,128)(2,1)}, bf16[128,2304]{1,0:T(8,128)(2,1)S(1)}, u32[]{:S(2)}, u32[]{:S(2)}) collective-permute-start(bf16[128,2304]{1,0:T(8,128)(2,1)} %get-tuple-element.42.refs_5_.refs_0_.refs_6_), channel_id=1, source_target_pairs={{0,16},{16,32},{32,48},{48,64},{64,80},{80,96},{96,112},{112,0},{1... | collective-permute-start | bytes 1769480 | tf_op jit(solution)/shard_map/ppermute | solution.py:36
  67.4 33.4 %collective-permute-start.20 = (bf16[8,576,128]{2,1,0:T(8,128)(2,1)}, bf16[8,576,128]{2,1,0:T(8,128)(2,1)}, u32[]{:S(2)}, u32[]{:S(2)}) collective-permute-start(bf16[8,576,128]{2,1,0:T(8,128)(2,1)} %stack.117.refs_3_.mine_ref), channel_id=1, source_target_pairs={{0,1},{1,0},{2,3},{3,2},{4,5},{5,4},{6,7},{7,6},{8,9},{9,8},{10,11... | collective-permute-start | bytes 3538952 | tf_op jit(solution)/shard_map/ppermute | solution.py:85
  73.9 16.0 %collective-permute-start.11 = (f32[3,576,128]{2,1,0:T(8,128)}, f32[3,576,128]{2,1,0:T(8,128)}, u32[]{:S(2)}, u32[]{:S(2)}) collective-permute-start(f32[3,576,128]{2,1,0:T(8,128)} %get-tuple-element.44), channel_id=1, source_target_pairs={{0,1},{1,0},{2,3},{3,2},{4,5},{5,4},{6,7},{7,6},{8,9},{9,8},{10,11... | collective-permute-start | bytes 2654216 | tf_op jit(solution)/shard_map/ppermute | solution.py:85
  84.3 2.4 %collective-permute-start.21 = (f32[1,576,128]{2,1,0:T(8,128)}, f32[1,576,128]{2,1,0:T(8,128)S(1)}, u32[]{:S(2)}, u32[]{:S(2)}) collective-permute-start(f32[1,576,128]{2,1,0:T(8,128)} %get-tuple-element.50), channel_id=1, source_target_pairs={{0,1},{1,0},{2,3},{3,2},{4,5},{5,4},{6,7},{7,6},{8,9},{9,8},{10,11... | collective-permute-start | bytes 884744 | tf_op jit(solution)/shard_map/ppermute | solution.py:85
  84.4 16.0 %collective-permute-start.19 = (bf16[128,2304]{1,0:T(8,128)(2,1)}, bf16[128,2304]{1,0:T(8,128)(2,1)S(1)}, u32[]{:S(2)}, u32[]{:S(2)}) collective-permute-start(bf16[128,2304]{1,0:T(8,128)(2,1)} %get-tuple-element.34.refs_4_), channel_id=1, source_target_pairs={{0,128},{16,144},{32,160},{48,176},{64,192},{80,208},{96,224},{112... | collective-permute-start | bytes 1769480 | tf_op jit(solution)/shard_map/ppermute | solution.py:44
  86.1 16.9 %collective-permute-start.17 = (bf16[128,2304]{1,0:T(8,128)(2,1)}, bf16[128,2304]{1,0:T(8,128)(2,1)}, u32[]{:S(2)}, u32[]{:S(2)}) collective-permute-start(bf16[128,2304]{1,0:T(8,128)(2,1)} %get-tuple-element.47.refs_0_.refs_11_), channel_id=1, source_target_pairs={{0,16},{16,32},{32,48},{48,64},{64,80},{80,96},{96,112},{112,0},{1... | collective-permute-start | bytes 1769480 | tf_op jit(solution)/shard_map/ppermute | solution.py:36
  86.7 16.4 %collective-permute-start.18 = (bf16[128,2304]{1,0:T(8,128)(2,1)}, bf16[128,2304]{1,0:T(8,128)(2,1)}, u32[]{:S(2)}, u32[]{:S(2)}) collective-permute-start(bf16[128,2304]{1,0:T(8,128)(2,1)} %get-tuple-element.48.refs_1_.refs_13_), channel_id=1, source_target_pairs={{0,112},{16,0},{32,16},{48,32},{64,48},{80,64},{96,80},{112,96},{1... | collective-permute-start | bytes 1769480 | tf_op jit(solution)/shard_map/ppermute | solution.py:40
  93.3 9.8 %collective-permute-start.22 = (f32[576,128]{1,0:T(8,128)}, f32[576,128]{1,0:T(8,128)S(1)}, u32[]{:S(2)}, u32[]{:S(2)}) collective-permute-start(f32[576,128]{1,0:T(8,128)} %get-tuple-element.52.refs_5_), channel_id=1, source_target_pairs={{0,4},{1,5},{2,6},{3,7},{4,8},{5,9},{6,10},{7,11},{8,12},{9,13},{1... | collective-permute-start | bytes 884744 | tf_op jit(solution)/shard_map/ppermute | solution.py:58
  100.4 9.0 %collective-permute-start.23 = (f32[576,128]{1,0:T(8,128)}, f32[576,128]{1,0:T(8,128)}, u32[]{:S(2)}, u32[]{:S(2)}) collective-permute-start(f32[576,128]{1,0:T(8,128)} %get-tuple-element.54.refs_7_), channel_id=1, source_target_pairs={{0,12},{1,13},{2,14},{3,15},{4,0},{5,1},{6,2},{7,3},{8,4},{9,5},{1... | collective-permute-start | bytes 884744 | tf_op jit(solution)/shard_map/ppermute | solution.py:58
  113.1 9.0 %collective-permute-start.24 = (f32[2,576,128]{2,1,0:T(8,128)}, f32[2,576,128]{2,1,0:T(8,128)S(1)}, u32[]{:S(2)}, u32[]{:S(2)}) collective-permute-start(f32[2,576,128]{2,1,0:T(8,128)} %chosen_sums.3), channel_id=1, source_target_pairs={{0,1},{1,0},{2,3},{3,2},{4,5},{5,4},{6,7},{7,6},{8,9},{9,8},{10,11... | collective-permute-start | bytes 1769480 | tf_op jit(solution)/shard_map/ppermute | solution.py:85
  113.2 16.6 %collective-permute-start.28 = (f32[576,128]{1,0:T(8,128)}, f32[576,128]{1,0:T(8,128)}, u32[]{:S(2)}, u32[]{:S(2)}) collective-permute-start(f32[576,128]{1,0:T(8,128)} %get-tuple-element.53.refs_6_), channel_id=1, source_target_pairs={{0,8},{1,9},{2,10},{3,11},{4,12},{5,13},{6,14},{7,15},{8,0},{9,1},... | collective-permute-start | bytes 884744 | tf_op jit(solution)/shard_map/ppermute | solution.py:58
  126.0 22.5 %collective-permute-start.25 = (f32[576,128]{1,0:T(8,128)}, f32[576,128]{1,0:T(8,128)S(1)}, u32[]{:S(2)}, u32[]{:S(2)}) collective-permute-start(f32[576,128]{1,0:T(8,128)} %get-tuple-element.59.refs_17_.refs_5_), channel_id=1, source_target_pairs={{0,4},{1,5},{2,6},{3,7},{4,8},{5,9},{6,10},{7,11},{8,12},{9,13},{1... | collective-permute-start | bytes 884744 | tf_op jit(solution)/shard_map/ppermute | solution.py:58
  126.0 22.5 %collective-permute-start.26 = (f32[576,128]{1,0:T(8,128)}, f32[576,128]{1,0:T(8,128)}, u32[]{:S(2)}, u32[]{:S(2)}) collective-permute-start(f32[576,128]{1,0:T(8,128)} %get-tuple-element.60.refs_19_.refs_7_), channel_id=1, source_target_pairs={{0,12},{1,13},{2,14},{3,15},{4,0},{5,1},{6,2},{7,3},{8,4},{9,5},{1... | collective-permute-start | bytes 884744 | tf_op jit(solution)/shard_map/ppermute | solution.py:58
  128.0 20.5 %collective-permute-start.27 = (f32[576,128]{1,0:T(8,128)}, f32[576,128]{1,0:T(8,128)}, u32[]{:S(2)}, u32[]{:S(2)}) collective-permute-start(f32[576,128]{1,0:T(8,128)} %get-tuple-element.61.refs_18_.refs_6_), channel_id=1, source_target_pairs={{0,8},{1,9},{2,10},{3,11},{4,12},{5,13},{6,14},{7,15},{8,0},{9,1},... | collective-permute-start | bytes 884744 | tf_op jit(solution)/shard_map/ppermute | solution.py:58
  131.9 29.7 %copy-start.7 = (f32[576,128]{1,0:T(8,128)S(1)}, f32[576,128]{1,0:T(8,128)}, u32[]{:S(2)}) copy-start(f32[576,128]{1,0:T(8,128)} %merge.2) | copy-start | bytes 884740
  131.9 16.6 %collective-permute-start.29 = (f32[576,128]{1,0:T(8,128)}, f32[576,128]{1,0:T(8,128)S(1)}, u32[]{:S(2)}, u32[]{:S(2)}) collective-permute-start(f32[576,128]{1,0:T(8,128)} %merge.2), channel_id=1, source_target_pairs={{0,2},{1,3},{4,6},{5,7},{8,10},{9,11},{12,14},{13,15},{17,19},{18,... | collective-permute-start | bytes 884744 | tf_op jit(solution)/shard_map/ppermute | solution.py:81
  151.3 10.3 %collective-permute-start.30 = (f32[576,128]{1,0:T(8,128)}, f32[576,128]{1,0:T(8,128)S(1)}, u32[]{:S(2)}, u32[]{:S(2)}) collective-permute-start(f32[576,128]{1,0:T(8,128)} %merge.3), channel_id=1, source_target_pairs={{2,0},{3,1},{6,4},{7,5},{10,8},{11,9},{14,12},{15,13},{16,18},{19,... | collective-permute-start | bytes 884744 | tf_op jit(solution)/shard_map/ppermute | solution.py:81
  (12 other events, 21.3 us)

commit v5 on v4

--- a/solution.py
+++ b/solution.py
@@ -10,6 +10,8 @@
 XL, Z = 2, 8
 Y, XH, C = 4, 2, 2
 VMEM_LIMIT = 63 << 20
+TAIL_LIMIT = 32 << 20
+NO_COST = pl.CostEstimate(flops=1, bytes_accessed=1, transcendentals=0)
 
 
 def gx_pairs(dxl, dz):
@@ -66,21 +68,6 @@
     return (z + (z % 2 != c)) // 2 % 2 == xh
 
 
-def in_xh_where(t, late):
-    pairs = []
-    for xl in range(XL):
-        for z in range(Z):
-            for y in range(Y):
-                for xh in range(XH):
-                    for c in range(C):
-                        if late_here(z, xh, c) == late:
-                            at = ((xl * Z + z) * Y + y) * XH
-                            pairs.append(
-                                ((at + xh) * C + c, (at + 1 - xh) * C + c)
-                            )
-    return lax.ppermute(t, ("gx", "gy"), pairs)
-
-
 def in_core(t):
     return lax.ppermute(t, "gy", gy_pairs(0, 0, 1))
 
@@ -91,19 +78,25 @@
 SCALAR = pl.BlockSpec(memory_space=pltpu.SMEM)
 
 
-def params():
-    return pltpu.CompilerParams(vmem_limit_bytes=VMEM_LIMIT)
+def params(limit=VMEM_LIMIT):
+    return pltpu.CompilerParams(vmem_limit_bytes=limit)
+
+
+def tie_kernel(*refs):
+    refs[-1][...] = jnp.zeros_like(refs[-1])
 
 
 def tie(values, after):
     n = len(values)
     return pl.pallas_call(
-        lambda *refs: None,
-        out_shape=[jax.ShapeDtypeStruct(v.shape, v.dtype) for v in values],
+        tie_kernel,
+        out_shape=[jax.ShapeDtypeStruct(v.shape, v.dtype) for v in values]
+        + [jax.ShapeDtypeStruct((8, 128), jnp.float32)],
         in_specs=[IN_HBM] * n + [ANYWHERE] * len(after),
-        out_specs=[IN_HBM] * n,
+        out_specs=[IN_HBM] * n + [VECTOR],
         input_output_aliases={k: k for k in range(n)},
         compiler_params=params(),
+        cost_estimate=NO_COST,
         name="tie",
     )(*values, *after)
 
@@ -119,6 +112,7 @@
         in_specs=[VECTOR],
         out_specs=VECTOR,
         compiler_params=params(),
+        cost_estimate=NO_COST,
         name="touch",
     )(a)
 
@@ -136,6 +130,7 @@
         in_specs=[VECTOR] * 2 + [ANYWHERE] * len(after),
         out_specs=VECTOR,
         compiler_params=params(),
+        cost_estimate=NO_COST,
         name="stack",
     )(a, b, *after)
 
@@ -211,16 +206,12 @@
             pltpu.SemaphoreType.DMA((n + PARTS,)),
         ],
         compiler_params=params(),
-        cost_estimate=pl.CostEstimate(
-            flops=2 * width * cols * rows * n,
-            bytes_accessed=2 * cols * (width + n * rows) + 8 * slots * width * rows,
-            transcendentals=0,
-        ),
+        cost_estimate=NO_COST,
         name="partial_sums",
     )(first, weight, *shards, *after)
 
 
-def chosen_kernel(n, s_ref, w_any, *refs):
+def chosen_kernel(n, own, s_ref, w_any, *refs):
     out_ref, w_ref, g_ref, sem = refs[-4:]
     rows = out_ref.shape[2]
     copies = load_weight(w_any, w_ref, sem, n)
@@ -228,7 +219,7 @@
         target = g_ref.at[pl.ds(k * rows, rows), :]
         for group in range(2):
 
-            @pl.when(s_ref[0] == group)
+            @pl.when((s_ref[0] == 1 - group) == own)
             def _(source=refs[group * n + k], target=target, k=k):
                 pltpu.make_async_copy(source, target, sem.at[k]).start()
 
@@ -240,12 +231,12 @@
         out_ref[k] = sums[:, k * rows : (k + 1) * rows]
 
 
-def chosen_sums(which, weight, groups, after):
+def chosen_sums(own, scalars, weight, groups, after):
     n = len(groups[0])
     rows, cols = groups[0][0].shape
     width = weight.shape[0]
     return pl.pallas_call(
-        functools.partial(chosen_kernel, n),
+        functools.partial(chosen_kernel, n, own),
         out_shape=jax.ShapeDtypeStruct((n, width, rows), jnp.float32),
         in_specs=[SCALAR] + [IN_HBM] * (1 + 2 * n) + [ANYWHERE] * len(after),
         out_specs=VECTOR,
@@ -255,18 +246,14 @@
             pltpu.SemaphoreType.DMA((n + PARTS,)),
         ],
         compiler_params=params(),
-        cost_estimate=pl.CostEstimate(
-            flops=2 * width * cols * rows * n,
-            bytes_accessed=2 * cols * (width + n * rows) + 4 * n * width * rows,
-            transcendentals=0,
-        ),
+        cost_estimate=NO_COST,
         name="chosen_sums",
-    )(which, weight, *groups[0], *groups[1], *after)
-
-
-def place_kernel(counts, s_ref, *refs):
-    pairs, outs = refs[: 2 * len(counts)], refs[2 * len(counts) :]
-    k = 0
+    )(scalars, weight, *groups[0], *groups[1], *after)
+
+
+def place_kernel(base, counts, s_ref, *refs):
+    pairs, outs = refs[: 2 * len(counts)], refs[-Y:]
+    k = base
     for group, n in enumerate(counts):
         keep_ref, got_ref = pairs[2 * group], pairs[2 * group + 1]
         for i in range(n):
@@ -279,36 +266,46 @@
             k += 1
 
 
-def place(ways, groups):
+def place(base, scalars, groups, limit, after):
     counts = [kept.shape[0] for kept, _ in groups]
     out = jax.ShapeDtypeStruct(groups[0][0].shape[1:], jnp.float32)
     return pl.pallas_call(
-        functools.partial(place_kernel, counts),
+        functools.partial(place_kernel, base, counts),
         out_shape=[out] * Y,
-        in_specs=[SCALAR] + [VECTOR] * (2 * len(counts)),
+        in_specs=[SCALAR] + [VECTOR] * (2 * len(counts)) + [ANYWHERE] * len(after),
         out_specs=[VECTOR] * Y,
-        compiler_params=params(),
+        compiler_params=params(limit),
+        cost_estimate=NO_COST,
         name="place",
-    )(ways, *[a for pair in groups for a in pair])
-
-
-def merge_kernel(*refs):
-    a, b, c, d = refs[:Y]
-    refs[-1][...] = (a[...] + b[...]) + (c[...] + d[...])
-
-
-def merge(parts, after):
-    return pl.pallas_call(
-        merge_kernel,
-        out_shape=jax.ShapeDtypeStruct(parts[0].shape, jnp.float32),
-        in_specs=[VECTOR] * Y + [ANYWHERE] * len(after),
-        out_specs=VECTOR,
-        compiler_params=params(),
+    )(scalars, *[a for pair in groups for a in pair], *after)
+
+
+def merge_kernel(base, s_ref, *refs):
+    late, early, (keep_ref, send_ref) = refs[:Y], refs[Y : 2 * Y], refs[-2:]
+
+    def total(parts):
+        return (parts[0][...] + parts[1][...]) + (parts[2][...] + parts[3][...])
+
+    a, b = total(late), total(early)
+    here = s_ref[base] == 1
+    keep_ref[...] = jnp.where(here, a, b)
+    send_ref[...] = jnp.where(here, b, a)
+
+
+def merge(base, scalars, late, early, after):
+    out = jax.ShapeDtypeStruct(late[0].shape, jnp.float32)
+    return pl.pallas_call(
+        functools.partial(merge_kernel, base),
+        out_shape=(out, out),
+        in_specs=[SCALAR] + [VECTOR] * (2 * Y) + [ANYWHERE] * len(after),
+        out_specs=(VECTOR, VECTOR),
+        compiler_params=params(TAIL_LIMIT),
+        cost_estimate=NO_COST,
         name="merge",
-    )(*parts, *after)
-
-
-def weight_kernel(n, tile, scale, s_ref, mine_ref, other_ref, *refs):
+    )(scalars, *late, *early, *after)
+
+
+def weight_kernel(base, n, tile, scale, s_ref, mine_ref, other_ref, *refs):
     pieces, (out_ref, token_ref) = refs[:n], refs[-7:-5]
     x_ref, g_ref, o_ref, in_sem, out_sem = refs[-5:]
     count, _, rows = mine_ref.shape
@@ -321,7 +318,7 @@
         copies.append(copy)
     token_ref[...] = jnp.zeros_like(token_ref)
     for k in range(n):
-        at = s_ref[k]
+        at = s_ref[base + k]
         here = slice(k * rows, (k + 1) * rows)
 
         @pl.when(at < count)
@@ -350,13 +347,13 @@
         copy.wait()
 
 
-def weight_sums(scalars, mine, other, shards, scale, after):
+def weight_sums(base, scalars, mine, other, shards, scale, after):
     n = len(shards)
     rows, cols = shards[0].shape
     width = mine.shape[1]
     tile = 768
     return pl.pallas_call(
-        functools.partial(weight_kernel, n, tile, scale),
+        functools.partial(weight_kernel, base, n, tile, scale),
         out_shape=(
             jax.ShapeDtypeStruct((width, cols), jnp.float32),
             jax.ShapeDtypeStruct((8, 128), jnp.float32),
@@ -370,12 +367,8 @@
             pltpu.SemaphoreType.DMA((n,)),
             pltpu.SemaphoreType.DMA((cols // tile,)),
         ],
-        compiler_params=params(),
-        cost_estimate=pl.CostEstimate(
-            flops=2 * width * cols * rows * n,
-            bytes_accessed=2 * rows * n * (cols + width) + 4 * width * cols,
-            transcendentals=0,
-        ),
+        compiler_params=params(TAIL_LIMIT),
+        cost_estimate=NO_COST,
         name="weight_sums",
     )(scalars, mine, other, *shards, *after)
 
@@ -404,12 +397,13 @@
         ("d3", "dx3", "u1", "ux1"),
     )
     even = z % 2 == c
-    first = jnp.stack([even]).astype(jnp.int32)
     h = {"g": grad_out}
 
-    def partials(a, b, *after):
-        groups = [h[s] for s in a], [h[s] for s in b]
-        return partial_sums(first, weight, groups, after)
+    first_early = (("d2", "u2"), ("u1", "ux1"))
+    mixed = (("dx2", "g", "gx"), ("d3", "d1", "u3"))
+    last_early = (("ux2",), ("dx3",))
+    last = (("u4", "dx4"), ("dx1", "ux3"))
+    order = [s for names in sets for s in names]
 
     def ways(*groups):
         slots = []
@@ -417,14 +411,38 @@
             for k in range(max(len(a), len(b), 1)):
                 way = [(where(s[k])[0] - y) % Y if k < len(s) else -1 for s in (a, b)]
                 slots.append(jnp.where(even, way[0], way[1]))
-        return jnp.stack(slots).astype(jnp.int32)
+        return slots
+
+    def of_inputs(name):
+        ty, txh, tc = where(name)
+        k = (ty // 2 != y // 2) * 4 + (ty % 2 != y % 2) * 2 + (txh != xh)
+        return jnp.where(tc == c, k, k + Y * XH)
+
+    none = ((), ())
+    lists = [
+        [even],
+        ways(first_early, (mixed[0][:1], mixed[1][:1]), none, none, last_early),
+        ways(none, (mixed[0][1:], mixed[1][1:]), last),
+        [of_inputs(s) for s in order],
+        [late_here(z, xh, c)],
+    ]
+    scalars = jnp.stack([jnp.int32(v) for values in lists for v in values])
+    _, at_early, at_late, at_inputs, at_here = (
+        sum(len(values) for values in lists[:k]) for k in range(len(lists))
+    )
+
+    def partials(a, b, *after):
+        groups = [h[s] for s in a], [h[s] for s in b]
+        return partial_sums(scalars, weight, groups, after)
 
     def over_y(parts):
         return [parts[0], in_y(parts[1], 1), in_y(parts[3], -1), in_y(parts[2], 2)]
 
     def phase(names, sends, *after):
         s = [h[name] for name in sends]
-        h.update(zip(names, tie([up(s[0]), down(s[1]), across(s[2])], after)))
+        *got, token = tie([up(s[0]), down(s[1]), across(s[2])], after)
+        h.update(zip(names, got))
+        return token
 
     mine = touch(inputs.T[None])
     pair = in_xh(mine)
@@ -434,43 +452,39 @@
     phase(("u2", "d2", "ux1"), ("u1", "d1", "u1"), pair)
     quad = stack(pair, quad, [h["u2"]])
     column = in_y(quad, 2)
-    first_early = (("d2", "u2"), ("u1", "ux1"))
     keep_a, send_a = partials(*first_early)
     got_a = in_core(send_a)
     phase(("u3", "d3", "dx2"), ("u2", "d2", "d2"), quad, keep_a)
     column = stack(quad, column, [h["u3"]])
     other = in_core(column)
-    mixed = (("dx2", "g", "gx"), ("d3", "d1", "u3"))
     keep_b, send_b = partials(*mixed)
     got_b = in_core(send_b)
-    phase(("u4", "dx3", "ux2"), ("u3", "dx2", "u2"), column, got_a, keep_b)
-    last_early = (("ux2",), ("dx3",))
-    keep_c, send_c = partials(*last_early)
+    token = phase(("u4", "dx3", "ux2"), ("u3", "dx2", "u2"), column, got_a, keep_b)
+    keep_c, send_c = partials(*last_early, in_core(token))
     got_c = in_core(send_c)
-    none = ((), ())
     early = place(
-        ways(first_early, (mixed[0][:1], mixed[1][:1]), none, none, last_early),
+        at_early,
+        scalars,
         [(keep_a, got_a), (keep_b, got_b), (keep_c, got_c)],
+        VMEM_LIMIT,
+        [],
     )
     phase(("ux3", "dx4", "dx1"), ("ux2", "dx3", "d1"), other, *early)
     early = over_y(early)
-    last = (("u4", "dx4"), ("dx1", "ux3"))
     groups = [[h[s] for s in group] for group in last]
-    got_d = in_core(chosen_sums(first, weight, groups, early[1:3]))
-    keep_d = chosen_sums(1 - first, weight, groups, [])
+    got_d = in_core(chosen_sums(False, scalars, weight, groups, []))
+    keep_d = chosen_sums(True, scalars, weight, groups, [])
     late = place(
-        ways(none, (mixed[0][1:], mixed[1][1:]), last),
+        at_late,
+        scalars,
         [(keep_b, got_b), (keep_d, got_d)],
-    )
-
-    def of_inputs(name):
-        ty, txh, tc = where(name)
-        k = (ty // 2 != y // 2) * 4 + (ty % 2 != y % 2) * 2 + (txh != xh)
-        return jnp.where(tc == c, k, k + column.shape[0])
-
-    order = [s for names in sets for s in names]
+        TAIL_LIMIT,
+        early[1:],
+    )
+
     grad_weight, token = weight_sums(
-        jnp.stack([of_inputs(s) for s in order]),
+        at_inputs,
+        scalars,
         column,
         other,
         [h[s] for s in order],
@@ -478,12 +492,9 @@
         late,
     )
 
-    early = merge(early, late)
-    got_early = in_xh_where(early, True)
-    late = merge(over_y(late), [token, got_early])
-    got_late = in_xh_where(late, False)
-    grad_in = jnp.where(late_here(z, xh, c), late + got_late, early + got_early)
-    return grad_in.astype(jnp.bfloat16).T, grad_weight
+    keep, send = merge(at_here, scalars, over_y(late), early, [token])
+    grad_in = (keep + in_xh(send)).astype(jnp.bfloat16)
+    return grad_in.T, grad_weight
 
 
 def solution(mesh):

time: 164 us -> 159 us (0.970)
  starting transfers between devices: 43.4 us -> 38.4 us
  local copies, waits for them, and re-layouts: 7.5 us -> 9.81 us
    ppermute x2 -> x0, waiting for transfers between devices: 8.98 us -> none  [in_xh_where(): return lax.ppermute(t, ('gx', 'gy'), pairs)]
    ppermute x1 -> x2, waiting for transfers between devices: 8.97 us -> 17.7 us  [in_xh(): return lax.ppermute(t, 'gy', gy_pairs(0, 1, 0))]
    ppermute x5, waiting for transfers between devices: 10.2 us -> 4.23 us  [across(): return lax.ppermute(t, 'gx', gx_pairs(1, 0))]
    ppermute x2 -> x0, starting transfers between devices: 4.87 us -> none  [in_xh_where(): return lax.ppermute(t, ('gx', 'gy'), pairs)]
    unnamed x26 -> x40, local copies, waits for them, and re-layouts: 5.66 us -> 9.18 us
    ppermute x7, waiting for transfers between devices: 6.91 us -> 9.35 us  [in_y(): return lax.ppermute(t, 'gy', gy_pairs(dy, 0, 0))]
    pallas_call x3, Pallas kernels: 15.5 us -> 17.6 us  [partial_sums(): pl.pallas_call(functools.partial(partial_kernel, places), out_shape=(out,...]
    ppermute x5 -> x6, waiting for transfers between devices: 0.01 us -> 1.79 us  [in_core(): return lax.ppermute(t, 'gy', gy_pairs(0, 0, 1))]
  transfers between devices with their start and end apart: 31 -> 31, of which waited for: 13 -> 15; matrix products, arithmetic and copies ran while one was open for 1% -> 0% of each run, Pallas kernels for 30% -> 29%
where the time goes in v5:
time: 159 us; the launch traced here: 158 us
  Pallas kernels  54.4 us (34%)
  waiting for transfers between devices  54.1 us (34%)
  starting transfers between devices  38.4 us (24%)
  local copies, waits for them, and re-layouts  9.81 us (6%)
    ppermute x2, waiting for transfers between devices, in_xh(): return lax.ppermute(t, 'gy', gy_pairs(0, 1, 0))  17.7 us
    pallas_call x3, Pallas kernels, partial_sums(): pl.pallas_call(functools.partial(partial_kernel, places), out_shape=(out,...  17.6 us
    ppermute x5, waiting for transfers between devices, down(): return lax.ppermute(t, 'gx', gx_pairs(0, -1))  13.5 us
    ppermute x5, starting transfers between devices, down(): return lax.ppermute(t, 'gx', gx_pairs(0, -1))  13.1 us
    pallas_call x1, Pallas kernels, weight_sums(): pl.pallas_call(functools.partial(weight_kernel, base, n, tile, scale), ou...  11.3 us
    ppermute x7, starting transfers between devices, in_y(): return lax.ppermute(t, 'gy', gy_pairs(dy, 0, 0))  11.2 us
    ppermute x7, waiting for transfers between devices, in_y(): return lax.ppermute(t, 'gy', gy_pairs(dy, 0, 0))  9.35 us
    unnamed x40, local copies, waits for them, and re-layouts  9.18 us
  transfers between devices with their start and end apart: 31, of which 15 were waited for; matrix products, arithmetic and copies ran while one was open for 0% of the time, Pallas kernels for 29%

profile of v5, /device:TPU:8, one launch (start us, length us, event | category | flops | bytes accessed | tf_op | source)
XLA Modules:
  0.0 158.3 jit_solution(1673123759351566056)
XLA Ops:
  2.2 5.9 %collective-permute-start.1 = (bf16[128,2304]{1,0:T(8,128)(2,1)}, bf16[128,2304]{1,0:T(8,128)(2,1)}, u32[]{:S(2)}, u32[]{:S(2)}) collective-permute-start(bf16[128,2304]{1,0:T(8,128)(2,1)} %refs_0_.1), channel_id=1, source_target_pairs={{0,112},{16,0},{32,16},{48,32},{64,48},{80,64},{96,80},{112,96},{1... | collective-permute-start | bytes 1769480 | tf_op jit(solution)/shard_map/ppermute | solution.py:42
  8.1 1.6 touch.1.a_ref
  9.6 2.7 %collective-permute-start.3 = (bf16[1,576,128]{2,1,0:T(8,128)(2,1)}, bf16[1,576,128]{2,1,0:T(8,128)(2,1)S(1)}, u32[]{:S(2)}, u32[]{:S(2)}) collective-permute-start(bf16[1,576,128]{2,1,0:T(8,128)(2,1)} %touch.1.a_ref), channel_id=1, source_target_pairs={{0,2},{1,3},{2,0},{3,1},{4,6},{5,7},{6,4},{7,5},{8,10},{9,11},{10,... | collective-permute-start | bytes 442376 | tf_op jit(solution)/shard_map/ppermute | solution.py:64
  12.4 9.0 %collective-permute-done.3.refs_3_.b_ref = bf16[1,576,128]{2,1,0:T(8,128)(2,1)S(1)} collective-permute-done((bf16[1,576,128]{2,1,0:T(8,128)(2,1)}, bf16[1,576,128]{2,1,0:T(8,128)(2,1)S(1)}, u32[]{:S(2)}, u32[]{:S(2)}) %collective-permute-start.3) | collective-permute-done | bytes 147488 | tf_op jit(solution)/shard_map/ppermute | solution.py:64
  21.4 2.6 %collective-permute-done.refs_0_ = bf16[128,2304]{1,0:T(8,128)(2,1)S(1)} collective-permute-done((bf16[128,2304]{1,0:T(8,128)(2,1)}, bf16[128,2304]{1,0:T(8,128)(2,1)S(1)}, u32[]{:S(2)}, u32[]{:S(2)}) %collective-permute-start) | collective-permute-done | bytes 589856 | tf_op jit(solution)/shard_map/ppermute | solution.py:38
  25.4 3.9 %collective-permute-start.5 = (bf16[128,2304]{1,0:T(8,128)(2,1)}, bf16[128,2304]{1,0:T(8,128)(2,1)}, u32[]{:S(2)}, u32[]{:S(2)}) collective-permute-start(bf16[128,2304]{1,0:T(8,128)(2,1)} %get-tuple-element.37.refs_4_), channel_id=1, source_target_pairs={{0,112},{16,0},{32,16},{48,32},{64,48},{80,64},{96,80},{112,96},{1... | collective-permute-start | bytes 1769480 | tf_op jit(solution)/shard_map/ppermute | solution.py:42
  29.5 1.7 %stack.124.refs_3_.a_ref = bf16[2,576,128]{2,1,0:T(8,128)(2,1)} custom-call(bf16[1,576,128]{2,1,0:T(8,128)(2,1)} %touch.1.a_ref, bf16[1,576,128]{2,1,0:T(8,128)(2,1)} %copy-done.16, bf16[128,2304]{1,0:T(8,128)(2,1)} %get-tuple-element.36.refs_0_.refs_2_.refs_14_), custom_call_target="tpu_custom_call" | custom-call | flops 1 | bytes 1 | tf_op jit(solution)/shard_map/stack/pallas_call | solution.py:127
  31.7 9.6 %collective-permute-done.5.refs_1_ = bf16[128,2304]{1,0:T(8,128)(2,1)} collective-permute-done((bf16[128,2304]{1,0:T(8,128)(2,1)}, bf16[128,2304]{1,0:T(8,128)(2,1)}, u32[]{:S(2)}, u32[]{:S(2)}) %collective-permute-start.5) | collective-permute-done | bytes 589856 | tf_op jit(solution)/shard_map/ppermute | solution.py:42
  41.3 2.2 %collective-permute-done.6.refs_2_ = bf16[128,2304]{1,0:T(8,128)(2,1)} collective-permute-done((bf16[128,2304]{1,0:T(8,128)(2,1)}, bf16[128,2304]{1,0:T(8,128)(2,1)}, u32[]{:S(2)}, u32[]{:S(2)}) %collective-permute-start.6) | collective-permute-done | bytes 589856 | tf_op jit(solution)/shard_map/ppermute | solution.py:46
  46.1 1.7 %collective-permute-start.9 = (bf16[128,2304]{1,0:T(8,128)(2,1)}, bf16[128,2304]{1,0:T(8,128)(2,1)}, u32[]{:S(2)}, u32[]{:S(2)}) collective-permute-start(bf16[128,2304]{1,0:T(8,128)(2,1)} %get-tuple-element.39.refs_0_.refs_8_), channel_id=1, source_target_pairs={{0,128},{16,144},{32,160},{48,176},{64,192},{80,208},{96,224},{112... | collective-permute-start | bytes 1769480 | tf_op jit(solution)/shard_map/ppermute | solution.py:46
  47.8 2.0 %collective-permute-start.7 = (bf16[128,2304]{1,0:T(8,128)(2,1)}, bf16[128,2304]{1,0:T(8,128)(2,1)S(1)}, u32[]{:S(2)}, u32[]{:S(2)}) collective-permute-start(bf16[128,2304]{1,0:T(8,128)(2,1)} %get-tuple-element.38.refs_0_.refs_1_.refs_10_), channel_id=1, source_target_pairs={{0,16},{16,32},{32,48},{48,64},{64,80},{80,96},{96,112},{112,0},{1... | collective-permute-start | bytes 1769480 | tf_op jit(solution)/shard_map/ppermute | solution.py:38
  50.6 1.9 %stack.125.refs_3_.a_ref = bf16[4,576,128]{2,1,0:T(8,128)(2,1)} custom-call(bf16[2,576,128]{2,1,0:T(8,128)(2,1)} %stack.124.refs_3_.a_ref, bf16[2,576,128]{2,1,0:T(8,128)(2,1)} %copy-done.17, bf16[128,2304]{1,0:T(8,128)(2,1)} %get-tuple-element.38.refs_0_.refs_1_.refs_10_), custom_call_target="tpu_custom_call" | custom-call | flops 1 | bytes 1 | tf_op jit(solution)/shard_map/stack/pallas_call | solution.py:127
  52.5 2.3 %collective-permute-start.15 = (bf16[4,576,128]{2,1,0:T(8,128)(2,1)}, bf16[4,576,128]{2,1,0:T(8,128)(2,1)}, u32[]{:S(2)}, u32[]{:S(2)}) collective-permute-start(bf16[4,576,128]{2,1,0:T(8,128)(2,1)} %stack.125.refs_3_.a_ref), channel_id=1, source_target_pairs={{0,8},{1,9},{2,10},{3,11},{4,12},{5,13},{6,14},{7,15},{8,0},{9,1},... | collective-permute-start | bytes 1769480 | tf_op jit(solution)/shard_map/ppermute | solution.py:60
  55.7 5.9 %partial_sums.3 = (f32[2,576,128]{2,1,0:T(8,128)}, f32[2,576,128]{2,1,0:T(8,128)}) custom-call(s32[29]{0:T(128)} %stack.121.s_ref, bf16[576,2304]{1,0:T(8,128)(2,1)} %w_any.9, bf16[128,2304]{1,0:T(8,128)(2,1)} %get-tuple-element.39.refs_0_.refs_8_, bf16[128,2304]{1,0:T(8,128)(2,1)} %get-tuple-element.38.refs_0_.refs_1_.refs_10_, ...), custom_call_target="tpu_custom_call" | custom-call | flops 1 | bytes 1 | tf_op jit(solution)/shard_map/partial_sums/pallas_call | solution.py:198
  66.1 7.2 %partial_sums.4 = (f32[3,576,128]{2,1,0:T(8,128)}, f32[3,576,128]{2,1,0:T(8,128)}) custom-call(s32[29]{0:T(128)} %stack.121.s_ref, bf16[576,2304]{1,0:T(8,128)(2,1)} %w_any.9, bf16[128,2304]{1,0:T(8,128)(2,1)} %get-tuple-element.42.refs_0_.refs_9_, bf16[128,2304]{1,0:T(8,128)(2,1)} %refs_0_.1, bf16[128,2304]{1,0:T(8,128)(2,1)} %get-tuple-element.43.refs_2_.refs_1_, ...), custom_call_target="tpu_custom_call" | custom-call | flops 1 | bytes 1 | tf_op jit(solution)/shard_map/partial_sums/pallas_call | solution.py:198
  73.5 2.3 %stack.126.refs_3_.mine_ref = bf16[8,576,128]{2,1,0:T(8,128)(2,1)} custom-call(bf16[4,576,128]{2,1,0:T(8,128)(2,1)} %stack.125.refs_3_.a_ref, bf16[4,576,128]{2,1,0:T(8,128)(2,1)} %collective-permute-done.15.b_ref, bf16[128,2304]{1,0:T(8,128)(2,1)} %get-tuple-element.45.refs_5_.refs_0_.refs_6_), custom_call_target="tpu_custom_call" | custom-call | flops 1 | bytes 1 | tf_op jit(solution)/shard_map/stack/pallas_call | solution.py:127
  76.3 3.8 %collective-permute-done.13.refs_1_ = bf16[128,2304]{1,0:T(8,128)(2,1)} collective-permute-done((bf16[128,2304]{1,0:T(8,128)(2,1)}, bf16[128,2304]{1,0:T(8,128)(2,1)}, u32[]{:S(2)}, u32[]{:S(2)}) %collective-permute-start.13) | collective-permute-done | bytes 589856 | tf_op jit(solution)/shard_map/ppermute | solution.py:42
  85.0 2.7 %collective-permute-start.18 = (bf16[128,2304]{1,0:T(8,128)(2,1)}, bf16[128,2304]{1,0:T(8,128)(2,1)}, u32[]{:S(2)}, u32[]{:S(2)}) collective-permute-start(bf16[128,2304]{1,0:T(8,128)(2,1)} %get-tuple-element.51.refs_1_.refs_13_), channel_id=1, source_target_pairs={{0,112},{16,0},{32,16},{48,32},{64,48},{80,64},{96,80},{112,96},{1... | collective-permute-start | bytes 1769480 | tf_op jit(solution)/shard_map/ppermute | solution.py:42
  87.7 4.5 %partial_sums.5 = (f32[1,576,128]{2,1,0:T(8,128)}, f32[1,576,128]{2,1,0:T(8,128)}) custom-call(s32[29]{0:T(128)} %stack.121.s_ref, bf16[576,2304]{1,0:T(8,128)(2,1)} %w_any.9, bf16[128,2304]{1,0:T(8,128)(2,1)} %get-tuple-element.50.refs_0_.refs_11_, bf16[128,2304]{1,0:T(8,128)(2,1)} %get-tuple-element.51.refs_1_.refs_13_, f32[8,128]{1,0:T(8,128)} %copy-done.19), custom_call_target="tpu_custom_call" | custom-call | flops 1 | bytes 1 | tf_op jit(solution)/shard_map/partial_sums/pallas_call | solution.py:198
  92.3 1.8 %collective-permute-done.22.refs_5_ = f32[1,576,128]{2,1,0:T(8,128)S(1)} collective-permute-done((f32[1,576,128]{2,1,0:T(8,128)}, f32[1,576,128]{2,1,0:T(8,128)S(1)}, u32[]{:S(2)}, u32[]{:S(2)}) %collective-permute-start.22) | collective-permute-done | bytes 294944 | tf_op jit(solution)/shard_map/ppermute | solution.py:72
  94.8 3.3 %place.2 = (f32[576,128]{1,0:T(8,128)}, f32[576,128]{1,0:T(8,128)}, f32[576,128]{1,0:T(8,128)}, f32[576,128]{1,0:T(8,128)}) custom-call(s32[29]{0:T(128)} %stack.121.s_ref, f32[2,576,128]{2,1,0:T(8,128)} %get-tuple-element.41.refs_4_.refs_0_, f32[2,576,128]{2,1,0:T(8,128)} %collective-permute-done.16.refs_4_.refs_1_, ...), custom_call_target="tpu_custom_call" | custom-call | flops 1 | bytes 1 | tf_op jit(solution)/shard_map/place/pallas_call | solution.py:272
  99.0 2.4 %collective-permute-done.17.refs_0_ = bf16[128,2304]{1,0:T(8,128)(2,1)} collective-permute-done((bf16[128,2304]{1,0:T(8,128)(2,1)}, bf16[128,2304]{1,0:T(8,128)(2,1)}, u32[]{:S(2)}, u32[]{:S(2)}) %collective-permute-start.17) | collective-permute-done | bytes 589856 | tf_op jit(solution)/shard_map/ppermute | solution.py:38
  102.0 4.5 %chosen_sums.3 = f32[2,576,128]{2,1,0:T(8,128)} custom-call(s32[29]{0:T(128)} %stack.121.s_ref, bf16[576,2304]{1,0:T(8,128)(2,1)} %w_any.9, bf16[128,2304]{1,0:T(8,128)(2,1)} %get-tuple-element.49.refs_0_.refs_2_, bf16[128,2304]{1,0:T(8,128)(2,1)} %get-tuple-element.59.refs_1_.refs_3_, bf16[128,2304]{1,0:T(8,128)(2,1)} %get-tuple-element.60.refs_2_.refs_5_, ...), custom_call_target="tpu_custom_call" | custom-call | flops 1 | bytes 1 | tf_op jit(solution)/shard_map/chosen_sums/pallas_call | solution.py:238
  106.6 1.7 %collective-permute-start.24 = (f32[576,128]{1,0:T(8,128)}, f32[576,128]{1,0:T(8,128)S(1)}, u32[]{:S(2)}, u32[]{:S(2)}) collective-permute-start(f32[576,128]{1,0:T(8,128)} %get-tuple-element.56.refs_5_), channel_id=1, source_target_pairs={{0,4},{1,5},{2,6},{3,7},{4,8},{5,9},{6,10},{7,11},{8,12},{9,13},{1... | collective-permute-start | bytes 884744 | tf_op jit(solution)/shard_map/ppermute | solution.py:60
  108.2 1.8 %collective-permute-start.26 = (f32[576,128]{1,0:T(8,128)}, f32[576,128]{1,0:T(8,128)}, u32[]{:S(2)}, u32[]{:S(2)}) collective-permute-start(f32[576,128]{1,0:T(8,128)} %get-tuple-element.57.refs_6_), channel_id=1, source_target_pairs={{0,8},{1,9},{2,10},{3,11},{4,12},{5,13},{6,14},{7,15},{8,0},{9,1},... | collective-permute-start | bytes 884744 | tf_op jit(solution)/shard_map/ppermute | solution.py:60
  111.6 4.5 %chosen_sums.2.refs_2_ = f32[2,576,128]{2,1,0:T(8,128)} custom-call(s32[29]{0:T(128)} %stack.121.s_ref, bf16[576,2304]{1,0:T(8,128)(2,1)} %w_any.9, bf16[128,2304]{1,0:T(8,128)(2,1)} %get-tuple-element.49.refs_0_.refs_2_, bf16[128,2304]{1,0:T(8,128)(2,1)} %get-tuple-element.59.refs_1_.refs_3_, bf16[128,2304]{1,0:T(8,128)(2,1)} %get-tuple-element.60.refs_2_.refs_5_, ...), custom_call_target="tpu_custom_call" | custom-call | flops 1 | bytes 1 | tf_op jit(solution)/shard_map/chosen_sums/pallas_call | solution.py:238
  116.7 3.3 %collective-permute-done.26.refs_6_.refs_7_ = f32[576,128]{1,0:T(8,128)} collective-permute-done((f32[576,128]{1,0:T(8,128)}, f32[576,128]{1,0:T(8,128)}, u32[]{:S(2)}, u32[]{:S(2)}) %collective-permute-start.26) | collective-permute-done | bytes 294944 | tf_op jit(solution)/shard_map/ppermute | solution.py:60
  120.0 5.5 %collective-permute-done.25.refs_5_.refs_6_ = f32[576,128]{1,0:T(8,128)} collective-permute-done((f32[576,128]{1,0:T(8,128)}, f32[576,128]{1,0:T(8,128)}, u32[]{:S(2)}, u32[]{:S(2)}) %collective-permute-start.25) | collective-permute-done | bytes 294944 | tf_op jit(solution)/shard_map/ppermute | solution.py:60
  127.7 1.6 %place.3 = (f32[576,128]{1,0:T(8,128)S(1)}, f32[576,128]{1,0:T(8,128)S(1)}, f32[576,128]{1,0:T(8,128)S(1)}, f32[576,128]{1,0:T(8,128)S(1)}) custom-call(s32[29]{0:T(128)S(1)} %copy-done.15, f32[3,576,128]{2,1,0:T(8,128)S(1)} %copy-done.11, f32[3,576,128]{2,1,0:T(8,128)} %collective-permute-done.11.refs_3_.refs_1_, f32[2,576,128]{2,1,0:T(8,128)S(1)} %copy-done.13, ...), custom_call_target="tpu_custom_call" | custom-call | flops 1 | bytes 1 | tf_op jit(solution)/shard_map/place/pallas_call | solution.py:272
  131.4 1.8 %collective-permute-start.29 = (f32[576,128]{1,0:T(8,128)S(1)}, f32[576,128]{1,0:T(8,128)S(1)}, u32[]{:S(2)}, u32[]{:S(2)}) collective-permute-start(f32[576,128]{1,0:T(8,128)S(1)} %get-tuple-element.65.refs_18_), channel_id=1, source_target_pairs={{0,8},{1,9},{2,10},{3,11},{4,12},{5,13},{6,14},{7,15},{8,0},{9,1},... | collective-permute-start | bytes 884744 | tf_op jit(solution)/shard_map/ppermute | solution.py:60
  135.4 11.3 %weight_sums.1 = (f32[576,2304]{1,0:T(8,128)}, f32[8,128]{1,0:T(8,128)S(1)}) custom-call(s32[29]{0:T(128)S(1)} %copy-done.15, bf16[8,576,128]{2,1,0:T(8,128)(2,1)S(1)} %copy-done, bf16[8,576,128]{2,1,0:T(8,128)(2,1)} %collective-permute-done.20.refs_3_.other_ref, bf16[128,2304]{1,0:T(8,128)(2,1)S(1)} %copy-done.12, ...), custom_call_target="tpu_custom_call" | custom-call | flops 1 | bytes 1 | tf_op jit(solution)/shard_map/weight_sums/pallas_call | solution.py:355
  148.9 8.7 %collective-permute-done.30 = f32[576,128]{1,0:T(8,128)S(1)} collective-permute-done((f32[576,128]{1,0:T(8,128)S(1)}, f32[576,128]{1,0:T(8,128)S(1)}, u32[]{:S(2)}, u32[]{:S(2)}) %collective-permute-start.30) | collective-permute-done | bytes 294944 | tf_op jit(solution)/shard_map/ppermute | solution.py:64
  (90 shorter events, 31.8 us)
Async XLA Ops:
  0.6 20.7 %collective-permute-start.2 = (bf16[128,2304]{1,0:T(8,128)(2,1)}, bf16[128,2304]{1,0:T(8,128)(2,1)}, u32[]{:S(2)}, u32[]{:S(2)}) collective-permute-start(bf16[128,2304]{1,0:T(8,128)(2,1)} %refs_0_.1), channel_id=1, source_target_pairs={{0,128},{16,144},{32,160},{48,176},{64,192},{80,208},{96,224},{112... | collective-permute-start | bytes 1769480 | tf_op jit(solution)/shard_map/ppermute | solution.py:46
  2.2 19.2 %collective-permute-start.1 = (bf16[128,2304]{1,0:T(8,128)(2,1)}, bf16[128,2304]{1,0:T(8,128)(2,1)}, u32[]{:S(2)}, u32[]{:S(2)}) collective-permute-start(bf16[128,2304]{1,0:T(8,128)(2,1)} %refs_0_.1), channel_id=1, source_target_pairs={{0,112},{16,0},{32,16},{48,32},{64,48},{80,64},{96,80},{112,96},{1... | collective-permute-start | bytes 1769480 | tf_op jit(solution)/shard_map/ppermute | solution.py:42
  8.1 15.9 %collective-permute-start = (bf16[128,2304]{1,0:T(8,128)(2,1)}, bf16[128,2304]{1,0:T(8,128)(2,1)S(1)}, u32[]{:S(2)}, u32[]{:S(2)}) collective-permute-start(bf16[128,2304]{1,0:T(8,128)(2,1)} %refs_0_.1), channel_id=1, source_target_pairs={{0,16},{16,32},{32,48},{48,64},{64,80},{80,96},{96,112},{112,0},{1... | collective-permute-start | bytes 1769480 | tf_op jit(solution)/shard_map/ppermute | solution.py:38
  9.6 11.7 %collective-permute-start.3 = (bf16[1,576,128]{2,1,0:T(8,128)(2,1)}, bf16[1,576,128]{2,1,0:T(8,128)(2,1)S(1)}, u32[]{:S(2)}, u32[]{:S(2)}) collective-permute-start(bf16[1,576,128]{2,1,0:T(8,128)(2,1)} %touch.1.a_ref), channel_id=1, source_target_pairs={{0,2},{1,3},{2,0},{3,1},{4,6},{5,7},{6,4},{7,5},{8,10},{9,11},{10,... | collective-permute-start | bytes 442376 | tf_op jit(solution)/shard_map/ppermute | solution.py:64
  25.4 15.9 %collective-permute-start.5 = (bf16[128,2304]{1,0:T(8,128)(2,1)}, bf16[128,2304]{1,0:T(8,128)(2,1)}, u32[]{:S(2)}, u32[]{:S(2)}) collective-permute-start(bf16[128,2304]{1,0:T(8,128)(2,1)} %get-tuple-element.37.refs_4_), channel_id=1, source_target_pairs={{0,112},{16,0},{32,16},{48,32},{64,48},{80,64},{96,80},{112,96},{1... | collective-permute-start | bytes 1769480 | tf_op jit(solution)/shard_map/ppermute | solution.py:42
  29.3 14.2 %collective-permute-start.6 = (bf16[128,2304]{1,0:T(8,128)(2,1)}, bf16[128,2304]{1,0:T(8,128)(2,1)}, u32[]{:S(2)}, u32[]{:S(2)}) collective-permute-start(bf16[128,2304]{1,0:T(8,128)(2,1)} %get-tuple-element.36.refs_0_.refs_2_.refs_14_), channel_id=1, source_target_pairs={{0,128},{16,144},{32,160},{48,176},{64,192},{80,208},{96,224},{112... | collective-permute-start | bytes 1769480 | tf_op jit(solution)/shard_map/ppermute | solution.py:46
  29.5 15.1 %collective-permute-start.4 = (bf16[128,2304]{1,0:T(8,128)(2,1)}, bf16[128,2304]{1,0:T(8,128)(2,1)S(1)}, u32[]{:S(2)}, u32[]{:S(2)}) collective-permute-start(bf16[128,2304]{1,0:T(8,128)(2,1)} %get-tuple-element.36.refs_0_.refs_2_.refs_14_), channel_id=1, source_target_pairs={{0,16},{16,32},{32,48},{48,64},{64,80},{80,96},{96,112},{112,0},{1... | collective-permute-start | bytes 1769480 | tf_op jit(solution)/shard_map/ppermute | solution.py:38
  31.2 18.6 %collective-permute-start.10 = (bf16[2,576,128]{2,1,0:T(8,128)(2,1)}, bf16[2,576,128]{2,1,0:T(8,128)(2,1)S(1)}, u32[]{:S(2)}, u32[]{:S(2)}) collective-permute-start(bf16[2,576,128]{2,1,0:T(8,128)(2,1)} %stack.124.refs_3_.a_ref), channel_id=1, source_target_pairs={{0,4},{1,5},{2,6},{3,7},{4,0},{5,1},{6,2},{7,3},{8,12},{9,13},{10,... | collective-permute-start | bytes 884744 | tf_op jit(solution)/shard_map/ppermute | solution.py:56
  46.1 16.6 %collective-permute-start.9 = (bf16[128,2304]{1,0:T(8,128)(2,1)}, bf16[128,2304]{1,0:T(8,128)(2,1)}, u32[]{:S(2)}, u32[]{:S(2)}) collective-permute-start(bf16[128,2304]{1,0:T(8,128)(2,1)} %get-tuple-element.39.refs_0_.refs_8_), channel_id=1, source_target_pairs={{0,128},{16,144},{32,160},{48,176},{64,192},{80,208},{96,224},{112... | collective-permute-start | bytes 1769480 | tf_op jit(solution)/shard_map/ppermute | solution.py:46
  47.8 14.8 %collective-permute-start.8 = (bf16[128,2304]{1,0:T(8,128)(2,1)}, bf16[128,2304]{1,0:T(8,128)(2,1)}, u32[]{:S(2)}, u32[]{:S(2)}) collective-permute-start(bf16[128,2304]{1,0:T(8,128)(2,1)} %get-tuple-element.39.refs_0_.refs_8_), channel_id=1, source_target_pairs={{0,112},{16,0},{32,16},{48,32},{64,48},{80,64},{96,80},{112,96},{1... | collective-permute-start | bytes 1769480 | tf_op jit(solution)/shard_map/ppermute | solution.py:42
  47.8 14.8 %collective-permute-start.7 = (bf16[128,2304]{1,0:T(8,128)(2,1)}, bf16[128,2304]{1,0:T(8,128)(2,1)S(1)}, u32[]{:S(2)}, u32[]{:S(2)}) collective-permute-start(bf16[128,2304]{1,0:T(8,128)(2,1)} %get-tuple-element.38.refs_0_.refs_1_.refs_10_), channel_id=1, source_target_pairs={{0,16},{16,32},{32,48},{48,64},{64,80},{80,96},{96,112},{112,0},{1... | collective-permute-start | bytes 1769480 | tf_op jit(solution)/shard_map/ppermute | solution.py:38
  52.5 20.9 %collective-permute-start.15 = (bf16[4,576,128]{2,1,0:T(8,128)(2,1)}, bf16[4,576,128]{2,1,0:T(8,128)(2,1)}, u32[]{:S(2)}, u32[]{:S(2)}) collective-permute-start(bf16[4,576,128]{2,1,0:T(8,128)(2,1)} %stack.125.refs_3_.a_ref), channel_id=1, source_target_pairs={{0,8},{1,9},{2,10},{3,11},{4,12},{5,13},{6,14},{7,15},{8,0},{9,1},... | collective-permute-start | bytes 1769480 | tf_op jit(solution)/shard_map/ppermute | solution.py:60
  54.8 21.0 %collective-permute-start.14 = (bf16[128,2304]{1,0:T(8,128)(2,1)}, bf16[128,2304]{1,0:T(8,128)(2,1)}, u32[]{:S(2)}, u32[]{:S(2)}) collective-permute-start(bf16[128,2304]{1,0:T(8,128)(2,1)} %get-tuple-element.38.refs_0_.refs_1_.refs_10_), channel_id=1, source_target_pairs={{0,128},{16,144},{32,160},{48,176},{64,192},{80,208},{96,224},{112... | collective-permute-start | bytes 1769480 | tf_op jit(solution)/shard_map/ppermute | solution.py:46
  62.6 13.7 %collective-permute-start.16 = (f32[2,576,128]{2,1,0:T(8,128)}, f32[2,576,128]{2,1,0:T(8,128)}, u32[]{:S(2)}, u32[]{:S(2)}) collective-permute-start(f32[2,576,128]{2,1,0:T(8,128)} %get-tuple-element.48), channel_id=1, source_target_pairs={{0,1},{1,0},{2,3},{3,2},{4,5},{5,4},{6,7},{7,6},{8,9},{9,8},{10,11... | collective-permute-start | bytes 1769480 | tf_op jit(solution)/shard_map/ppermute | solution.py:72
  64.1 16.1 %collective-permute-start.13 = (bf16[128,2304]{1,0:T(8,128)(2,1)}, bf16[128,2304]{1,0:T(8,128)(2,1)}, u32[]{:S(2)}, u32[]{:S(2)}) collective-permute-start(bf16[128,2304]{1,0:T(8,128)(2,1)} %get-tuple-element.42.refs_0_.refs_9_), channel_id=1, source_target_pairs={{0,112},{16,0},{32,16},{48,32},{64,48},{80,64},{96,80},{112,96},{1... | collective-permute-start | bytes 1769480 | tf_op jit(solution)/shard_map/ppermute | solution.py:42
  64.7 16.9 %collective-permute-start.12 = (bf16[128,2304]{1,0:T(8,128)(2,1)}, bf16[128,2304]{1,0:T(8,128)(2,1)S(1)}, u32[]{:S(2)}, u32[]{:S(2)}) collective-permute-start(bf16[128,2304]{1,0:T(8,128)(2,1)} %get-tuple-element.45.refs_5_.refs_0_.refs_6_), channel_id=1, source_target_pairs={{0,16},{16,32},{32,48},{48,64},{64,80},{80,96},{96,112},{112,0},{1... | collective-permute-start | bytes 1769480 | tf_op jit(solution)/shard_map/ppermute | solution.py:38
  73.4 18.8 %collective-permute-start.11 = (f32[3,576,128]{2,1,0:T(8,128)}, f32[3,576,128]{2,1,0:T(8,128)}, u32[]{:S(2)}, u32[]{:S(2)}) collective-permute-start(f32[3,576,128]{2,1,0:T(8,128)} %get-tuple-element.47), channel_id=1, source_target_pairs={{0,1},{1,0},{2,3},{3,2},{4,5},{5,4},{6,7},{7,6},{8,9},{9,8},{10,11... | collective-permute-start | bytes 2654216 | tf_op jit(solution)/shard_map/ppermute | solution.py:72
  75.8 23.2 %collective-permute-start.20 = (bf16[8,576,128]{2,1,0:T(8,128)(2,1)}, bf16[8,576,128]{2,1,0:T(8,128)(2,1)}, u32[]{:S(2)}, u32[]{:S(2)}) collective-permute-start(bf16[8,576,128]{2,1,0:T(8,128)(2,1)} %stack.126.refs_3_.mine_ref), channel_id=1, source_target_pairs={{0,1},{1,0},{2,3},{3,2},{4,5},{5,4},{6,7},{7,6},{8,9},{9,8},{10,11... | collective-permute-start | bytes 3538952 | tf_op jit(solution)/shard_map/ppermute | solution.py:72
  83.0 1.9 %collective-permute-start.21 = (f32[8,128]{1,0:T(8,128)}, f32[8,128]{1,0:T(8,128)S(1)}, u32[]{:S(2)}, u32[]{:S(2)}) collective-permute-start(f32[8,128]{1,0:T(8,128)} %get-tuple-element.52), channel_id=1, source_target_pairs={{0,1},{1,0},{2,3},{3,2},{4,5},{5,4},{6,7},{7,6},{8,9},{9,8},{10,11... | collective-permute-start | bytes 12296 | tf_op jit(solution)/shard_map/ppermute | solution.py:72
  83.0 16.0 %collective-permute-start.19 = (bf16[128,2304]{1,0:T(8,128)(2,1)}, bf16[128,2304]{1,0:T(8,128)(2,1)S(1)}, u32[]{:S(2)}, u32[]{:S(2)}) collective-permute-start(bf16[128,2304]{1,0:T(8,128)(2,1)} %get-tuple-element.37.refs_4_), channel_id=1, source_target_pairs={{0,128},{16,144},{32,160},{48,176},{64,192},{80,208},{96,224},{112... | collective-permute-start | bytes 1769480 | tf_op jit(solution)/shard_map/ppermute | solution.py:46
  84.4 17.0 %collective-permute-start.17 = (bf16[128,2304]{1,0:T(8,128)(2,1)}, bf16[128,2304]{1,0:T(8,128)(2,1)}, u32[]{:S(2)}, u32[]{:S(2)}) collective-permute-start(bf16[128,2304]{1,0:T(8,128)(2,1)} %get-tuple-element.50.refs_0_.refs_11_), channel_id=1, source_target_pairs={{0,16},{16,32},{32,48},{48,64},{64,80},{80,96},{96,112},{112,0},{1... | collective-permute-start | bytes 1769480 | tf_op jit(solution)/shard_map/ppermute | solution.py:38
  85.0 16.5 %collective-permute-start.18 = (bf16[128,2304]{1,0:T(8,128)(2,1)}, bf16[128,2304]{1,0:T(8,128)(2,1)}, u32[]{:S(2)}, u32[]{:S(2)}) collective-permute-start(bf16[128,2304]{1,0:T(8,128)(2,1)} %get-tuple-element.51.refs_1_.refs_13_), channel_id=1, source_target_pairs={{0,112},{16,0},{32,16},{48,32},{64,48},{80,64},{96,80},{112,96},{1... | collective-permute-start | bytes 1769480 | tf_op jit(solution)/shard_map/ppermute | solution.py:42
  92.2 1.9 %collective-permute-start.22 = (f32[1,576,128]{2,1,0:T(8,128)}, f32[1,576,128]{2,1,0:T(8,128)S(1)}, u32[]{:S(2)}, u32[]{:S(2)}) collective-permute-start(f32[1,576,128]{2,1,0:T(8,128)} %get-tuple-element.54), channel_id=1, source_target_pairs={{0,1},{1,0},{2,3},{3,2},{4,5},{5,4},{6,7},{7,6},{8,9},{9,8},{10,11... | collective-permute-start | bytes 884744 | tf_op jit(solution)/shard_map/ppermute | solution.py:72
  106.5 19.0 %copy-start.15 = (s32[29]{0:T(128)S(1)}, s32[29]{0:T(128)}, u32[]{:S(2)}) copy-start(s32[29]{0:T(128)} %stack.121.s_ref) | copy-start | bytes 352
  106.5 19.0 %collective-permute-start.23 = (f32[2,576,128]{2,1,0:T(8,128)}, f32[2,576,128]{2,1,0:T(8,128)}, u32[]{:S(2)}, u32[]{:S(2)}) collective-permute-start(f32[2,576,128]{2,1,0:T(8,128)} %chosen_sums.3), channel_id=1, source_target_pairs={{0,1},{1,0},{2,3},{3,2},{4,5},{5,4},{6,7},{7,6},{8,9},{9,8},{10,11... | collective-permute-start | bytes 1769480 | tf_op jit(solution)/shard_map/ppermute | solution.py:72
  106.6 10.1 %collective-permute-start.24 = (f32[576,128]{1,0:T(8,128)}, f32[576,128]{1,0:T(8,128)S(1)}, u32[]{:S(2)}, u32[]{:S(2)}) collective-permute-start(f32[576,128]{1,0:T(8,128)} %get-tuple-element.56.refs_5_), channel_id=1, source_target_pairs={{0,4},{1,5},{2,6},{3,7},{4,8},{5,9},{6,10},{7,11},{8,12},{9,13},{1... | collective-permute-start | bytes 884744 | tf_op jit(solution)/shard_map/ppermute | solution.py:60
  108.2 11.7 %collective-permute-start.26 = (f32[576,128]{1,0:T(8,128)}, f32[576,128]{1,0:T(8,128)}, u32[]{:S(2)}, u32[]{:S(2)}) collective-permute-start(f32[576,128]{1,0:T(8,128)} %get-tuple-element.57.refs_6_), channel_id=1, source_target_pairs={{0,8},{1,9},{2,10},{3,11},{4,12},{5,13},{6,14},{7,15},{8,0},{9,1},... | collective-permute-start | bytes 884744 | tf_op jit(solution)/shard_map/ppermute | solution.py:60
  110.0 15.4 %collective-permute-start.25 = (f32[576,128]{1,0:T(8,128)}, f32[576,128]{1,0:T(8,128)}, u32[]{:S(2)}, u32[]{:S(2)}) collective-permute-start(f32[576,128]{1,0:T(8,128)} %get-tuple-element.58.refs_7_), channel_id=1, source_target_pairs={{0,12},{1,13},{2,14},{3,15},{4,0},{5,1},{6,2},{7,3},{8,4},{9,5},{1... | collective-permute-start | bytes 884744 | tf_op jit(solution)/shard_map/ppermute | solution.py:60
  129.3 17.4 %collective-permute-start.27 = (f32[576,128]{1,0:T(8,128)S(1)}, f32[576,128]{1,0:T(8,128)S(1)}, u32[]{:S(2)}, u32[]{:S(2)}) collective-permute-start(f32[576,128]{1,0:T(8,128)S(1)} %get-tuple-element.63.refs_17_), channel_id=1, source_target_pairs={{0,4},{1,5},{2,6},{3,7},{4,8},{5,9},{6,10},{7,11},{8,12},{9,13},{1... | collective-permute-start | bytes 884744 | tf_op jit(solution)/shard_map/ppermute | solution.py:60
  130.0 16.7 %collective-permute-start.28 = (f32[576,128]{1,0:T(8,128)S(1)}, f32[576,128]{1,0:T(8,128)S(1)}, u32[]{:S(2)}, u32[]{:S(2)}) collective-permute-start(f32[576,128]{1,0:T(8,128)S(1)} %get-tuple-element.64.refs_19_), channel_id=1, source_target_pairs={{0,12},{1,13},{2,14},{3,15},{4,0},{5,1},{6,2},{7,3},{8,4},{9,5},{1... | collective-permute-start | bytes 884744 | tf_op jit(solution)/shard_map/ppermute | solution.py:60
  131.4 15.3 %collective-permute-start.29 = (f32[576,128]{1,0:T(8,128)S(1)}, f32[576,128]{1,0:T(8,128)S(1)}, u32[]{:S(2)}, u32[]{:S(2)}) collective-permute-start(f32[576,128]{1,0:T(8,128)S(1)} %get-tuple-element.65.refs_18_), channel_id=1, source_target_pairs={{0,8},{1,9},{2,10},{3,11},{4,12},{5,13},{6,14},{7,15},{8,0},{9,1},... | collective-permute-start | bytes 884744 | tf_op jit(solution)/shard_map/ppermute | solution.py:60
  148.0 9.7 %collective-permute-start.30 = (f32[576,128]{1,0:T(8,128)S(1)}, f32[576,128]{1,0:T(8,128)S(1)}, u32[]{:S(2)}, u32[]{:S(2)}) collective-permute-start(f32[576,128]{1,0:T(8,128)S(1)} %get-tuple-element.68), channel_id=1, source_target_pairs={{0,2},{1,3},{2,0},{3,1},{4,6},{5,7},{6,4},{7,5},{8,10},{9,11},{10,... | collective-permute-start | bytes 884744 | tf_op jit(solution)/shard_map/ppermute | solution.py:64
  (19 other events, 114.0 us)

commit v6 on v5

--- a/solution.py
+++ b/solution.py
@@ -9,7 +9,7 @@
 
 XL, Z = 2, 8
 Y, XH, C = 4, 2, 2
-VMEM_LIMIT = 63 << 20
+VMEM_LIMIT = 127 << 19
 TAIL_LIMIT = 32 << 20
 NO_COST = pl.CostEstimate(flops=1, bytes_accessed=1, transcendentals=0)
 
@@ -82,18 +82,19 @@
     return pltpu.CompilerParams(vmem_limit_bytes=limit)
 
 
-def tie_kernel(*refs):
-    refs[-1][...] = jnp.zeros_like(refs[-1])
-
-
-def tie(values, after):
+def tie_kernel(n, *refs):
+    for token_ref in refs[n:]:
+        token_ref[...] = jnp.zeros_like(token_ref)
+
+
+def tie(values, after, tokens):
     n = len(values)
     return pl.pallas_call(
-        tie_kernel,
+        functools.partial(tie_kernel, 2 * n + len(after)),
         out_shape=[jax.ShapeDtypeStruct(v.shape, v.dtype) for v in values]
-        + [jax.ShapeDtypeStruct((8, 128), jnp.float32)],
+        + [jax.ShapeDtypeStruct((8, 128), jnp.float32)] * tokens,
         in_specs=[IN_HBM] * n + [ANYWHERE] * len(after),
-        out_specs=[IN_HBM] * n + [VECTOR],
+        out_specs=[IN_HBM] * n + [VECTOR] * tokens,
         input_output_aliases={k: k for k in range(n)},
         compiler_params=params(),
         cost_estimate=NO_COST,
@@ -367,7 +368,7 @@
             pltpu.SemaphoreType.DMA((n,)),
             pltpu.SemaphoreType.DMA((cols // tile,)),
         ],
-        compiler_params=params(TAIL_LIMIT),
+        compiler_params=params(),
         cost_estimate=NO_COST,
         name="weight_sums",
     )(scalars, mine, other, *shards, *after)
@@ -438,11 +439,11 @@
     def over_y(parts):
         return [parts[0], in_y(parts[1], 1), in_y(parts[3], -1), in_y(parts[2], 2)]
 
-    def phase(names, sends, *after):
+    def phase(names, sends, *after, tokens=0):
         s = [h[name] for name in sends]
-        *got, token = tie([up(s[0]), down(s[1]), across(s[2])], after)
+        got = tie([up(s[0]), down(s[1]), across(s[2])], after, tokens)
         h.update(zip(names, got))
-        return token
+        return got[3:]
 
     mine = touch(inputs.T[None])
     pair = in_xh(mine)
@@ -459,8 +460,10 @@
     other = in_core(column)
     keep_b, send_b = partials(*mixed)
     got_b = in_core(send_b)
-    token = phase(("u4", "dx3", "ux2"), ("u3", "dx2", "u2"), column, got_a, keep_b)
-    keep_c, send_c = partials(*last_early, in_core(token))
+    (token,) = phase(
+        ("u4", "dx3", "ux2"), ("u3", "dx2", "u2"), column, got_a, keep_b, tokens=1
+    )
+    keep_c, send_c = partials(*last_early, in_core(token), other)
     got_c = in_core(send_c)
     early = place(
         at_early,
@@ -478,8 +481,8 @@
         at_late,
         scalars,
         [(keep_b, got_b), (keep_d, got_d)],
-        TAIL_LIMIT,
-        early[1:],
+        VMEM_LIMIT,
+        [],
     )
 
     grad_weight, token = weight_sums(

time: 159 us -> 154 us (0.969)
  local copies, waits for them, and re-layouts: 9.81 us -> 5.43 us
    unnamed x40 -> x20, local copies, waits for them, and re-layouts: 9.18 us -> 4.78 us
    ppermute x7, waiting for transfers between devices: 9.35 us -> 5.31 us  [in_y(): return lax.ppermute(t, 'gy', gy_pairs(dy, 0, 0))]
    pallas_call x5, Pallas kernels: 2.97 us -> 0.6 us  [tie(): pl.pallas_call(functools.partial(tie_kernel, 2 * n + len(after)), out_sha...]
    ppermute x5, waiting for transfers between devices: 13.5 us -> 15.9 us  [down(): return lax.ppermute(t, 'gx', gx_pairs(0, -1))]
    pallas_call x1, Pallas kernels: 11.3 us -> 13 us  [weight_sums(): pl.pallas_call(functools.partial(weight_kernel, base, n, tile, scale), ou...]
  transfers between devices with their start and end apart: 31 -> 31, of which waited for: 15 -> 15; matrix products, arithmetic and copies ran while one was open for 0% -> 0% of each run, Pallas kernels for 29% -> 32%
where the time goes in v6:
time: 154 us; the launch traced here: 153 us
  Pallas kernels  55.3 us (36%)
  waiting for transfers between devices  54.2 us (35%)
  starting transfers between devices  37 us (24%)
  local copies, waits for them, and re-layouts  5.43 us (4%)
    ppermute x2, waiting for transfers between devices, in_xh(): return lax.ppermute(t, 'gy', gy_pairs(0, 1, 0))  17.7 us
    pallas_call x3, Pallas kernels, partial_sums(): pl.pallas_call(functools.partial(partial_kernel, places), out_shape=(out,...  17.5 us
    ppermute x5, waiting for transfers between devices, down(): return lax.ppermute(t, 'gx', gx_pairs(0, -1))  15.9 us
    ppermute x5, starting transfers between devices, down(): return lax.ppermute(t, 'gx', gx_pairs(0, -1))  13.9 us
    pallas_call x1, Pallas kernels, weight_sums(): pl.pallas_call(functools.partial(weight_kernel, base, n, tile, scale), ou...  13 us
    ppermute x7, starting transfers between devices, in_y(): return lax.ppermute(t, 'gy', gy_pairs(dy, 0, 0))  10.7 us
    pallas_call x2, Pallas kernels, chosen_sums(): pl.pallas_call(functools.partial(chosen_kernel, n, own), out_shape=jax.Sh...  8.94 us
    ppermute x5, waiting for transfers between devices, up(): return lax.ppermute(t, 'gx', gx_pairs(0, 1))  8.23 us
  transfers between devices with their start and end apart: 31, of which 15 were waited for; matrix products, arithmetic and copies ran while one was open for 0% of the time, Pallas kernels for 32%

profile of v6, /device:TPU:8, one launch (start us, length us, event | category | flops | bytes accessed | tf_op | source)
XLA Modules:
  0.0 153.5 jit_solution(13579711528474801618)
XLA Ops:
  2.2 5.9 %collective-permute-start.1 = (bf16[128,2304]{1,0:T(8,128)(2,1)}, bf16[128,2304]{1,0:T(8,128)(2,1)}, u32[]{:S(2)}, u32[]{:S(2)}) collective-permute-start(bf16[128,2304]{1,0:T(8,128)(2,1)} %refs_0_.1), channel_id=1, source_target_pairs={{0,112},{16,0},{32,16},{48,32},{64,48},{80,64},{96,80},{112,96},{1... | collective-permute-start | bytes 1769480 | tf_op jit(solution)/shard_map/ppermute | solution.py:42
  9.6 2.7 %collective-permute-start.3 = (bf16[1,576,128]{2,1,0:T(8,128)(2,1)}, bf16[1,576,128]{2,1,0:T(8,128)(2,1)S(1)}, u32[]{:S(2)}, u32[]{:S(2)}) collective-permute-start(bf16[1,576,128]{2,1,0:T(8,128)(2,1)} %touch.1.a_ref), channel_id=1, source_target_pairs={{0,2},{1,3},{2,0},{3,1},{4,6},{5,7},{6,4},{7,5},{8,10},{9,11},{10,... | collective-permute-start | bytes 442376 | tf_op jit(solution)/shard_map/ppermute | solution.py:64
  12.4 9.0 %collective-permute-done.3.refs_3_.b_ref = bf16[1,576,128]{2,1,0:T(8,128)(2,1)S(1)} collective-permute-done((bf16[1,576,128]{2,1,0:T(8,128)(2,1)}, bf16[1,576,128]{2,1,0:T(8,128)(2,1)S(1)}, u32[]{:S(2)}, u32[]{:S(2)}) %collective-permute-start.3) | collective-permute-done | bytes 147488 | tf_op jit(solution)/shard_map/ppermute | solution.py:64
  21.4 2.7 %collective-permute-done.refs_0_ = bf16[128,2304]{1,0:T(8,128)(2,1)} collective-permute-done((bf16[128,2304]{1,0:T(8,128)(2,1)}, bf16[128,2304]{1,0:T(8,128)(2,1)}, u32[]{:S(2)}, u32[]{:S(2)}) %collective-permute-start) | collective-permute-done | bytes 589856 | tf_op jit(solution)/shard_map/ppermute | solution.py:38
  24.1 3.8 %collective-permute-start.5 = (bf16[128,2304]{1,0:T(8,128)(2,1)}, bf16[128,2304]{1,0:T(8,128)(2,1)}, u32[]{:S(2)}, u32[]{:S(2)}) collective-permute-start(bf16[128,2304]{1,0:T(8,128)(2,1)} %get-tuple-element.37.refs_4_), channel_id=1, source_target_pairs={{0,112},{16,0},{32,16},{48,32},{64,48},{80,64},{96,80},{112,96},{1... | collective-permute-start | bytes 1769480 | tf_op jit(solution)/shard_map/ppermute | solution.py:42
  28.1 1.7 %stack.124.refs_3_.a_ref = bf16[2,576,128]{2,1,0:T(8,128)(2,1)} custom-call(bf16[1,576,128]{2,1,0:T(8,128)(2,1)} %touch.1.a_ref, bf16[1,576,128]{2,1,0:T(8,128)(2,1)} %copy-done.6, bf16[128,2304]{1,0:T(8,128)(2,1)} %get-tuple-element.36.refs_0_.refs_2_.refs_14_), custom_call_target="tpu_custom_call" | custom-call | flops 1 | bytes 1 | tf_op jit(solution)/shard_map/stack/pallas_call | solution.py:128
  30.3 9.6 %collective-permute-done.5.refs_1_ = bf16[128,2304]{1,0:T(8,128)(2,1)} collective-permute-done((bf16[128,2304]{1,0:T(8,128)(2,1)}, bf16[128,2304]{1,0:T(8,128)(2,1)}, u32[]{:S(2)}, u32[]{:S(2)}) %collective-permute-start.5) | collective-permute-done | bytes 589856 | tf_op jit(solution)/shard_map/ppermute | solution.py:42
  39.9 2.2 %collective-permute-done.6.refs_2_ = bf16[128,2304]{1,0:T(8,128)(2,1)} collective-permute-done((bf16[128,2304]{1,0:T(8,128)(2,1)}, bf16[128,2304]{1,0:T(8,128)(2,1)}, u32[]{:S(2)}, u32[]{:S(2)}) %collective-permute-start.6) | collective-permute-done | bytes 589856 | tf_op jit(solution)/shard_map/ppermute | solution.py:46
  43.3 1.7 %collective-permute-start.9 = (bf16[128,2304]{1,0:T(8,128)(2,1)}, bf16[128,2304]{1,0:T(8,128)(2,1)}, u32[]{:S(2)}, u32[]{:S(2)}) collective-permute-start(bf16[128,2304]{1,0:T(8,128)(2,1)} %get-tuple-element.39.refs_0_.refs_8_), channel_id=1, source_target_pairs={{0,128},{16,144},{32,160},{48,176},{64,192},{80,208},{96,224},{112... | collective-permute-start | bytes 1769480 | tf_op jit(solution)/shard_map/ppermute | solution.py:46
  45.1 2.0 %collective-permute-start.7 = (bf16[128,2304]{1,0:T(8,128)(2,1)}, bf16[128,2304]{1,0:T(8,128)(2,1)}, u32[]{:S(2)}, u32[]{:S(2)}) collective-permute-start(bf16[128,2304]{1,0:T(8,128)(2,1)} %get-tuple-element.38.refs_0_.refs_1_.refs_10_), channel_id=1, source_target_pairs={{0,16},{16,32},{32,48},{48,64},{64,80},{80,96},{96,112},{112,0},{1... | collective-permute-start | bytes 1769480 | tf_op jit(solution)/shard_map/ppermute | solution.py:38
  47.8 1.9 %stack.125.refs_3_.a_ref = bf16[4,576,128]{2,1,0:T(8,128)(2,1)} custom-call(bf16[2,576,128]{2,1,0:T(8,128)(2,1)} %stack.124.refs_3_.a_ref, bf16[2,576,128]{2,1,0:T(8,128)(2,1)} %copy-done.7, bf16[128,2304]{1,0:T(8,128)(2,1)} %get-tuple-element.38.refs_0_.refs_1_.refs_10_), custom_call_target="tpu_custom_call" | custom-call | flops 1 | bytes 1 | tf_op jit(solution)/shard_map/stack/pallas_call | solution.py:128
  49.7 2.3 %collective-permute-start.15 = (bf16[4,576,128]{2,1,0:T(8,128)(2,1)}, bf16[4,576,128]{2,1,0:T(8,128)(2,1)}, u32[]{:S(2)}, u32[]{:S(2)}) collective-permute-start(bf16[4,576,128]{2,1,0:T(8,128)(2,1)} %stack.125.refs_3_.a_ref), channel_id=1, source_target_pairs={{0,8},{1,9},{2,10},{3,11},{4,12},{5,13},{6,14},{7,15},{8,0},{9,1},... | collective-permute-start | bytes 1769480 | tf_op jit(solution)/shard_map/ppermute | solution.py:60
  52.9 5.8 %partial_sums.3 = (f32[2,576,128]{2,1,0:T(8,128)}, f32[2,576,128]{2,1,0:T(8,128)}) custom-call(s32[29]{0:T(128)} %stack.121.s_ref, bf16[576,2304]{1,0:T(8,128)(2,1)} %w_any.9, bf16[128,2304]{1,0:T(8,128)(2,1)} %get-tuple-element.39.refs_0_.refs_8_, bf16[128,2304]{1,0:T(8,128)(2,1)} %get-tuple-element.38.refs_0_.refs_1_.refs_10_, ...), custom_call_target="tpu_custom_call" | custom-call | flops 1 | bytes 1 | tf_op jit(solution)/shard_map/partial_sums/pallas_call | solution.py:199
  59.9 3.5 %collective-permute-done.15.b_ref = bf16[4,576,128]{2,1,0:T(8,128)(2,1)} collective-permute-done((bf16[4,576,128]{2,1,0:T(8,128)(2,1)}, bf16[4,576,128]{2,1,0:T(8,128)(2,1)}, u32[]{:S(2)}, u32[]{:S(2)}) %collective-permute-start.15) | collective-permute-done | bytes 589856 | tf_op jit(solution)/shard_map/ppermute | solution.py:60
  63.4 2.3 %stack.126.refs_3_.mine_ref = bf16[8,576,128]{2,1,0:T(8,128)(2,1)} custom-call(bf16[4,576,128]{2,1,0:T(8,128)(2,1)} %stack.125.refs_3_.a_ref, bf16[4,576,128]{2,1,0:T(8,128)(2,1)} %collective-permute-done.15.b_ref, bf16[128,2304]{1,0:T(8,128)(2,1)} %get-tuple-element.45.refs_5_.refs_0_.refs_6_), custom_call_target="tpu_custom_call" | custom-call | flops 1 | bytes 1 | tf_op jit(solution)/shard_map/stack/pallas_call | solution.py:128
  68.3 7.2 %partial_sums.4 = (f32[3,576,128]{2,1,0:T(8,128)}, f32[3,576,128]{2,1,0:T(8,128)}) custom-call(s32[29]{0:T(128)} %stack.121.s_ref, bf16[576,2304]{1,0:T(8,128)(2,1)} %w_any.9, bf16[128,2304]{1,0:T(8,128)(2,1)} %get-tuple-element.42.refs_0_.refs_9_, bf16[128,2304]{1,0:T(8,128)(2,1)} %refs_0_.1, bf16[128,2304]{1,0:T(8,128)(2,1)} %get-tuple-element.43.refs_2_.refs_1_, ...), custom_call_target="tpu_custom_call" | custom-call | flops 1 | bytes 1 | tf_op jit(solution)/shard_map/partial_sums/pallas_call | solution.py:199
  75.6 6.2 %collective-permute-done.13.refs_1_ = bf16[128,2304]{1,0:T(8,128)(2,1)} collective-permute-done((bf16[128,2304]{1,0:T(8,128)(2,1)}, bf16[128,2304]{1,0:T(8,128)(2,1)}, u32[]{:S(2)}, u32[]{:S(2)}) %collective-permute-start.13) | collective-permute-done | bytes 589856 | tf_op jit(solution)/shard_map/ppermute | solution.py:42
  81.8 2.4 %collective-permute-done.12.refs_0_ = bf16[128,2304]{1,0:T(8,128)(2,1)} collective-permute-done((bf16[128,2304]{1,0:T(8,128)(2,1)}, bf16[128,2304]{1,0:T(8,128)(2,1)}, u32[]{:S(2)}, u32[]{:S(2)}) %collective-permute-start.12) | collective-permute-done | bytes 589856 | tf_op jit(solution)/shard_map/ppermute | solution.py:38
  86.2 2.8 %collective-permute-start.18 = (bf16[128,2304]{1,0:T(8,128)(2,1)}, bf16[128,2304]{1,0:T(8,128)(2,1)}, u32[]{:S(2)}, u32[]{:S(2)}) collective-permute-start(bf16[128,2304]{1,0:T(8,128)(2,1)} %get-tuple-element.51.refs_1_.refs_13_), channel_id=1, source_target_pairs={{0,112},{16,0},{32,16},{48,32},{64,48},{80,64},{96,80},{112,96},{1... | collective-permute-start | bytes 1769480 | tf_op jit(solution)/shard_map/ppermute | solution.py:42
  89.0 4.5 %partial_sums.5 = (f32[1,576,128]{2,1,0:T(8,128)}, f32[1,576,128]{2,1,0:T(8,128)}) custom-call(s32[29]{0:T(128)} %stack.121.s_ref, bf16[576,2304]{1,0:T(8,128)(2,1)} %w_any.9, bf16[128,2304]{1,0:T(8,128)(2,1)} %get-tuple-element.50.refs_0_.refs_11_, bf16[128,2304]{1,0:T(8,128)(2,1)} %get-tuple-element.51.refs_1_.refs_13_, f32[8,128]{1,0:T(8,128)} %copy-done.9, ...), custom_call_target="tpu_custom_call" | custom-call | flops 1 | bytes 1 | tf_op jit(solution)/shard_map/partial_sums/pallas_call | solution.py:199
  93.6 1.8 %collective-permute-done.22.refs_5_ = f32[1,576,128]{2,1,0:T(8,128)S(1)} collective-permute-done((f32[1,576,128]{2,1,0:T(8,128)}, f32[1,576,128]{2,1,0:T(8,128)S(1)}, u32[]{:S(2)}, u32[]{:S(2)}) %collective-permute-start.22) | collective-permute-done | bytes 294944 | tf_op jit(solution)/shard_map/ppermute | solution.py:72
  96.1 3.3 %place.2 = (f32[576,128]{1,0:T(8,128)}, f32[576,128]{1,0:T(8,128)}, f32[576,128]{1,0:T(8,128)}, f32[576,128]{1,0:T(8,128)}) custom-call(s32[29]{0:T(128)} %stack.121.s_ref, f32[2,576,128]{2,1,0:T(8,128)} %get-tuple-element.41.refs_4_.refs_0_, f32[2,576,128]{2,1,0:T(8,128)} %collective-permute-done.16.refs_4_.refs_1_, ...), custom_call_target="tpu_custom_call" | custom-call | flops 1 | bytes 1 | tf_op jit(solution)/shard_map/place/pallas_call | solution.py:273
  100.9 1.9 %collective-permute-done.17.refs_0_ = bf16[128,2304]{1,0:T(8,128)(2,1)} collective-permute-done((bf16[128,2304]{1,0:T(8,128)(2,1)}, bf16[128,2304]{1,0:T(8,128)(2,1)}, u32[]{:S(2)}, u32[]{:S(2)}) %collective-permute-start.17) | collective-permute-done | bytes 589856 | tf_op jit(solution)/shard_map/ppermute | solution.py:38
  102.7 4.5 %chosen_sums.3 = f32[2,576,128]{2,1,0:T(8,128)} custom-call(s32[29]{0:T(128)} %stack.121.s_ref, bf16[576,2304]{1,0:T(8,128)(2,1)} %w_any.9, bf16[128,2304]{1,0:T(8,128)(2,1)} %get-tuple-element.49.refs_0_.refs_2_, bf16[128,2304]{1,0:T(8,128)(2,1)} %get-tuple-element.59.refs_1_.refs_3_, bf16[128,2304]{1,0:T(8,128)(2,1)} %get-tuple-element.60.refs_2_.refs_5_, ...), custom_call_target="tpu_custom_call" | custom-call | flops 1 | bytes 1 | tf_op jit(solution)/shard_map/chosen_sums/pallas_call | solution.py:239
  107.3 1.7 %collective-permute-start.27 = (f32[576,128]{1,0:T(8,128)}, f32[576,128]{1,0:T(8,128)S(1)}, u32[]{:S(2)}, u32[]{:S(2)}) collective-permute-start(f32[576,128]{1,0:T(8,128)} %get-tuple-element.56.refs_5_), channel_id=1, source_target_pairs={{0,4},{1,5},{2,6},{3,7},{4,8},{5,9},{6,10},{7,11},{8,12},{9,13},{1... | collective-permute-start | bytes 884744 | tf_op jit(solution)/shard_map/ppermute | solution.py:60
  109.9 2.4 %collective-permute-start.28 = (f32[576,128]{1,0:T(8,128)}, f32[576,128]{1,0:T(8,128)}, u32[]{:S(2)}, u32[]{:S(2)}) collective-permute-start(f32[576,128]{1,0:T(8,128)} %get-tuple-element.58.refs_7_), channel_id=1, source_target_pairs={{0,12},{1,13},{2,14},{3,15},{4,0},{5,1},{6,2},{7,3},{8,4},{9,5},{1... | collective-permute-start | bytes 884744 | tf_op jit(solution)/shard_map/ppermute | solution.py:60
  112.3 4.5 %chosen_sums.2.refs_2_ = f32[2,576,128]{2,1,0:T(8,128)} custom-call(s32[29]{0:T(128)} %stack.121.s_ref, bf16[576,2304]{1,0:T(8,128)(2,1)} %w_any.9, bf16[128,2304]{1,0:T(8,128)(2,1)} %get-tuple-element.49.refs_0_.refs_2_, bf16[128,2304]{1,0:T(8,128)(2,1)} %get-tuple-element.59.refs_1_.refs_3_, bf16[128,2304]{1,0:T(8,128)(2,1)} %get-tuple-element.60.refs_2_.refs_5_, ...), custom_call_target="tpu_custom_call" | custom-call | flops 1 | bytes 1 | tf_op jit(solution)/shard_map/chosen_sums/pallas_call | solution.py:239
  116.8 3.0 %place.3 = (f32[576,128]{1,0:T(8,128)}, f32[576,128]{1,0:T(8,128)}, f32[576,128]{1,0:T(8,128)}, f32[576,128]{1,0:T(8,128)}) custom-call(s32[29]{0:T(128)} %stack.121.s_ref, f32[3,576,128]{2,1,0:T(8,128)} %get-tuple-element.46.refs_5_.refs_2_.refs_0_, f32[3,576,128]{2,1,0:T(8,128)} %collective-permute-done.11.refs_3_.refs_1_, ...), custom_call_target="tpu_custom_call" | custom-call | flops 1 | bytes 1 | tf_op jit(solution)/shard_map/place/pallas_call | solution.py:273
  119.8 2.0 %collective-permute-start.25 = (f32[576,128]{1,0:T(8,128)}, f32[576,128]{1,0:T(8,128)}, u32[]{:S(2)}, u32[]{:S(2)}) collective-permute-start(f32[576,128]{1,0:T(8,128)} %get-tuple-element.64.refs_19_), channel_id=1, source_target_pairs={{0,12},{1,13},{2,14},{3,15},{4,0},{5,1},{6,2},{7,3},{8,4},{9,5},{1... | collective-permute-start | bytes 884744 | tf_op jit(solution)/shard_map/ppermute | solution.py:60
  124.0 13.0 %weight_sums.1 = (f32[576,2304]{1,0:T(8,128)}, f32[8,128]{1,0:T(8,128)}) custom-call(s32[29]{0:T(128)} %stack.121.s_ref, bf16[8,576,128]{2,1,0:T(8,128)(2,1)} %stack.126.refs_3_.mine_ref, bf16[8,576,128]{2,1,0:T(8,128)(2,1)} %collective-permute-done.20.refs_3_.other_ref, bf16[128,2304]{1,0:T(8,128)(2,1)} %refs_0_.1, ...), custom_call_target="tpu_custom_call" | custom-call | flops 1 | bytes 1 | tf_op jit(solution)/shard_map/weight_sums/pallas_call | solution.py:356
  137.1 1.8 %collective-permute-done.26.refs_3_ = f32[576,128]{1,0:T(8,128)} collective-permute-done((f32[576,128]{1,0:T(8,128)}, f32[576,128]{1,0:T(8,128)}, u32[]{:S(2)}, u32[]{:S(2)}) %collective-permute-start.26) | collective-permute-done | bytes 294944 | tf_op jit(solution)/shard_map/ppermute | solution.py:60
  144.0 8.7 %collective-permute-done.30 = f32[576,128]{1,0:T(8,128)S(1)} collective-permute-done((f32[576,128]{1,0:T(8,128)S(1)}, f32[576,128]{1,0:T(8,128)S(1)}, u32[]{:S(2)}, u32[]{:S(2)}) %collective-permute-start.30) | collective-permute-done | bytes 294944 | tf_op jit(solution)/shard_map/ppermute | solution.py:64
  (70 shorter events, 23.8 us)
Async XLA Ops:
  0.6 20.7 %collective-permute-start.2 = (bf16[128,2304]{1,0:T(8,128)(2,1)}, bf16[128,2304]{1,0:T(8,128)(2,1)}, u32[]{:S(2)}, u32[]{:S(2)}) collective-permute-start(bf16[128,2304]{1,0:T(8,128)(2,1)} %refs_0_.1), channel_id=1, source_target_pairs={{0,128},{16,144},{32,160},{48,176},{64,192},{80,208},{96,224},{112... | collective-permute-start | bytes 1769480 | tf_op jit(solution)/shard_map/ppermute | solution.py:46
  2.2 19.2 %collective-permute-start.1 = (bf16[128,2304]{1,0:T(8,128)(2,1)}, bf16[128,2304]{1,0:T(8,128)(2,1)}, u32[]{:S(2)}, u32[]{:S(2)}) collective-permute-start(bf16[128,2304]{1,0:T(8,128)(2,1)} %refs_0_.1), channel_id=1, source_target_pairs={{0,112},{16,0},{32,16},{48,32},{64,48},{80,64},{96,80},{112,96},{1... | collective-permute-start | bytes 1769480 | tf_op jit(solution)/shard_map/ppermute | solution.py:42
  8.1 16.0 %collective-permute-start = (bf16[128,2304]{1,0:T(8,128)(2,1)}, bf16[128,2304]{1,0:T(8,128)(2,1)}, u32[]{:S(2)}, u32[]{:S(2)}) collective-permute-start(bf16[128,2304]{1,0:T(8,128)(2,1)} %refs_0_.1), channel_id=1, source_target_pairs={{0,16},{16,32},{32,48},{48,64},{64,80},{80,96},{96,112},{112,0},{1... | collective-permute-start | bytes 1769480 | tf_op jit(solution)/shard_map/ppermute | solution.py:38
  9.6 11.7 %collective-permute-start.3 = (bf16[1,576,128]{2,1,0:T(8,128)(2,1)}, bf16[1,576,128]{2,1,0:T(8,128)(2,1)S(1)}, u32[]{:S(2)}, u32[]{:S(2)}) collective-permute-start(bf16[1,576,128]{2,1,0:T(8,128)(2,1)} %touch.1.a_ref), channel_id=1, source_target_pairs={{0,2},{1,3},{2,0},{3,1},{4,6},{5,7},{6,4},{7,5},{8,10},{9,11},{10,... | collective-permute-start | bytes 442376 | tf_op jit(solution)/shard_map/ppermute | solution.py:64
  24.1 15.8 %collective-permute-start.5 = (bf16[128,2304]{1,0:T(8,128)(2,1)}, bf16[128,2304]{1,0:T(8,128)(2,1)}, u32[]{:S(2)}, u32[]{:S(2)}) collective-permute-start(bf16[128,2304]{1,0:T(8,128)(2,1)} %get-tuple-element.37.refs_4_), channel_id=1, source_target_pairs={{0,112},{16,0},{32,16},{48,32},{64,48},{80,64},{96,80},{112,96},{1... | collective-permute-start | bytes 1769480 | tf_op jit(solution)/shard_map/ppermute | solution.py:42
  27.9 14.2 %collective-permute-start.6 = (bf16[128,2304]{1,0:T(8,128)(2,1)}, bf16[128,2304]{1,0:T(8,128)(2,1)}, u32[]{:S(2)}, u32[]{:S(2)}) collective-permute-start(bf16[128,2304]{1,0:T(8,128)(2,1)} %get-tuple-element.36.refs_0_.refs_2_.refs_14_), channel_id=1, source_target_pairs={{0,128},{16,144},{32,160},{48,176},{64,192},{80,208},{96,224},{112... | collective-permute-start | bytes 1769480 | tf_op jit(solution)/shard_map/ppermute | solution.py:46
  28.1 15.2 %collective-permute-start.4 = (bf16[128,2304]{1,0:T(8,128)(2,1)}, bf16[128,2304]{1,0:T(8,128)(2,1)}, u32[]{:S(2)}, u32[]{:S(2)}) collective-permute-start(bf16[128,2304]{1,0:T(8,128)(2,1)} %get-tuple-element.36.refs_0_.refs_2_.refs_14_), channel_id=1, source_target_pairs={{0,16},{16,32},{32,48},{48,64},{64,80},{80,96},{96,112},{112,0},{1... | collective-permute-start | bytes 1769480 | tf_op jit(solution)/shard_map/ppermute | solution.py:38
  29.8 17.3 %collective-permute-start.10 = (bf16[2,576,128]{2,1,0:T(8,128)(2,1)}, bf16[2,576,128]{2,1,0:T(8,128)(2,1)S(1)}, u32[]{:S(2)}, u32[]{:S(2)}) collective-permute-start(bf16[2,576,128]{2,1,0:T(8,128)(2,1)} %stack.124.refs_3_.a_ref), channel_id=1, source_target_pairs={{0,4},{1,5},{2,6},{3,7},{4,0},{5,1},{6,2},{7,3},{8,12},{9,13},{10,... | collective-permute-start | bytes 884744 | tf_op jit(solution)/shard_map/ppermute | solution.py:56
  43.3 16.6 %collective-permute-start.9 = (bf16[128,2304]{1,0:T(8,128)(2,1)}, bf16[128,2304]{1,0:T(8,128)(2,1)}, u32[]{:S(2)}, u32[]{:S(2)}) collective-permute-start(bf16[128,2304]{1,0:T(8,128)(2,1)} %get-tuple-element.39.refs_0_.refs_8_), channel_id=1, source_target_pairs={{0,128},{16,144},{32,160},{48,176},{64,192},{80,208},{96,224},{112... | collective-permute-start | bytes 1769480 | tf_op jit(solution)/shard_map/ppermute | solution.py:46
  45.1 14.8 %collective-permute-start.8 = (bf16[128,2304]{1,0:T(8,128)(2,1)}, bf16[128,2304]{1,0:T(8,128)(2,1)}, u32[]{:S(2)}, u32[]{:S(2)}) collective-permute-start(bf16[128,2304]{1,0:T(8,128)(2,1)} %get-tuple-element.39.refs_0_.refs_8_), channel_id=1, source_target_pairs={{0,112},{16,0},{32,16},{48,32},{64,48},{80,64},{96,80},{112,96},{1... | collective-permute-start | bytes 1769480 | tf_op jit(solution)/shard_map/ppermute | solution.py:42
  45.1 14.8 %collective-permute-start.7 = (bf16[128,2304]{1,0:T(8,128)(2,1)}, bf16[128,2304]{1,0:T(8,128)(2,1)}, u32[]{:S(2)}, u32[]{:S(2)}) collective-permute-start(bf16[128,2304]{1,0:T(8,128)(2,1)} %get-tuple-element.38.refs_0_.refs_1_.refs_10_), channel_id=1, source_target_pairs={{0,16},{16,32},{32,48},{48,64},{64,80},{80,96},{96,112},{112,0},{1... | collective-permute-start | bytes 1769480 | tf_op jit(solution)/shard_map/ppermute | solution.py:38
  49.7 13.7 %collective-permute-start.15 = (bf16[4,576,128]{2,1,0:T(8,128)(2,1)}, bf16[4,576,128]{2,1,0:T(8,128)(2,1)}, u32[]{:S(2)}, u32[]{:S(2)}) collective-permute-start(bf16[4,576,128]{2,1,0:T(8,128)(2,1)} %stack.125.refs_3_.a_ref), channel_id=1, source_target_pairs={{0,8},{1,9},{2,10},{3,11},{4,12},{5,13},{6,14},{7,15},{8,0},{9,1},... | collective-permute-start | bytes 1769480 | tf_op jit(solution)/shard_map/ppermute | solution.py:60
  52.6 22.8 %collective-permute-start.14 = (bf16[128,2304]{1,0:T(8,128)(2,1)}, bf16[128,2304]{1,0:T(8,128)(2,1)}, u32[]{:S(2)}, u32[]{:S(2)}) collective-permute-start(bf16[128,2304]{1,0:T(8,128)(2,1)} %get-tuple-element.38.refs_0_.refs_1_.refs_10_), channel_id=1, source_target_pairs={{0,128},{16,144},{32,160},{48,176},{64,192},{80,208},{96,224},{112... | collective-permute-start | bytes 1769480 | tf_op jit(solution)/shard_map/ppermute | solution.py:46
  65.7 23.3 %collective-permute-start.20 = (bf16[8,576,128]{2,1,0:T(8,128)(2,1)}, bf16[8,576,128]{2,1,0:T(8,128)(2,1)}, u32[]{:S(2)}, u32[]{:S(2)}) collective-permute-start(bf16[8,576,128]{2,1,0:T(8,128)(2,1)} %stack.126.refs_3_.mine_ref), channel_id=1, source_target_pairs={{0,1},{1,0},{2,3},{3,2},{4,5},{5,4},{6,7},{7,6},{8,9},{9,8},{10,11... | collective-permute-start | bytes 3538952 | tf_op jit(solution)/shard_map/ppermute | solution.py:72
  65.7 9.9 %collective-permute-start.16 = (f32[2,576,128]{2,1,0:T(8,128)}, f32[2,576,128]{2,1,0:T(8,128)}, u32[]{:S(2)}, u32[]{:S(2)}) collective-permute-start(f32[2,576,128]{2,1,0:T(8,128)} %get-tuple-element.48), channel_id=1, source_target_pairs={{0,1},{1,0},{2,3},{3,2},{4,5},{5,4},{6,7},{7,6},{8,9},{9,8},{10,11... | collective-permute-start | bytes 1769480 | tf_op jit(solution)/shard_map/ppermute | solution.py:72
  66.2 15.6 %collective-permute-start.13 = (bf16[128,2304]{1,0:T(8,128)(2,1)}, bf16[128,2304]{1,0:T(8,128)(2,1)}, u32[]{:S(2)}, u32[]{:S(2)}) collective-permute-start(bf16[128,2304]{1,0:T(8,128)(2,1)} %get-tuple-element.42.refs_0_.refs_9_), channel_id=1, source_target_pairs={{0,112},{16,0},{32,16},{48,32},{64,48},{80,64},{96,80},{112,96},{1... | collective-permute-start | bytes 1769480 | tf_op jit(solution)/shard_map/ppermute | solution.py:42
  67.7 16.5 %collective-permute-start.12 = (bf16[128,2304]{1,0:T(8,128)(2,1)}, bf16[128,2304]{1,0:T(8,128)(2,1)}, u32[]{:S(2)}, u32[]{:S(2)}) collective-permute-start(bf16[128,2304]{1,0:T(8,128)(2,1)} %get-tuple-element.45.refs_5_.refs_0_.refs_6_), channel_id=1, source_target_pairs={{0,16},{16,32},{32,48},{48,64},{64,80},{80,96},{96,112},{112,0},{1... | collective-permute-start | bytes 1769480 | tf_op jit(solution)/shard_map/ppermute | solution.py:38
  75.5 18.1 %collective-permute-start.11 = (f32[3,576,128]{2,1,0:T(8,128)}, f32[3,576,128]{2,1,0:T(8,128)}, u32[]{:S(2)}, u32[]{:S(2)}) collective-permute-start(f32[3,576,128]{2,1,0:T(8,128)} %get-tuple-element.47), channel_id=1, source_target_pairs={{0,1},{1,0},{2,3},{3,2},{4,5},{5,4},{6,7},{7,6},{8,9},{9,8},{10,11... | collective-permute-start | bytes 2654216 | tf_op jit(solution)/shard_map/ppermute | solution.py:72
  84.8 1.4 collective-permute-start.21
  84.8 16.1 %collective-permute-start.19 = (bf16[128,2304]{1,0:T(8,128)(2,1)}, bf16[128,2304]{1,0:T(8,128)(2,1)}, u32[]{:S(2)}, u32[]{:S(2)}) collective-permute-start(bf16[128,2304]{1,0:T(8,128)(2,1)} %get-tuple-element.37.refs_4_), channel_id=1, source_target_pairs={{0,128},{16,144},{32,160},{48,176},{64,192},{80,208},{96,224},{112... | collective-permute-start | bytes 1769480 | tf_op jit(solution)/shard_map/ppermute | solution.py:46
  85.7 17.0 %collective-permute-start.17 = (bf16[128,2304]{1,0:T(8,128)(2,1)}, bf16[128,2304]{1,0:T(8,128)(2,1)}, u32[]{:S(2)}, u32[]{:S(2)}) collective-permute-start(bf16[128,2304]{1,0:T(8,128)(2,1)} %get-tuple-element.50.refs_0_.refs_11_), channel_id=1, source_target_pairs={{0,16},{16,32},{32,48},{48,64},{64,80},{80,96},{96,112},{112,0},{1... | collective-permute-start | bytes 1769480 | tf_op jit(solution)/shard_map/ppermute | solution.py:38
  86.2 16.5 %collective-permute-start.18 = (bf16[128,2304]{1,0:T(8,128)(2,1)}, bf16[128,2304]{1,0:T(8,128)(2,1)}, u32[]{:S(2)}, u32[]{:S(2)}) collective-permute-start(bf16[128,2304]{1,0:T(8,128)(2,1)} %get-tuple-element.51.refs_1_.refs_13_), channel_id=1, source_target_pairs={{0,112},{16,0},{32,16},{48,32},{64,48},{80,64},{96,80},{112,96},{1... | collective-permute-start | bytes 1769480 | tf_op jit(solution)/shard_map/ppermute | solution.py:42
  93.5 1.9 %collective-permute-start.22 = (f32[1,576,128]{2,1,0:T(8,128)}, f32[1,576,128]{2,1,0:T(8,128)S(1)}, u32[]{:S(2)}, u32[]{:S(2)}) collective-permute-start(f32[1,576,128]{2,1,0:T(8,128)} %get-tuple-element.54), channel_id=1, source_target_pairs={{0,1},{1,0},{2,3},{3,2},{4,5},{5,4},{6,7},{7,6},{8,9},{9,8},{10,11... | collective-permute-start | bytes 884744 | tf_op jit(solution)/shard_map/ppermute | solution.py:72
  107.2 9.6 %collective-permute-start.23 = (f32[2,576,128]{2,1,0:T(8,128)}, f32[2,576,128]{2,1,0:T(8,128)}, u32[]{:S(2)}, u32[]{:S(2)}) collective-permute-start(f32[2,576,128]{2,1,0:T(8,128)} %chosen_sums.3), channel_id=1, source_target_pairs={{0,1},{1,0},{2,3},{3,2},{4,5},{5,4},{6,7},{7,6},{8,9},{9,8},{10,11... | collective-permute-start | bytes 1769480 | tf_op jit(solution)/shard_map/ppermute | solution.py:72
  107.3 14.6 %collective-permute-start.27 = (f32[576,128]{1,0:T(8,128)}, f32[576,128]{1,0:T(8,128)S(1)}, u32[]{:S(2)}, u32[]{:S(2)}) collective-permute-start(f32[576,128]{1,0:T(8,128)} %get-tuple-element.56.refs_5_), channel_id=1, source_target_pairs={{0,4},{1,5},{2,6},{3,7},{4,8},{5,9},{6,10},{7,11},{8,12},{9,13},{1... | collective-permute-start | bytes 884744 | tf_op jit(solution)/shard_map/ppermute | solution.py:60
  109.0 28.1 %collective-permute-start.29 = (f32[576,128]{1,0:T(8,128)}, f32[576,128]{1,0:T(8,128)}, u32[]{:S(2)}, u32[]{:S(2)}) collective-permute-start(f32[576,128]{1,0:T(8,128)} %get-tuple-element.57.refs_6_), channel_id=1, source_target_pairs={{0,8},{1,9},{2,10},{3,11},{4,12},{5,13},{6,14},{7,15},{8,0},{9,1},... | collective-permute-start | bytes 884744 | tf_op jit(solution)/shard_map/ppermute | solution.py:60
  109.9 27.1 %collective-permute-start.28 = (f32[576,128]{1,0:T(8,128)}, f32[576,128]{1,0:T(8,128)}, u32[]{:S(2)}, u32[]{:S(2)}) collective-permute-start(f32[576,128]{1,0:T(8,128)} %get-tuple-element.58.refs_7_), channel_id=1, source_target_pairs={{0,12},{1,13},{2,14},{3,15},{4,0},{5,1},{6,2},{7,3},{8,4},{9,5},{1... | collective-permute-start | bytes 884744 | tf_op jit(solution)/shard_map/ppermute | solution.py:60
  119.8 17.2 %collective-permute-start.24 = (f32[576,128]{1,0:T(8,128)}, f32[576,128]{1,0:T(8,128)}, u32[]{:S(2)}, u32[]{:S(2)}) collective-permute-start(f32[576,128]{1,0:T(8,128)} %get-tuple-element.63.refs_17_), channel_id=1, source_target_pairs={{0,4},{1,5},{2,6},{3,7},{4,8},{5,9},{6,10},{7,11},{8,12},{9,13},{1... | collective-permute-start | bytes 884744 | tf_op jit(solution)/shard_map/ppermute | solution.py:60
  119.8 17.2 %collective-permute-start.25 = (f32[576,128]{1,0:T(8,128)}, f32[576,128]{1,0:T(8,128)}, u32[]{:S(2)}, u32[]{:S(2)}) collective-permute-start(f32[576,128]{1,0:T(8,128)} %get-tuple-element.64.refs_19_), channel_id=1, source_target_pairs={{0,12},{1,13},{2,14},{3,15},{4,0},{5,1},{6,2},{7,3},{8,4},{9,5},{1... | collective-permute-start | bytes 884744 | tf_op jit(solution)/shard_map/ppermute | solution.py:60
  122.6 16.3 %collective-permute-start.26 = (f32[576,128]{1,0:T(8,128)}, f32[576,128]{1,0:T(8,128)}, u32[]{:S(2)}, u32[]{:S(2)}) collective-permute-start(f32[576,128]{1,0:T(8,128)} %get-tuple-element.65.refs_18_), channel_id=1, source_target_pairs={{0,8},{1,9},{2,10},{3,11},{4,12},{5,13},{6,14},{7,15},{8,0},{9,1},... | collective-permute-start | bytes 884744 | tf_op jit(solution)/shard_map/ppermute | solution.py:60
  124.0 14.9 %copy-start.4 = (s32[29]{0:T(128)S(1)}, s32[29]{0:T(128)}, u32[]{:S(2)}) copy-start(s32[29]{0:T(128)} %stack.121.s_ref) | copy-start | bytes 352
  142.9 9.8 %collective-permute-start.30 = (f32[576,128]{1,0:T(8,128)S(1)}, f32[576,128]{1,0:T(8,128)S(1)}, u32[]{:S(2)}, u32[]{:S(2)}) collective-permute-start(f32[576,128]{1,0:T(8,128)S(1)} %get-tuple-element.68), channel_id=1, source_target_pairs={{0,2},{1,3},{2,0},{3,1},{4,6},{5,7},{6,4},{7,5},{8,10},{9,11},{10,... | collective-permute-start | bytes 884744 | tf_op jit(solution)/shard_map/ppermute | solution.py:64
  (9 other events, 25.2 us)

commit v7 on v6

v7 whole, which is shorter than its diff:
```python
import functools

import jax
import jax.numpy as jnp
from jax import lax
from jax.experimental import pallas as pl
from jax.experimental.pallas import tpu as pltpu
from jax.sharding import PartitionSpec as P

XL, Z = 2, 8
Y, XH, C = 4, 2, 2
VMEM_LIMIT = 127 << 19
NO_COST = pl.CostEstimate(flops=1, bytes_accessed=1, transcendentals=0)


def gx_pairs(dxl, dz):
    return [
        (xl * Z + z, (xl + dxl) % XL * Z + (z + dz) % Z)
        for xl in range(XL)
        for z in range(Z)
    ]


def gy_pairs(dy, dxh, dc):
    return [
        (
            (y * XH + xh) * C + c,
            ((y + dy) % Y * XH + (xh + dxh) % XH) * C + (c + dc) % C,
        )
        for y in range(Y)
        for xh in range(XH)
        for c in range(C)
    ]


def up(t):
    return lax.ppermute(t, "gx", gx_pairs(0, 1))


def down(t):
    return lax.ppermute(t, "gx", gx_pairs(0, -1))


def across(t):
    return lax.ppermute(t, "gx", gx_pairs(1, 0))


def in_y_pair(t):
    pairs = [
        ((y * XH + xh) * C + c, ((y ^ 1) * XH + xh) * C + c)
        for y in range(Y)
        for xh in range(XH)
        for c in range(C)
    ]
    return lax.ppermute(t, "gy", pairs)


def in_y(t, dy):
    return lax.ppermute(t, "gy", gy_pairs(dy, 0, 0))


def in_xh(t):
    return lax.ppermute(t, "gy", gy_pairs(0, 1, 0))


def in_core(t):
    return lax.ppermute(t, "gy", gy_pairs(0, 0, 1))


AT = {"g": (0, 0), "gx": (1, 0)}
for _k in range(1, 5):
    AT[f"u{_k}"], AT[f"ux{_k}"] = (0, -_k), (1, -_k)
    AT[f"d{_k}"], AT[f"dx{_k}"] = (0, _k), (1, _k)


def position():
    ix, iy = lax.axis_index("gx"), lax.axis_index("gy")
    return ix >> 3, ix & 7, iy >> 2, (iy >> 1) & 1, iy & 1


def where(here, name):
    side, dz = AT[name]
    at = (here[1] + dz + Z) & 7
    return (here[0] ^ side) * 2 + (at >> 2), (at >> 1) & 1, at & 1


def keeps_even(here):
    return (here[1] & 1) == here[4]


def way(here, name):
    return (where(here, name)[0] - here[2]) & 3


def of_inputs(here, name):
    y, xh, c = where(here, name)
    dy = y ^ here[2]
    return (c ^ here[4]) * 8 + (dy >> 1) * 4 + (dy & 1) * 2 + (xh ^ here[3])


def ends_late(here):
    _, z, _, xh, c = here
    return ((z + ((z & 1) ^ c)) >> 1) & 1 == xh


IN_HBM = pl.BlockSpec(memory_space=pltpu.HBM)
ANYWHERE = pl.BlockSpec(memory_space=pl.ANY)
VECTOR = pl.BlockSpec(memory_space=pltpu.VMEM)


def params():
    return pltpu.CompilerParams(vmem_limit_bytes=VMEM_LIMIT)


def tie_kernel(n, *refs):
    for token_ref in refs[n:]:
        token_ref[...] = jnp.zeros_like(token_ref)


def tie(values, after, tokens):
    n = len(values)
    return pl.pallas_call(
        functools.partial(tie_kernel, 2 * n + len(after)),
        out_shape=[jax.ShapeDtypeStruct(v.shape, v.dtype) for v in values]
        + [jax.ShapeDtypeStruct((8, 128), jnp.float32)] * tokens,
        in_specs=[IN_HBM] * n + [ANYWHERE] * len(after),
        out_specs=[IN_HBM] * n + [VECTOR] * tokens,
        input_output_aliases={k: k for k in range(n)},
        compiler_params=params(),
        cost_estimate=NO_COST,
        name="tie",
    )(*values, *after)


def touch_kernel(a_ref, out_ref):
    out_ref[...] = a_ref[...]


def touch(a):
    return pl.pallas_call(
        touch_kernel,
        out_shape=jax.ShapeDtypeStruct(a.shape, a.dtype),
        in_specs=[VECTOR],
        out_specs=VECTOR,
        compiler_params=params(),
        cost_estimate=NO_COST,
        name="touch",
    )(a)


def stack_kernel(a_ref, b_ref, *refs):
    n = a_ref.shape[0]
    refs[-1][:n] = a_ref[...]
    refs[-1][n:] = b_ref[...]


def stack(a, b, after):
    return pl.pallas_call(
        stack_kernel,
        out_shape=jax.ShapeDtypeStruct((2 * a.shape[0],) + a.shape[1:], a.dtype),
        in_specs=[VECTOR] * 2 + [ANYWHERE] * len(after),
        out_specs=VECTOR,
        compiler_params=params(),
        cost_estimate=NO_COST,
        name="stack",
    )(a, b, *after)


PARTS = 4


def load_weight(w_any, w_ref, sem, first):
    part = w_ref.shape[0] // PARTS
    copies = []
    for k in range(PARTS):
        rows = pl.ds(k * part, part)
        copy = pltpu.make_async_copy(
            w_any.at[rows, :], w_ref.at[rows, :], sem.at[first + k]
        )
        copy.start()
        copies.append(copy)
    return copies


def product(w_ref, g_ref):
    return lax.dot_general(
        w_ref[...],
        g_ref[...],
        (((1,), (1,)), ((), ())),
        preferred_element_type=jnp.float32,
    )


def partial_kernel(places, w_any, *refs):
    n = len(places)
    pieces = refs[:n]
    keep_ref, send_ref, w_ref, g_ref, sem = refs[-5:]
    rows = keep_ref.shape[2]
    copies = load_weight(w_any, w_ref, sem, n)
    for k in range(n):
        copy = pltpu.make_async_copy(
            pieces[k], g_ref.at[pl.ds(k * rows, rows), :], sem.at[k]
        )
        copy.start()
        copies.append(copy)
    even = keeps_even(position())
    for copy in copies:
        copy.wait()
    sums = product(w_ref, g_ref)
    for k in range(n):
        group, slot = places[k]
        value = sums[:, k * rows : (k + 1) * rows]

        @pl.when(even == (group == 0))
        def _(slot=slot, value=value):
            keep_ref[slot] = value

        @pl.when(even == (group == 1))
        def _(slot=slot, value=value):
            send_ref[slot] = value


def partial_sums(weight, groups, after):
    places = [(g, k) for g, shards in enumerate(groups) for k in range(len(shards))]
    shards = [s for group in groups for s in group]
    n, slots = len(shards), max(len(group) for group in groups)
    rows, cols = shards[0].shape
    width = weight.shape[0]
    out = jax.ShapeDtypeStruct((slots, width, rows), jnp.float32)
    return pl.pallas_call(
        functools.partial(partial_kernel, places),
        out_shape=(out, out),
        in_specs=[IN_HBM] * (1 + n) + [ANYWHERE] * len(after),
        out_specs=(VECTOR, VECTOR),
        scratch_shapes=[
            pltpu.VMEM((width, cols), jnp.bfloat16),
            pltpu.VMEM((n * rows, cols), jnp.bfloat16),
            pltpu.SemaphoreType.DMA((n + PARTS,)),
        ],
        compiler_params=params(),
        cost_estimate=NO_COST,
        name="partial_sums",
    )(weight, *shards, *after)


def place_kernel(groups, *refs):
    pairs, outs = refs[: 2 * len(groups)], refs[-Y:]
    here = position()
    even = keeps_even(here)
    for group, slots in enumerate(groups):
        keep_ref, got_ref = pairs[2 * group], pairs[2 * group + 1]
        for i, names in slots:
            to = [-1 if name is None else way(here, name) for name in names]
            to = jnp.where(even, to[0], to[1])
            for r, out_ref in enumerate(outs):

                @pl.when(to == r)
                def _(keep_ref=keep_ref, got_ref=got_ref, i=i, out_ref=out_ref):
                    out_ref[...] = keep_ref[i] + got_ref[i]


def place(groups):
    arrays = [a for kept, got, _ in groups for a in (kept, got)]
    out = jax.ShapeDtypeStruct(arrays[0].shape[1:], jnp.float32)
    return pl.pallas_call(
        functools.partial(place_kernel, [slots for _, _, slots in groups]),
        out_shape=[out] * Y,
        in_specs=[VECTOR] * len(arrays),
        out_specs=[VECTOR] * Y,
        compiler_params=params(),
        cost_estimate=NO_COST,
        name="place",
    )(*arrays)


def merge_kernel(*refs):
    late, early, (keep_ref, send_ref) = refs[:Y], refs[Y : 2 * Y], refs[-2:]

    def total(parts):
        return (parts[0][...] + parts[1][...]) + (parts[2][...] + parts[3][...])

    a, b = total(late), total(early)
    here = ends_late(position())
    keep_ref[...] = jnp.where(here, a, b)
    send_ref[...] = jnp.where(here, b, a)


def merge(late, early, after):
    out = jax.ShapeDtypeStruct(late[0].shape, jnp.float32)
    return pl.pallas_call(
        merge_kernel,
        out_shape=(out, out),
        in_specs=[VECTOR] * (2 * Y) + [ANYWHERE] * len(after),
        out_specs=(VECTOR, VECTOR),
        compiler_params=params(),
        cost_estimate=NO_COST,
        name="merge",
    )(*late, *early, *after)


def weight_kernel(names, tile, scale, mine_ref, other_ref, *refs):
    n = len(names)
    pieces, (out_ref, token_ref) = refs[:n], refs[-7:-5]
    x_ref, g_ref, o_ref, in_sem, out_sem = refs[-5:]
    count, _, rows = mine_ref.shape
    tiles = g_ref.shape[1] // tile
    copies = []
    for t in range(tiles):
        columns = pl.ds(t * tile, tile)
        for k in range(n):
            copy = pltpu.make_async_copy(
                pieces[k].at[:, columns],
                g_ref.at[pl.ds(k * rows, rows), columns],
                in_sem.at[t * n + k],
            )
            copy.start()
            copies.append(copy)
    token_ref[...] = jnp.zeros_like(token_ref)
    here = position()
    for k, name in enumerate(names):
        at = of_inputs(here, name)
        target = slice(k * rows, (k + 1) * rows)

        @pl.when(at < count)
        def _(at=at, target=target):
            x_ref[:, target] = mine_ref[jnp.minimum(at, count - 1)]

        @pl.when(at >= count)
        def _(at=at, target=target):
            x_ref[:, target] = other_ref[jnp.maximum(at - count, 0)]

    results = []
    for t in range(tiles):
        columns = slice(t * tile, (t + 1) * tile)
        for copy in copies[t * n : (t + 1) * n]:
            copy.wait()
        sums = jnp.dot(
            x_ref[...], g_ref[:, columns], preferred_element_type=jnp.float32
        )
        o_ref[:, columns] = sums * scale
        copy = pltpu.make_async_copy(
            o_ref.at[:, columns], out_ref.at[:, columns], out_sem.at[t]
        )
        copy.start()
        results.append(copy)
    for copy in results:
        copy.wait()


def weight_sums(names, mine, other, shards, scale, after):
    n = len(shards)
    rows, cols = shards[0].shape
    width = mine.shape[1]
    tile = 768
    return pl.pallas_call(
        functools.partial(weight_kernel, names, tile, scale),
        out_shape=(
            jax.ShapeDtypeStruct((width, cols), jnp.float32),
            jax.ShapeDtypeStruct((8, 128), jnp.float32),
        ),
        in_specs=[VECTOR, VECTOR] + [IN_HBM] * n + [ANYWHERE] * len(after),
        out_specs=(IN_HBM, VECTOR),
        scratch_shapes=[
            pltpu.VMEM((width, n * rows), jnp.bfloat16),
            pltpu.VMEM((n * rows, cols), jnp.bfloat16),
            pltpu.VMEM((width, cols), jnp.float32),
            pltpu.SemaphoreType.DMA((n * (cols // tile),)),
            pltpu.SemaphoreType.DMA((cols // tile,)),
        ],
        compiler_params=params(),
        cost_estimate=NO_COST,
        name="weight_sums",
    )(mine, other, *shards, *after)


def body(grad_out, inputs, weight):
    rows = grad_out.shape[0]
    h = {"g": grad_out}

    first_early = (("d2", "u2"), ("u1", "ux1"))
    mixed = (("dx2", "g", "gx"), ("d3", "d1", "u3"))
    last_early = (("ux2",), ("dx3",))
    last = (("u4", "dx4"), ("dx1", "ux3"))

    def partials(groups, *after):
        return partial_sums(weight, [[h[s] for s in group] for group in groups], after)

    def slots(groups, *chosen):
        return [(k, (groups[0][k], groups[1][k])) for k in chosen]

    def over_y(parts):
        return [parts[0], in_y(parts[1], 1), in_y(parts[3], -1), in_y(parts[2], 2)]

    def phase(names, sends, *after, tokens=0):
        s = [h[name] for name in sends]
        got = tie([up(s[0]), down(s[1]), across(s[2])], after, tokens)
        h.update(zip(names, got))
        return got[3:]

    mine = touch(inputs.T[None])
    pair = in_xh(mine)
    phase(("u1", "d1", "gx"), ("g", "g", "g"), pair)
    pair = stack(mine, pair, [h["u1"]])
    quad = in_y_pair(pair)
    phase(("u2", "d2", "ux1"), ("u1", "d1", "u1"), pair)
    quad = stack(pair, quad, [h["u2"]])
    column = in_y(quad, 2)
    keep_a, send_a = partials(first_early)
    got_a = in_core(send_a)
    phase(("u3", "d3", "dx2"), ("u2", "d2", "d2"), quad, keep_a)
    column = stack(quad, column, [h["u3"]])
    other = in_core(column)
    keep_b, send_b = partials(mixed)
    got_b = in_core(send_b)
    (token,) = phase(
        ("u4", "dx3", "ux2"), ("u3", "dx2", "u2"), column, got_a, keep_b, tokens=1
    )
    keep_c, send_c = partials(last_early, in_core(token))
    got_c = in_core(send_c)
    early = place(
        [
            (keep_a, got_a, slots(first_early, 0, 1)),
            (keep_b, got_b, slots(mixed, 0)),
            (keep_c, got_c, slots(last_early, 0)),
        ]
    )
    phase(("ux3", "dx4", "dx1"), ("ux2", "dx3", "d1"), other, *early)
    early = over_y(early)
    keep_d, send_d = partials(last)
    got_d = in_core(send_d)
    late = place(
        [(keep_b, got_b, slots(mixed, 1, 2)), (keep_d, got_d, slots(last, 0, 1))]
    )

    order = [s for groups in (first_early, mixed, last_early, last) for group in groups for s in group]
    grad_weight, token = weight_sums(
        order,
        column,
        other,
        [h[s] for s in order],
        1.0 / (Y * XH * C * rows),
        late,
    )

    keep, send = merge(over_y(late), early, [token])
    grad_in = (keep + in_xh(send)).astype(jnp.bfloat16)
    return grad_in.T, grad_weight


def solution(mesh):
    return jax.shard_map(
        body,
        mesh=mesh,
        in_specs=(P("gx", "gy"), P("gy", "gx"), P("gx", "gy")),
        out_specs=(P("gy", "gx"), P("gx", "gy")),
        check_vma=False,
    )
```

time: 154 us -> 148 us (0.961)
  Pallas kernels: 55.3 us -> 50.6 us
  local copies, waits for them, and re-layouts: 5.43 us -> 1.48 us
  waiting for transfers between devices: 54.2 us -> 56.5 us
    pallas_call x6 -> x4, Pallas kernels: 29.7 us -> 21.7 us  [the longest x1 13 us: weight_sums(): pl.pallas_call(functools.partial(weight_kernel, names, tile, scale), out_...]
    unnamed x20 -> x10, local copies, waits for them, and re-layouts: 4.78 us -> 1.48 us
    ppermute x7, waiting for transfers between devices: 5.31 us -> 8.46 us  [in_y(): return lax.ppermute(t, 'gy', gy_pairs(dy, 0, 0))]
    pallas_call x3 -> x4, Pallas kernels: 17.5 us -> 20.7 us  [partial_sums(): pl.pallas_call(functools.partial(partial_kernel, places), out_shape=(out,...]
    ppermute x5, waiting for transfers between devices: 15.9 us -> 14.1 us  [down(): return lax.ppermute(t, 'gx', gx_pairs(0, -1))]
  transfers between devices with their start and end apart: 31 -> 31, of which waited for: 15 -> 14; matrix products, arithmetic and copies ran while one was open for 0% -> 0% of each run, Pallas kernels for 32% -> 29%
where the time goes in v7:
time: 148 us
  waiting for transfers between devices  56.5 us (38%)
  Pallas kernels  50.6 us (34%)
  starting transfers between devices  36.8 us (25%)
  other arithmetic  1.67 us (1%)
  local copies, waits for them, and re-layouts  1.48 us (1%)
    pallas_call x4, Pallas kernels, partial_sums(): pl.pallas_call(functools.partial(partial_kernel, places), out_shape=(out,...  20.7 us
    ppermute x2, waiting for transfers between devices, in_xh(): return lax.ppermute(t, 'gy', gy_pairs(0, 1, 0))  18 us
    ppermute x5, waiting for transfers between devices, down(): return lax.ppermute(t, 'gx', gx_pairs(0, -1))  14.1 us
    pallas_call x1, Pallas kernels, weight_sums(): pl.pallas_call(functools.partial(weight_kernel, names, tile, scale), out_...  13 us
    ppermute x5, starting transfers between devices, down(): return lax.ppermute(t, 'gx', gx_pairs(0, -1))  13 us
    ppermute x7, starting transfers between devices, in_y(): return lax.ppermute(t, 'gy', gy_pairs(dy, 0, 0))  9.32 us
    ppermute x7, waiting for transfers between devices, in_y(): return lax.ppermute(t, 'gy', gy_pairs(dy, 0, 0))  8.46 us
    ppermute x5, waiting for transfers between devices, up(): return lax.ppermute(t, 'gx', gx_pairs(0, 1))  8.09 us
  transfers between devices with their start and end apart: 31, of which 14 were waited for; matrix products, arithmetic and copies ran while one was open for 0% of the time, Pallas kernels for 29%

profile of v7, /device:TPU:8, one launch (start us, length us, event | category | flops | bytes accessed | tf_op | source)
XLA Modules:
  0.0 147.8 jit_solution(967674554316525235)
XLA Ops:
  2.2 5.9 %collective-permute-start.1 = (bf16[128,2304]{1,0:T(8,128)(2,1)}, bf16[128,2304]{1,0:T(8,128)(2,1)}, u32[]{:S(2)}, u32[]{:S(2)}) collective-permute-start(bf16[128,2304]{1,0:T(8,128)(2,1)} %refs_5_.1), channel_id=1, source_target_pairs={{0,112},{16,0},{32,16},{48,32},{64,48},{80,64},{96,80},{112,96},{1... | collective-permute-start | bytes 1769480 | tf_op jit(solution)/shard_map/ppermute | solution.py:41
  9.6 2.7 %collective-permute-start.3 = (bf16[1,576,128]{2,1,0:T(8,128)(2,1)}, bf16[1,576,128]{2,1,0:T(8,128)(2,1)S(1)}, u32[]{:S(2)}, u32[]{:S(2)}) collective-permute-start(bf16[1,576,128]{2,1,0:T(8,128)(2,1)} %touch.1.a_ref), channel_id=1, source_target_pairs={{0,2},{1,3},{2,0},{3,1},{4,6},{5,7},{6,4},{7,5},{8,10},{9,11},{10,... | collective-permute-start | bytes 442376 | tf_op jit(solution)/shard_map/ppermute | solution.py:63
  12.4 9.0 %collective-permute-done.3.refs_3_.b_ref = bf16[1,576,128]{2,1,0:T(8,128)(2,1)S(1)} collective-permute-done((bf16[1,576,128]{2,1,0:T(8,128)(2,1)}, bf16[1,576,128]{2,1,0:T(8,128)(2,1)S(1)}, u32[]{:S(2)}, u32[]{:S(2)}) %collective-permute-start.3) | collective-permute-done | bytes 147488 | tf_op jit(solution)/shard_map/ppermute | solution.py:63
  21.4 2.7 %collective-permute-done.refs_0_ = bf16[128,2304]{1,0:T(8,128)(2,1)} collective-permute-done((bf16[128,2304]{1,0:T(8,128)(2,1)}, bf16[128,2304]{1,0:T(8,128)(2,1)}, u32[]{:S(2)}, u32[]{:S(2)}) %collective-permute-start) | collective-permute-done | bytes 589856 | tf_op jit(solution)/shard_map/ppermute | solution.py:37
  24.1 3.8 %collective-permute-start.5 = (bf16[128,2304]{1,0:T(8,128)(2,1)}, bf16[128,2304]{1,0:T(8,128)(2,1)}, u32[]{:S(2)}, u32[]{:S(2)}) collective-permute-start(bf16[128,2304]{1,0:T(8,128)(2,1)} %get-tuple-element.39.refs_4_.refs_8_), channel_id=1, source_target_pairs={{0,112},{16,0},{32,16},{48,32},{64,48},{80,64},{96,80},{112,96},{1... | collective-permute-start | bytes 1769480 | tf_op jit(solution)/shard_map/ppermute | solution.py:41
  28.1 1.7 %stack.3.refs_3_.a_ref = bf16[2,576,128]{2,1,0:T(8,128)(2,1)} custom-call(bf16[1,576,128]{2,1,0:T(8,128)(2,1)} %touch.1.a_ref, bf16[1,576,128]{2,1,0:T(8,128)(2,1)} %copy-done, bf16[128,2304]{1,0:T(8,128)(2,1)} %get-tuple-element.38.refs_0_.refs_2_), custom_call_target="tpu_custom_call" | custom-call | flops 1 | bytes 1 | tf_op jit(solution)/shard_map/stack/pallas_call | solution.py:158
  30.2 9.6 %collective-permute-done.5.refs_1_ = bf16[128,2304]{1,0:T(8,128)(2,1)} collective-permute-done((bf16[128,2304]{1,0:T(8,128)(2,1)}, bf16[128,2304]{1,0:T(8,128)(2,1)}, u32[]{:S(2)}, u32[]{:S(2)}) %collective-permute-start.5) | collective-permute-done | bytes 589856 | tf_op jit(solution)/shard_map/ppermute | solution.py:41
  39.9 2.2 %collective-permute-done.6.refs_2_ = bf16[128,2304]{1,0:T(8,128)(2,1)} collective-permute-done((bf16[128,2304]{1,0:T(8,128)(2,1)}, bf16[128,2304]{1,0:T(8,128)(2,1)}, u32[]{:S(2)}, u32[]{:S(2)}) %collective-permute-start.6) | collective-permute-done | bytes 589856 | tf_op jit(solution)/shard_map/ppermute | solution.py:45
  43.3 1.7 %collective-permute-start.9 = (bf16[128,2304]{1,0:T(8,128)(2,1)}, bf16[128,2304]{1,0:T(8,128)(2,1)}, u32[]{:S(2)}, u32[]{:S(2)}) collective-permute-start(bf16[128,2304]{1,0:T(8,128)(2,1)} %get-tuple-element.41.refs_0_), channel_id=1, source_target_pairs={{0,128},{16,144},{32,160},{48,176},{64,192},{80,208},{96,224},{112... | collective-permute-start | bytes 1769480 | tf_op jit(solution)/shard_map/ppermute | solution.py:45
  45.0 2.0 %collective-permute-start.7 = (bf16[128,2304]{1,0:T(8,128)(2,1)}, bf16[128,2304]{1,0:T(8,128)(2,1)}, u32[]{:S(2)}, u32[]{:S(2)}) collective-permute-start(bf16[128,2304]{1,0:T(8,128)(2,1)} %get-tuple-element.40.refs_0_.refs_1_), channel_id=1, source_target_pairs={{0,16},{16,32},{32,48},{48,64},{64,80},{80,96},{96,112},{112,0},{1... | collective-permute-start | bytes 1769480 | tf_op jit(solution)/shard_map/ppermute | solution.py:37
  47.8 2.0 %stack.4.refs_3_.a_ref = bf16[4,576,128]{2,1,0:T(8,128)(2,1)} custom-call(bf16[2,576,128]{2,1,0:T(8,128)(2,1)} %stack.3.refs_3_.a_ref, bf16[2,576,128]{2,1,0:T(8,128)(2,1)} %copy-done.3, bf16[128,2304]{1,0:T(8,128)(2,1)} %get-tuple-element.40.refs_0_.refs_1_), custom_call_target="tpu_custom_call" | custom-call | flops 1 | bytes 1 | tf_op jit(solution)/shard_map/stack/pallas_call | solution.py:158
  49.8 2.3 %collective-permute-start.15 = (bf16[4,576,128]{2,1,0:T(8,128)(2,1)}, bf16[4,576,128]{2,1,0:T(8,128)(2,1)}, u32[]{:S(2)}, u32[]{:S(2)}) collective-permute-start(bf16[4,576,128]{2,1,0:T(8,128)(2,1)} %stack.4.refs_3_.a_ref), channel_id=1, source_target_pairs={{0,8},{1,9},{2,10},{3,11},{4,12},{5,13},{6,14},{7,15},{8,0},{9,1},... | collective-permute-start | bytes 1769480 | tf_op jit(solution)/shard_map/ppermute | solution.py:59
  52.4 5.1 %partial_sums.4 = (f32[2,576,128]{2,1,0:T(8,128)}, f32[2,576,128]{2,1,0:T(8,128)}) custom-call(bf16[576,2304]{1,0:T(8,128)(2,1)} %w_any.7, bf16[128,2304]{1,0:T(8,128)(2,1)} %get-tuple-element.41.refs_0_, bf16[128,2304]{1,0:T(8,128)(2,1)} %get-tuple-element.40.refs_0_.refs_1_, bf16[128,2304]{1,0:T(8,128)(2,1)} %get-tuple-element.38.refs_0_.refs_2_, ...), custom_call_target="tpu_custom_call" | custom-call | flops 1 | bytes 1 | tf_op jit(solution)/shard_map/partial_sums/pallas_call | solution.py:230
  57.5 2.4 %collective-permute-done.9.refs_2_ = bf16[128,2304]{1,0:T(8,128)(2,1)} collective-permute-done((bf16[128,2304]{1,0:T(8,128)(2,1)}, bf16[128,2304]{1,0:T(8,128)(2,1)}, u32[]{:S(2)}, u32[]{:S(2)}) %collective-permute-start.9) | collective-permute-done | bytes 589856 | tf_op jit(solution)/shard_map/ppermute | solution.py:45
  62.0 6.5 %partial_sums.5 = (f32[3,576,128]{2,1,0:T(8,128)}, f32[3,576,128]{2,1,0:T(8,128)}) custom-call(bf16[576,2304]{1,0:T(8,128)(2,1)} %w_any.7, bf16[128,2304]{1,0:T(8,128)(2,1)} %get-tuple-element.44.refs_0_.refs_4_, bf16[128,2304]{1,0:T(8,128)(2,1)} %refs_5_.1, bf16[128,2304]{1,0:T(8,128)(2,1)} %get-tuple-element.45.refs_2_.refs_6_, ...), custom_call_target="tpu_custom_call" | custom-call | flops 1 | bytes 1 | tf_op jit(solution)/shard_map/partial_sums/pallas_call | solution.py:230
  68.6 2.4 %stack.5.refs_3_.mine_ref = bf16[8,576,128]{2,1,0:T(8,128)(2,1)} custom-call(bf16[4,576,128]{2,1,0:T(8,128)(2,1)} %stack.4.refs_3_.a_ref, bf16[4,576,128]{2,1,0:T(8,128)(2,1)} %collective-permute-done.15.b_ref, bf16[128,2304]{1,0:T(8,128)(2,1)} %get-tuple-element.47.refs_5_.refs_0_.refs_9_), custom_call_target="tpu_custom_call" | custom-call | flops 1 | bytes 1 | tf_op jit(solution)/shard_map/stack/pallas_call | solution.py:158
  71.6 4.4 %collective-permute-done.13.refs_1_ = bf16[128,2304]{1,0:T(8,128)(2,1)} collective-permute-done((bf16[128,2304]{1,0:T(8,128)(2,1)}, bf16[128,2304]{1,0:T(8,128)(2,1)}, u32[]{:S(2)}, u32[]{:S(2)}) %collective-permute-start.13) | collective-permute-done | bytes 589856 | tf_op jit(solution)/shard_map/ppermute | solution.py:41
  78.0 1.8 %collective-permute-start.19 = (bf16[128,2304]{1,0:T(8,128)(2,1)}, bf16[128,2304]{1,0:T(8,128)(2,1)}, u32[]{:S(2)}, u32[]{:S(2)}) collective-permute-start(bf16[128,2304]{1,0:T(8,128)(2,1)} %get-tuple-element.39.refs_4_.refs_8_), channel_id=1, source_target_pairs={{0,128},{16,144},{32,160},{48,176},{64,192},{80,208},{96,224},{112... | collective-permute-start | bytes 1769480 | tf_op jit(solution)/shard_map/ppermute | solution.py:45
  80.1 3.0 %collective-permute-start.18 = (bf16[128,2304]{1,0:T(8,128)(2,1)}, bf16[128,2304]{1,0:T(8,128)(2,1)}, u32[]{:S(2)}, u32[]{:S(2)}) collective-permute-start(bf16[128,2304]{1,0:T(8,128)(2,1)} %get-tuple-element.53.refs_1_.refs_11_), channel_id=1, source_target_pairs={{0,112},{16,0},{32,16},{48,32},{64,48},{80,64},{96,80},{112,96},{1... | collective-permute-start | bytes 1769480 | tf_op jit(solution)/shard_map/ppermute | solution.py:41
  83.0 3.8 %partial_sums.6 = (f32[1,576,128]{2,1,0:T(8,128)}, f32[1,576,128]{2,1,0:T(8,128)}) custom-call(bf16[576,2304]{1,0:T(8,128)(2,1)} %w_any.7, bf16[128,2304]{1,0:T(8,128)(2,1)} %get-tuple-element.52.refs_0_.refs_10_, bf16[128,2304]{1,0:T(8,128)(2,1)} %get-tuple-element.53.refs_1_.refs_11_, f32[8,128]{1,0:T(8,128)} %copy-done.4), custom_call_target="tpu_custom_call" | custom-call | flops 1 | bytes 1 | tf_op jit(solution)/shard_map/partial_sums/pallas_call | solution.py:230
  87.0 1.8 %collective-permute-done.22.refs_5_ = f32[1,576,128]{2,1,0:T(8,128)S(1)} collective-permute-done((f32[1,576,128]{2,1,0:T(8,128)}, f32[1,576,128]{2,1,0:T(8,128)S(1)}, u32[]{:S(2)}, u32[]{:S(2)}) %collective-permute-start.22) | collective-permute-done | bytes 294944 | tf_op jit(solution)/shard_map/ppermute | solution.py:67
  89.5 3.2 %place.2 = (f32[576,128]{1,0:T(8,128)}, f32[576,128]{1,0:T(8,128)}, f32[576,128]{1,0:T(8,128)}, f32[576,128]{1,0:T(8,128)}) custom-call(f32[2,576,128]{2,1,0:T(8,128)} %get-tuple-element.43.refs_4_.refs_0_, f32[2,576,128]{2,1,0:T(8,128)} %collective-permute-done.16.refs_4_.refs_1_, f32[3,576,128]{2,1,0:T(8,128)} %get-tuple-element.48.refs_5_.refs_2_.refs_0_, ...), custom_call_target="tpu_custom_call" | custom-call | flops 1 | bytes 1 | tf_op jit(solution)/shard_map/place/pallas_call | solution.py:265
  94.1 2.7 %collective-permute-done.17.refs_0_ = bf16[128,2304]{1,0:T(8,128)(2,1)} collective-permute-done((bf16[128,2304]{1,0:T(8,128)(2,1)}, bf16[128,2304]{1,0:T(8,128)(2,1)}, u32[]{:S(2)}, u32[]{:S(2)}) %collective-permute-start.17) | collective-permute-done | bytes 589856 | tf_op jit(solution)/shard_map/ppermute | solution.py:37
  96.8 5.2 %partial_sums.7 = (f32[2,576,128]{2,1,0:T(8,128)}, f32[2,576,128]{2,1,0:T(8,128)}) custom-call(bf16[576,2304]{1,0:T(8,128)(2,1)} %w_any.7, bf16[128,2304]{1,0:T(8,128)(2,1)} %get-tuple-element.51.refs_0_.refs_12_, bf16[128,2304]{1,0:T(8,128)(2,1)} %get-tuple-element.61.refs_1_.refs_13_, bf16[128,2304]{1,0:T(8,128)(2,1)} %get-tuple-element.62.refs_2_.refs_14_, ...), custom_call_target="tpu_custom_call" | custom-call | flops 1 | bytes 1 | tf_op jit(solution)/shard_map/partial_sums/pallas_call | solution.py:230
  104.7 2.4 %collective-permute-start.28 = (f32[576,128]{1,0:T(8,128)S(1)}, f32[576,128]{1,0:T(8,128)}, u32[]{:S(2)}, u32[]{:S(2)}) collective-permute-start(f32[576,128]{1,0:T(8,128)S(1)} %copy-done.1), channel_id=1, source_target_pairs={{0,12},{1,13},{2,14},{3,15},{4,0},{5,1},{6,2},{7,3},{8,4},{9,5},{1... | collective-permute-start | bytes 884744 | tf_op jit(solution)/shard_map/ppermute | solution.py:59
  107.1 3.0 %place.3 = (f32[576,128]{1,0:T(8,128)}, f32[576,128]{1,0:T(8,128)}, f32[576,128]{1,0:T(8,128)}, f32[576,128]{1,0:T(8,128)}) custom-call(f32[3,576,128]{2,1,0:T(8,128)} %get-tuple-element.48.refs_5_.refs_2_.refs_0_, f32[3,576,128]{2,1,0:T(8,128)} %collective-permute-done.11.refs_3_.refs_1_, f32[2,576,128]{2,1,0:T(8,128)} %get-tuple-element.64.refs_2_, ...), custom_call_target="tpu_custom_call" | custom-call | flops 1 | bytes 1 | tf_op jit(solution)/shard_map/place/pallas_call | solution.py:265
  110.1 2.0 %collective-permute-start.25 = (f32[576,128]{1,0:T(8,128)}, f32[576,128]{1,0:T(8,128)}, u32[]{:S(2)}, u32[]{:S(2)}) collective-permute-start(f32[576,128]{1,0:T(8,128)} %get-tuple-element.68.refs_19_), channel_id=1, source_target_pairs={{0,12},{1,13},{2,14},{3,15},{4,0},{5,1},{6,2},{7,3},{8,4},{9,5},{1... | collective-permute-start | bytes 884744 | tf_op jit(solution)/shard_map/ppermute | solution.py:59
  112.1 5.2 %collective-permute-done.27.refs_5_ = f32[576,128]{1,0:T(8,128)} collective-permute-done((f32[576,128]{1,0:T(8,128)}, f32[576,128]{1,0:T(8,128)}, u32[]{:S(2)}, u32[]{:S(2)}) %collective-permute-start.27) | collective-permute-done | bytes 294944 | tf_op jit(solution)/shard_map/ppermute | solution.py:59
  117.3 13.0 %weight_sums.1 = (f32[576,2304]{1,0:T(8,128)}, f32[8,128]{1,0:T(8,128)}) custom-call(bf16[8,576,128]{2,1,0:T(8,128)(2,1)} %stack.5.refs_3_.mine_ref, bf16[8,576,128]{2,1,0:T(8,128)(2,1)} %collective-permute-done.20.refs_3_.other_ref, bf16[128,2304]{1,0:T(8,128)(2,1)} %get-tuple-element.41.refs_0_, bf16[128,2304]{1,0:T(8,128)(2,1)} %get-tuple-element.40.refs_0_.refs_1_, ...), custom_call_target="tpu_custom_call" | custom-call | flops 1 | bytes 1 | tf_op jit(solution)/shard_map/weight_sums/pallas_call | solution.py:355
  130.4 3.3 %collective-permute-done.26.refs_3_ = f32[576,128]{1,0:T(8,128)} collective-permute-done((f32[576,128]{1,0:T(8,128)}, f32[576,128]{1,0:T(8,128)}, u32[]{:S(2)}, u32[]{:S(2)}) %collective-permute-start.26) | collective-permute-done | bytes 294944 | tf_op jit(solution)/shard_map/ppermute | solution.py:59
  133.6 2.5 %merge.1 = (f32[576,128]{1,0:T(8,128)}, f32[576,128]{1,0:T(8,128)}) custom-call(f32[576,128]{1,0:T(8,128)} %get-tuple-element.66.refs_16_.refs_0_, f32[576,128]{1,0:T(8,128)} %collective-permute-done.24.refs_1_, f32[576,128]{1,0:T(8,128)} %collective-permute-done.25.refs_2_, f32[576,128]{1,0:T(8,128)} %collective-permute-done.26.refs_3_, ...), custom_call_target="tpu_custom_call" | custom-call | flops 1 | bytes 1 | tf_op jit(solution)/shard_map/merge/pallas_call | solution.py:290
  137.1 9.0 %collective-permute-done.30 = f32[576,128]{1,0:T(8,128)S(1)} collective-permute-done((f32[576,128]{1,0:T(8,128)}, f32[576,128]{1,0:T(8,128)S(1)}, u32[]{:S(2)}, u32[]{:S(2)}) %collective-permute-start.30) | collective-permute-done | bytes 294944 | tf_op jit(solution)/shard_map/ppermute | solution.py:63
  (58 shorter events, 18.7 us)
Async XLA Ops:
  0.6 20.7 %collective-permute-start.2 = (bf16[128,2304]{1,0:T(8,128)(2,1)}, bf16[128,2304]{1,0:T(8,128)(2,1)}, u32[]{:S(2)}, u32[]{:S(2)}) collective-permute-start(bf16[128,2304]{1,0:T(8,128)(2,1)} %refs_5_.1), channel_id=1, source_target_pairs={{0,128},{16,144},{32,160},{48,176},{64,192},{80,208},{96,224},{112... | collective-permute-start | bytes 1769480 | tf_op jit(solution)/shard_map/ppermute | solution.py:45
  2.2 19.2 %collective-permute-start.1 = (bf16[128,2304]{1,0:T(8,128)(2,1)}, bf16[128,2304]{1,0:T(8,128)(2,1)}, u32[]{:S(2)}, u32[]{:S(2)}) collective-permute-start(bf16[128,2304]{1,0:T(8,128)(2,1)} %refs_5_.1), channel_id=1, source_target_pairs={{0,112},{16,0},{32,16},{48,32},{64,48},{80,64},{96,80},{112,96},{1... | collective-permute-start | bytes 1769480 | tf_op jit(solution)/shard_map/ppermute | solution.py:41
  8.1 16.0 %collective-permute-start = (bf16[128,2304]{1,0:T(8,128)(2,1)}, bf16[128,2304]{1,0:T(8,128)(2,1)}, u32[]{:S(2)}, u32[]{:S(2)}) collective-permute-start(bf16[128,2304]{1,0:T(8,128)(2,1)} %refs_5_.1), channel_id=1, source_target_pairs={{0,16},{16,32},{32,48},{48,64},{64,80},{80,96},{96,112},{112,0},{1... | collective-permute-start | bytes 1769480 | tf_op jit(solution)/shard_map/ppermute | solution.py:37
  9.6 11.7 %collective-permute-start.3 = (bf16[1,576,128]{2,1,0:T(8,128)(2,1)}, bf16[1,576,128]{2,1,0:T(8,128)(2,1)S(1)}, u32[]{:S(2)}, u32[]{:S(2)}) collective-permute-start(bf16[1,576,128]{2,1,0:T(8,128)(2,1)} %touch.1.a_ref), channel_id=1, source_target_pairs={{0,2},{1,3},{2,0},{3,1},{4,6},{5,7},{6,4},{7,5},{8,10},{9,11},{10,... | collective-permute-start | bytes 442376 | tf_op jit(solution)/shard_map/ppermute | solution.py:63
  24.1 15.8 %collective-permute-start.5 = (bf16[128,2304]{1,0:T(8,128)(2,1)}, bf16[128,2304]{1,0:T(8,128)(2,1)}, u32[]{:S(2)}, u32[]{:S(2)}) collective-permute-start(bf16[128,2304]{1,0:T(8,128)(2,1)} %get-tuple-element.39.refs_4_.refs_8_), channel_id=1, source_target_pairs={{0,112},{16,0},{32,16},{48,32},{64,48},{80,64},{96,80},{112,96},{1... | collective-permute-start | bytes 1769480 | tf_op jit(solution)/shard_map/ppermute | solution.py:41
  27.9 14.2 %collective-permute-start.6 = (bf16[128,2304]{1,0:T(8,128)(2,1)}, bf16[128,2304]{1,0:T(8,128)(2,1)}, u32[]{:S(2)}, u32[]{:S(2)}) collective-permute-start(bf16[128,2304]{1,0:T(8,128)(2,1)} %get-tuple-element.38.refs_0_.refs_2_), channel_id=1, source_target_pairs={{0,128},{16,144},{32,160},{48,176},{64,192},{80,208},{96,224},{112... | collective-permute-start | bytes 1769480 | tf_op jit(solution)/shard_map/ppermute | solution.py:45
  28.1 15.2 %collective-permute-start.4 = (bf16[128,2304]{1,0:T(8,128)(2,1)}, bf16[128,2304]{1,0:T(8,128)(2,1)}, u32[]{:S(2)}, u32[]{:S(2)}) collective-permute-start(bf16[128,2304]{1,0:T(8,128)(2,1)} %get-tuple-element.38.refs_0_.refs_2_), channel_id=1, source_target_pairs={{0,16},{16,32},{32,48},{48,64},{64,80},{80,96},{96,112},{112,0},{1... | collective-permute-start | bytes 1769480 | tf_op jit(solution)/shard_map/ppermute | solution.py:37
  29.8 17.3 %collective-permute-start.10 = (bf16[2,576,128]{2,1,0:T(8,128)(2,1)}, bf16[2,576,128]{2,1,0:T(8,128)(2,1)S(1)}, u32[]{:S(2)}, u32[]{:S(2)}) collective-permute-start(bf16[2,576,128]{2,1,0:T(8,128)(2,1)} %stack.3.refs_3_.a_ref), channel_id=1, source_target_pairs={{0,4},{1,5},{2,6},{3,7},{4,0},{5,1},{6,2},{7,3},{8,12},{9,13},{10,... | collective-permute-start | bytes 884744 | tf_op jit(solution)/shard_map/ppermute | solution.py:55
  43.3 16.6 %collective-permute-start.9 = (bf16[128,2304]{1,0:T(8,128)(2,1)}, bf16[128,2304]{1,0:T(8,128)(2,1)}, u32[]{:S(2)}, u32[]{:S(2)}) collective-permute-start(bf16[128,2304]{1,0:T(8,128)(2,1)} %get-tuple-element.41.refs_0_), channel_id=1, source_target_pairs={{0,128},{16,144},{32,160},{48,176},{64,192},{80,208},{96,224},{112... | collective-permute-start | bytes 1769480 | tf_op jit(solution)/shard_map/ppermute | solution.py:45
  45.0 14.8 %collective-permute-start.8 = (bf16[128,2304]{1,0:T(8,128)(2,1)}, bf16[128,2304]{1,0:T(8,128)(2,1)}, u32[]{:S(2)}, u32[]{:S(2)}) collective-permute-start(bf16[128,2304]{1,0:T(8,128)(2,1)} %get-tuple-element.41.refs_0_), channel_id=1, source_target_pairs={{0,112},{16,0},{32,16},{48,32},{64,48},{80,64},{96,80},{112,96},{1... | collective-permute-start | bytes 1769480 | tf_op jit(solution)/shard_map/ppermute | solution.py:41
  45.0 14.8 %collective-permute-start.7 = (bf16[128,2304]{1,0:T(8,128)(2,1)}, bf16[128,2304]{1,0:T(8,128)(2,1)}, u32[]{:S(2)}, u32[]{:S(2)}) collective-permute-start(bf16[128,2304]{1,0:T(8,128)(2,1)} %get-tuple-element.40.refs_0_.refs_1_), channel_id=1, source_target_pairs={{0,16},{16,32},{32,48},{48,64},{64,80},{80,96},{96,112},{112,0},{1... | collective-permute-start | bytes 1769480 | tf_op jit(solution)/shard_map/ppermute | solution.py:37
  49.8 18.7 %collective-permute-start.15 = (bf16[4,576,128]{2,1,0:T(8,128)(2,1)}, bf16[4,576,128]{2,1,0:T(8,128)(2,1)}, u32[]{:S(2)}, u32[]{:S(2)}) collective-permute-start(bf16[4,576,128]{2,1,0:T(8,128)(2,1)} %stack.4.refs_3_.a_ref), channel_id=1, source_target_pairs={{0,8},{1,9},{2,10},{3,11},{4,12},{5,13},{6,14},{7,15},{8,0},{9,1},... | collective-permute-start | bytes 1769480 | tf_op jit(solution)/shard_map/ppermute | solution.py:59
  52.1 19.0 %collective-permute-start.14 = (bf16[128,2304]{1,0:T(8,128)(2,1)}, bf16[128,2304]{1,0:T(8,128)(2,1)}, u32[]{:S(2)}, u32[]{:S(2)}) collective-permute-start(bf16[128,2304]{1,0:T(8,128)(2,1)} %get-tuple-element.40.refs_0_.refs_1_), channel_id=1, source_target_pairs={{0,128},{16,144},{32,160},{48,176},{64,192},{80,208},{96,224},{112... | collective-permute-start | bytes 1769480 | tf_op jit(solution)/shard_map/ppermute | solution.py:45
  59.9 11.7 %collective-permute-start.16 = (f32[2,576,128]{2,1,0:T(8,128)}, f32[2,576,128]{2,1,0:T(8,128)}, u32[]{:S(2)}, u32[]{:S(2)}) collective-permute-start(f32[2,576,128]{2,1,0:T(8,128)} %get-tuple-element.50), channel_id=1, source_target_pairs={{0,1},{1,0},{2,3},{3,2},{4,5},{5,4},{6,7},{7,6},{8,9},{9,8},{10,11... | collective-permute-start | bytes 1769480 | tf_op jit(solution)/shard_map/ppermute | solution.py:67
  59.9 16.1 %collective-permute-start.13 = (bf16[128,2304]{1,0:T(8,128)(2,1)}, bf16[128,2304]{1,0:T(8,128)(2,1)}, u32[]{:S(2)}, u32[]{:S(2)}) collective-permute-start(bf16[128,2304]{1,0:T(8,128)(2,1)} %get-tuple-element.44.refs_0_.refs_4_), channel_id=1, source_target_pairs={{0,112},{16,0},{32,16},{48,32},{64,48},{80,64},{96,80},{112,96},{1... | collective-permute-start | bytes 1769480 | tf_op jit(solution)/shard_map/ppermute | solution.py:41
  60.3 17.1 %collective-permute-start.12 = (bf16[128,2304]{1,0:T(8,128)(2,1)}, bf16[128,2304]{1,0:T(8,128)(2,1)}, u32[]{:S(2)}, u32[]{:S(2)}) collective-permute-start(bf16[128,2304]{1,0:T(8,128)(2,1)} %get-tuple-element.47.refs_5_.refs_0_.refs_9_), channel_id=1, source_target_pairs={{0,16},{16,32},{32,48},{48,64},{64,80},{80,96},{96,112},{112,0},{1... | collective-permute-start | bytes 1769480 | tf_op jit(solution)/shard_map/ppermute | solution.py:37
  68.5 18.3 %collective-permute-start.11 = (f32[3,576,128]{2,1,0:T(8,128)}, f32[3,576,128]{2,1,0:T(8,128)}, u32[]{:S(2)}, u32[]{:S(2)}) collective-permute-start(f32[3,576,128]{2,1,0:T(8,128)} %get-tuple-element.49), channel_id=1, source_target_pairs={{0,1},{1,0},{2,3},{3,2},{4,5},{5,4},{6,7},{7,6},{8,9},{9,8},{10,11... | collective-permute-start | bytes 2654216 | tf_op jit(solution)/shard_map/ppermute | solution.py:67
  71.1 23.0 %collective-permute-start.20 = (bf16[8,576,128]{2,1,0:T(8,128)(2,1)}, bf16[8,576,128]{2,1,0:T(8,128)(2,1)}, u32[]{:S(2)}, u32[]{:S(2)}) collective-permute-start(bf16[8,576,128]{2,1,0:T(8,128)(2,1)} %stack.5.refs_3_.mine_ref), channel_id=1, source_target_pairs={{0,1},{1,0},{2,3},{3,2},{4,5},{5,4},{6,7},{7,6},{8,9},{9,8},{10,11... | collective-permute-start | bytes 3538952 | tf_op jit(solution)/shard_map/ppermute | solution.py:67
  78.0 2.0 %collective-permute-start.21 = (f32[8,128]{1,0:T(8,128)}, f32[8,128]{1,0:T(8,128)S(1)}, u32[]{:S(2)}, u32[]{:S(2)}) collective-permute-start(f32[8,128]{1,0:T(8,128)} %get-tuple-element.54), channel_id=1, source_target_pairs={{0,1},{1,0},{2,3},{3,2},{4,5},{5,4},{6,7},{7,6},{8,9},{9,8},{10,11... | collective-permute-start | bytes 12296 | tf_op jit(solution)/shard_map/ppermute | solution.py:67
  78.0 16.1 %collective-permute-start.19 = (bf16[128,2304]{1,0:T(8,128)(2,1)}, bf16[128,2304]{1,0:T(8,128)(2,1)}, u32[]{:S(2)}, u32[]{:S(2)}) collective-permute-start(bf16[128,2304]{1,0:T(8,128)(2,1)} %get-tuple-element.39.refs_4_.refs_8_), channel_id=1, source_target_pairs={{0,128},{16,144},{32,160},{48,176},{64,192},{80,208},{96,224},{112... | collective-permute-start | bytes 1769480 | tf_op jit(solution)/shard_map/ppermute | solution.py:45
  79.8 17.0 %collective-permute-start.17 = (bf16[128,2304]{1,0:T(8,128)(2,1)}, bf16[128,2304]{1,0:T(8,128)(2,1)}, u32[]{:S(2)}, u32[]{:S(2)}) collective-permute-start(bf16[128,2304]{1,0:T(8,128)(2,1)} %get-tuple-element.52.refs_0_.refs_10_), channel_id=1, source_target_pairs={{0,16},{16,32},{32,48},{48,64},{64,80},{80,96},{96,112},{112,0},{1... | collective-permute-start | bytes 1769480 | tf_op jit(solution)/shard_map/ppermute | solution.py:37
  80.1 16.7 %collective-permute-start.18 = (bf16[128,2304]{1,0:T(8,128)(2,1)}, bf16[128,2304]{1,0:T(8,128)(2,1)}, u32[]{:S(2)}, u32[]{:S(2)}) collective-permute-start(bf16[128,2304]{1,0:T(8,128)(2,1)} %get-tuple-element.53.refs_1_.refs_11_), channel_id=1, source_target_pairs={{0,112},{16,0},{32,16},{48,32},{64,48},{80,64},{96,80},{112,96},{1... | collective-permute-start | bytes 1769480 | tf_op jit(solution)/shard_map/ppermute | solution.py:41
  86.9 1.9 %collective-permute-start.22 = (f32[1,576,128]{2,1,0:T(8,128)}, f32[1,576,128]{2,1,0:T(8,128)S(1)}, u32[]{:S(2)}, u32[]{:S(2)}) collective-permute-start(f32[1,576,128]{2,1,0:T(8,128)} %get-tuple-element.56), channel_id=1, source_target_pairs={{0,1},{1,0},{2,3},{3,2},{4,5},{5,4},{6,7},{7,6},{8,9},{9,8},{10,11... | collective-permute-start | bytes 884744 | tf_op jit(solution)/shard_map/ppermute | solution.py:67
  96.8 7.9 %copy-start.1 = (f32[576,128]{1,0:T(8,128)S(1)}, f32[576,128]{1,0:T(8,128)}, u32[]{:S(2)}) copy-start(f32[576,128]{1,0:T(8,128)} %get-tuple-element.60.refs_7_) | copy-start | bytes 884740
  102.0 5.1 %collective-permute-start.23 = (f32[2,576,128]{2,1,0:T(8,128)}, f32[2,576,128]{2,1,0:T(8,128)}, u32[]{:S(2)}, u32[]{:S(2)}) collective-permute-start(f32[2,576,128]{2,1,0:T(8,128)} %get-tuple-element.65), channel_id=1, source_target_pairs={{0,1},{1,0},{2,3},{3,2},{4,5},{5,4},{6,7},{7,6},{8,9},{9,8},{10,11... | collective-permute-start | bytes 1769480 | tf_op jit(solution)/shard_map/ppermute | solution.py:67
  102.1 15.2 %collective-permute-start.27 = (f32[576,128]{1,0:T(8,128)}, f32[576,128]{1,0:T(8,128)}, u32[]{:S(2)}, u32[]{:S(2)}) collective-permute-start(f32[576,128]{1,0:T(8,128)} %get-tuple-element.58.refs_5_), channel_id=1, source_target_pairs={{0,4},{1,5},{2,6},{3,7},{4,8},{5,9},{6,10},{7,11},{8,12},{9,13},{1... | collective-permute-start | bytes 884744 | tf_op jit(solution)/shard_map/ppermute | solution.py:59
  103.7 26.6 %collective-permute-start.29 = (f32[576,128]{1,0:T(8,128)}, f32[576,128]{1,0:T(8,128)}, u32[]{:S(2)}, u32[]{:S(2)}) collective-permute-start(f32[576,128]{1,0:T(8,128)} %get-tuple-element.59.refs_6_), channel_id=1, source_target_pairs={{0,8},{1,9},{2,10},{3,11},{4,12},{5,13},{6,14},{7,15},{8,0},{9,1},... | collective-permute-start | bytes 884744 | tf_op jit(solution)/shard_map/ppermute | solution.py:59
  104.7 25.6 %collective-permute-start.28 = (f32[576,128]{1,0:T(8,128)S(1)}, f32[576,128]{1,0:T(8,128)}, u32[]{:S(2)}, u32[]{:S(2)}) collective-permute-start(f32[576,128]{1,0:T(8,128)S(1)} %copy-done.1), channel_id=1, source_target_pairs={{0,12},{1,13},{2,14},{3,15},{4,0},{5,1},{6,2},{7,3},{8,4},{9,5},{1... | collective-permute-start | bytes 884744 | tf_op jit(solution)/shard_map/ppermute | solution.py:59
  110.1 20.3 %collective-permute-start.24 = (f32[576,128]{1,0:T(8,128)}, f32[576,128]{1,0:T(8,128)}, u32[]{:S(2)}, u32[]{:S(2)}) collective-permute-start(f32[576,128]{1,0:T(8,128)} %get-tuple-element.67.refs_17_), channel_id=1, source_target_pairs={{0,4},{1,5},{2,6},{3,7},{4,8},{5,9},{6,10},{7,11},{8,12},{9,13},{1... | collective-permute-start | bytes 884744 | tf_op jit(solution)/shard_map/ppermute | solution.py:59
  110.1 20.3 %collective-permute-start.25 = (f32[576,128]{1,0:T(8,128)}, f32[576,128]{1,0:T(8,128)}, u32[]{:S(2)}, u32[]{:S(2)}) collective-permute-start(f32[576,128]{1,0:T(8,128)} %get-tuple-element.68.refs_19_), channel_id=1, source_target_pairs={{0,12},{1,13},{2,14},{3,15},{4,0},{5,1},{6,2},{7,3},{8,4},{9,5},{1... | collective-permute-start | bytes 884744 | tf_op jit(solution)/shard_map/ppermute | solution.py:59
  117.3 16.4 %collective-permute-start.26 = (f32[576,128]{1,0:T(8,128)}, f32[576,128]{1,0:T(8,128)}, u32[]{:S(2)}, u32[]{:S(2)}) collective-permute-start(f32[576,128]{1,0:T(8,128)} %get-tuple-element.69.refs_18_), channel_id=1, source_target_pairs={{0,8},{1,9},{2,10},{3,11},{4,12},{5,13},{6,14},{7,15},{8,0},{9,1},... | collective-permute-start | bytes 884744 | tf_op jit(solution)/shard_map/ppermute | solution.py:59
  136.2 10.0 %collective-permute-start.30 = (f32[576,128]{1,0:T(8,128)}, f32[576,128]{1,0:T(8,128)S(1)}, u32[]{:S(2)}, u32[]{:S(2)}) collective-permute-start(f32[576,128]{1,0:T(8,128)} %get-tuple-element.72), channel_id=1, source_target_pairs={{0,2},{1,3},{2,0},{3,1},{4,6},{5,7},{6,4},{7,5},{8,10},{9,11},{10,... | collective-permute-start | bytes 884744 | tf_op jit(solution)/shard_map/ppermute | solution.py:63
  (4 other events, 7.2 us)

commit v8 on v7

--- a/solution.py
+++ b/solution.py
@@ -244,7 +244,11 @@
 
 
 def place_kernel(groups, *refs):
-    pairs, outs = refs[: 2 * len(groups)], refs[-Y:]
+    n = 2 * len(groups)
+    pairs, outs = refs[:n], refs[-Y:]
+    extra = refs[n : n + (len(refs) - n - Y) // 2]
+    for k, extra_ref in enumerate(extra):
+        refs[-Y - 1 - k][...] = extra_ref[...]
     here = position()
     even = keeps_even(here)
     for group, slots in enumerate(groups):
@@ -259,18 +263,18 @@
                     out_ref[...] = keep_ref[i] + got_ref[i]
 
 
-def place(groups):
+def place(groups, extra):
     arrays = [a for kept, got, _ in groups for a in (kept, got)]
     out = jax.ShapeDtypeStruct(arrays[0].shape[1:], jnp.float32)
     return pl.pallas_call(
         functools.partial(place_kernel, [slots for _, _, slots in groups]),
-        out_shape=[out] * Y,
-        in_specs=[VECTOR] * len(arrays),
-        out_specs=[VECTOR] * Y,
+        out_shape=[out] * (len(extra) + Y),
+        in_specs=[VECTOR] * (len(arrays) + len(extra)),
+        out_specs=[VECTOR] * (len(extra) + Y),
         compiler_params=params(),
         cost_estimate=NO_COST,
         name="place",
-    )(*arrays)
+    )(*arrays, *extra)
 
 
 def merge_kernel(*refs):
@@ -389,13 +393,14 @@
         return [(k, (groups[0][k], groups[1][k])) for k in chosen]
 
     def over_y(parts):
-        return [parts[0], in_y(parts[1], 1), in_y(parts[3], -1), in_y(parts[2], 2)]
+        return [parts[0], in_y(parts[1], 1), in_y(parts[3], -1)]
 
     def phase(names, sends, *after, tokens=0):
         s = [h[name] for name in sends]
-        got = tie([up(s[0]), down(s[1]), across(s[2])], after, tokens)
+        moved = [up(s[0]), down(s[1])] + [across(v) for v in s[2:]]
+        got = tie(moved + [h[n] for n in names[len(s) :]], after, tokens)
         h.update(zip(names, got))
-        return got[3:]
+        return got[len(names) :]
 
     mine = touch(inputs.T[None])
     pair = in_xh(mine)
@@ -407,7 +412,7 @@
     column = in_y(quad, 2)
     keep_a, send_a = partials(first_early)
     got_a = in_core(send_a)
-    phase(("u3", "d3", "dx2"), ("u2", "d2", "d2"), quad, keep_a)
+    phase(("u3", "d3", "dx2", "u2"), ("u2", "d2", "d2"), quad, keep_a)
     column = stack(quad, column, [h["u3"]])
     other = in_core(column)
     keep_b, send_b = partials(mixed)
@@ -422,14 +427,17 @@
             (keep_a, got_a, slots(first_early, 0, 1)),
             (keep_b, got_b, slots(mixed, 0)),
             (keep_c, got_c, slots(last_early, 0)),
-        ]
+        ],
+        [],
     )
     phase(("ux3", "dx4", "dx1"), ("ux2", "dx3", "d1"), other, *early)
+    two_on = early[2]
     early = over_y(early)
     keep_d, send_d = partials(last)
     got_d = in_core(send_d)
-    late = place(
-        [(keep_b, got_b, slots(mixed, 1, 2)), (keep_d, got_d, slots(last, 0, 1))]
+    two_on, *late = place(
+        [(keep_b, got_b, slots(mixed, 1, 2)), (keep_d, got_d, slots(last, 0, 1))],
+        [two_on],
     )
 
     order = [s for groups in (first_early, mixed, last_early, last) for group in groups for s in group]
@@ -442,7 +450,9 @@
         late,
     )
 
-    keep, send = merge(over_y(late), early, [token])
+    early.append(in_y(two_on, 2))
+    late = over_y(late) + [in_y(late[2], 2)]
+    keep, send = merge(late, early, [token])
     grad_in = (keep + in_xh(send)).astype(jnp.bfloat16)
     return grad_in.T, grad_weight
 

time: 148 us -> 146 us (0.986)
  waiting for transfers between devices: 56.5 us -> 51.4 us
  starting transfers between devices: 36.8 us -> 38.8 us
    ppermute x5, starting transfers between devices: 13 us -> 18.5 us  [down(): return lax.ppermute(t, 'gx', gx_pairs(0, -1))]
    ppermute x5, waiting for transfers between devices: 14.1 us -> 9.74 us  [down(): return lax.ppermute(t, 'gx', gx_pairs(0, -1))]
    ppermute x5, starting transfers between devices: 3.96 us -> 0.54 us  [up(): return lax.ppermute(t, 'gx', gx_pairs(0, 1))]
    ppermute x7, waiting for transfers between devices: 8.46 us -> 6.69 us  [in_y(): return lax.ppermute(t, 'gy', gy_pairs(dy, 0, 0))]
  transfers between devices with their start and end apart: 31 -> 31, of which waited for: 14 -> 15; matrix products, arithmetic and copies ran while one was open for 0% -> 0% of each run, Pallas kernels for 29% -> 30%
where the time goes in v8:
time: 146 us; the launch traced here: 145 us
  waiting for transfers between devices  51.4 us (35%)
  Pallas kernels  50.8 us (35%)
  starting transfers between devices  38.8 us (27%)
  other arithmetic  1.67 us (1%)
    pallas_call x4, Pallas kernels, partial_sums(): pl.pallas_call(functools.partial(partial_kernel, places), out_shape=(out,...  20.7 us
    ppermute x5, starting transfers between devices, down(): return lax.ppermute(t, 'gx', gx_pairs(0, -1))  18.5 us
    ppermute x2, waiting for transfers between devices, in_xh(): return lax.ppermute(t, 'gy', gy_pairs(0, 1, 0))  18.3 us
    pallas_call x1, Pallas kernels, weight_sums(): pl.pallas_call(functools.partial(weight_kernel, names, tile, scale), out_...  13 us
    ppermute x5, waiting for transfers between devices, down(): return lax.ppermute(t, 'gx', gx_pairs(0, -1))  9.74 us
    ppermute x7, starting transfers between devices, in_y(): return lax.ppermute(t, 'gy', gy_pairs(dy, 0, 0))  9.06 us
    ppermute x5, waiting for transfers between devices, up(): return lax.ppermute(t, 'gx', gx_pairs(0, 1))  7.75 us
    ppermute x5, waiting for transfers between devices, across(): return lax.ppermute(t, 'gx', gx_pairs(1, 0))  6.87 us
  transfers between devices with their start and end apart: 31, of which 15 were waited for; matrix products, arithmetic and copies ran while one was open for 0% of the time, Pallas kernels for 30%

profile of v8, /device:TPU:8, one launch (start us, length us, event | category | flops | bytes accessed | tf_op | source)
XLA Modules:
  0.0 144.9 jit_solution(11916985464306445613)
XLA Ops:
  2.2 5.9 %collective-permute-start.1 = (bf16[128,2304]{1,0:T(8,128)(2,1)}, bf16[128,2304]{1,0:T(8,128)(2,1)}, u32[]{:S(2)}, u32[]{:S(2)}) collective-permute-start(bf16[128,2304]{1,0:T(8,128)(2,1)} %refs_5_.1), channel_id=1, source_target_pairs={{0,112},{16,0},{32,16},{48,32},{64,48},{80,64},{96,80},{112,96},{1... | collective-permute-start | bytes 1769480 | tf_op jit(solution)/shard_map/ppermute | solution.py:41
  9.6 2.7 %collective-permute-start.3 = (bf16[1,576,128]{2,1,0:T(8,128)(2,1)}, bf16[1,576,128]{2,1,0:T(8,128)(2,1)S(1)}, u32[]{:S(2)}, u32[]{:S(2)}) collective-permute-start(bf16[1,576,128]{2,1,0:T(8,128)(2,1)} %touch.1.a_ref), channel_id=1, source_target_pairs={{0,2},{1,3},{2,0},{3,1},{4,6},{5,7},{6,4},{7,5},{8,10},{9,11},{10,... | collective-permute-start | bytes 442376 | tf_op jit(solution)/shard_map/ppermute | solution.py:63
  12.4 9.0 %collective-permute-done.3.refs_3_.b_ref = bf16[1,576,128]{2,1,0:T(8,128)(2,1)S(1)} collective-permute-done((bf16[1,576,128]{2,1,0:T(8,128)(2,1)}, bf16[1,576,128]{2,1,0:T(8,128)(2,1)S(1)}, u32[]{:S(2)}, u32[]{:S(2)}) %collective-permute-start.3) | collective-permute-done | bytes 147488 | tf_op jit(solution)/shard_map/ppermute | solution.py:63
  21.4 2.7 %collective-permute-done.refs_0_ = bf16[128,2304]{1,0:T(8,128)(2,1)} collective-permute-done((bf16[128,2304]{1,0:T(8,128)(2,1)}, bf16[128,2304]{1,0:T(8,128)(2,1)}, u32[]{:S(2)}, u32[]{:S(2)}) %collective-permute-start) | collective-permute-done | bytes 589856 | tf_op jit(solution)/shard_map/ppermute | solution.py:37
  24.1 3.8 %collective-permute-start.5 = (bf16[128,2304]{1,0:T(8,128)(2,1)}, bf16[128,2304]{1,0:T(8,128)(2,1)}, u32[]{:S(2)}, u32[]{:S(2)}) collective-permute-start(bf16[128,2304]{1,0:T(8,128)(2,1)} %get-tuple-element.41.refs_4_.refs_8_), channel_id=1, source_target_pairs={{0,112},{16,0},{32,16},{48,32},{64,48},{80,64},{96,80},{112,96},{1... | collective-permute-start | bytes 1769480 | tf_op jit(solution)/shard_map/ppermute | solution.py:41
  28.1 1.7 %stack.3.refs_3_.a_ref = bf16[2,576,128]{2,1,0:T(8,128)(2,1)} custom-call(bf16[1,576,128]{2,1,0:T(8,128)(2,1)} %touch.1.a_ref, bf16[1,576,128]{2,1,0:T(8,128)(2,1)} %copy-done, bf16[128,2304]{1,0:T(8,128)(2,1)} %get-tuple-element.40.refs_0_.refs_2_), custom_call_target="tpu_custom_call" | custom-call | flops 1 | bytes 1 | tf_op jit(solution)/shard_map/stack/pallas_call | solution.py:158
  30.2 9.6 %collective-permute-done.5.refs_1_ = bf16[128,2304]{1,0:T(8,128)(2,1)} collective-permute-done((bf16[128,2304]{1,0:T(8,128)(2,1)}, bf16[128,2304]{1,0:T(8,128)(2,1)}, u32[]{:S(2)}, u32[]{:S(2)}) %collective-permute-start.5) | collective-permute-done | bytes 589856 | tf_op jit(solution)/shard_map/ppermute | solution.py:41
  39.9 2.2 %collective-permute-done.6.refs_2_ = bf16[128,2304]{1,0:T(8,128)(2,1)} collective-permute-done((bf16[128,2304]{1,0:T(8,128)(2,1)}, bf16[128,2304]{1,0:T(8,128)(2,1)}, u32[]{:S(2)}, u32[]{:S(2)}) %collective-permute-start.6) | collective-permute-done | bytes 589856 | tf_op jit(solution)/shard_map/ppermute | solution.py:45
  43.3 1.7 %collective-permute-start.9 = (bf16[128,2304]{1,0:T(8,128)(2,1)}, bf16[128,2304]{1,0:T(8,128)(2,1)}, u32[]{:S(2)}, u32[]{:S(2)}) collective-permute-start(bf16[128,2304]{1,0:T(8,128)(2,1)} %get-tuple-element.43.refs_0_), channel_id=1, source_target_pairs={{0,128},{16,144},{32,160},{48,176},{64,192},{80,208},{96,224},{112... | collective-permute-start | bytes 1769480 | tf_op jit(solution)/shard_map/ppermute | solution.py:45
  45.1 3.2 %collective-permute-start.8 = (bf16[128,2304]{1,0:T(8,128)(2,1)}, bf16[128,2304]{1,0:T(8,128)(2,1)}, u32[]{:S(2)}, u32[]{:S(2)}) collective-permute-start(bf16[128,2304]{1,0:T(8,128)(2,1)} %get-tuple-element.43.refs_0_), channel_id=1, source_target_pairs={{0,112},{16,0},{32,16},{48,32},{64,48},{80,64},{96,80},{112,96},{1... | collective-permute-start | bytes 1769480 | tf_op jit(solution)/shard_map/ppermute | solution.py:41
  49.0 2.0 %stack.4.refs_4_.a_ref = bf16[4,576,128]{2,1,0:T(8,128)(2,1)} custom-call(bf16[2,576,128]{2,1,0:T(8,128)(2,1)} %stack.3.refs_3_.a_ref, bf16[2,576,128]{2,1,0:T(8,128)(2,1)} %copy-done.3, bf16[128,2304]{1,0:T(8,128)(2,1)} %get-tuple-element.42.refs_0_.refs_1_.refs_3_), custom_call_target="tpu_custom_call" | custom-call | flops 1 | bytes 1 | tf_op jit(solution)/shard_map/stack/pallas_call | solution.py:158
  51.0 2.3 %collective-permute-start.15 = (bf16[4,576,128]{2,1,0:T(8,128)(2,1)}, bf16[4,576,128]{2,1,0:T(8,128)(2,1)}, u32[]{:S(2)}, u32[]{:S(2)}) collective-permute-start(bf16[4,576,128]{2,1,0:T(8,128)(2,1)} %stack.4.refs_4_.a_ref), channel_id=1, source_target_pairs={{0,8},{1,9},{2,10},{3,11},{4,12},{5,13},{6,14},{7,15},{8,0},{9,1},... | collective-permute-start | bytes 1769480 | tf_op jit(solution)/shard_map/ppermute | solution.py:59
  53.2 5.2 %partial_sums.4 = (f32[2,576,128]{2,1,0:T(8,128)}, f32[2,576,128]{2,1,0:T(8,128)}) custom-call(bf16[576,2304]{1,0:T(8,128)(2,1)} %w_any.7, bf16[128,2304]{1,0:T(8,128)(2,1)} %get-tuple-element.43.refs_0_, bf16[128,2304]{1,0:T(8,128)(2,1)} %get-tuple-element.42.refs_0_.refs_1_.refs_3_, bf16[128,2304]{1,0:T(8,128)(2,1)} %get-tuple-element.40.refs_0_.refs_2_, ...), custom_call_target="tpu_custom_call" | custom-call | flops 1 | bytes 1 | tf_op jit(solution)/shard_map/partial_sums/pallas_call | solution.py:230
  59.4 2.9 %collective-permute-start.13 = (bf16[128,2304]{1,0:T(8,128)(2,1)}, bf16[128,2304]{1,0:T(8,128)(2,1)}, u32[]{:S(2)}, u32[]{:S(2)}) collective-permute-start(bf16[128,2304]{1,0:T(8,128)(2,1)} %get-tuple-element.46.refs_0_.refs_4_), channel_id=1, source_target_pairs={{0,112},{16,0},{32,16},{48,32},{64,48},{80,64},{96,80},{112,96},{1... | collective-permute-start | bytes 1769480 | tf_op jit(solution)/shard_map/ppermute | solution.py:41
  62.3 6.5 %partial_sums.5 = (f32[3,576,128]{2,1,0:T(8,128)}, f32[3,576,128]{2,1,0:T(8,128)}) custom-call(bf16[576,2304]{1,0:T(8,128)(2,1)} %w_any.7, bf16[128,2304]{1,0:T(8,128)(2,1)} %get-tuple-element.46.refs_0_.refs_4_, bf16[128,2304]{1,0:T(8,128)(2,1)} %refs_5_.1, bf16[128,2304]{1,0:T(8,128)(2,1)} %get-tuple-element.47.refs_2_.refs_6_, ...), custom_call_target="tpu_custom_call" | custom-call | flops 1 | bytes 1 | tf_op jit(solution)/shard_map/partial_sums/pallas_call | solution.py:230
  68.9 2.4 %stack.5.refs_3_.mine_ref = bf16[8,576,128]{2,1,0:T(8,128)(2,1)} custom-call(bf16[4,576,128]{2,1,0:T(8,128)(2,1)} %stack.4.refs_4_.a_ref, bf16[4,576,128]{2,1,0:T(8,128)(2,1)} %collective-permute-done.15.b_ref, bf16[128,2304]{1,0:T(8,128)(2,1)} %get-tuple-element.49.refs_5_.refs_0_.refs_9_), custom_call_target="tpu_custom_call" | custom-call | flops 1 | bytes 1 | tf_op jit(solution)/shard_map/stack/pallas_call | solution.py:158
  71.9 2.8 %collective-permute-done.14.refs_2_ = bf16[128,2304]{1,0:T(8,128)(2,1)} collective-permute-done((bf16[128,2304]{1,0:T(8,128)(2,1)}, bf16[128,2304]{1,0:T(8,128)(2,1)}, u32[]{:S(2)}, u32[]{:S(2)}) %collective-permute-start.14) | collective-permute-done | bytes 589856 | tf_op jit(solution)/shard_map/ppermute | solution.py:45
  78.8 2.7 %collective-permute-start.18 = (bf16[128,2304]{1,0:T(8,128)(2,1)}, bf16[128,2304]{1,0:T(8,128)(2,1)}, u32[]{:S(2)}, u32[]{:S(2)}) collective-permute-start(bf16[128,2304]{1,0:T(8,128)(2,1)} %get-tuple-element.56.refs_1_.refs_11_), channel_id=1, source_target_pairs={{0,112},{16,0},{32,16},{48,32},{64,48},{80,64},{96,80},{112,96},{1... | collective-permute-start | bytes 1769480 | tf_op jit(solution)/shard_map/ppermute | solution.py:41
  81.5 3.8 %partial_sums.6 = (f32[1,576,128]{2,1,0:T(8,128)}, f32[1,576,128]{2,1,0:T(8,128)}) custom-call(bf16[576,2304]{1,0:T(8,128)(2,1)} %w_any.7, bf16[128,2304]{1,0:T(8,128)(2,1)} %get-tuple-element.55.refs_0_.refs_10_, bf16[128,2304]{1,0:T(8,128)(2,1)} %get-tuple-element.56.refs_1_.refs_11_, f32[8,128]{1,0:T(8,128)} %copy-done.4), custom_call_target="tpu_custom_call" | custom-call | flops 1 | bytes 1 | tf_op jit(solution)/shard_map/partial_sums/pallas_call | solution.py:230
  85.4 1.8 %collective-permute-done.22.refs_5_ = f32[1,576,128]{2,1,0:T(8,128)S(1)} collective-permute-done((f32[1,576,128]{2,1,0:T(8,128)}, f32[1,576,128]{2,1,0:T(8,128)S(1)}, u32[]{:S(2)}, u32[]{:S(2)}) %collective-permute-start.22) | collective-permute-done | bytes 294944 | tf_op jit(solution)/shard_map/ppermute | solution.py:67
  87.9 3.2 %place.2 = (f32[576,128]{1,0:T(8,128)}, f32[576,128]{1,0:T(8,128)}, f32[576,128]{1,0:T(8,128)}, f32[576,128]{1,0:T(8,128)}) custom-call(f32[2,576,128]{2,1,0:T(8,128)} %get-tuple-element.45.refs_5_.refs_0_, f32[2,576,128]{2,1,0:T(8,128)} %collective-permute-done.16.refs_4_.refs_1_, f32[3,576,128]{2,1,0:T(8,128)} %get-tuple-element.50.refs_5_.refs_2_.refs_0_, ...), custom_call_target="tpu_custom_call" | custom-call | flops 1 | bytes 1 | tf_op jit(solution)/shard_map/place/pallas_call | solution.py:269
  91.1 1.8 %collective-permute-done.19.refs_2_ = bf16[128,2304]{1,0:T(8,128)(2,1)} collective-permute-done((bf16[128,2304]{1,0:T(8,128)(2,1)}, bf16[128,2304]{1,0:T(8,128)(2,1)}, u32[]{:S(2)}, u32[]{:S(2)}) %collective-permute-start.19) | collective-permute-done | bytes 589856 | tf_op jit(solution)/shard_map/ppermute | solution.py:45
  92.9 2.3 %collective-permute-done.17.refs_0_ = bf16[128,2304]{1,0:T(8,128)(2,1)} collective-permute-done((bf16[128,2304]{1,0:T(8,128)(2,1)}, bf16[128,2304]{1,0:T(8,128)(2,1)}, u32[]{:S(2)}, u32[]{:S(2)}) %collective-permute-start.17) | collective-permute-done | bytes 589856 | tf_op jit(solution)/shard_map/ppermute | solution.py:37
  95.2 5.2 %partial_sums.7 = (f32[2,576,128]{2,1,0:T(8,128)}, f32[2,576,128]{2,1,0:T(8,128)}) custom-call(bf16[576,2304]{1,0:T(8,128)(2,1)} %w_any.7, bf16[128,2304]{1,0:T(8,128)(2,1)} %get-tuple-element.54.refs_0_.refs_12_, bf16[128,2304]{1,0:T(8,128)(2,1)} %get-tuple-element.64.refs_1_.refs_13_, bf16[128,2304]{1,0:T(8,128)(2,1)} %get-tuple-element.65.refs_2_.refs_14_, ...), custom_call_target="tpu_custom_call" | custom-call | flops 1 | bytes 1 | tf_op jit(solution)/shard_map/partial_sums/pallas_call | solution.py:230
  100.7 1.9 %collective-permute-start.28 = (f32[576,128]{1,0:T(8,128)S(1)}, f32[576,128]{1,0:T(8,128)}, u32[]{:S(2)}, u32[]{:S(2)}) collective-permute-start(f32[576,128]{1,0:T(8,128)S(1)} %copy-done.1), channel_id=1, source_target_pairs={{0,12},{1,13},{2,14},{3,15},{4,0},{5,1},{6,2},{7,3},{8,4},{9,5},{1... | collective-permute-start | bytes 884744 | tf_op jit(solution)/shard_map/ppermute | solution.py:59
  102.9 3.2 %place.3 = (f32[576,128]{1,0:T(8,128)}, f32[576,128]{1,0:T(8,128)}, f32[576,128]{1,0:T(8,128)}, f32[576,128]{1,0:T(8,128)}, f32[576,128]{1,0:T(8,128)}) custom-call(f32[3,576,128]{2,1,0:T(8,128)} %get-tuple-element.50.refs_5_.refs_2_.refs_0_, f32[3,576,128]{2,1,0:T(8,128)} %collective-permute-done.11.refs_3_.refs_1_, ...), custom_call_target="tpu_custom_call" | custom-call | flops 1 | bytes 1 | tf_op jit(solution)/shard_map/place/pallas_call | solution.py:269
  107.3 2.6 %collective-permute-start.24 = (f32[576,128]{1,0:T(8,128)}, f32[576,128]{1,0:T(8,128)}, u32[]{:S(2)}, u32[]{:S(2)}) collective-permute-start(f32[576,128]{1,0:T(8,128)} %get-tuple-element.70.refs_17_), channel_id=1, source_target_pairs={{0,4},{1,5},{2,6},{3,7},{4,8},{5,9},{6,10},{7,11},{8,12},{9,13},{1... | collective-permute-start | bytes 884744 | tf_op jit(solution)/shard_map/ppermute | solution.py:59
  111.6 13.0 %weight_sums.1 = (f32[576,2304]{1,0:T(8,128)}, f32[8,128]{1,0:T(8,128)}) custom-call(bf16[8,576,128]{2,1,0:T(8,128)(2,1)} %stack.5.refs_3_.mine_ref, bf16[8,576,128]{2,1,0:T(8,128)(2,1)} %collective-permute-done.20.refs_3_.other_ref, bf16[128,2304]{1,0:T(8,128)(2,1)} %get-tuple-element.43.refs_0_, bf16[128,2304]{1,0:T(8,128)(2,1)} %get-tuple-element.52.refs_1_, ...), custom_call_target="tpu_custom_call" | custom-call | flops 1 | bytes 1 | tf_op jit(solution)/shard_map/weight_sums/pallas_call | solution.py:359
  124.7 5.8 %collective-permute-done.26.refs_3_ = f32[576,128]{1,0:T(8,128)} collective-permute-done((f32[576,128]{1,0:T(8,128)}, f32[576,128]{1,0:T(8,128)}, u32[]{:S(2)}, u32[]{:S(2)}) %collective-permute-start.26) | collective-permute-done | bytes 294944 | tf_op jit(solution)/shard_map/ppermute | solution.py:59
  130.5 2.5 %merge.1 = (f32[576,128]{1,0:T(8,128)}, f32[576,128]{1,0:T(8,128)}) custom-call(f32[576,128]{1,0:T(8,128)} %get-tuple-element.69.refs_16_.refs_0_, f32[576,128]{1,0:T(8,128)} %collective-permute-done.24.refs_1_, f32[576,128]{1,0:T(8,128)} %collective-permute-done.25.refs_2_, f32[576,128]{1,0:T(8,128)} %collective-permute-done.26.refs_3_, ...), custom_call_target="tpu_custom_call" | custom-call | flops 1 | bytes 1 | tf_op jit(solution)/shard_map/merge/pallas_call | solution.py:294
  133.9 9.4 %collective-permute-done.30 = f32[576,128]{1,0:T(8,128)S(1)} collective-permute-done((f32[576,128]{1,0:T(8,128)}, f32[576,128]{1,0:T(8,128)S(1)}, u32[]{:S(2)}, u32[]{:S(2)}) %collective-permute-start.30) | collective-permute-done | bytes 294944 | tf_op jit(solution)/shard_map/ppermute | solution.py:63
  143.3 1.7 %fusion = bf16[128,576]{0,1:T(8,128)(2,1)} fusion(f32[576,128]{1,0:T(8,128)} %get-tuple-element.75, f32[576,128]{1,0:T(8,128)S(1)} %collective-permute-done.30), kind=kLoop, calls=%fused_computation.1 | loop fusion | flops 147456 | bytes 737280 | tf_op jit(solution)/shard_map/transpose | solution.py:457
  (58 shorter events, 16.6 us)
Async XLA Ops:
  0.6 20.7 %collective-permute-start.2 = (bf16[128,2304]{1,0:T(8,128)(2,1)}, bf16[128,2304]{1,0:T(8,128)(2,1)}, u32[]{:S(2)}, u32[]{:S(2)}) collective-permute-start(bf16[128,2304]{1,0:T(8,128)(2,1)} %refs_5_.1), channel_id=1, source_target_pairs={{0,128},{16,144},{32,160},{48,176},{64,192},{80,208},{96,224},{112... | collective-permute-start | bytes 1769480 | tf_op jit(solution)/shard_map/ppermute | solution.py:45
  2.2 19.2 %collective-permute-start.1 = (bf16[128,2304]{1,0:T(8,128)(2,1)}, bf16[128,2304]{1,0:T(8,128)(2,1)}, u32[]{:S(2)}, u32[]{:S(2)}) collective-permute-start(bf16[128,2304]{1,0:T(8,128)(2,1)} %refs_5_.1), channel_id=1, source_target_pairs={{0,112},{16,0},{32,16},{48,32},{64,48},{80,64},{96,80},{112,96},{1... | collective-permute-start | bytes 1769480 | tf_op jit(solution)/shard_map/ppermute | solution.py:41
  8.1 16.0 %collective-permute-start = (bf16[128,2304]{1,0:T(8,128)(2,1)}, bf16[128,2304]{1,0:T(8,128)(2,1)}, u32[]{:S(2)}, u32[]{:S(2)}) collective-permute-start(bf16[128,2304]{1,0:T(8,128)(2,1)} %refs_5_.1), channel_id=1, source_target_pairs={{0,16},{16,32},{32,48},{48,64},{64,80},{80,96},{96,112},{112,0},{1... | collective-permute-start | bytes 1769480 | tf_op jit(solution)/shard_map/ppermute | solution.py:37
  9.6 11.7 %collective-permute-start.3 = (bf16[1,576,128]{2,1,0:T(8,128)(2,1)}, bf16[1,576,128]{2,1,0:T(8,128)(2,1)S(1)}, u32[]{:S(2)}, u32[]{:S(2)}) collective-permute-start(bf16[1,576,128]{2,1,0:T(8,128)(2,1)} %touch.1.a_ref), channel_id=1, source_target_pairs={{0,2},{1,3},{2,0},{3,1},{4,6},{5,7},{6,4},{7,5},{8,10},{9,11},{10,... | collective-permute-start | bytes 442376 | tf_op jit(solution)/shard_map/ppermute | solution.py:63
  24.1 15.8 %collective-permute-start.5 = (bf16[128,2304]{1,0:T(8,128)(2,1)}, bf16[128,2304]{1,0:T(8,128)(2,1)}, u32[]{:S(2)}, u32[]{:S(2)}) collective-permute-start(bf16[128,2304]{1,0:T(8,128)(2,1)} %get-tuple-element.41.refs_4_.refs_8_), channel_id=1, source_target_pairs={{0,112},{16,0},{32,16},{48,32},{64,48},{80,64},{96,80},{112,96},{1... | collective-permute-start | bytes 1769480 | tf_op jit(solution)/shard_map/ppermute | solution.py:41
  27.9 14.2 %collective-permute-start.6 = (bf16[128,2304]{1,0:T(8,128)(2,1)}, bf16[128,2304]{1,0:T(8,128)(2,1)}, u32[]{:S(2)}, u32[]{:S(2)}) collective-permute-start(bf16[128,2304]{1,0:T(8,128)(2,1)} %get-tuple-element.40.refs_0_.refs_2_), channel_id=1, source_target_pairs={{0,128},{16,144},{32,160},{48,176},{64,192},{80,208},{96,224},{112... | collective-permute-start | bytes 1769480 | tf_op jit(solution)/shard_map/ppermute | solution.py:45
  28.1 15.2 %collective-permute-start.4 = (bf16[128,2304]{1,0:T(8,128)(2,1)}, bf16[128,2304]{1,0:T(8,128)(2,1)}, u32[]{:S(2)}, u32[]{:S(2)}) collective-permute-start(bf16[128,2304]{1,0:T(8,128)(2,1)} %get-tuple-element.40.refs_0_.refs_2_), channel_id=1, source_target_pairs={{0,16},{16,32},{32,48},{48,64},{64,80},{80,96},{96,112},{112,0},{1... | collective-permute-start | bytes 1769480 | tf_op jit(solution)/shard_map/ppermute | solution.py:37
  29.8 18.5 %collective-permute-start.10 = (bf16[2,576,128]{2,1,0:T(8,128)(2,1)}, bf16[2,576,128]{2,1,0:T(8,128)(2,1)S(1)}, u32[]{:S(2)}, u32[]{:S(2)}) collective-permute-start(bf16[2,576,128]{2,1,0:T(8,128)(2,1)} %stack.3.refs_3_.a_ref), channel_id=1, source_target_pairs={{0,4},{1,5},{2,6},{3,7},{4,0},{5,1},{6,2},{7,3},{8,12},{9,13},{10,... | collective-permute-start | bytes 884744 | tf_op jit(solution)/shard_map/ppermute | solution.py:55
  43.3 15.2 %collective-permute-start.7 = (bf16[128,2304]{1,0:T(8,128)(2,1)}, bf16[128,2304]{1,0:T(8,128)(2,1)}, u32[]{:S(2)}, u32[]{:S(2)}) collective-permute-start(bf16[128,2304]{1,0:T(8,128)(2,1)} %get-tuple-element.42.refs_0_.refs_1_.refs_3_), channel_id=1, source_target_pairs={{0,16},{16,32},{32,48},{48,64},{64,80},{80,96},{96,112},{112,0},{1... | collective-permute-start | bytes 1769480 | tf_op jit(solution)/shard_map/ppermute | solution.py:37
  43.3 15.2 %collective-permute-start.9 = (bf16[128,2304]{1,0:T(8,128)(2,1)}, bf16[128,2304]{1,0:T(8,128)(2,1)}, u32[]{:S(2)}, u32[]{:S(2)}) collective-permute-start(bf16[128,2304]{1,0:T(8,128)(2,1)} %get-tuple-element.43.refs_0_), channel_id=1, source_target_pairs={{0,128},{16,144},{32,160},{48,176},{64,192},{80,208},{96,224},{112... | collective-permute-start | bytes 1769480 | tf_op jit(solution)/shard_map/ppermute | solution.py:45
  45.1 13.5 %collective-permute-start.8 = (bf16[128,2304]{1,0:T(8,128)(2,1)}, bf16[128,2304]{1,0:T(8,128)(2,1)}, u32[]{:S(2)}, u32[]{:S(2)}) collective-permute-start(bf16[128,2304]{1,0:T(8,128)(2,1)} %get-tuple-element.43.refs_0_), channel_id=1, source_target_pairs={{0,112},{16,0},{32,16},{48,32},{64,48},{80,64},{96,80},{112,96},{1... | collective-permute-start | bytes 1769480 | tf_op jit(solution)/shard_map/ppermute | solution.py:41
  51.0 17.9 %collective-permute-start.15 = (bf16[4,576,128]{2,1,0:T(8,128)(2,1)}, bf16[4,576,128]{2,1,0:T(8,128)(2,1)}, u32[]{:S(2)}, u32[]{:S(2)}) collective-permute-start(bf16[4,576,128]{2,1,0:T(8,128)(2,1)} %stack.4.refs_4_.a_ref), channel_id=1, source_target_pairs={{0,8},{1,9},{2,10},{3,11},{4,12},{5,13},{6,14},{7,15},{8,0},{9,1},... | collective-permute-start | bytes 1769480 | tf_op jit(solution)/shard_map/ppermute | solution.py:59
  58.4 12.9 %collective-permute-start.16 = (f32[2,576,128]{2,1,0:T(8,128)}, f32[2,576,128]{2,1,0:T(8,128)}, u32[]{:S(2)}, u32[]{:S(2)}) collective-permute-start(f32[2,576,128]{2,1,0:T(8,128)} %get-tuple-element.53), channel_id=1, source_target_pairs={{0,1},{1,0},{2,3},{3,2},{4,5},{5,4},{6,7},{7,6},{8,9},{9,8},{10,11... | collective-permute-start | bytes 1769480 | tf_op jit(solution)/shard_map/ppermute | solution.py:67
  58.6 16.1 %collective-permute-start.14 = (bf16[128,2304]{1,0:T(8,128)(2,1)}, bf16[128,2304]{1,0:T(8,128)(2,1)}, u32[]{:S(2)}, u32[]{:S(2)}) collective-permute-start(bf16[128,2304]{1,0:T(8,128)(2,1)} %get-tuple-element.52.refs_1_), channel_id=1, source_target_pairs={{0,128},{16,144},{32,160},{48,176},{64,192},{80,208},{96,224},{112... | collective-permute-start | bytes 1769480 | tf_op jit(solution)/shard_map/ppermute | solution.py:45
  59.4 15.4 %collective-permute-start.13 = (bf16[128,2304]{1,0:T(8,128)(2,1)}, bf16[128,2304]{1,0:T(8,128)(2,1)}, u32[]{:S(2)}, u32[]{:S(2)}) collective-permute-start(bf16[128,2304]{1,0:T(8,128)(2,1)} %get-tuple-element.46.refs_0_.refs_4_), channel_id=1, source_target_pairs={{0,112},{16,0},{32,16},{48,32},{64,48},{80,64},{96,80},{112,96},{1... | collective-permute-start | bytes 1769480 | tf_op jit(solution)/shard_map/ppermute | solution.py:41
  62.3 14.0 %collective-permute-start.12 = (bf16[128,2304]{1,0:T(8,128)(2,1)}, bf16[128,2304]{1,0:T(8,128)(2,1)}, u32[]{:S(2)}, u32[]{:S(2)}) collective-permute-start(bf16[128,2304]{1,0:T(8,128)(2,1)} %get-tuple-element.49.refs_5_.refs_0_.refs_9_), channel_id=1, source_target_pairs={{0,16},{16,32},{32,48},{48,64},{64,80},{80,96},{96,112},{112,0},{1... | collective-permute-start | bytes 1769480 | tf_op jit(solution)/shard_map/ppermute | solution.py:37
  68.8 16.5 %collective-permute-start.11 = (f32[3,576,128]{2,1,0:T(8,128)}, f32[3,576,128]{2,1,0:T(8,128)}, u32[]{:S(2)}, u32[]{:S(2)}) collective-permute-start(f32[3,576,128]{2,1,0:T(8,128)} %get-tuple-element.51), channel_id=1, source_target_pairs={{0,1},{1,0},{2,3},{3,2},{4,5},{5,4},{6,7},{7,6},{8,9},{9,8},{10,11... | collective-permute-start | bytes 2654216 | tf_op jit(solution)/shard_map/ppermute | solution.py:67
  71.4 21.6 %collective-permute-start.20 = (bf16[8,576,128]{2,1,0:T(8,128)(2,1)}, bf16[8,576,128]{2,1,0:T(8,128)(2,1)}, u32[]{:S(2)}, u32[]{:S(2)}) collective-permute-start(bf16[8,576,128]{2,1,0:T(8,128)(2,1)} %stack.5.refs_3_.mine_ref), channel_id=1, source_target_pairs={{0,1},{1,0},{2,3},{3,2},{4,5},{5,4},{6,7},{7,6},{8,9},{9,8},{10,11... | collective-permute-start | bytes 3538952 | tf_op jit(solution)/shard_map/ppermute | solution.py:67
  76.9 1.9 %collective-permute-start.21 = (f32[8,128]{1,0:T(8,128)}, f32[8,128]{1,0:T(8,128)S(1)}, u32[]{:S(2)}, u32[]{:S(2)}) collective-permute-start(f32[8,128]{1,0:T(8,128)} %get-tuple-element.57), channel_id=1, source_target_pairs={{0,1},{1,0},{2,3},{3,2},{4,5},{5,4},{6,7},{7,6},{8,9},{9,8},{10,11... | collective-permute-start | bytes 12296 | tf_op jit(solution)/shard_map/ppermute | solution.py:67
  76.9 16.1 %collective-permute-start.19 = (bf16[128,2304]{1,0:T(8,128)(2,1)}, bf16[128,2304]{1,0:T(8,128)(2,1)}, u32[]{:S(2)}, u32[]{:S(2)}) collective-permute-start(bf16[128,2304]{1,0:T(8,128)(2,1)} %get-tuple-element.41.refs_4_.refs_8_), channel_id=1, source_target_pairs={{0,128},{16,144},{32,160},{48,176},{64,192},{80,208},{96,224},{112... | collective-permute-start | bytes 1769480 | tf_op jit(solution)/shard_map/ppermute | solution.py:45
  78.3 17.0 %collective-permute-start.17 = (bf16[128,2304]{1,0:T(8,128)(2,1)}, bf16[128,2304]{1,0:T(8,128)(2,1)}, u32[]{:S(2)}, u32[]{:S(2)}) collective-permute-start(bf16[128,2304]{1,0:T(8,128)(2,1)} %get-tuple-element.55.refs_0_.refs_10_), channel_id=1, source_target_pairs={{0,16},{16,32},{32,48},{48,64},{64,80},{80,96},{96,112},{112,0},{1... | collective-permute-start | bytes 1769480 | tf_op jit(solution)/shard_map/ppermute | solution.py:37
  78.8 16.5 %collective-permute-start.18 = (bf16[128,2304]{1,0:T(8,128)(2,1)}, bf16[128,2304]{1,0:T(8,128)(2,1)}, u32[]{:S(2)}, u32[]{:S(2)}) collective-permute-start(bf16[128,2304]{1,0:T(8,128)(2,1)} %get-tuple-element.56.refs_1_.refs_11_), channel_id=1, source_target_pairs={{0,112},{16,0},{32,16},{48,32},{64,48},{80,64},{96,80},{112,96},{1... | collective-permute-start | bytes 1769480 | tf_op jit(solution)/shard_map/ppermute | solution.py:41
  85.3 1.9 %collective-permute-start.22 = (f32[1,576,128]{2,1,0:T(8,128)}, f32[1,576,128]{2,1,0:T(8,128)S(1)}, u32[]{:S(2)}, u32[]{:S(2)}) collective-permute-start(f32[1,576,128]{2,1,0:T(8,128)} %get-tuple-element.59), channel_id=1, source_target_pairs={{0,1},{1,0},{2,3},{3,2},{4,5},{5,4},{6,7},{7,6},{8,9},{9,8},{10,11... | collective-permute-start | bytes 884744 | tf_op jit(solution)/shard_map/ppermute | solution.py:67
  95.2 5.5 %copy-start.1 = (f32[576,128]{1,0:T(8,128)S(1)}, f32[576,128]{1,0:T(8,128)}, u32[]{:S(2)}) copy-start(f32[576,128]{1,0:T(8,128)} %get-tuple-element.63.refs_7_) | copy-start | bytes 884740
  100.5 2.4 %collective-permute-start.23 = (f32[2,576,128]{2,1,0:T(8,128)}, f32[2,576,128]{2,1,0:T(8,128)}, u32[]{:S(2)}, u32[]{:S(2)}) collective-permute-start(f32[2,576,128]{2,1,0:T(8,128)} %get-tuple-element.68), channel_id=1, source_target_pairs={{0,1},{1,0},{2,3},{3,2},{4,5},{5,4},{6,7},{7,6},{8,9},{9,8},{10,11... | collective-permute-start | bytes 1769480 | tf_op jit(solution)/shard_map/ppermute | solution.py:67
  100.6 10.2 %collective-permute-start.27 = (f32[576,128]{1,0:T(8,128)}, f32[576,128]{1,0:T(8,128)}, u32[]{:S(2)}, u32[]{:S(2)}) collective-permute-start(f32[576,128]{1,0:T(8,128)} %get-tuple-element.61.refs_5_), channel_id=1, source_target_pairs={{0,4},{1,5},{2,6},{3,7},{4,8},{5,9},{6,10},{7,11},{8,12},{9,13},{1... | collective-permute-start | bytes 884744 | tf_op jit(solution)/shard_map/ppermute | solution.py:59
  100.7 23.9 %collective-permute-start.28 = (f32[576,128]{1,0:T(8,128)S(1)}, f32[576,128]{1,0:T(8,128)}, u32[]{:S(2)}, u32[]{:S(2)}) collective-permute-start(f32[576,128]{1,0:T(8,128)S(1)} %copy-done.1), channel_id=1, source_target_pairs={{0,12},{1,13},{2,14},{3,15},{4,0},{5,1},{6,2},{7,3},{8,4},{9,5},{1... | collective-permute-start | bytes 884744 | tf_op jit(solution)/shard_map/ppermute | solution.py:59
  106.1 18.6 %collective-permute-start.29 = (f32[576,128]{1,0:T(8,128)}, f32[576,128]{1,0:T(8,128)}, u32[]{:S(2)}, u32[]{:S(2)}) collective-permute-start(f32[576,128]{1,0:T(8,128)} %get-tuple-element.73), channel_id=1, source_target_pairs={{0,8},{1,9},{2,10},{3,11},{4,12},{5,13},{6,14},{7,15},{8,0},{9,1},... | collective-permute-start | bytes 884744 | tf_op jit(solution)/shard_map/ppermute | solution.py:59
  107.3 17.4 %collective-permute-start.24 = (f32[576,128]{1,0:T(8,128)}, f32[576,128]{1,0:T(8,128)}, u32[]{:S(2)}, u32[]{:S(2)}) collective-permute-start(f32[576,128]{1,0:T(8,128)} %get-tuple-element.70.refs_17_), channel_id=1, source_target_pairs={{0,4},{1,5},{2,6},{3,7},{4,8},{5,9},{6,10},{7,11},{8,12},{9,13},{1... | collective-permute-start | bytes 884744 | tf_op jit(solution)/shard_map/ppermute | solution.py:59
  109.9 14.8 %collective-permute-start.25 = (f32[576,128]{1,0:T(8,128)}, f32[576,128]{1,0:T(8,128)}, u32[]{:S(2)}, u32[]{:S(2)}) collective-permute-start(f32[576,128]{1,0:T(8,128)} %get-tuple-element.71.refs_19_), channel_id=1, source_target_pairs={{0,12},{1,13},{2,14},{3,15},{4,0},{5,1},{6,2},{7,3},{8,4},{9,5},{1... | collective-permute-start | bytes 884744 | tf_op jit(solution)/shard_map/ppermute | solution.py:59
  110.8 19.7 %collective-permute-start.26 = (f32[576,128]{1,0:T(8,128)}, f32[576,128]{1,0:T(8,128)}, u32[]{:S(2)}, u32[]{:S(2)}) collective-permute-start(f32[576,128]{1,0:T(8,128)} %get-tuple-element.72.refs_18_), channel_id=1, source_target_pairs={{0,8},{1,9},{2,10},{3,11},{4,12},{5,13},{6,14},{7,15},{8,0},{9,1},... | collective-permute-start | bytes 884744 | tf_op jit(solution)/shard_map/ppermute | solution.py:59
  133.0 10.3 %collective-permute-start.30 = (f32[576,128]{1,0:T(8,128)}, f32[576,128]{1,0:T(8,128)S(1)}, u32[]{:S(2)}, u32[]{:S(2)}) collective-permute-start(f32[576,128]{1,0:T(8,128)} %get-tuple-element.76), channel_id=1, source_target_pairs={{0,2},{1,3},{2,0},{3,1},{4,6},{5,7},{6,4},{7,5},{8,10},{9,11},{10,... | collective-permute-start | bytes 884744 | tf_op jit(solution)/shard_map/ppermute | solution.py:63
  (4 other events, 6.9 us)

commit v9 on v8

--- a/solution.py
+++ b/solution.py
@@ -277,29 +277,43 @@
     )(*arrays, *extra)
 
 
+def total_kernel(*refs):
+    a, b, c, d = refs[:Y]
+    refs[-1][...] = (a[...] + b[...]) + (c[...] + d[...])
+
+
+def total(parts, after):
+    return pl.pallas_call(
+        total_kernel,
+        out_shape=jax.ShapeDtypeStruct(parts[0].shape, jnp.float32),
+        in_specs=[VECTOR] * Y + [ANYWHERE] * len(after),
+        out_specs=VECTOR,
+        compiler_params=params(),
+        cost_estimate=NO_COST,
+        name="total",
+    )(*parts, *after)
+
+
 def merge_kernel(*refs):
-    late, early, (keep_ref, send_ref) = refs[:Y], refs[Y : 2 * Y], refs[-2:]
-
-    def total(parts):
-        return (parts[0][...] + parts[1][...]) + (parts[2][...] + parts[3][...])
-
-    a, b = total(late), total(early)
+    late, early_ref, (keep_ref, send_ref) = refs[:Y], refs[Y], refs[-2:]
+    a = (late[0][...] + late[1][...]) + (late[2][...] + late[3][...])
+    b = early_ref[...]
     here = ends_late(position())
     keep_ref[...] = jnp.where(here, a, b)
     send_ref[...] = jnp.where(here, b, a)
 
 
-def merge(late, early, after):
+def merge(late, early):
     out = jax.ShapeDtypeStruct(late[0].shape, jnp.float32)
     return pl.pallas_call(
         merge_kernel,
         out_shape=(out, out),
-        in_specs=[VECTOR] * (2 * Y) + [ANYWHERE] * len(after),
+        in_specs=[VECTOR] * (Y + 1),
         out_specs=(VECTOR, VECTOR),
         compiler_params=params(),
         cost_estimate=NO_COST,
         name="merge",
-    )(*late, *early, *after)
+    )(*late, early)
 
 
 def weight_kernel(names, tile, scale, mine_ref, other_ref, *refs):
@@ -452,7 +466,7 @@
 
     early.append(in_y(two_on, 2))
     late = over_y(late) + [in_y(late[2], 2)]
-    keep, send = merge(late, early, [token])
+    keep, send = merge(late, total(early, [token]))
     grad_in = (keep + in_xh(send)).astype(jnp.bfloat16)
     return grad_in.T, grad_weight
 

time: 146 us -> 146 us (level)
  waiting for transfers between devices: 51.4 us -> 49.3 us
  Pallas kernels: 50.8 us -> 52.4 us
    ppermute x7, waiting for transfers between devices: 6.69 us -> 4.59 us  [in_y(): return lax.ppermute(t, 'gy', gy_pairs(dy, 0, 0))]
    pallas_call x1 -> x2, Pallas kernels: 2.52 us -> 4.21 us  [the longest x1 2.22 us: merge(): pl.pallas_call(merge_kernel, out_shape=(out, out), in_specs=[VECTOR] * (Y...]
  transfers between devices with their start and end apart: 31 -> 31, of which waited for: 15 -> 15; matrix products, arithmetic and copies ran while one was open for 0% -> 0% of each run, Pallas kernels for 30% -> 31%
where the time goes in v9:
time: 146 us; the launch traced here: 145 us
  Pallas kernels  52.4 us (36%)
  waiting for transfers between devices  49.3 us (34%)
  starting transfers between devices  38.9 us (27%)
  other arithmetic  1.67 us (1%)
    pallas_call x4, Pallas kernels, partial_sums(): pl.pallas_call(functools.partial(partial_kernel, places), out_shape=(out,...  20.6 us
    ppermute x5, starting transfers between devices, down(): return lax.ppermute(t, 'gx', gx_pairs(0, -1))  18.5 us
    ppermute x2, waiting for transfers between devices, in_xh(): return lax.ppermute(t, 'gy', gy_pairs(0, 1, 0))  18.3 us
    pallas_call x1, Pallas kernels, weight_sums(): pl.pallas_call(functools.partial(weight_kernel, names, tile, scale), out_...  13 us
    ppermute x5, waiting for transfers between devices, down(): return lax.ppermute(t, 'gx', gx_pairs(0, -1))  9.74 us
    ppermute x7, starting transfers between devices, in_y(): return lax.ppermute(t, 'gy', gy_pairs(dy, 0, 0))  9.12 us
    ppermute x5, waiting for transfers between devices, up(): return lax.ppermute(t, 'gx', gx_pairs(0, 1))  7.75 us
    ppermute x5, waiting for transfers between devices, across(): return lax.ppermute(t, 'gx', gx_pairs(1, 0))  6.85 us
  transfers between devices with their start and end apart: 31, of which 15 were waited for; matrix products, arithmetic and copies ran while one was open for 0% of the time, Pallas kernels for 31%

profile of v9, /device:TPU:8, one launch (start us, length us, event | category | flops | bytes accessed | tf_op | source)
XLA Modules:
  0.0 144.6 jit_solution(8742290538481099224)
XLA Ops:
  2.2 5.9 %collective-permute-start.1 = (bf16[128,2304]{1,0:T(8,128)(2,1)}, bf16[128,2304]{1,0:T(8,128)(2,1)}, u32[]{:S(2)}, u32[]{:S(2)}) collective-permute-start(bf16[128,2304]{1,0:T(8,128)(2,1)} %refs_5_.1), channel_id=1, source_target_pairs={{0,112},{16,0},{32,16},{48,32},{64,48},{80,64},{96,80},{112,96},{1... | collective-permute-start | bytes 1769480 | tf_op jit(solution)/shard_map/ppermute | solution.py:41
  9.6 2.7 %collective-permute-start.3 = (bf16[1,576,128]{2,1,0:T(8,128)(2,1)}, bf16[1,576,128]{2,1,0:T(8,128)(2,1)S(1)}, u32[]{:S(2)}, u32[]{:S(2)}) collective-permute-start(bf16[1,576,128]{2,1,0:T(8,128)(2,1)} %touch.1.a_ref), channel_id=1, source_target_pairs={{0,2},{1,3},{2,0},{3,1},{4,6},{5,7},{6,4},{7,5},{8,10},{9,11},{10,... | collective-permute-start | bytes 442376 | tf_op jit(solution)/shard_map/ppermute | solution.py:63
  12.4 9.0 %collective-permute-done.3.refs_3_.b_ref = bf16[1,576,128]{2,1,0:T(8,128)(2,1)S(1)} collective-permute-done((bf16[1,576,128]{2,1,0:T(8,128)(2,1)}, bf16[1,576,128]{2,1,0:T(8,128)(2,1)S(1)}, u32[]{:S(2)}, u32[]{:S(2)}) %collective-permute-start.3) | collective-permute-done | bytes 147488 | tf_op jit(solution)/shard_map/ppermute | solution.py:63
  21.4 2.7 %collective-permute-done.refs_0_ = bf16[128,2304]{1,0:T(8,128)(2,1)} collective-permute-done((bf16[128,2304]{1,0:T(8,128)(2,1)}, bf16[128,2304]{1,0:T(8,128)(2,1)}, u32[]{:S(2)}, u32[]{:S(2)}) %collective-permute-start) | collective-permute-done | bytes 589856 | tf_op jit(solution)/shard_map/ppermute | solution.py:37
  24.1 3.8 %collective-permute-start.5 = (bf16[128,2304]{1,0:T(8,128)(2,1)}, bf16[128,2304]{1,0:T(8,128)(2,1)}, u32[]{:S(2)}, u32[]{:S(2)}) collective-permute-start(bf16[128,2304]{1,0:T(8,128)(2,1)} %get-tuple-element.41.refs_4_.refs_8_), channel_id=1, source_target_pairs={{0,112},{16,0},{32,16},{48,32},{64,48},{80,64},{96,80},{112,96},{1... | collective-permute-start | bytes 1769480 | tf_op jit(solution)/shard_map/ppermute | solution.py:41
  28.1 1.7 %stack.3.refs_3_.a_ref = bf16[2,576,128]{2,1,0:T(8,128)(2,1)} custom-call(bf16[1,576,128]{2,1,0:T(8,128)(2,1)} %touch.1.a_ref, bf16[1,576,128]{2,1,0:T(8,128)(2,1)} %copy-done, bf16[128,2304]{1,0:T(8,128)(2,1)} %get-tuple-element.40.refs_0_.refs_2_), custom_call_target="tpu_custom_call" | custom-call | flops 1 | bytes 1 | tf_op jit(solution)/shard_map/stack/pallas_call | solution.py:158
  30.3 9.6 %collective-permute-done.5.refs_1_ = bf16[128,2304]{1,0:T(8,128)(2,1)} collective-permute-done((bf16[128,2304]{1,0:T(8,128)(2,1)}, bf16[128,2304]{1,0:T(8,128)(2,1)}, u32[]{:S(2)}, u32[]{:S(2)}) %collective-permute-start.5) | collective-permute-done | bytes 589856 | tf_op jit(solution)/shard_map/ppermute | solution.py:41
  39.9 2.2 %collective-permute-done.6.refs_2_ = bf16[128,2304]{1,0:T(8,128)(2,1)} collective-permute-done((bf16[128,2304]{1,0:T(8,128)(2,1)}, bf16[128,2304]{1,0:T(8,128)(2,1)}, u32[]{:S(2)}, u32[]{:S(2)}) %collective-permute-start.6) | collective-permute-done | bytes 589856 | tf_op jit(solution)/shard_map/ppermute | solution.py:45
  43.3 1.7 %collective-permute-start.9 = (bf16[128,2304]{1,0:T(8,128)(2,1)}, bf16[128,2304]{1,0:T(8,128)(2,1)}, u32[]{:S(2)}, u32[]{:S(2)}) collective-permute-start(bf16[128,2304]{1,0:T(8,128)(2,1)} %get-tuple-element.43.refs_0_), channel_id=1, source_target_pairs={{0,128},{16,144},{32,160},{48,176},{64,192},{80,208},{96,224},{112... | collective-permute-start | bytes 1769480 | tf_op jit(solution)/shard_map/ppermute | solution.py:45
  45.1 3.2 %collective-permute-start.8 = (bf16[128,2304]{1,0:T(8,128)(2,1)}, bf16[128,2304]{1,0:T(8,128)(2,1)}, u32[]{:S(2)}, u32[]{:S(2)}) collective-permute-start(bf16[128,2304]{1,0:T(8,128)(2,1)} %get-tuple-element.43.refs_0_), channel_id=1, source_target_pairs={{0,112},{16,0},{32,16},{48,32},{64,48},{80,64},{96,80},{112,96},{1... | collective-permute-start | bytes 1769480 | tf_op jit(solution)/shard_map/ppermute | solution.py:41
  49.0 1.9 %stack.4.refs_4_.a_ref = bf16[4,576,128]{2,1,0:T(8,128)(2,1)} custom-call(bf16[2,576,128]{2,1,0:T(8,128)(2,1)} %stack.3.refs_3_.a_ref, bf16[2,576,128]{2,1,0:T(8,128)(2,1)} %copy-done.3, bf16[128,2304]{1,0:T(8,128)(2,1)} %get-tuple-element.42.refs_0_.refs_1_.refs_3_), custom_call_target="tpu_custom_call" | custom-call | flops 1 | bytes 1 | tf_op jit(solution)/shard_map/stack/pallas_call | solution.py:158
  50.9 2.3 %collective-permute-start.15 = (bf16[4,576,128]{2,1,0:T(8,128)(2,1)}, bf16[4,576,128]{2,1,0:T(8,128)(2,1)}, u32[]{:S(2)}, u32[]{:S(2)}) collective-permute-start(bf16[4,576,128]{2,1,0:T(8,128)(2,1)} %stack.4.refs_4_.a_ref), channel_id=1, source_target_pairs={{0,8},{1,9},{2,10},{3,11},{4,12},{5,13},{6,14},{7,15},{8,0},{9,1},... | collective-permute-start | bytes 1769480 | tf_op jit(solution)/shard_map/ppermute | solution.py:59
  53.2 5.2 %partial_sums.4 = (f32[2,576,128]{2,1,0:T(8,128)}, f32[2,576,128]{2,1,0:T(8,128)}) custom-call(bf16[576,2304]{1,0:T(8,128)(2,1)} %w_any.7, bf16[128,2304]{1,0:T(8,128)(2,1)} %get-tuple-element.43.refs_0_, bf16[128,2304]{1,0:T(8,128)(2,1)} %get-tuple-element.42.refs_0_.refs_1_.refs_3_, bf16[128,2304]{1,0:T(8,128)(2,1)} %get-tuple-element.40.refs_0_.refs_2_, ...), custom_call_target="tpu_custom_call" | custom-call | flops 1 | bytes 1 | tf_op jit(solution)/shard_map/partial_sums/pallas_call | solution.py:230
  59.4 2.9 %collective-permute-start.13 = (bf16[128,2304]{1,0:T(8,128)(2,1)}, bf16[128,2304]{1,0:T(8,128)(2,1)}, u32[]{:S(2)}, u32[]{:S(2)}) collective-permute-start(bf16[128,2304]{1,0:T(8,128)(2,1)} %get-tuple-element.46.refs_0_.refs_4_), channel_id=1, source_target_pairs={{0,112},{16,0},{32,16},{48,32},{64,48},{80,64},{96,80},{112,96},{1... | collective-permute-start | bytes 1769480 | tf_op jit(solution)/shard_map/ppermute | solution.py:41
  62.3 6.5 %partial_sums.5 = (f32[3,576,128]{2,1,0:T(8,128)}, f32[3,576,128]{2,1,0:T(8,128)}) custom-call(bf16[576,2304]{1,0:T(8,128)(2,1)} %w_any.7, bf16[128,2304]{1,0:T(8,128)(2,1)} %get-tuple-element.46.refs_0_.refs_4_, bf16[128,2304]{1,0:T(8,128)(2,1)} %refs_5_.1, bf16[128,2304]{1,0:T(8,128)(2,1)} %get-tuple-element.47.refs_2_.refs_6_, ...), custom_call_target="tpu_custom_call" | custom-call | flops 1 | bytes 1 | tf_op jit(solution)/shard_map/partial_sums/pallas_call | solution.py:230
  68.9 2.4 %stack.5.refs_3_.mine_ref = bf16[8,576,128]{2,1,0:T(8,128)(2,1)} custom-call(bf16[4,576,128]{2,1,0:T(8,128)(2,1)} %stack.4.refs_4_.a_ref, bf16[4,576,128]{2,1,0:T(8,128)(2,1)} %collective-permute-done.15.b_ref, bf16[128,2304]{1,0:T(8,128)(2,1)} %get-tuple-element.49.refs_5_.refs_0_.refs_9_), custom_call_target="tpu_custom_call" | custom-call | flops 1 | bytes 1 | tf_op jit(solution)/shard_map/stack/pallas_call | solution.py:158
  71.8 2.8 %collective-permute-done.14.refs_2_ = bf16[128,2304]{1,0:T(8,128)(2,1)} collective-permute-done((bf16[128,2304]{1,0:T(8,128)(2,1)}, bf16[128,2304]{1,0:T(8,128)(2,1)}, u32[]{:S(2)}, u32[]{:S(2)}) %collective-permute-start.14) | collective-permute-done | bytes 589856 | tf_op jit(solution)/shard_map/ppermute | solution.py:45
  78.7 2.7 %collective-permute-start.18 = (bf16[128,2304]{1,0:T(8,128)(2,1)}, bf16[128,2304]{1,0:T(8,128)(2,1)}, u32[]{:S(2)}, u32[]{:S(2)}) collective-permute-start(bf16[128,2304]{1,0:T(8,128)(2,1)} %get-tuple-element.56.refs_1_.refs_11_), channel_id=1, source_target_pairs={{0,112},{16,0},{32,16},{48,32},{64,48},{80,64},{96,80},{112,96},{1... | collective-permute-start | bytes 1769480 | tf_op jit(solution)/shard_map/ppermute | solution.py:41
  81.4 3.8 %partial_sums.6 = (f32[1,576,128]{2,1,0:T(8,128)}, f32[1,576,128]{2,1,0:T(8,128)}) custom-call(bf16[576,2304]{1,0:T(8,128)(2,1)} %w_any.7, bf16[128,2304]{1,0:T(8,128)(2,1)} %get-tuple-element.55.refs_0_.refs_10_, bf16[128,2304]{1,0:T(8,128)(2,1)} %get-tuple-element.56.refs_1_.refs_11_, f32[8,128]{1,0:T(8,128)} %copy-done.4), custom_call_target="tpu_custom_call" | custom-call | flops 1 | bytes 1 | tf_op jit(solution)/shard_map/partial_sums/pallas_call | solution.py:230
  85.4 1.8 %collective-permute-done.22.refs_5_ = f32[1,576,128]{2,1,0:T(8,128)S(1)} collective-permute-done((f32[1,576,128]{2,1,0:T(8,128)}, f32[1,576,128]{2,1,0:T(8,128)S(1)}, u32[]{:S(2)}, u32[]{:S(2)}) %collective-permute-start.22) | collective-permute-done | bytes 294944 | tf_op jit(solution)/shard_map/ppermute | solution.py:67
  87.9 3.2 %place.2 = (f32[576,128]{1,0:T(8,128)}, f32[576,128]{1,0:T(8,128)}, f32[576,128]{1,0:T(8,128)}, f32[576,128]{1,0:T(8,128)}) custom-call(f32[2,576,128]{2,1,0:T(8,128)} %get-tuple-element.45.refs_5_.refs_0_, f32[2,576,128]{2,1,0:T(8,128)} %collective-permute-done.16.refs_4_.refs_1_, f32[3,576,128]{2,1,0:T(8,128)} %get-tuple-element.50.refs_5_.refs_2_.refs_0_, ...), custom_call_target="tpu_custom_call" | custom-call | flops 1 | bytes 1 | tf_op jit(solution)/shard_map/place/pallas_call | solution.py:269
  91.1 1.8 %collective-permute-done.19.refs_2_ = bf16[128,2304]{1,0:T(8,128)(2,1)} collective-permute-done((bf16[128,2304]{1,0:T(8,128)(2,1)}, bf16[128,2304]{1,0:T(8,128)(2,1)}, u32[]{:S(2)}, u32[]{:S(2)}) %collective-permute-start.19) | collective-permute-done | bytes 589856 | tf_op jit(solution)/shard_map/ppermute | solution.py:45
  92.9 2.3 %collective-permute-done.17.refs_0_ = bf16[128,2304]{1,0:T(8,128)(2,1)} collective-permute-done((bf16[128,2304]{1,0:T(8,128)(2,1)}, bf16[128,2304]{1,0:T(8,128)(2,1)}, u32[]{:S(2)}, u32[]{:S(2)}) %collective-permute-start.17) | collective-permute-done | bytes 589856 | tf_op jit(solution)/shard_map/ppermute | solution.py:37
  95.2 5.2 %partial_sums.7 = (f32[2,576,128]{2,1,0:T(8,128)}, f32[2,576,128]{2,1,0:T(8,128)}) custom-call(bf16[576,2304]{1,0:T(8,128)(2,1)} %w_any.7, bf16[128,2304]{1,0:T(8,128)(2,1)} %get-tuple-element.54.refs_0_.refs_12_, bf16[128,2304]{1,0:T(8,128)(2,1)} %get-tuple-element.64.refs_1_.refs_13_, bf16[128,2304]{1,0:T(8,128)(2,1)} %get-tuple-element.65.refs_2_.refs_14_, ...), custom_call_target="tpu_custom_call" | custom-call | flops 1 | bytes 1 | tf_op jit(solution)/shard_map/partial_sums/pallas_call | solution.py:230
  100.7 1.8 %collective-permute-start.28 = (f32[576,128]{1,0:T(8,128)S(1)}, f32[576,128]{1,0:T(8,128)}, u32[]{:S(2)}, u32[]{:S(2)}) collective-permute-start(f32[576,128]{1,0:T(8,128)S(1)} %copy-done.1), channel_id=1, source_target_pairs={{0,12},{1,13},{2,14},{3,15},{4,0},{5,1},{6,2},{7,3},{8,4},{9,5},{1... | collective-permute-start | bytes 884744 | tf_op jit(solution)/shard_map/ppermute | solution.py:59
  102.8 3.2 %place.3 = (f32[576,128]{1,0:T(8,128)}, f32[576,128]{1,0:T(8,128)}, f32[576,128]{1,0:T(8,128)}, f32[576,128]{1,0:T(8,128)}, f32[576,128]{1,0:T(8,128)}) custom-call(f32[3,576,128]{2,1,0:T(8,128)} %get-tuple-element.50.refs_5_.refs_2_.refs_0_, f32[3,576,128]{2,1,0:T(8,128)} %collective-permute-done.11.refs_3_.refs_1_, ...), custom_call_target="tpu_custom_call" | custom-call | flops 1 | bytes 1 | tf_op jit(solution)/shard_map/place/pallas_call | solution.py:269
  107.3 2.6 %collective-permute-start.24 = (f32[576,128]{1,0:T(8,128)}, f32[576,128]{1,0:T(8,128)}, u32[]{:S(2)}, u32[]{:S(2)}) collective-permute-start(f32[576,128]{1,0:T(8,128)} %get-tuple-element.70.refs_17_), channel_id=1, source_target_pairs={{0,4},{1,5},{2,6},{3,7},{4,8},{5,9},{6,10},{7,11},{8,12},{9,13},{1... | collective-permute-start | bytes 884744 | tf_op jit(solution)/shard_map/ppermute | solution.py:59
  111.6 13.0 %weight_sums.1 = (f32[576,2304]{1,0:T(8,128)}, f32[8,128]{1,0:T(8,128)}) custom-call(bf16[8,576,128]{2,1,0:T(8,128)(2,1)} %stack.5.refs_3_.mine_ref, bf16[8,576,128]{2,1,0:T(8,128)(2,1)} %collective-permute-done.20.refs_3_.other_ref, bf16[128,2304]{1,0:T(8,128)(2,1)} %get-tuple-element.43.refs_0_, bf16[128,2304]{1,0:T(8,128)(2,1)} %get-tuple-element.52.refs_1_, ...), custom_call_target="tpu_custom_call" | custom-call | flops 1 | bytes 1 | tf_op jit(solution)/shard_map/weight_sums/pallas_call | solution.py:373
  124.6 2.0 %total.1.refs_4_ = f32[576,128]{1,0:T(8,128)} custom-call(f32[576,128]{1,0:T(8,128)} %get-tuple-element.60.refs_4_.refs_0_, f32[576,128]{1,0:T(8,128)} %collective-permute-done.27.refs_1_, f32[576,128]{1,0:T(8,128)} %collective-permute-done.28.refs_2_, f32[576,128]{1,0:T(8,128)} %collective-permute-done.29.refs_3_, f32[8,128]{1,0:T(8,128)} %get-tuple-element.74.refs_4_), custom_call_target="tpu_custom_call" | custom-call | flops 1 | bytes 1 | tf_op jit(solution)/shard_map/total/pallas_call | solution.py:286
  126.6 3.7 %collective-permute-done.26.refs_3_ = f32[576,128]{1,0:T(8,128)} collective-permute-done((f32[576,128]{1,0:T(8,128)}, f32[576,128]{1,0:T(8,128)}, u32[]{:S(2)}, u32[]{:S(2)}) %collective-permute-start.26) | collective-permute-done | bytes 294944 | tf_op jit(solution)/shard_map/ppermute | solution.py:59
  130.4 2.2 %merge.1 = (f32[576,128]{1,0:T(8,128)}, f32[576,128]{1,0:T(8,128)}) custom-call(f32[576,128]{1,0:T(8,128)} %get-tuple-element.69.refs_16_.refs_0_, f32[576,128]{1,0:T(8,128)} %collective-permute-done.24.refs_1_, f32[576,128]{1,0:T(8,128)} %collective-permute-done.25.refs_2_, f32[576,128]{1,0:T(8,128)} %collective-permute-done.26.refs_3_, ...), custom_call_target="tpu_custom_call" | custom-call | flops 1 | bytes 1 | tf_op jit(solution)/shard_map/merge/pallas_call | solution.py:308
  133.5 9.4 %collective-permute-done.30 = f32[576,128]{1,0:T(8,128)S(1)} collective-permute-done((f32[576,128]{1,0:T(8,128)}, f32[576,128]{1,0:T(8,128)S(1)}, u32[]{:S(2)}, u32[]{:S(2)}) %collective-permute-start.30) | collective-permute-done | bytes 294944 | tf_op jit(solution)/shard_map/ppermute | solution.py:63
  (59 shorter events, 18.5 us)
Async XLA Ops:
  0.6 20.7 %collective-permute-start.2 = (bf16[128,2304]{1,0:T(8,128)(2,1)}, bf16[128,2304]{1,0:T(8,128)(2,1)}, u32[]{:S(2)}, u32[]{:S(2)}) collective-permute-start(bf16[128,2304]{1,0:T(8,128)(2,1)} %refs_5_.1), channel_id=1, source_target_pairs={{0,128},{16,144},{32,160},{48,176},{64,192},{80,208},{96,224},{112... | collective-permute-start | bytes 1769480 | tf_op jit(solution)/shard_map/ppermute | solution.py:45
  2.2 19.2 %collective-permute-start.1 = (bf16[128,2304]{1,0:T(8,128)(2,1)}, bf16[128,2304]{1,0:T(8,128)(2,1)}, u32[]{:S(2)}, u32[]{:S(2)}) collective-permute-start(bf16[128,2304]{1,0:T(8,128)(2,1)} %refs_5_.1), channel_id=1, source_target_pairs={{0,112},{16,0},{32,16},{48,32},{64,48},{80,64},{96,80},{112,96},{1... | collective-permute-start | bytes 1769480 | tf_op jit(solution)/shard_map/ppermute | solution.py:41
  8.1 16.0 %collective-permute-start = (bf16[128,2304]{1,0:T(8,128)(2,1)}, bf16[128,2304]{1,0:T(8,128)(2,1)}, u32[]{:S(2)}, u32[]{:S(2)}) collective-permute-start(bf16[128,2304]{1,0:T(8,128)(2,1)} %refs_5_.1), channel_id=1, source_target_pairs={{0,16},{16,32},{32,48},{48,64},{64,80},{80,96},{96,112},{112,0},{1... | collective-permute-start | bytes 1769480 | tf_op jit(solution)/shard_map/ppermute | solution.py:37
  9.6 11.7 %collective-permute-start.3 = (bf16[1,576,128]{2,1,0:T(8,128)(2,1)}, bf16[1,576,128]{2,1,0:T(8,128)(2,1)S(1)}, u32[]{:S(2)}, u32[]{:S(2)}) collective-permute-start(bf16[1,576,128]{2,1,0:T(8,128)(2,1)} %touch.1.a_ref), channel_id=1, source_target_pairs={{0,2},{1,3},{2,0},{3,1},{4,6},{5,7},{6,4},{7,5},{8,10},{9,11},{10,... | collective-permute-start | bytes 442376 | tf_op jit(solution)/shard_map/ppermute | solution.py:63
  24.1 15.8 %collective-permute-start.5 = (bf16[128,2304]{1,0:T(8,128)(2,1)}, bf16[128,2304]{1,0:T(8,128)(2,1)}, u32[]{:S(2)}, u32[]{:S(2)}) collective-permute-start(bf16[128,2304]{1,0:T(8,128)(2,1)} %get-tuple-element.41.refs_4_.refs_8_), channel_id=1, source_target_pairs={{0,112},{16,0},{32,16},{48,32},{64,48},{80,64},{96,80},{112,96},{1... | collective-permute-start | bytes 1769480 | tf_op jit(solution)/shard_map/ppermute | solution.py:41
  27.9 14.2 %collective-permute-start.6 = (bf16[128,2304]{1,0:T(8,128)(2,1)}, bf16[128,2304]{1,0:T(8,128)(2,1)}, u32[]{:S(2)}, u32[]{:S(2)}) collective-permute-start(bf16[128,2304]{1,0:T(8,128)(2,1)} %get-tuple-element.40.refs_0_.refs_2_), channel_id=1, source_target_pairs={{0,128},{16,144},{32,160},{48,176},{64,192},{80,208},{96,224},{112... | collective-permute-start | bytes 1769480 | tf_op jit(solution)/shard_map/ppermute | solution.py:45
  28.1 15.2 %collective-permute-start.4 = (bf16[128,2304]{1,0:T(8,128)(2,1)}, bf16[128,2304]{1,0:T(8,128)(2,1)}, u32[]{:S(2)}, u32[]{:S(2)}) collective-permute-start(bf16[128,2304]{1,0:T(8,128)(2,1)} %get-tuple-element.40.refs_0_.refs_2_), channel_id=1, source_target_pairs={{0,16},{16,32},{32,48},{48,64},{64,80},{80,96},{96,112},{112,0},{1... | collective-permute-start | bytes 1769480 | tf_op jit(solution)/shard_map/ppermute | solution.py:37
  29.8 18.5 %collective-permute-start.10 = (bf16[2,576,128]{2,1,0:T(8,128)(2,1)}, bf16[2,576,128]{2,1,0:T(8,128)(2,1)S(1)}, u32[]{:S(2)}, u32[]{:S(2)}) collective-permute-start(bf16[2,576,128]{2,1,0:T(8,128)(2,1)} %stack.3.refs_3_.a_ref), channel_id=1, source_target_pairs={{0,4},{1,5},{2,6},{3,7},{4,0},{5,1},{6,2},{7,3},{8,12},{9,13},{10,... | collective-permute-start | bytes 884744 | tf_op jit(solution)/shard_map/ppermute | solution.py:55
  43.3 15.2 %collective-permute-start.7 = (bf16[128,2304]{1,0:T(8,128)(2,1)}, bf16[128,2304]{1,0:T(8,128)(2,1)}, u32[]{:S(2)}, u32[]{:S(2)}) collective-permute-start(bf16[128,2304]{1,0:T(8,128)(2,1)} %get-tuple-element.42.refs_0_.refs_1_.refs_3_), channel_id=1, source_target_pairs={{0,16},{16,32},{32,48},{48,64},{64,80},{80,96},{96,112},{112,0},{1... | collective-permute-start | bytes 1769480 | tf_op jit(solution)/shard_map/ppermute | solution.py:37
  43.3 15.2 %collective-permute-start.9 = (bf16[128,2304]{1,0:T(8,128)(2,1)}, bf16[128,2304]{1,0:T(8,128)(2,1)}, u32[]{:S(2)}, u32[]{:S(2)}) collective-permute-start(bf16[128,2304]{1,0:T(8,128)(2,1)} %get-tuple-element.43.refs_0_), channel_id=1, source_target_pairs={{0,128},{16,144},{32,160},{48,176},{64,192},{80,208},{96,224},{112... | collective-permute-start | bytes 1769480 | tf_op jit(solution)/shard_map/ppermute | solution.py:45
  45.1 13.4 %collective-permute-start.8 = (bf16[128,2304]{1,0:T(8,128)(2,1)}, bf16[128,2304]{1,0:T(8,128)(2,1)}, u32[]{:S(2)}, u32[]{:S(2)}) collective-permute-start(bf16[128,2304]{1,0:T(8,128)(2,1)} %get-tuple-element.43.refs_0_), channel_id=1, source_target_pairs={{0,112},{16,0},{32,16},{48,32},{64,48},{80,64},{96,80},{112,96},{1... | collective-permute-start | bytes 1769480 | tf_op jit(solution)/shard_map/ppermute | solution.py:41
  50.9 17.9 %collective-permute-start.15 = (bf16[4,576,128]{2,1,0:T(8,128)(2,1)}, bf16[4,576,128]{2,1,0:T(8,128)(2,1)}, u32[]{:S(2)}, u32[]{:S(2)}) collective-permute-start(bf16[4,576,128]{2,1,0:T(8,128)(2,1)} %stack.4.refs_4_.a_ref), channel_id=1, source_target_pairs={{0,8},{1,9},{2,10},{3,11},{4,12},{5,13},{6,14},{7,15},{8,0},{9,1},... | collective-permute-start | bytes 1769480 | tf_op jit(solution)/shard_map/ppermute | solution.py:59
  58.4 12.9 %collective-permute-start.16 = (f32[2,576,128]{2,1,0:T(8,128)}, f32[2,576,128]{2,1,0:T(8,128)}, u32[]{:S(2)}, u32[]{:S(2)}) collective-permute-start(f32[2,576,128]{2,1,0:T(8,128)} %get-tuple-element.53), channel_id=1, source_target_pairs={{0,1},{1,0},{2,3},{3,2},{4,5},{5,4},{6,7},{7,6},{8,9},{9,8},{10,11... | collective-permute-start | bytes 1769480 | tf_op jit(solution)/shard_map/ppermute | solution.py:67
  58.5 16.1 %collective-permute-start.14 = (bf16[128,2304]{1,0:T(8,128)(2,1)}, bf16[128,2304]{1,0:T(8,128)(2,1)}, u32[]{:S(2)}, u32[]{:S(2)}) collective-permute-start(bf16[128,2304]{1,0:T(8,128)(2,1)} %get-tuple-element.52.refs_1_), channel_id=1, source_target_pairs={{0,128},{16,144},{32,160},{48,176},{64,192},{80,208},{96,224},{112... | collective-permute-start | bytes 1769480 | tf_op jit(solution)/shard_map/ppermute | solution.py:45
  59.4 15.3 %collective-permute-start.13 = (bf16[128,2304]{1,0:T(8,128)(2,1)}, bf16[128,2304]{1,0:T(8,128)(2,1)}, u32[]{:S(2)}, u32[]{:S(2)}) collective-permute-start(bf16[128,2304]{1,0:T(8,128)(2,1)} %get-tuple-element.46.refs_0_.refs_4_), channel_id=1, source_target_pairs={{0,112},{16,0},{32,16},{48,32},{64,48},{80,64},{96,80},{112,96},{1... | collective-permute-start | bytes 1769480 | tf_op jit(solution)/shard_map/ppermute | solution.py:41
  62.3 13.9 %collective-permute-start.12 = (bf16[128,2304]{1,0:T(8,128)(2,1)}, bf16[128,2304]{1,0:T(8,128)(2,1)}, u32[]{:S(2)}, u32[]{:S(2)}) collective-permute-start(bf16[128,2304]{1,0:T(8,128)(2,1)} %get-tuple-element.49.refs_5_.refs_0_.refs_9_), channel_id=1, source_target_pairs={{0,16},{16,32},{32,48},{48,64},{64,80},{80,96},{96,112},{112,0},{1... | collective-permute-start | bytes 1769480 | tf_op jit(solution)/shard_map/ppermute | solution.py:37
  68.8 16.4 %collective-permute-start.11 = (f32[3,576,128]{2,1,0:T(8,128)}, f32[3,576,128]{2,1,0:T(8,128)}, u32[]{:S(2)}, u32[]{:S(2)}) collective-permute-start(f32[3,576,128]{2,1,0:T(8,128)} %get-tuple-element.51), channel_id=1, source_target_pairs={{0,1},{1,0},{2,3},{3,2},{4,5},{5,4},{6,7},{7,6},{8,9},{9,8},{10,11... | collective-permute-start | bytes 2654216 | tf_op jit(solution)/shard_map/ppermute | solution.py:67
  71.3 21.6 %collective-permute-start.20 = (bf16[8,576,128]{2,1,0:T(8,128)(2,1)}, bf16[8,576,128]{2,1,0:T(8,128)(2,1)}, u32[]{:S(2)}, u32[]{:S(2)}) collective-permute-start(bf16[8,576,128]{2,1,0:T(8,128)(2,1)} %stack.5.refs_3_.mine_ref), channel_id=1, source_target_pairs={{0,1},{1,0},{2,3},{3,2},{4,5},{5,4},{6,7},{7,6},{8,9},{9,8},{10,11... | collective-permute-start | bytes 3538952 | tf_op jit(solution)/shard_map/ppermute | solution.py:67
  76.8 1.9 %collective-permute-start.21 = (f32[8,128]{1,0:T(8,128)}, f32[8,128]{1,0:T(8,128)S(1)}, u32[]{:S(2)}, u32[]{:S(2)}) collective-permute-start(f32[8,128]{1,0:T(8,128)} %get-tuple-element.57), channel_id=1, source_target_pairs={{0,1},{1,0},{2,3},{3,2},{4,5},{5,4},{6,7},{7,6},{8,9},{9,8},{10,11... | collective-permute-start | bytes 12296 | tf_op jit(solution)/shard_map/ppermute | solution.py:67
  76.8 16.1 %collective-permute-start.19 = (bf16[128,2304]{1,0:T(8,128)(2,1)}, bf16[128,2304]{1,0:T(8,128)(2,1)}, u32[]{:S(2)}, u32[]{:S(2)}) collective-permute-start(bf16[128,2304]{1,0:T(8,128)(2,1)} %get-tuple-element.41.refs_4_.refs_8_), channel_id=1, source_target_pairs={{0,128},{16,144},{32,160},{48,176},{64,192},{80,208},{96,224},{112... | collective-permute-start | bytes 1769480 | tf_op jit(solution)/shard_map/ppermute | solution.py:45
  78.2 17.0 %collective-permute-start.17 = (bf16[128,2304]{1,0:T(8,128)(2,1)}, bf16[128,2304]{1,0:T(8,128)(2,1)}, u32[]{:S(2)}, u32[]{:S(2)}) collective-permute-start(bf16[128,2304]{1,0:T(8,128)(2,1)} %get-tuple-element.55.refs_0_.refs_10_), channel_id=1, source_target_pairs={{0,16},{16,32},{32,48},{48,64},{64,80},{80,96},{96,112},{112,0},{1... | collective-permute-start | bytes 1769480 | tf_op jit(solution)/shard_map/ppermute | solution.py:37
  78.7 16.5 %collective-permute-start.18 = (bf16[128,2304]{1,0:T(8,128)(2,1)}, bf16[128,2304]{1,0:T(8,128)(2,1)}, u32[]{:S(2)}, u32[]{:S(2)}) collective-permute-start(bf16[128,2304]{1,0:T(8,128)(2,1)} %get-tuple-element.56.refs_1_.refs_11_), channel_id=1, source_target_pairs={{0,112},{16,0},{32,16},{48,32},{64,48},{80,64},{96,80},{112,96},{1... | collective-permute-start | bytes 1769480 | tf_op jit(solution)/shard_map/ppermute | solution.py:41
  85.3 1.9 %collective-permute-start.22 = (f32[1,576,128]{2,1,0:T(8,128)}, f32[1,576,128]{2,1,0:T(8,128)S(1)}, u32[]{:S(2)}, u32[]{:S(2)}) collective-permute-start(f32[1,576,128]{2,1,0:T(8,128)} %get-tuple-element.59), channel_id=1, source_target_pairs={{0,1},{1,0},{2,3},{3,2},{4,5},{5,4},{6,7},{7,6},{8,9},{9,8},{10,11... | collective-permute-start | bytes 884744 | tf_op jit(solution)/shard_map/ppermute | solution.py:67
  95.2 5.6 %copy-start.1 = (f32[576,128]{1,0:T(8,128)S(1)}, f32[576,128]{1,0:T(8,128)}, u32[]{:S(2)}) copy-start(f32[576,128]{1,0:T(8,128)} %get-tuple-element.63.refs_7_) | copy-start | bytes 884740
  100.4 2.4 %collective-permute-start.23 = (f32[2,576,128]{2,1,0:T(8,128)}, f32[2,576,128]{2,1,0:T(8,128)}, u32[]{:S(2)}, u32[]{:S(2)}) collective-permute-start(f32[2,576,128]{2,1,0:T(8,128)} %get-tuple-element.68), channel_id=1, source_target_pairs={{0,1},{1,0},{2,3},{3,2},{4,5},{5,4},{6,7},{7,6},{8,9},{9,8},{10,11... | collective-permute-start | bytes 1769480 | tf_op jit(solution)/shard_map/ppermute | solution.py:67
  100.5 10.2 %collective-permute-start.27 = (f32[576,128]{1,0:T(8,128)}, f32[576,128]{1,0:T(8,128)}, u32[]{:S(2)}, u32[]{:S(2)}) collective-permute-start(f32[576,128]{1,0:T(8,128)} %get-tuple-element.61.refs_5_), channel_id=1, source_target_pairs={{0,4},{1,5},{2,6},{3,7},{4,8},{5,9},{6,10},{7,11},{8,12},{9,13},{1... | collective-permute-start | bytes 884744 | tf_op jit(solution)/shard_map/ppermute | solution.py:59
  100.7 23.9 %collective-permute-start.28 = (f32[576,128]{1,0:T(8,128)S(1)}, f32[576,128]{1,0:T(8,128)}, u32[]{:S(2)}, u32[]{:S(2)}) collective-permute-start(f32[576,128]{1,0:T(8,128)S(1)} %copy-done.1), channel_id=1, source_target_pairs={{0,12},{1,13},{2,14},{3,15},{4,0},{5,1},{6,2},{7,3},{8,4},{9,5},{1... | collective-permute-start | bytes 884744 | tf_op jit(solution)/shard_map/ppermute | solution.py:59
  106.0 18.6 %collective-permute-start.29 = (f32[576,128]{1,0:T(8,128)}, f32[576,128]{1,0:T(8,128)}, u32[]{:S(2)}, u32[]{:S(2)}) collective-permute-start(f32[576,128]{1,0:T(8,128)} %get-tuple-element.73), channel_id=1, source_target_pairs={{0,8},{1,9},{2,10},{3,11},{4,12},{5,13},{6,14},{7,15},{8,0},{9,1},... | collective-permute-start | bytes 884744 | tf_op jit(solution)/shard_map/ppermute | solution.py:59
  107.3 19.4 %collective-permute-start.24 = (f32[576,128]{1,0:T(8,128)}, f32[576,128]{1,0:T(8,128)}, u32[]{:S(2)}, u32[]{:S(2)}) collective-permute-start(f32[576,128]{1,0:T(8,128)} %get-tuple-element.70.refs_17_), channel_id=1, source_target_pairs={{0,4},{1,5},{2,6},{3,7},{4,8},{5,9},{6,10},{7,11},{8,12},{9,13},{1... | collective-permute-start | bytes 884744 | tf_op jit(solution)/shard_map/ppermute | solution.py:59
  109.8 16.8 %collective-permute-start.25 = (f32[576,128]{1,0:T(8,128)}, f32[576,128]{1,0:T(8,128)}, u32[]{:S(2)}, u32[]{:S(2)}) collective-permute-start(f32[576,128]{1,0:T(8,128)} %get-tuple-element.71.refs_19_), channel_id=1, source_target_pairs={{0,12},{1,13},{2,14},{3,15},{4,0},{5,1},{6,2},{7,3},{8,4},{9,5},{1... | collective-permute-start | bytes 884744 | tf_op jit(solution)/shard_map/ppermute | solution.py:59
  110.7 19.7 %collective-permute-start.26 = (f32[576,128]{1,0:T(8,128)}, f32[576,128]{1,0:T(8,128)}, u32[]{:S(2)}, u32[]{:S(2)}) collective-permute-start(f32[576,128]{1,0:T(8,128)} %get-tuple-element.72.refs_18_), channel_id=1, source_target_pairs={{0,8},{1,9},{2,10},{3,11},{4,12},{5,13},{6,14},{7,15},{8,0},{9,1},... | collective-permute-start | bytes 884744 | tf_op jit(solution)/shard_map/ppermute | solution.py:59
  132.6 10.3 %collective-permute-start.30 = (f32[576,128]{1,0:T(8,128)}, f32[576,128]{1,0:T(8,128)S(1)}, u32[]{:S(2)}, u32[]{:S(2)}) collective-permute-start(f32[576,128]{1,0:T(8,128)} %get-tuple-element.76), channel_id=1, source_target_pairs={{0,2},{1,3},{2,0},{3,1},{4,6},{5,7},{6,4},{7,5},{8,10},{9,11},{10,... | collective-permute-start | bytes 884744 | tf_op jit(solution)/shard_map/ppermute | solution.py:63
  (4 other events, 6.9 us)
